TPU v7x, 32 devices: a whole 2x2x4 slice. The times are simulated.
32 devices in a mesh: groups: 2 (over x), dp: 8 (over z, y), tensor: 2 (over core).
Axes of the slice: x: 2, y: 2, z: 4, core: 2. Of those that a mesh axis runs over, the one named last changes fastest.
Arguments:
- activations: bfloat16 [4096, 28672], P(('groups', 'dp'), 'tensor'), parts along dimension 0, may hold values from -6 to 6
- out_grads: bfloat16 [4096, 8192], P(('groups', 'dp'), 'tensor'), parts along dimension 0, may hold values from -6 to 6
- proj_in: bfloat16 [28672, 64], P('tensor'), may hold values from -0.03125 to 0.03125
- proj_out: bfloat16 [8192, 64], P('tensor'), may hold values from -0.0625 to 0.0625
- stored: bfloat16 [16384, 4096], P(('groups', 'dp')), parts along dimension 0, may hold values from -0.375 to 0.375
- counts: int32 [256], P(('groups', 'dp')), parts along dimension 0, may hold values from 1 to 16
- query_ids: int32 [512], P('groups'), parts along dimension 0, may hold values from 0 to 127
Outputs:
- gram: float32 [8192, 4096], P(('groups', 'dp'), 'tensor'), parts along dimension 0
- scores: float32 [512, 128], P('groups', 'dp'), parts along dimension 0
There are 2 independent parts, one for each index of `groups`. A program takes and returns all parts, laid end to end along the dimension named above; an argument that names none is the same for every part. Nothing has to cross between parts.
All inputs are finite; a program needn't handle non-finite values.
Results may differ from a plain program's by a relative error of at most 0.015.
Values may be sent and summed in bfloat16 or wider, within the bound.
No kernel may reach another device: no remote copies, remote signals or barrier semaphores. Data moves between devices by JAX's collectives and lax.ppermute only.
A program may use at most 192 MiB of HBM per device.

v0:
```python
import jax
import jax.numpy as jnp
from jax import lax
from jax.sharding import PartitionSpec as P

R = 64
SEQ = 16


damping = 1.0


def spread(value, axis, source):
    kept = jnp.where(lax.axis_index(axis) == source, value, 0).astype(value.dtype)
    return lax.psum(kept, axis)


def example_vectors(act_proj, grad_proj, counts, seq_len):
    examples = counts.shape[0]
    rank = act_proj.shape[1]
    position = jnp.arange(seq_len, dtype=jnp.int32)[None, :]
    count_f = counts.astype(jnp.float32)[:, None]
    weights = jnp.where(position < counts[:, None], 1.0 / count_f, jnp.float32(0.0))
    outer = jnp.einsum(
        "es,esi,esj->eij",
        weights,
        act_proj.reshape(examples, seq_len, rank),
        grad_proj.reshape(examples, seq_len, rank),
    )
    return outer.reshape(examples, rank * rank).astype(jnp.bfloat16)


def lead_dot(left, right, precision=None):
    return lax.dot_general(
        left,
        right,
        (((0,), (0,)), ((), ())),
        precision=precision,
        preferred_element_type=jnp.float32,
    )


def diagonal_mask(row_anchor, col_anchor, row_total, col_total):
    row_ids = row_anchor + jnp.arange(row_total, dtype=jnp.int32)[:, None]
    col_ids = col_anchor + jnp.arange(col_total, dtype=jnp.int32)[None, :]
    return (row_ids == col_ids).astype(jnp.float32)


def local(activations, out_grads, proj_in, proj_out, stored, counts, query_ids):
    highest = lax.Precision.HIGHEST
    act_part = jnp.dot(activations, proj_in, preferred_element_type=jnp.float32)
    grad_part = jnp.dot(out_grads, proj_out, preferred_element_type=jnp.float32)
    act_proj, grad_proj = lax.psum((act_part, grad_part), "tensor")
    vectors = example_vectors(act_proj, grad_proj, counts, SEQ)
    full_width = vectors.shape[1]
    tensor_count = lax.axis_size("tensor")
    block_count = lax.axis_size("dp")
    half_cols = full_width // tensor_count
    tensor_index = lax.axis_index("tensor")
    dp_index = lax.axis_index("dp")
    col_anchor = tensor_index * half_cols
    width = full_width // block_count
    stored_cols = lax.dynamic_slice_in_dim(stored, col_anchor, half_cols, 1)
    vector_cols = lax.dynamic_slice_in_dim(vectors, col_anchor, half_cols, 1)

    def gram_rows(row_count):
        stored_rows = lax.slice_in_dim(stored, 0, row_count, axis=1)
        vector_rows = lax.slice_in_dim(vectors, 0, row_count, axis=1)
        return lead_dot(stored_rows, stored_cols) + lead_dot(vector_rows, vector_cols)

    owned = lax.psum_scatter(
        gram_rows(width * lax.axis_size("dp")), "dp", scatter_dimension=0, tiled=True
    )
    owned = owned + damping * diagonal_mask(dp_index * width, col_anchor, width, half_cols)
    panel_block = lax.psum(gram_rows(width), "dp")
    panel_block = panel_block + damping * diagonal_mask(0, col_anchor, width, half_cols)
    corner_block = spread(panel_block[:, :width], "tensor", 0)
    corner = jnp.linalg.cholesky(corner_block)
    whiten = lax.linalg.triangular_solve(corner, panel_block, left_side=True, lower=True)
    train_cols = vectors.astype(jnp.float32).T
    u_train = lax.linalg.triangular_solve(corner, train_cols[:width, :], left_side=True, lower=True)
    r_train = vector_cols.astype(jnp.float32).T - lead_dot(whiten, u_train, highest)
    gathered = lax.all_gather(vectors, "dp", axis=0, tiled=True)
    queries = jnp.take(gathered, query_ids, axis=0).astype(jnp.float32)
    query_cols = queries.T
    u_query = lax.linalg.triangular_solve(corner, query_cols[:width, :], left_side=True, lower=True)
    query_half = lax.dynamic_slice_in_dim(query_cols, col_anchor, half_cols, 0)
    r_query = query_half - lead_dot(whiten, u_query, highest)
    partial_scores = lead_dot(r_query, r_train, highest) + 0.5 * lead_dot(u_query, u_train, highest)
    scores = lax.psum(partial_scores, "tensor")
    return (owned, scores / R)


def solution(mesh):
    placed = (
        P(("groups", "dp"), "tensor"),
        P(("groups", "dp"), "tensor"),
        P("tensor", None),
        P("tensor", None),
        P(("groups", "dp"), None),
        P(("groups", "dp")),
        P("groups"),
    )
    return jax.shard_map(
        local,
        mesh=mesh,
        in_specs=placed,
        out_specs=(P(("groups", "dp"), "tensor"), P("groups", "dp")),
        check_vma=False,
    )
```

profile of v0, /device:TPU:0, one launch (start us, length us, event | category | flops | bytes accessed | tf_op | source)
XLA Modules:
  0.0 989.9 jit_solution(1292435943558623020)
XLA Ops:
  7.2 6.4 fusion.91
  13.9 0.7 fusion.92
  14.6 4.1 psum.36
  18.7 15.8 %all-reduce.5.cloned.1.call-done = f32[16,16,64]{2,1,0:T(8,128)} async-done(((f32[16,16,64]{2,1,0:T(8,128)}), f32[16,16,64]{2,1,0:T(8,128)}) %all-reduce.5.cloned.1.call-update) | async-done | bytes 65552 | tf_op jit(solution)/shard_map/psum | solution.py:53
  34.5 1.4 convolution_convert_fusion
  35.8 0.9 convert_element_type.27
  36.9 5.0 fusion
  41.9 2.8 bitcast_add_fusion.1
  44.9 13.2 %fusion.64 = f32[4096,2048]{0,1:T(8,128)} fusion(bf16[16,4096]{1,0:T(8,128)(2,1)S(1)} %copy-done.4, s32[]{:T(128)S(6)} %select_n.35), kind=kOutput, calls=%fused_computation.107 | convolution fusion | flops 268435456 | bytes 33751044 | tf_op jit(solution)/shard_map/dot_general | solution.py:34
  58.1 32.8 %bitcast_add_fusion = f32[4096,2048]{0,1:T(8,128)} fusion(f32[4096,2048]{0,1:T(8,128)} %fusion.64, bf16[1024,4096]{1,0:T(8,128)(2,1)} %param.11, s32[]{:T(128)S(6)} %select_n.35), kind=kOutput, calls=%fused_computation.3 | convolution fusion | flops 17188257792 | bytes 79691776 | tf_op jit(solution)/shard_map/dot_general | solution.py:34
  91.7 5.2 gather_fusion
  96.9 140.7 %all-reduce.7.cloned.1.call-done = f32[512,2048]{0,1:T(8,128)} async-done(((f32[512,2048]{0,1:T(8,128)}), f32[512,2048]{0,1:T(8,128)}) %all-reduce.7.cloned.1.call-update) | async-done | bytes 4194320 | tf_op jit(solution)/shard_map/psum | solution.py:75
  237.7 545.7 %reduce-scatter.2.cloned.1.call-done = f32[512,2048]{0,1:T(8,128)} async-done(((f32[4096,2048]{0,1:T(8,128)}), f32[512,2048]{0,1:T(8,128)}) %reduce-scatter.2.cloned.1.call-update) | async-done | bytes 4194320 | tf_op jit(solution)/shard_map/reduce_scatter | solution.py:71
  783.4 5.2 convert_add_fusion
  788.6 1.9 copy-done.2
  790.6 1.1 slice_select_fusion
  791.7 3.1 bitcast_convert_fusion.1
  794.7 5.5 copy.36
  800.3 10.3 %all-reduce.9.cloned.1.call-done = f32[512,512]{0,1:T(8,128)} async-done(((f32[512,512]{0,1:T(8,128)}), f32[512,512]{0,1:T(8,128)}) %all-reduce.9.cloned.1.call-update) | async-done | bytes 1048592 | tf_op jit(solution)/shard_map/psum | solution.py:15
  810.6 1.6 copy.27
  812.1 1.4 fusion.19
  813.6 11.7 %cholesky.103 = f32[128,128]{1,0:T(8,128)S(1)} custom-call(f32[128,128]{1,0:T(8,128)S(1)} %cholesky.263), custom_call_target="Cholesky" | custom-call | tf_op jit(solution)/shard_map/jit(cholesky)/cholesky | solution.py:78
  825.4 9.8 custom-call.34
  835.8 11.7 %cholesky.215 = f32[128,128]{1,0:T(8,128)S(1)} custom-call(f32[128,128]{1,0:T(8,128)S(1)} %cholesky.267), custom_call_target="Cholesky" | custom-call | tf_op jit(solution)/shard_map/jit(cholesky)/cholesky | solution.py:78
  847.9 10.3 %custom-call.35 = f32[1,128,128]{1,2,0:T(8,128)S(1)} custom-call(f32[1,128,128]{2,1,0:T(8,128)S(1)} %get-tuple-element.37), custom_call_target="InvertDiagBlocksLowerTriangular" | custom-call | tf_op jit(solution)/shard_map/jit(cholesky)/cholesky | solution.py:78
  859.3 11.7 %cholesky.236 = f32[128,128]{1,0:T(8,128)S(1)} custom-call(f32[128,128]{1,0:T(8,128)S(1)} %cholesky.272), custom_call_target="Cholesky" | custom-call | tf_op jit(solution)/shard_map/jit(cholesky)/cholesky | solution.py:78
  871.1 9.8 custom-call.36
  881.7 11.9 %cholesky.253 = f32[128,128]{1,0:T(8,128)S(1)} custom-call(f32[128,128]{1,0:T(8,128)S(1)} %convolution_subtract_fusion.8), custom_call_target="Cholesky" | custom-call | tf_op jit(solution)/shard_map/jit(cholesky)/cholesky | solution.py:78
  898.2 8.1 while.1
  898.8 1.3 dynamic-slice.13
  900.8 1.3 dynamic-slice.13
  902.9 1.3 dynamic-slice.13
  904.9 1.3 dynamic-slice.13
  906.3 39.3 %custom-call.37 = f32[4,128,128]{1,2,0:T(8,128)S(1)} custom-call(f32[4,128,128]{2,1,0:T(8,128)S(1)} %get-tuple-element.9), custom_call_target="InvertDiagBlocksLowerTriangular" | custom-call | tf_op jit(solution)/shard_map/triangular_solve | solution.py:79
  945.6 2.4 fusion.17
  948.1 3.0 convolution_subtract_fusion.2
  951.1 1.1 fusion.53
  952.2 3.6 convolution_subtract_fusion.1
  955.8 1.1 fusion.56
  956.9 5.6 fusion.9
  962.5 1.1 fusion.59
  965.2 1.3 convolution_subtract_fusion.7
  966.8 1.5 convolution_subtract_fusion.5
  968.6 1.7 convolution_subtract_fusion.4
  970.7 2.3 fusion.13
  973.0 4.0 convolution_subtract_fusion
  977.4 1.7 convolution_add_fusion
  979.1 3.4 psum.39
  (95 shorter events, 12.7 us)
Async XLA Ops:
  7.2 6.7 copy-start
  7.2 6.6 copy-start.8
  7.2 6.7 copy-start.6
  7.2 27.3 %all-reduce.5.cloned.1.call-start = ((), (), s32[]{:S(2)}) async-start(), calls=%async_computation.1 | async-start | bytes 262144 | tf_op jit(solution)/shard_map/psum | solution.py:53
  13.7 78.0 %all-gather.2.cloned.1.call-start = ((), (), s32[]{:S(2)}) async-start(), calls=%async_computation.3 | async-start | bytes 1179648 | tf_op jit(solution)/shard_map/all_gather | solution.py:83
  36.8 200.9 %all-reduce.7.cloned.1.call-start = ((), (), s32[]{:S(2)}) async-start(), calls=%async_computation.4 | async-start | bytes 8388608 | tf_op jit(solution)/shard_map/psum | solution.py:75
  36.9 5.0 copy-start.4
  44.7 738.7 %reduce-scatter.2.cloned.1.call-start = ((), (), s32[]{:S(2)}) async-start(), calls=%async_computation.2 | async-start | bytes 37748736 | tf_op jit(solution)/shard_map/reduce_scatter | solution.py:71
  90.9 0.7 copy-start.7
  90.9 719.6 %all-reduce.9.cloned.1.call-start = ((), (), s32[]{:S(2)}) async-start(), calls=%async_computation.5 | async-start | bytes 2097152 | tf_op jit(solution)/shard_map/psum | solution.py:15
  788.6 1.9 copy-start.2
  945.6 6.6 copy-start.3
  956.9 8.0 copy-start.5
  973.0 10.1 %copy-start.1 = (bf16[256,4096]{1,0:T(8,128)(2,1)S(1)}, bf16[256,4096]{1,0:T(8,128)(2,1)}, u32[]{:S(2)}) copy-start(bf16[256,4096]{1,0:T(8,128)(2,1)} %param.8) | copy-start | bytes 6291460
Sparse Core Ops, SparseCore 0:
  13.8 20.6 all-reduce.4
  36.9 41.3 all-gather.1
  82.6 155.0 all-reduce.6
  241.3 542.0 reduce-scatter.1
  791.8 18.7 all-reduce.8
where the time goes:
time: 995 us; the launch traced here: 990 us
  waiting for transfers between devices  713 us (72%)
  other arithmetic  130 us (13%)
  matrix products  97.9 us (10%)
  local copies, waits for them, and re-layouts  24.4 us (2%)
  between operations  16.9 us (2%)
    reduce_scatter x1, waiting for transfers between devices, local(): lax.psum_scatter(gram_rows(width * lax.axis_size('dp')), 'dp', scatter_di...  546 us
    psum x1, waiting for transfers between devices, local(): panel_block = lax.psum(gram_rows(width), 'dp')  141 us
    another operation x14, other arithmetic, local(): corner = jnp.linalg.cholesky(corner_block)  78.9 us
    dot_general x8, matrix products, lead_dot(): lax.dot_general(left, right, (((0,), (0,)), ((), ())), precision=precisio...  62.2 us
    another operation x3, other arithmetic, local(): lax.linalg.triangular_solve(corner, panel_block, left_side=True, lower=True)  39.4 us
  transfers between devices with their start and end apart: 5, of which 4 were waited for; matrix products, arithmetic and copies ran while one was open for 7% of the time, Pallas kernels for 0%

commit v1 on v0

v1 whole, which is shorter than its diff:
```python
import jax
import jax.numpy as jnp
from jax import lax
from jax.experimental import pallas as pl
from jax.experimental.pallas import tpu as pltpu
from jax.sharding import PartitionSpec as P

R = 64
SEQ = 16
damping = 1.0
EXACT = lax.Precision.HIGHEST
SWAP = [(0, 1), (1, 0)]
VMEM_BYTES = 40 * 1024 * 1024


def ring_order(mesh):
    count = mesh.shape["dp"]
    coords = [getattr(device, "coords", None) for device in mesh.devices[0, :, 0]]
    if None in coords:
        return list(range(count))
    moving = [axis for axis in range(3) if len({place[axis] for place in coords}) > 1]
    fast = [axis for axis in moving if coords[0][axis] != coords[1][axis]]
    if len(moving) == 2 and len(fast) == 1 and len({place[fast[0]] for place in coords}) == 2:
        return list(range(0, count, 2)) + list(range(1, count, 2))[::-1]
    return list(range(count))


def lead_dot(left, right, precision=None):
    return lax.dot_general(
        left, right, (((0,), (0,)), ((), ())), precision=precision, preferred_element_type=jnp.float32
    )


def exact_dot(left, right):
    return jnp.dot(left, right, precision=EXACT, preferred_element_type=jnp.float32)


def panel_kernel(place_ref, left_ref, right_ref, out_ref):
    out_ref[0] = jnp.dot(left_ref[...].T, right_ref[...], preferred_element_type=jnp.float32)


def panel_parts(stored, tensor_index, owners, group, width):
    rows = stored.shape[0]
    return pl.pallas_call(
        panel_kernel,
        grid_spec=pltpu.PrefetchScalarGridSpec(
            num_scalar_prefetch=1,
            grid=(owners,),
            in_specs=[
                pl.BlockSpec((rows, group), lambda o, place: (0, 2 * o + place[0])),
                pl.BlockSpec((rows, width), lambda o, place: (0, 0)),
            ],
            out_specs=pl.BlockSpec((1, group, width), lambda o, place: (o, 0, 0)),
        ),
        out_shape=jax.ShapeDtypeStruct((owners, group, width), jnp.float32),
        compiler_params=pltpu.CompilerParams(vmem_limit_bytes=VMEM_BYTES),
        cost_estimate=pl.CostEstimate(
            flops=2 * rows * owners * group * width,
            bytes_accessed=2 * rows * group * owners + 4 * owners * group * width,
            transcendentals=0,
        ),
        name="panel_parts",
    )(jnp.reshape(tensor_index, (1,)).astype(jnp.int32), stored, stored)


def window_part(stored, owner, first, count, arrived, last=False):
    rows, full = stored.shape
    groups = full // owner[1]
    group = owner[1]

    def kernel(place_ref, left_ref, right_ref, *refs):
        turned = refs[-1]

        @pl.when(pl.program_id(0) == 0)
        def _():
            turned[...] = left_ref[...].T

        total = jnp.dot(turned[...], right_ref[...], preferred_element_type=jnp.float32)
        for ref in refs[: len(arrived)]:
            total = total + ref[...].astype(jnp.float32)
        if last:
            refs[-3][...] = total
            refs[-2][0] = total.T.astype(jnp.bfloat16)
        else:
            refs[-2][...] = total.astype(jnp.bfloat16)

    block = pl.BlockSpec((group, group), lambda k, place: (0, k))
    if last:
        out_specs = [block, pl.BlockSpec((1, group, group), lambda k, place: (k, 0, 0))]
        out_shape = [
            jax.ShapeDtypeStruct((group, count * group), jnp.float32),
            jax.ShapeDtypeStruct((count, group, group), jnp.bfloat16),
        ]
    else:
        out_specs = block
        out_shape = jax.ShapeDtypeStruct((group, count * group), jnp.bfloat16)
    return pl.pallas_call(
        kernel,
        grid_spec=pltpu.PrefetchScalarGridSpec(
            num_scalar_prefetch=1,
            grid=(count,),
            in_specs=[
                pl.BlockSpec((rows, group), lambda k, place: (0, place[0])),
                pl.BlockSpec((rows, group), lambda k, place: (0, lax.rem(place[0] + first + k, groups))),
            ]
            + [block] * len(arrived),
            out_specs=out_specs,
            scratch_shapes=[pltpu.VMEM((group, rows), jnp.bfloat16)],
        ),
        out_shape=out_shape,
        compiler_params=pltpu.CompilerParams(vmem_limit_bytes=VMEM_BYTES),
        cost_estimate=pl.CostEstimate(
            flops=2 * rows * count * group * group,
            bytes_accessed=2 * rows * group * (count + 1) + 4 * count * group * group,
            transcendentals=0,
        ),
        name="window_part",
    )(jnp.reshape(owner[0], (1,)).astype(jnp.int32), stored, stored, *arrived)


def solve_kernel(matrix_ref, right_ref, out_ref, work, inverse, residual):
    size = matrix_ref.shape[0]
    block = inverse.shape[0]
    work[...] = matrix_ref[...]
    out_ref[...] = right_ref[...]
    row_ids = lax.broadcasted_iota(jnp.int32, (block, block), 0)
    col_ids = lax.broadcasted_iota(jnp.int32, (block, block), 1)
    eye = (row_ids == col_ids).astype(jnp.float32)
    for start in range(0, size, block):
        here = slice(start, start + block)
        rest = slice(start + block, size)
        corner = work[here, here]
        norm = jnp.max(jnp.sum(jnp.abs(corner), axis=0))
        inverse[...] = eye / norm
        residual[...] = eye - corner / norm

        def unfinished(state):
            step, worst = state
            return jnp.logical_and(step < 40, worst > 1e-5)

        def improve(state):
            step, _ = state
            better = inverse[...] + exact_dot(inverse[...], residual[...])
            left_over = eye - exact_dot(work[here, here], better)
            inverse[...] = better
            residual[...] = left_over
            return step + 1, jnp.max(jnp.abs(left_over))

        lax.while_loop(unfinished, improve, (jnp.int32(0), jnp.float32(1.0)))
        found = inverse[...] + exact_dot(inverse[...], residual[...])
        solved = exact_dot(found, out_ref[here, :])
        out_ref[here, :] = solved
        if start + block < size:
            across = exact_dot(found, work[here, rest])
            down = work[rest, here]
            work[rest, rest] = work[rest, rest] - exact_dot(down, across)
            out_ref[rest, :] = out_ref[rest, :] - exact_dot(down, solved)
            work[here, rest] = across
    for start in range(size - 2 * block, -1, -block):
        here = slice(start, start + block)
        rest = slice(start + block, size)
        out_ref[here, :] = out_ref[here, :] - exact_dot(work[here, rest], out_ref[rest, :])


def solve(matrix, right):
    size, columns = right.shape
    block = 128
    return pl.pallas_call(
        solve_kernel,
        out_shape=jax.ShapeDtypeStruct((size, columns), jnp.float32),
        scratch_shapes=[
            pltpu.VMEM((size, size), jnp.float32),
            pltpu.VMEM((block, block), jnp.float32),
            pltpu.VMEM((block, block), jnp.float32),
        ],
        compiler_params=pltpu.CompilerParams(vmem_limit_bytes=VMEM_BYTES),
        cost_estimate=pl.CostEstimate(flops=12 * size**3, bytes_accessed=4 * size * (size + 2 * columns), transcendentals=0),
        name="solve",
    )(matrix, right)


def full_rows(place, near, far, turned, group):
    near_count = near.shape[1] // group
    far_count = far.shape[1] // group
    turned_count = turned.shape[0]
    half = near_count + far_count - 1
    groups = 2 * half

    def offset(c, place, mine):
        side = place[1] if mine else 1 - place[1]
        return lax.rem(side * half + c - place[0] + groups, groups)

    def near_map(mine):
        return lambda c, place: (0, jnp.minimum(offset(c, place, mine), near_count - 1))

    def far_map(mine):
        return lambda c, place: (0, jnp.clip(offset(c, place, mine) - near_count, 0, far_count - 1))

    def turned_map(mine):
        return lambda c, place: (jnp.clip(groups - 1 - offset(c, place, mine), 0, turned_count - 1), 0, 0)

    def kernel(place_ref, near_a, far_a, turned_a, near_b, far_b, turned_b, mine_ref, send_ref):
        c = pl.program_id(0)

        def pick(which, near_ref, far_ref, turned_ref, out_ref):
            step = offset(c, place_ref, which)

            @pl.when(step < near_count)
            def _():
                out_ref[...] = near_ref[...].astype(out_ref.dtype)

            @pl.when(jnp.logical_and(step >= near_count, step <= half))
            def _():
                out_ref[...] = far_ref[...].astype(out_ref.dtype)

            @pl.when(step > half)
            def _():
                out_ref[...] = turned_ref[0].astype(out_ref.dtype)

        pick(True, near_a, far_a, turned_a, mine_ref)
        pick(False, near_b, far_b, turned_b, send_ref)

    def sources(mine):
        return [
            pl.BlockSpec((group, group), near_map(mine)),
            pl.BlockSpec((group, group), far_map(mine)),
            pl.BlockSpec((1, group, group), turned_map(mine)),
        ]

    block = pl.BlockSpec((group, group), lambda c, place: (0, c))
    return pl.pallas_call(
        kernel,
        grid_spec=pltpu.PrefetchScalarGridSpec(
            num_scalar_prefetch=1,
            grid=(half,),
            in_specs=sources(True) + sources(False),
            out_specs=[block, block],
        ),
        out_shape=[
            jax.ShapeDtypeStruct((group, half * group), jnp.float32),
            jax.ShapeDtypeStruct((group, half * group), jnp.bfloat16),
        ],
        compiler_params=pltpu.CompilerParams(vmem_limit_bytes=VMEM_BYTES),
        name="full_rows",
    )(place, near, far, turned, near, far, turned)


def finish(place, mine, other, vectors, group):
    examples = vectors.shape[0]
    half_cols = mine.shape[1]
    wide = half_cols // 2

    def kernel(place_ref, mine_ref, other_ref, rows_ref, cols_ref, out_ref):
        r, c = pl.program_id(0), pl.program_id(1)
        added = jnp.dot(rows_ref[...].T, cols_ref[...], preferred_element_type=jnp.float32)
        row_ids = (place_ref[0] - place_ref[1] + r) * group + lax.broadcasted_iota(jnp.int32, (group, wide), 0)
        col_ids = place_ref[1] * half_cols + c * wide + lax.broadcasted_iota(jnp.int32, (group, wide), 1)
        added = added + jnp.where(row_ids == col_ids, jnp.float32(damping), jnp.float32(0.0))

        @pl.when(r == place_ref[1])
        def _():
            out_ref[...] = added + mine_ref[...]

        @pl.when(r != place_ref[1])
        def _():
            out_ref[...] = added + other_ref[...].astype(jnp.float32)

    return pl.pallas_call(
        kernel,
        grid_spec=pltpu.PrefetchScalarGridSpec(
            num_scalar_prefetch=1,
            grid=(2, 2),
            in_specs=[
                pl.BlockSpec((group, wide), lambda r, c, place: (0, c)),
                pl.BlockSpec((group, wide), lambda r, c, place: (0, c)),
                pl.BlockSpec((examples, group), lambda r, c, place: (0, place[0] - place[1] + r)),
                pl.BlockSpec((examples, wide), lambda r, c, place: (0, 2 * place[1] + c)),
            ],
            out_specs=pl.BlockSpec((group, wide), lambda r, c, place: (r, c)),
        ),
        out_shape=jax.ShapeDtypeStruct((2 * group, half_cols), jnp.float32),
        compiler_params=pltpu.CompilerParams(vmem_limit_bytes=VMEM_BYTES),
        name="finish",
    )(place, mine, other, vectors, vectors)


def in_order(tensor_index, mine, other, axis):
    return jnp.where(
        tensor_index == 0,
        jnp.concatenate([mine, other], axis=axis),
        jnp.concatenate([other, mine], axis=axis),
    )


def local(ring, activations, out_grads, proj_in, proj_out, stored, counts, query_ids):
    owners = len(ring)
    full = stored.shape[1]
    width = full // owners
    group = width // 2
    groups = 2 * owners
    half = owners // 2
    t = lax.axis_index("tensor")
    d = lax.axis_index("dp")
    g = 2 * d + t
    place = jnp.stack([g, t]).astype(jnp.int32)
    around = jnp.array(ring + ring + ring, jnp.int32)
    spot = jnp.array([ring.index(index) for index in range(owners)], jnp.int32)[d]
    ahead = [(ring[p], ring[(p + 1) % owners]) for p in range(owners)]
    back = [(ring[(p + 1) % owners], ring[p]) for p in range(owners)]

    def owner_at(step):
        return around[spot + owners + step]

    sides = jnp.concatenate(
        [
            jnp.dot(activations, proj_in, preferred_element_type=jnp.float32),
            jnp.dot(out_grads, proj_out, preferred_element_type=jnp.float32),
        ],
        axis=1,
    )
    sides = sides + lax.ppermute(sides, "tensor", SWAP)

    panels = panel_parts(stored, t, owners, group, width)
    corner_rows = lax.psum(panels[0], "dp")

    def panel_at(step):
        return lax.dynamic_index_in_dim(panels, owner_at(step), 0, keepdims=False)

    examples = counts.shape[0]
    rank = proj_in.shape[1]
    position = jnp.arange(SEQ, dtype=jnp.int32)[None, :]
    weights = jnp.where(
        position < counts[:, None], 1.0 / counts.astype(jnp.float32)[:, None], jnp.float32(0.0)
    )
    act_half = lax.dynamic_slice_in_dim(sides, t * (rank // 2), rank // 2, 1)
    outer = jnp.einsum(
        "es,esi,esj->eij",
        weights,
        act_half.reshape(examples, SEQ, rank // 2),
        sides[:, rank:].reshape(examples, SEQ, rank),
        precision=EXACT,
    )
    vectors_half = outer.reshape(examples, full // 2).astype(jnp.bfloat16)
    gathered_half = lax.all_gather(vectors_half, "dp", axis=0, tiled=True)
    vectors = in_order(t, gathered_half, lax.ppermute(gathered_half, "tensor", SWAP), 1)

    near_count = groups // 4 + 1
    far_count = groups // 2 + 1 - near_count

    def window(step, first, count, arrived):
        return window_part(stored, (2 * owner_at(step) + t, group), first, count, arrived)

    far_ahead, far_back, near_ahead, near_back = [], [], [], []
    panel_ahead = panel_back = None
    for step in range(half, 0, -1):
        whole_step = step < half
        part_ahead, part_back = panel_at(step), panel_at(-step)
        if not whole_step:
            part_ahead, part_back = part_ahead[:, :group], part_back[:, group:]
        elif step == half - 1:
            blank = jnp.zeros_like(panel_ahead)
            part_ahead = part_ahead + jnp.concatenate([panel_ahead, blank], axis=1)
            part_back = part_back + jnp.concatenate([blank, panel_back], axis=1)
        else:
            part_ahead, part_back = part_ahead + panel_ahead, part_back + panel_back
        panel_ahead = lax.ppermute(part_ahead, "dp", ahead)
        panel_back = lax.ppermute(part_back, "dp", back)
        far_ahead = [lax.ppermute(window(step, near_count, far_count, far_ahead), "dp", ahead)]
        if whole_step:
            far_back = [lax.ppermute(window(-step, near_count, far_count, far_back), "dp", back)]
    for step in range(half, 0, -1):
        near_back = [lax.ppermute(window(-step, 0, near_count, near_back), "dp", back)]
        if step < half:
            near_ahead = [lax.ppermute(window(step, 0, near_count, near_ahead), "dp", ahead)]

    corner = in_order(t, corner_rows, lax.ppermute(corner_rows, "tensor", SWAP), 0)
    first_cols = vectors[:, :width]
    eye = jnp.eye(width, dtype=jnp.float32)
    corner = corner + lead_dot(first_cols, first_cols) + damping * eye
    scale = lax.rsqrt(jnp.sum(corner * eye, axis=1))
    first_rows = first_cols.astype(jnp.float32).T
    solved = solve(corner * scale[:, None] * scale[None, :], first_rows * scale[:, None]) * scale[:, None]
    own_cols = lax.dynamic_slice_in_dim(vectors, g * group, group, 1)
    row_ids = g * group + jnp.arange(group, dtype=jnp.int32)[:, None]
    damped = jnp.where(row_ids == jnp.arange(width, dtype=jnp.int32)[None, :], jnp.float32(damping), 0.0)
    panel = panel_at(0) + panel_ahead + panel_back + lead_dot(own_cols, first_cols) + damped
    rest = own_cols.astype(jnp.float32).T - exact_dot(panel, solved)
    pairs = lead_dot(rest, rest, EXACT)
    pairs = pairs + jnp.where(g == 0, lead_dot(first_rows, solved, EXACT), 0.0)
    pairs = lax.psum(pairs, ("dp", "tensor"))
    own_pairs = lax.dynamic_slice_in_dim(pairs, d * examples, examples, 1)
    chosen = (query_ids[:, None] == jnp.arange(pairs.shape[0], dtype=jnp.int32)[None, :]).astype(jnp.float32)
    scores = exact_dot(chosen, own_pairs) / R

    far, far_turned = window_part(
        stored, (g, group), near_count, far_count, far_ahead + far_back, last=True
    )
    near, near_turned = window_part(stored, (g, group), 0, near_count, near_ahead + near_back, last=True)
    turned = []
    for shift in range(1, groups // 2):
        block = near_turned[shift] if shift < near_count else far_turned[shift - near_count]
        turned.append(
            lax.ppermute(block, ("dp", "tensor"), [(h, (h + shift) % groups) for h in range(groups)])
        )
    mine, send = full_rows(place, near, far, jnp.stack(turned), group)
    other = lax.ppermute(send, "tensor", SWAP)
    return finish(place, mine, other, vectors, group), scores


def solution(mesh):
    placed = (
        P(("groups", "dp"), "tensor"),
        P(("groups", "dp"), "tensor"),
        P("tensor", None),
        P("tensor", None),
        P(("groups", "dp"), None),
        P(("groups", "dp")),
        P("groups"),
    )
    ring = ring_order(mesh)

    def program(*args):
        return local(ring, *args)

    return jax.shard_map(
        program,
        mesh=mesh,
        in_specs=placed,
        out_specs=(P(("groups", "dp"), "tensor"), P("groups", "dp")),
        check_vma=False,
    )
```

time: 995 us -> 415 us (0.42)
  waiting for transfers between devices: 713 us -> 155 us
  other arithmetic: 130 us -> 5.37 us
  matrix products: 97.9 us -> 11.9 us
  Pallas kernels: 0 us -> 84.3 us
  blocking collectives: 7.55 us -> 39.5 us
  between operations: 16.9 us -> 48 us
  starting transfers between devices: 0.38 us -> 25.9 us
  local copies, waits for them, and re-layouts: 24.4 us -> 39.8 us
    reduce_scatter x1 -> x0, waiting for transfers between devices: 546 us -> none  [local(): lax.psum_scatter(gram_rows(width * lax.axis_size('dp')), 'dp', scatter_di...]
    another operation x17 -> x1, other arithmetic: 118 us -> 0.08 us  [local(): place = jnp.stack([g, t]).astype(jnp.int32)]
    psum x3 -> x2, waiting for transfers between devices: 167 us -> 82.4 us  [the longest x1 82.4 us: local(): pairs = lax.psum(pairs, ('dp', 'tensor'))]
    pallas_call x0 -> x20, Pallas kernels: none -> 84.3 us  [the longest x16 47.5 us: window_part(): pl.pallas_call(kernel, grid_spec=pltpu.PrefetchScalarGridSpec(num_scalar_...]
    ppermute x0 -> x33, waiting for transfers between devices: none -> 73.1 us  [the longest x7 27.6 us: local(): lax.ppermute(block, ('dp', 'tensor'), [(h, (h + shift) % groups) for h in...]
    dot_general x8 -> x4, matrix products: 62.2 us -> 2.16 us  [lead_dot(): lax.dot_general(left, right, (((0,), (0,)), ((), ())), precision=precisio...]
    all_gather x0 -> x1, blocking collectives: none -> 39.5 us  [local(): gathered_half = lax.all_gather(vectors_half, 'dp', axis=0, tiled=True)]
    another operation x27 -> x0, matrix products: 27.2 us -> none  [the longest x7 17.9 us: local(): lax.linalg.triangular_solve(corner, panel_block, left_side=True, lower=True)]
  transfers between devices with their start and end apart: 5 -> 35, of which waited for: 4 -> 12; matrix products, arithmetic and copies ran while one was open for 7% -> 5% of each run, Pallas kernels for 0% -> 18%
where the time goes in v1:
time: 415 us; the launch traced here: 410 us
  waiting for transfers between devices  155 us (37%)
  Pallas kernels  84.3 us (20%)
  between operations  48 us (12%)
  local copies, waits for them, and re-layouts  39.8 us (10%)
  blocking collectives  39.5 us (10%)
  starting transfers between devices  25.9 us (6%)
  matrix products  11.9 us (3%)
  other arithmetic  5.37 us (1%)
    psum x1, waiting for transfers between devices, local(): pairs = lax.psum(pairs, ('dp', 'tensor'))  82.4 us
    pallas_call x16, Pallas kernels, window_part(): pl.pallas_call(kernel, grid_spec=pltpu.PrefetchScalarGridSpec(num_scalar_...  47.5 us
    all_gather x1, blocking collectives, local(): gathered_half = lax.all_gather(vectors_half, 'dp', axis=0, tiled=True)  39.5 us
    unnamed x46, local copies, waits for them, and re-layouts  32.1 us
    ppermute x7, waiting for transfers between devices, local(): lax.ppermute(block, ('dp', 'tensor'), [(h, (h + shift) % groups) for h in...  27.6 us
    pallas_call x1, Pallas kernels, solve(): pl.pallas_call(solve_kernel, out_shape=jax.ShapeDtypeStruct((size, column...  22.6 us
    ppermute x4, waiting for transfers between devices, local(): lax.ppermute(window(step, near_count, far_count, far_ahead), 'dp', ahead)  18.9 us
    ppermute x4, waiting for transfers between devices, local(): panel_back = lax.ppermute(part_back, 'dp', back)  12.6 us
  transfers between devices with their start and end apart: 35, of which 12 were waited for; matrix products, arithmetic and copies ran while one was open for 5% of the time, Pallas kernels for 18%

profile of v1, /device:TPU:0, one launch (start us, length us, event | category | flops | bytes accessed | tf_op | source)
XLA Modules:
  0.0 410.2 jit_solution(818508376605070455)
XLA Ops:
  25.7 3.4 copy-done.2
  29.1 4.5 %panel_parts.1 = f32[8,256,512]{2,1,0:T(8,128)S(1)} custom-call(s32[1]{0:T(128)} %bitcast.1.place_ref, bf16[1024,4096]{1,0:T(8,128)(2,1)S(1)} %copy-done.2, bf16[1024,4096]{1,0:T(8,128)(2,1)S(1)} %copy-done.2), custom_call_target="tpu_custom_call" | custom-call | flops 2147483648 | bytes 8388608 | tf_op jit(solution)/shard_map/panel_parts/pallas_call | solution.py:44
  36.7 6.0 %fusion.35 = f32[256,64]{0,1:T(8,128)S(1)} fusion(bf16[256,14336]{1,0:T(8,128)(2,1)} %param.9, bf16[14336,64]{0,1:T(8,128)(2,1)} %param.11), kind=kOutput, calls=%fused_computation.75 | convolution fusion | flops 469762048 | bytes 9240576 | tf_op jit(solution)/shard_map/dot_general | solution.py:316
  45.3 2.6 collective-permute-start.24
  48.6 3.4 copy-done.3
  52.0 2.4 window_part.19
  55.0 3.4 copy-done.4
  58.4 2.8 window_part.24
  61.2 2.0 collective-permute-start.7
  63.8 3.4 copy-done.5
  67.2 2.8 window_part.28
  71.9 39.5 %all_gather.3 = bf16[128,2048]{1,0:T(8,128)(2,1)S(1)} all-gather(bf16[16,2048]{1,0:T(8,128)(2,1)S(1)} %convert_element_type.19), channel_id=1, replica_groups=mesh['groups'=2,'dp'=8,'tensor'=2] {'dp'}, dimensions={0}, use_global_device_ids=true | all-gather | bytes 589824 | tf_op jit(solution)/shard_map/all_gather | solution.py:344
  111.8 3.4 copy-done.6
  115.2 2.4 window_part.16
  135.1 3.4 copy-done.7
  138.5 4.1 window_part.25
  144.0 3.4 copy-done.8
  147.3 4.1 %window_part.29 = bf16[256,1024]{1,0:T(8,128)(2,1)} custom-call(s32[1]{0:T(128)} %bitcast.21.place_ref, bf16[1024,4096]{1,0:T(8,128)(2,1)S(1)} %copy-done.8, bf16[1024,4096]{1,0:T(8,128)(2,1)S(1)} %copy-done.8, bf16[256,1024]{1,0:T(8,128)(2,1)} %collective-permute-done.11.refs_0_), custom_call_target="tpu_custom_call" | custom-call | flops 536870912 | bytes 3670016 | tf_op jit(solution)/shard_map/window_part/pallas_call | solution.py:97
  152.1 3.5 window_part.20
  157.1 5.6 %collective-permute-done.25 = f32[256,512]{1,0:T(8,128)} collective-permute-done((f32[256,512]{1,0:T(8,128)S(1)}, f32[256,512]{1,0:T(8,128)}, u32[]{:S(2)}, u32[]{:S(2)}) %collective-permute-start.25) | collective-permute-done | bytes 524320 | tf_op jit(solution)/shard_map/ppermute | solution.py:366
  164.1 2.1 collective-permute-start.26
  166.4 3.4 copy-done.9
  169.7 4.2 %window_part.17 = bf16[256,1280]{1,0:T(8,128)(2,1)S(1)} custom-call(s32[1]{0:T(128)} %bitcast.9.place_ref, bf16[1024,4096]{1,0:T(8,128)(2,1)S(1)} %copy-done.9, bf16[1024,4096]{1,0:T(8,128)(2,1)S(1)} %copy-done.9, bf16[256,1280]{1,0:T(8,128)(2,1)} %collective-permute-done.refs_0_), custom_call_target="tpu_custom_call" | custom-call | flops 671088640 | bytes 4456448 | tf_op jit(solution)/shard_map/window_part/pallas_call | solution.py:97
  174.5 2.1 collective-permute-start.1
  176.5 3.3 window_part.26
  180.7 2.4 window_part.21
  185.2 3.4 window_part.30
  189.3 2.1 collective-permute-start.29
  191.6 7.6 %collective-permute-done.1.refs_0_ = bf16[256,1280]{1,0:T(8,128)(2,1)S(1)} collective-permute-done((bf16[256,1280]{1,0:T(8,128)(2,1)S(1)}, bf16[256,1280]{1,0:T(8,128)(2,1)S(1)}, u32[]{:S(2)}, u32[]{:S(2)}) %collective-permute-start.1) | collective-permute-done | bytes 655392 | tf_op jit(solution)/shard_map/ppermute | solution.py:374
  199.2 2.4 window_part.18
  201.7 8.7 %collective-permute-done.9.refs_0_ = bf16[256,1024]{1,0:T(8,128)(2,1)S(1)} collective-permute-done((bf16[256,1024]{1,0:T(8,128)(2,1)S(1)}, bf16[256,1024]{1,0:T(8,128)(2,1)S(1)}, u32[]{:S(2)}, u32[]{:S(2)}) %collective-permute-start.9) | collective-permute-done | bytes 524320 | tf_op jit(solution)/shard_map/ppermute | solution.py:368
  210.4 2.0 window_part.27
  212.6 2.4 window_part.22
  217.1 6.2 %collective-permute-done.29 = f32[256,512]{1,0:T(8,128)S(1)} collective-permute-done((f32[256,512]{1,0:T(8,128)S(1)}, f32[256,512]{1,0:T(8,128)S(1)}, u32[]{:S(2)}, u32[]{:S(2)}) %collective-permute-start.29) | collective-permute-done | bytes 524320 | tf_op jit(solution)/shard_map/ppermute | solution.py:367
  223.4 2.1 collective-permute-start.30
  225.5 10.2 %collective-permute-done.10.refs_0_ = bf16[256,1024]{1,0:T(8,128)(2,1)S(1)} collective-permute-done((bf16[256,1024]{1,0:T(8,128)(2,1)S(1)}, bf16[256,1024]{1,0:T(8,128)(2,1)S(1)}, u32[]{:S(2)}, u32[]{:S(2)}) %collective-permute-start.10) | collective-permute-done | bytes 524320 | tf_op jit(solution)/shard_map/ppermute | solution.py:368
  235.7 2.4 window_part.31
  238.3 3.6 collective-permute-start.20
  241.9 2.8 window_part.23
  244.8 6.4 %collective-permute-done.30 = f32[256,512]{1,0:T(8,128)S(1)} collective-permute-done((f32[256,512]{1,0:T(8,128)S(1)}, f32[256,512]{1,0:T(8,128)S(1)}, u32[]{:S(2)}, u32[]{:S(2)}) %collective-permute-start.30) | collective-permute-done | bytes 524320 | tf_op jit(solution)/shard_map/ppermute | solution.py:367
  251.3 7.1 %collective-permute-done.14 = bf16[256,256]{1,0:T(8,128)(2,1)S(1)} collective-permute-done((bf16[256,256]{1,0:T(8,128)(2,1)S(1)}, bf16[256,256]{1,0:T(8,128)(2,1)S(1)}, u32[]{:S(2)}, u32[]{:S(2)}) %collective-permute-start.14) | collective-permute-done | bytes 131104 | tf_op jit(solution)/shard_map/ppermute | solution.py:403
  258.4 7.6 %collective-permute-done.15 = bf16[256,256]{1,0:T(8,128)(2,1)S(1)} collective-permute-done((bf16[256,256]{1,0:T(8,128)(2,1)S(1)}, bf16[256,256]{1,0:T(8,128)(2,1)S(1)}, u32[]{:S(2)}, u32[]{:S(2)}) %collective-permute-start.15) | collective-permute-done | bytes 131104 | tf_op jit(solution)/shard_map/ppermute | solution.py:403
  266.0 6.2 %collective-permute-done.16 = bf16[256,256]{1,0:T(8,128)(2,1)S(1)} collective-permute-done((bf16[256,256]{1,0:T(8,128)(2,1)S(1)}, bf16[256,256]{1,0:T(8,128)(2,1)S(1)}, u32[]{:S(2)}, u32[]{:S(2)}) %collective-permute-start.16) | collective-permute-done | bytes 131104 | tf_op jit(solution)/shard_map/ppermute | solution.py:403
  272.3 6.7 %collective-permute-done.17 = bf16[256,256]{1,0:T(8,128)(2,1)S(1)} collective-permute-done((bf16[256,256]{1,0:T(8,128)(2,1)S(1)}, bf16[256,256]{1,0:T(8,128)(2,1)S(1)}, u32[]{:S(2)}, u32[]{:S(2)}) %collective-permute-start.17) | collective-permute-done | bytes 131104 | tf_op jit(solution)/shard_map/ppermute | solution.py:403
  280.4 4.1 full_rows.1
  285.9 22.6 %solve.1 = f32[512,128]{1,0:T(8,128)S(1)} custom-call(f32[512,512]{1,0:T(8,128)S(1)} %multiply_multiply_fusion.matrix_ref, f32[512,128]{1,0:T(8,128)S(1)} %multiply_bitcast_fusion.right_ref), custom_call_target="tpu_custom_call" | custom-call | flops 1610612736 | bytes 1572864 | tf_op jit(solution)/shard_map/solve/pallas_call | solution.py:168
  312.3 82.4 %all-reduce.7.cloned.1.call-done = f32[128,128]{0,1:T(8,128)} async-done(((f32[128,128]{0,1:T(8,128)}), f32[128,128]{0,1:T(8,128)}) %all-reduce.7.cloned.1.call-update) | async-done | bytes 65552 | tf_op jit(solution)/shard_map/psum | solution.py:390
  397.8 5.6 %finish.1 = f32[512,2048]{1,0:T(8,128)} custom-call(s32[2]{0:T(128)S(1)} %pad_add_fusion.place_ref, f32[256,2048]{1,0:T(8,128)S(1)} %copy-done.13, bf16[256,2048]{1,0:T(8,128)(2,1)} %collective-permute-done.21.other_ref, bf16[128,4096]{1,0:T(8,128)(2,1)S(1)} %copy.27.rows_ref.cols_ref, bf16[128,4096]{1,0:T(8,128)(2,1)S(1)} %copy.27.rows_ref.cols_ref), custom_call_target="tpu_custom_call" | custom-call | tf_op jit(solution)/shard_map/finish/pallas_call | solution.py:268
  (130 shorter events, 34.3 us)
Async XLA Ops:
  7.2 35.5 %copy-start = (bf16[256,4096]{1,0:T(8,128)(2,1)S(1)}, bf16[256,4096]{1,0:T(8,128)(2,1)}, u32[]{:S(2)}) copy-start(bf16[256,4096]{1,0:T(8,128)(2,1)} %param.10) | copy-start | bytes 6291460
  7.2 148.4 %all-reduce.5.cloned.1.call-start = ((), (), s32[]{:S(2)}) async-start(), calls=%async_computation | async-start | bytes 1048576 | tf_op jit(solution)/shard_map/psum | solution.py:324
  25.7 3.4 copy-start.2
  36.7 358.0 %all-reduce.7.cloned.1.call-start = ((), (), s32[]{:S(2)}) async-start(), calls=%async_computation.1 | async-start | bytes 131072 | tf_op jit(solution)/shard_map/psum | solution.py:390
  36.7 6.0 %copy-start.15 = (bf16[4096,64]{0,1:T(8,128)(2,1)S(1)}, bf16[4096,64]{0,1:T(8,128)(2,1)}, u32[]{:S(2)}) copy-start(bf16[4096,64]{0,1:T(8,128)(2,1)} %param.12) | copy-start | bytes 1572868
  44.1 26.6 %collective-permute-start.22 = (f32[256,128]{0,1:T(8,128)}, f32[256,128]{0,1:T(8,128)S(1)}, u32[]{:S(2)}, u32[]{:S(2)}) collective-permute-start(f32[256,128]{0,1:T(8,128)} %pad_maximum_fusion), channel_id=1, source_target_pairs={{0,1},{1,0},{2,3},{3,2},{4,5},{5,4},{6,7},{7,6},{8,9},{9,8},{10,11... | collective-permute-start | bytes 393224 | tf_op jit(solution)/shard_map/ppermute | solution.py:321
  45.3 88.5 %collective-permute-start.24 = (f32[256,256]{1,0:T(8,128)}, f32[256,256]{1,0:T(8,128)S(1)}, u32[]{:S(2)}, u32[]{:S(2)}) collective-permute-start(f32[256,256]{1,0:T(8,128)} %slice.49), channel_id=1, source_target_pairs={{0,4},{4,8},{8,12},{12,14},{14,10},{10,6},{6,2},{2,0},{1,5},{5,9},... | collective-permute-start | bytes 786440 | tf_op jit(solution)/shard_map/ppermute | solution.py:366
  48.6 3.4 copy-start.3
  54.3 97.1 %collective-permute-start.3 = (bf16[256,1280]{1,0:T(8,128)(2,1)S(1)}, bf16[256,1280]{1,0:T(8,128)(2,1)S(1)}, u32[]{:S(2)}, u32[]{:S(2)}) collective-permute-start(bf16[256,1280]{1,0:T(8,128)(2,1)S(1)} %window_part.19), channel_id=1, source_target_pairs={{4,0},{8,4},{12,8},{14,12},{10,14},{6,10},{2,6},{0,2},{5,1},{9,5},... | collective-permute-start | bytes 1966088 | tf_op jit(solution)/shard_map/ppermute | solution.py:372
  55.0 3.4 copy-start.4
  61.2 73.8 %collective-permute-start.7 = (bf16[256,1024]{1,0:T(8,128)(2,1)}, bf16[256,1024]{1,0:T(8,128)(2,1)}, u32[]{:S(2)}, u32[]{:S(2)}) collective-permute-start(bf16[256,1024]{1,0:T(8,128)(2,1)} %window_part.24), channel_id=1, source_target_pairs={{0,4},{4,8},{8,12},{12,14},{14,10},{10,6},{6,2},{2,0},{1,5},{5,9},... | collective-permute-start | bytes 1572872 | tf_op jit(solution)/shard_map/ppermute | solution.py:368
  63.8 3.4 copy-start.5
  70.1 72.5 %collective-permute-start.11 = (bf16[256,1024]{1,0:T(8,128)(2,1)}, bf16[256,1024]{1,0:T(8,128)(2,1)}, u32[]{:S(2)}, u32[]{:S(2)}) collective-permute-start(bf16[256,1024]{1,0:T(8,128)(2,1)} %window_part.28), channel_id=1, source_target_pairs={{4,0},{8,4},{12,8},{14,12},{10,14},{6,10},{2,6},{0,2},{5,1},{9,5},... | collective-permute-start | bytes 1572872 | tf_op jit(solution)/shard_map/ppermute | solution.py:370
  111.7 43.9 %collective-permute-start.23 = (bf16[128,2048]{0,1:T(8,128)(2,1)S(1)}, bf16[128,2048]{0,1:T(8,128)(2,1)}, u32[]{:S(2)}, u32[]{:S(2)}) collective-permute-start(bf16[128,2048]{0,1:T(8,128)(2,1)S(1)} %copy.25), channel_id=1, source_target_pairs={{0,1},{1,0},{2,3},{3,2},{4,5},{5,4},{6,7},{7,6},{8,9},{9,8},{10,11... | collective-permute-start | bytes 1572872 | tf_op jit(solution)/shard_map/ppermute | solution.py:345
  111.8 3.4 copy-start.6
  133.9 30.2 %collective-permute-start = (bf16[256,1280]{1,0:T(8,128)(2,1)S(1)}, bf16[256,1280]{1,0:T(8,128)(2,1)}, u32[]{:S(2)}, u32[]{:S(2)}) collective-permute-start(bf16[256,1280]{1,0:T(8,128)(2,1)S(1)} %window_part.16), channel_id=1, source_target_pairs={{0,4},{4,8},{8,12},{12,14},{14,10},{10,6},{6,2},{2,0},{1,5},{5,9},... | collective-permute-start | bytes 1966088 | tf_op jit(solution)/shard_map/ppermute | solution.py:374
  135.0 27.7 %collective-permute-start.25 = (f32[256,512]{1,0:T(8,128)S(1)}, f32[256,512]{1,0:T(8,128)}, u32[]{:S(2)}, u32[]{:S(2)}) collective-permute-start(f32[256,512]{1,0:T(8,128)S(1)} %bitcast_add_fusion.3), channel_id=1, source_target_pairs={{0,4},{4,8},{8,12},{12,14},{14,10},{10,6},{6,2},{2,0},{1,5},{5,9},... | collective-permute-start | bytes 1572872 | tf_op jit(solution)/shard_map/ppermute | solution.py:366
  142.6 31.9 %collective-permute-start.8 = (bf16[256,1024]{1,0:T(8,128)(2,1)}, bf16[256,1024]{1,0:T(8,128)(2,1)}, u32[]{:S(2)}, u32[]{:S(2)}) collective-permute-start(bf16[256,1024]{1,0:T(8,128)(2,1)} %window_part.25), channel_id=1, source_target_pairs={{0,4},{4,8},{8,12},{12,14},{14,10},{10,6},{6,2},{2,0},{1,5},{5,9},... | collective-permute-start | bytes 1572872 | tf_op jit(solution)/shard_map/ppermute | solution.py:368
  151.5 31.7 %collective-permute-start.12 = (bf16[256,1024]{1,0:T(8,128)(2,1)}, bf16[256,1024]{1,0:T(8,128)(2,1)}, u32[]{:S(2)}, u32[]{:S(2)}) collective-permute-start(bf16[256,1024]{1,0:T(8,128)(2,1)} %window_part.29), channel_id=1, source_target_pairs={{4,0},{8,4},{12,8},{14,12},{10,14},{6,10},{2,6},{0,2},{5,1},{9,5},... | collective-permute-start | bytes 1572872 | tf_op jit(solution)/shard_map/ppermute | solution.py:370
  155.6 18.3 %collective-permute-start.32 = (f32[256,512]{1,0:T(8,128)}, f32[256,512]{1,0:T(8,128)S(1)}, u32[]{:S(2)}, u32[]{:S(2)}) collective-permute-start(f32[256,512]{1,0:T(8,128)} %all-reduce.5.cloned.1.call-done), channel_id=1, source_target_pairs={{0,1},{1,0},{2,3},{3,2},{4,5},{5,4},{6,7},{7,6},{8,9},{9,8},{10,11... | collective-permute-start | bytes 1572872 | tf_op jit(solution)/shard_map/ppermute | solution.py:376
  157.1 151.9 %copy-start.14 = (bf16[128,4096]{0,1:T(8,128)(2,1)}, bf16[128,4096]{0,1:T(8,128)(2,1)S(1)}, u32[]{:S(2)}) copy-start(bf16[128,4096]{0,1:T(8,128)(2,1)S(1)} %maximum_select_fusion) | copy-start | bytes 3145732
  162.8 17.9 %collective-permute-start.4 = (bf16[256,1280]{1,0:T(8,128)(2,1)}, bf16[256,1280]{1,0:T(8,128)(2,1)S(1)}, u32[]{:S(2)}, u32[]{:S(2)}) collective-permute-start(bf16[256,1280]{1,0:T(8,128)(2,1)} %window_part.20), channel_id=1, source_target_pairs={{4,0},{8,4},{12,8},{14,12},{10,14},{6,10},{2,6},{0,2},{5,1},{9,5},... | collective-permute-start | bytes 1966088 | tf_op jit(solution)/shard_map/ppermute | solution.py:372
  164.1 25.1 %collective-permute-start.26 = (f32[256,512]{1,0:T(8,128)S(1)}, f32[256,512]{1,0:T(8,128)S(1)}, u32[]{:S(2)}, u32[]{:S(2)}) collective-permute-start(f32[256,512]{1,0:T(8,128)S(1)} %bitcast_add_fusion.4), channel_id=1, source_target_pairs={{0,4},{4,8},{8,12},{12,14},{14,10},{10,6},{6,2},{2,0},{1,5},{5,9},... | collective-permute-start | bytes 1572872 | tf_op jit(solution)/shard_map/ppermute | solution.py:366
  169.7 4.2 %copy-start.16 = (f32[256,256]{1,0:T(8,128)S(1)}, f32[256,256]{1,0:T(8,128)}, u32[]{:S(2)}) copy-start(f32[256,256]{1,0:T(8,128)} %slice.50) | copy-start | bytes 786436
  169.7 4.3 %copy-start.18 = (f32[256,512]{1,0:T(8,128)S(1)}, f32[256,512]{1,0:T(8,128)}, u32[]{:S(2)}) copy-start(f32[256,512]{1,0:T(8,128)} %all-reduce.5.cloned.1.call-done) | copy-start | bytes 1572868
  174.0 14.6 %collective-permute-start.28 = (f32[256,256]{1,0:T(8,128)S(1)}, f32[256,256]{1,0:T(8,128)S(1)}, u32[]{:S(2)}, u32[]{:S(2)}) collective-permute-start(f32[256,256]{1,0:T(8,128)S(1)} %copy-done.16), channel_id=1, source_target_pairs={{4,0},{8,4},{12,8},{14,12},{10,14},{6,10},{2,6},{0,2},{5,1},{9,5},... | collective-permute-start | bytes 786440 | tf_op jit(solution)/shard_map/ppermute | solution.py:367
  174.5 24.7 %collective-permute-start.1 = (bf16[256,1280]{1,0:T(8,128)(2,1)S(1)}, bf16[256,1280]{1,0:T(8,128)(2,1)S(1)}, u32[]{:S(2)}, u32[]{:S(2)}) collective-permute-start(bf16[256,1280]{1,0:T(8,128)(2,1)S(1)} %window_part.17), channel_id=1, source_target_pairs={{0,4},{4,8},{8,12},{12,14},{14,10},{10,6},{6,2},{2,0},{1,5},{5,9},... | collective-permute-start | bytes 1966088 | tf_op jit(solution)/shard_map/ppermute | solution.py:374
  180.6 29.8 %collective-permute-start.9 = (bf16[256,1024]{1,0:T(8,128)(2,1)S(1)}, bf16[256,1024]{1,0:T(8,128)(2,1)S(1)}, u32[]{:S(2)}, u32[]{:S(2)}) collective-permute-start(bf16[256,1024]{1,0:T(8,128)(2,1)S(1)} %window_part.26), channel_id=1, source_target_pairs={{0,4},{4,8},{8,12},{12,14},{14,10},{10,6},{6,2},{2,0},{1,5},{5,9},... | collective-permute-start | bytes 1572872 | tf_op jit(solution)/shard_map/ppermute | solution.py:368
  183.1 29.5 %collective-permute-start.5 = (bf16[256,1280]{1,0:T(8,128)(2,1)S(1)}, bf16[256,1280]{1,0:T(8,128)(2,1)S(1)}, u32[]{:S(2)}, u32[]{:S(2)}) collective-permute-start(bf16[256,1280]{1,0:T(8,128)(2,1)S(1)} %window_part.21), channel_id=1, source_target_pairs={{4,0},{8,4},{12,8},{14,12},{10,14},{6,10},{2,6},{0,2},{5,1},{9,5},... | collective-permute-start | bytes 1966088 | tf_op jit(solution)/shard_map/ppermute | solution.py:372
  185.2 4.0 copy-start.11
  188.6 34.8 %collective-permute-start.13 = (bf16[256,1024]{1,0:T(8,128)(2,1)S(1)}, bf16[256,1024]{1,0:T(8,128)(2,1)S(1)}, u32[]{:S(2)}, u32[]{:S(2)}) collective-permute-start(bf16[256,1024]{1,0:T(8,128)(2,1)S(1)} %window_part.30), channel_id=1, source_target_pairs={{4,0},{8,4},{12,8},{14,12},{10,14},{6,10},{2,6},{0,2},{5,1},{9,5},... | collective-permute-start | bytes 1572872 | tf_op jit(solution)/shard_map/ppermute | solution.py:370
  189.3 34.0 %collective-permute-start.29 = (f32[256,512]{1,0:T(8,128)S(1)}, f32[256,512]{1,0:T(8,128)S(1)}, u32[]{:S(2)}, u32[]{:S(2)}) collective-permute-start(f32[256,512]{1,0:T(8,128)S(1)} %get-tuple-element.15), channel_id=1, source_target_pairs={{4,0},{8,4},{12,8},{14,12},{10,14},{6,10},{2,6},{0,2},{5,1},{9,5},... | collective-permute-start | bytes 1572872 | tf_op jit(solution)/shard_map/ppermute | solution.py:367
  201.6 36.6 %collective-permute-start.2 = (bf16[256,1280]{1,0:T(8,128)(2,1)S(1)}, bf16[256,1280]{1,0:T(8,128)(2,1)S(1)}, u32[]{:S(2)}, u32[]{:S(2)}) collective-permute-start(bf16[256,1280]{1,0:T(8,128)(2,1)S(1)} %window_part.18), channel_id=1, source_target_pairs={{0,4},{4,8},{8,12},{12,14},{14,10},{10,6},{6,2},{2,0},{1,5},{5,9},... | collective-permute-start | bytes 1966088 | tf_op jit(solution)/shard_map/ppermute | solution.py:374
  212.5 23.2 %collective-permute-start.10 = (bf16[256,1024]{1,0:T(8,128)(2,1)S(1)}, bf16[256,1024]{1,0:T(8,128)(2,1)S(1)}, u32[]{:S(2)}, u32[]{:S(2)}) collective-permute-start(bf16[256,1024]{1,0:T(8,128)(2,1)S(1)} %window_part.27), channel_id=1, source_target_pairs={{0,4},{4,8},{8,12},{12,14},{14,10},{10,6},{6,2},{2,0},{1,5},{5,9},... | collective-permute-start | bytes 1572872 | tf_op jit(solution)/shard_map/ppermute | solution.py:368
  215.0 23.3 %collective-permute-start.6 = (bf16[256,1280]{1,0:T(8,128)(2,1)S(1)}, bf16[256,1280]{1,0:T(8,128)(2,1)S(1)}, u32[]{:S(2)}, u32[]{:S(2)}) collective-permute-start(bf16[256,1280]{1,0:T(8,128)(2,1)S(1)} %window_part.22), channel_id=1, source_target_pairs={{4,0},{8,4},{12,8},{14,12},{10,14},{6,10},{2,6},{0,2},{5,1},{9,5},... | collective-permute-start | bytes 1966088 | tf_op jit(solution)/shard_map/ppermute | solution.py:372
  223.3 85.7 %collective-permute-start.27 = (f32[256,512]{1,0:T(8,128)S(1)}, f32[256,512]{1,0:T(8,128)S(1)}, u32[]{:S(2)}, u32[]{:S(2)}) collective-permute-start(f32[256,512]{1,0:T(8,128)S(1)} %get-tuple-element.14), channel_id=1, source_target_pairs={{0,4},{4,8},{8,12},{12,14},{14,10},{10,6},{6,2},{2,0},{1,5},{5,9},... | collective-permute-start | bytes 1572872 | tf_op jit(solution)/shard_map/ppermute | solution.py:366
  223.4 27.7 %collective-permute-start.30 = (f32[256,512]{1,0:T(8,128)S(1)}, f32[256,512]{1,0:T(8,128)S(1)}, u32[]{:S(2)}, u32[]{:S(2)}) collective-permute-start(f32[256,512]{1,0:T(8,128)S(1)} %bitcast_add_fusion.1), channel_id=1, source_target_pairs={{4,0},{8,4},{12,8},{14,12},{10,14},{6,10},{2,6},{0,2},{5,1},{9,5},... | collective-permute-start | bytes 1572872 | tf_op jit(solution)/shard_map/ppermute | solution.py:367
  238.1 42.2 %collective-permute-start.18 = (bf16[256,256]{1,0:T(8,128)(2,1)S(1)}, bf16[256,256]{1,0:T(8,128)(2,1)S(1)}, u32[]{:S(2)}, u32[]{:S(2)}) collective-permute-start(bf16[256,256]{1,0:T(8,128)(2,1)S(1)} %get-tuple-element.25), channel_id=1, source_target_pairs={{0,5},{1,6},{2,7},{3,8},{4,9},{5,10},{6,11},{7,12},{8,13},{9,14},{... | collective-permute-start | bytes 393224 | tf_op jit(solution)/shard_map/ppermute | solution.py:403
  238.2 42.2 %collective-permute-start.19 = (bf16[256,256]{1,0:T(8,128)(2,1)S(1)}, bf16[256,256]{1,0:T(8,128)(2,1)S(1)}, u32[]{:S(2)}, u32[]{:S(2)}) collective-permute-start(bf16[256,256]{1,0:T(8,128)(2,1)S(1)} %get-tuple-element.24), channel_id=1, source_target_pairs={{0,6},{1,7},{2,8},{3,9},{4,10},{5,11},{6,12},{7,13},{8,14},{9,15},... | collective-permute-start | bytes 393224 | tf_op jit(solution)/shard_map/ppermute | solution.py:403
  238.3 42.1 %collective-permute-start.20 = (bf16[256,256]{1,0:T(8,128)(2,1)S(1)}, bf16[256,256]{1,0:T(8,128)(2,1)S(1)}, u32[]{:S(2)}, u32[]{:S(2)}) collective-permute-start(bf16[256,256]{1,0:T(8,128)(2,1)S(1)} %get-tuple-element.23), channel_id=1, source_target_pairs={{0,7},{1,8},{2,9},{3,10},{4,11},{5,12},{6,13},{7,14},{8,15},{9,0},... | collective-permute-start | bytes 393224 | tf_op jit(solution)/shard_map/ppermute | solution.py:403
  251.2 7.2 %collective-permute-start.14 = (bf16[256,256]{1,0:T(8,128)(2,1)S(1)}, bf16[256,256]{1,0:T(8,128)(2,1)S(1)}, u32[]{:S(2)}, u32[]{:S(2)}) collective-permute-start(bf16[256,256]{1,0:T(8,128)(2,1)S(1)} %get-tuple-element.22), channel_id=1, source_target_pairs={{0,1},{1,2},{2,3},{3,4},{4,5},{5,6},{6,7},{7,8},{8,9},{9,10},{10,1... | collective-permute-start | bytes 393224 | tf_op jit(solution)/shard_map/ppermute | solution.py:403
  258.4 7.7 %collective-permute-start.15 = (bf16[256,256]{1,0:T(8,128)(2,1)S(1)}, bf16[256,256]{1,0:T(8,128)(2,1)S(1)}, u32[]{:S(2)}, u32[]{:S(2)}) collective-permute-start(bf16[256,256]{1,0:T(8,128)(2,1)S(1)} %get-tuple-element.21), channel_id=1, source_target_pairs={{0,2},{1,3},{2,4},{3,5},{4,6},{5,7},{6,8},{7,9},{8,10},{9,11},{10,... | collective-permute-start | bytes 393224 | tf_op jit(solution)/shard_map/ppermute | solution.py:403
  266.0 6.2 %collective-permute-start.16 = (bf16[256,256]{1,0:T(8,128)(2,1)S(1)}, bf16[256,256]{1,0:T(8,128)(2,1)S(1)}, u32[]{:S(2)}, u32[]{:S(2)}) collective-permute-start(bf16[256,256]{1,0:T(8,128)(2,1)S(1)} %get-tuple-element.20), channel_id=1, source_target_pairs={{0,3},{1,4},{2,5},{3,6},{4,7},{5,8},{6,9},{7,10},{8,11},{9,12},{10... | collective-permute-start | bytes 393224 | tf_op jit(solution)/shard_map/ppermute | solution.py:403
  272.2 6.8 %collective-permute-start.17 = (bf16[256,256]{1,0:T(8,128)(2,1)S(1)}, bf16[256,256]{1,0:T(8,128)(2,1)S(1)}, u32[]{:S(2)}, u32[]{:S(2)}) collective-permute-start(bf16[256,256]{1,0:T(8,128)(2,1)S(1)} %get-tuple-element.19), channel_id=1, source_target_pairs={{0,4},{1,5},{2,6},{3,7},{4,8},{5,9},{6,10},{7,11},{8,12},{9,13},{1... | collective-permute-start | bytes 393224 | tf_op jit(solution)/shard_map/ppermute | solution.py:403
  279.0 30.0 %collective-permute-start.31 = (f32[256,512]{1,0:T(8,128)S(1)}, f32[256,512]{1,0:T(8,128)S(1)}, u32[]{:S(2)}, u32[]{:S(2)}) collective-permute-start(f32[256,512]{1,0:T(8,128)S(1)} %bitcast_add_fusion.2), channel_id=1, source_target_pairs={{4,0},{8,4},{12,8},{14,12},{10,14},{6,10},{2,6},{0,2},{5,1},{9,5},... | collective-permute-start | bytes 1572872 | tf_op jit(solution)/shard_map/ppermute | solution.py:367
  285.9 110.4 %collective-permute-start.21 = (bf16[256,2048]{1,0:T(8,128)(2,1)}, bf16[256,2048]{1,0:T(8,128)(2,1)}, u32[]{:S(2)}, u32[]{:S(2)}) collective-permute-start(bf16[256,2048]{1,0:T(8,128)(2,1)} %get-tuple-element.13), channel_id=1, source_target_pairs={{0,1},{1,0},{2,3},{3,2},{4,5},{5,4},{6,7},{7,6},{8,9},{9,8},{10,11... | collective-permute-start | bytes 3145736 | tf_op jit(solution)/shard_map/ppermute | solution.py:406
  309.0 85.7 %copy-start.19 = (s32[256]{0:T(256)S(1)}, s32[256]{0:T(256)}, u32[]{:S(2)}) copy-start(s32[256]{0:T(256)} %param.15) | copy-start | bytes 3076
  397.8 5.6 %copy-start.1 = (bf16[256,4096]{1,0:T(8,128)(2,1)S(1)}, bf16[256,4096]{1,0:T(8,128)(2,1)}, u32[]{:S(2)}) copy-start(bf16[256,4096]{1,0:T(8,128)(2,1)} %param.10) | copy-start | bytes 6291460
  (7 other events, 18.0 us)
Sparse Core Ops, SparseCore 0:
  36.8 77.8 all-reduce.4
  310.9 83.6 all-reduce.6

commit v2 on v0

v2 whole, which is shorter than its diff:
```python
import jax
import jax.numpy as jnp
from jax import lax
from jax.experimental import pallas as pl
from jax.experimental.pallas import tpu as pltpu
from jax.sharding import PartitionSpec as P

R = 64
SEQ = 16
damping = 1.0
EXACT = lax.Precision.HIGHEST
SWAP = [(0, 1), (1, 0)]
VMEM_BYTES = 56 * 1024 * 1024


class Ring:
    def __init__(self, mesh):
        self.count = mesh.shape["dp"]
        self.half = self.count // 2
        coords = [getattr(device, "coords", None) for device in mesh.devices[0, :, 0]]
        self.folded = False
        if None not in coords:
            moving = [axis for axis in range(3) if len({place[axis] for place in coords}) > 1]
            fast = [axis for axis in moving if coords[0][axis] != coords[1][axis]]
            self.folded = len(moving) == 2 and len(fast) == 1 and len({place[fast[0]] for place in coords}) == 2
        reach = [0, 0]
        self.offsets = []
        for distance in range(self.half - 1, 0, -1):
            side = 0 if reach[0] <= reach[1] else 1
            reach[side] += distance
            self.offsets.append(distance if side == 0 else -distance)

    def index_at(self, position):
        if isinstance(position, int):
            position = position % self.count
            if not self.folded:
                return position
            return 2 * position if position < self.half else 2 * (self.count - 1 - position) + 1
        position = lax.rem(position + 2 * self.count, self.count)
        if not self.folded:
            return position
        return jnp.where(position < self.half, 2 * position, 2 * (self.count - 1 - position) + 1)

    def position_of(self, index):
        if not self.folded:
            return index
        return jnp.where(lax.rem(index, 2) == 0, index // 2, self.count - 1 - index // 2)

    def shift(self, step):
        return [(self.index_at(p), self.index_at(p + step)) for p in range(self.count)]


def lead_dot(left, right, precision=None):
    return lax.dot_general(
        left, right, (((0,), (0,)), ((), ())), precision=precision, preferred_element_type=jnp.float32
    )


def exact_dot(left, right):
    return jnp.dot(left, right, precision=EXACT, preferred_element_type=jnp.float32)


def trail_dot(left, right):
    return lax.dot_general(
        left, right, (((1,), (1,)), ((), ())), precision=EXACT, preferred_element_type=jnp.float32
    )


def window_part(ring, place, stored, group, step, slots, arrived, last=False):
    rows = stored.shape[0]
    count = len(slots)

    def position(ref):
        return lax.rem(ring.position_of(ref[0]) + step + 2 * ring.count, ring.count)

    def left_map(ref):
        return 2 * ring.index_at(position(ref)) + ref[1]

    def right_map(slot, ref):
        offset, core = slot
        owner = position(ref)
        if core is None:
            core = jnp.where(owner < ring.half, ref[1], 1 - ref[1])
        return 2 * ring.index_at(owner + offset) + core

    def kernel(place_ref, left_ref, *refs):
        rights, refs = refs[:count], refs[count:]
        sums, outs = refs[: len(arrived)], refs[len(arrived) :]
        turned = left_ref[...].T
        for k in range(count):
            cols = slice(k * group, (k + 1) * group)
            total = jnp.dot(turned, rights[k][...], preferred_element_type=jnp.float32)
            for ref in sums:
                total = total + ref[:, cols].astype(jnp.float32)
            total = total.astype(jnp.bfloat16)
            if last:
                outs[0][k] = total
                outs[1][k] = total.T
            else:
                outs[0][:, cols] = total

    flat = pl.BlockSpec((group, count * group), lambda i, ref: (0, 0))
    if last:
        out_specs = [pl.BlockSpec((count, group, group), lambda i, ref: (0, 0, 0))] * 2
        out_shape = [jax.ShapeDtypeStruct((count, group, group), jnp.bfloat16)] * 2
    else:
        out_specs = flat
        out_shape = jax.ShapeDtypeStruct((group, count * group), jnp.bfloat16)
    in_specs = [pl.BlockSpec((rows, group), lambda i, ref: (0, left_map(ref)))]
    for slot in slots:
        in_specs.append(pl.BlockSpec((rows, group), lambda i, ref, slot=slot: (0, right_map(slot, ref))))
    return pl.pallas_call(
        kernel,
        grid_spec=pltpu.PrefetchScalarGridSpec(
            num_scalar_prefetch=1,
            grid=(1,),
            in_specs=in_specs + [flat] * len(arrived),
            out_specs=out_specs,
        ),
        out_shape=out_shape,
        compiler_params=pltpu.CompilerParams(vmem_limit_bytes=VMEM_BYTES),
        cost_estimate=pl.CostEstimate(
            flops=2 * rows * count * group * group,
            bytes_accessed=2 * rows * group * (count + 1) + 4 * count * group * group,
            transcendentals=0,
        ),
        name="window_part",
    )(place, *([stored] * (count + 1)), *arrived)


def solve_kernel(matrix_ref, right_ref, out_ref, work, inverse, residual):
    size = matrix_ref.shape[0]
    block = inverse.shape[0]
    work[...] = matrix_ref[...]
    out_ref[...] = right_ref[...]
    row_ids = lax.broadcasted_iota(jnp.int32, (block, block), 0)
    col_ids = lax.broadcasted_iota(jnp.int32, (block, block), 1)
    eye = (row_ids == col_ids).astype(jnp.float32)
    for start in range(0, size, block):
        here = slice(start, start + block)
        rest = slice(start + block, size)
        corner = work[here, here]
        norm = jnp.max(jnp.sum(jnp.abs(corner), axis=0))
        inverse[...] = eye / norm
        residual[...] = eye - corner / norm

        def unfinished(state):
            step, worst = state
            return jnp.logical_and(step < 40, worst > 1e-5)

        def improve(state):
            step, _ = state
            better = inverse[...] + exact_dot(inverse[...], residual[...])
            left_over = eye - exact_dot(work[here, here], better)
            inverse[...] = better
            residual[...] = left_over
            return step + 1, jnp.max(jnp.abs(left_over))

        lax.while_loop(unfinished, improve, (jnp.int32(0), jnp.float32(1.0)))
        found = inverse[...] + exact_dot(inverse[...], residual[...])
        solved = exact_dot(found, out_ref[here, :])
        out_ref[here, :] = solved
        if start + block < size:
            across = exact_dot(found, work[here, rest])
            down = work[rest, here]
            work[rest, rest] = work[rest, rest] - exact_dot(down, across)
            out_ref[rest, :] = out_ref[rest, :] - exact_dot(down, solved)
            work[here, rest] = across
    for start in range(size - 2 * block, -1, -block):
        here = slice(start, start + block)
        rest = slice(start + block, size)
        out_ref[here, :] = out_ref[here, :] - exact_dot(work[here, rest], out_ref[rest, :])


def solve(matrix, right):
    size, columns = right.shape
    block = 128
    return pl.pallas_call(
        solve_kernel,
        out_shape=jax.ShapeDtypeStruct((size, columns), jnp.float32),
        scratch_shapes=[
            pltpu.VMEM((size, size), jnp.float32),
            pltpu.VMEM((block, block), jnp.float32),
            pltpu.VMEM((block, block), jnp.float32),
        ],
        compiler_params=pltpu.CompilerParams(vmem_limit_bytes=VMEM_BYTES),
        cost_estimate=pl.CostEstimate(flops=12 * size**3, bytes_accessed=4 * size * (size + 2 * columns), transcendentals=0),
        name="solve",
    )(matrix, right)


def split_terms(value):
    high = value.astype(jnp.bfloat16)
    value = value - high.astype(jnp.float32)
    middle = value.astype(jnp.bfloat16)
    value = value - middle.astype(jnp.float32)
    return high, middle, value.astype(jnp.bfloat16)


def spread_back(place, stored, solved, owners, group):
    rows = stored.shape[0]
    width, examples = solved.shape

    def kernel(place_ref, first_ref, solved_ref, cols_ref, out_ref, terms):
        @pl.when(pl.program_id(0) == 0)
        def _():
            total = jnp.zeros((rows, examples), jnp.float32)
            for term in split_terms(solved_ref[...]):
                total = total + jnp.dot(first_ref[...], term, preferred_element_type=jnp.float32)
            for index, term in enumerate(split_terms(total.T)):
                terms[index * examples : (index + 1) * examples, :] = term

        product = jnp.dot(terms[...], cols_ref[...], preferred_element_type=jnp.float32)
        out_ref[0] = product[:examples] + product[examples : 2 * examples] + product[2 * examples :]

    return pl.pallas_call(
        kernel,
        grid_spec=pltpu.PrefetchScalarGridSpec(
            num_scalar_prefetch=1,
            grid=(owners,),
            in_specs=[
                pl.BlockSpec((rows, width), lambda o, ref: (0, 0)),
                pl.BlockSpec((width, examples), lambda o, ref: (0, 0)),
                pl.BlockSpec((rows, group), lambda o, ref: (0, 2 * o + ref[1])),
            ],
            out_specs=pl.BlockSpec((1, examples, group), lambda o, ref: (o, 0, 0)),
            scratch_shapes=[pltpu.VMEM((3 * examples, rows), jnp.bfloat16)],
        ),
        out_shape=jax.ShapeDtypeStruct((owners, examples, group), jnp.float32),
        compiler_params=pltpu.CompilerParams(vmem_limit_bytes=VMEM_BYTES),
        cost_estimate=pl.CostEstimate(
            flops=6 * rows * examples * (width + owners * group),
            bytes_accessed=2 * rows * (width + owners * group) + 4 * owners * examples * group,
            transcendentals=0,
        ),
        name="spread_back",
    )(place, stored, solved, stored)


def source_table(ring, slots):
    table = [0] * ring.count
    held = [0] * ring.count
    for index, (offset, core) in enumerate(slots):
        if core is None:
            table[ring.half] = index
            held[ring.half] = -1
        elif core == 0:
            table[offset % ring.count] = index
    place = len(slots)
    for offset in ring.offsets:
        table[-offset % ring.count] = place
        held[-offset % ring.count] = 1
        place += 2
    return table, held, place


def for_sibling(ring, place, table, held, arrived_quarter, blocks, group):
    fetch = block_fetch(ring, table, arrived_quarter)

    def chip(c, ref):
        return (1 - ref[1]) * ring.half + c

    def kernel(place_ref, first_ref, second_ref, out_ref):
        out_ref[0] = first_ref[0]
        out_ref[1] = second_ref[0]

    return pl.pallas_call(
        kernel,
        grid_spec=pltpu.PrefetchScalarGridSpec(
            num_scalar_prefetch=1,
            grid=(ring.half,),
            in_specs=[
                pl.BlockSpec((1, group, group), lambda c, ref, j=j: (fetch(chip(c, ref), j, ref), 0, 0)) for j in (0, 1)
            ],
            out_specs=pl.BlockSpec((2, group, group), lambda c, ref: (c, 0, 0)),
        ),
        out_shape=jax.ShapeDtypeStruct((2 * ring.half, group, group), jnp.bfloat16),
        compiler_params=pltpu.CompilerParams(vmem_limit_bytes=VMEM_BYTES),
        name="for_sibling",
    )(place, blocks, blocks)


def block_fetch(ring, table, arrived_quarter):
    def fetch(chip, j, ref):
        here = ring.position_of(ref[0])
        offset = lax.rem(ring.position_of(chip) - here + 2 * ring.count, ring.count)
        found = jnp.int32(0)
        for index, start in enumerate(table):
            found = jnp.where(offset == index, start, found)
        own = (j == ref[1]) == (here < ring.half)
        quarter = jnp.where(own, table[ring.half], arrived_quarter)
        return jnp.where(offset == ring.half, quarter, found + j)

    return fetch


def finish(ring, place, table, held, arrived_quarter, blocks, other, vectors, group):
    examples = vectors.shape[0]
    fetch = block_fetch(ring, table, arrived_quarter)

    def chip(c, ref):
        return ref[1] * ring.half + c

    def by_columns(c, ref):
        here = ring.position_of(ref[0])
        offset = lax.rem(ring.position_of(chip(c, ref)) - here + 2 * ring.count, ring.count)
        found = jnp.int32(0)
        for index, kind in enumerate(held):
            if kind == 1:
                found = jnp.where(offset == index, 1, found)
        return jnp.where(offset == ring.half, (here < ring.half).astype(jnp.int32), found) == 1

    def local_map(c, r, u, ref):
        return fetch(chip(c, ref), jnp.where(by_columns(c, ref), r, u), ref), 0, 0

    def other_map(c, r, u, ref):
        return 2 * c + jnp.where(by_columns(c, ref), r, u), 0, 0

    def kernel(place_ref, local_a, local_b, other_a, other_b, rows_ref, cols_ref, out_ref):
        c, r = pl.program_id(0), pl.program_id(1)
        added = jnp.dot(rows_ref[...].T, cols_ref[...], preferred_element_type=jnp.float32)
        row_ids = (2 * place_ref[0] + r) * group + lax.broadcasted_iota(jnp.int32, added.shape, 0)
        col_ids = 2 * chip(c, place_ref) * group + lax.broadcasted_iota(jnp.int32, added.shape, 1)
        added = added + jnp.where(row_ids == col_ids, jnp.float32(damping), jnp.float32(0.0))
        columns = by_columns(c, place_ref)
        for u, local_ref, other_ref in ((0, local_a, other_a), (1, local_b, other_b)):
            cols = slice(u * group, (u + 1) * group)
            mine = jnp.where(columns, u, r) == place_ref[1]

            @pl.when(mine)
            def _():
                out_ref[:, cols] = added[:, cols] + local_ref[0].astype(jnp.float32)

            @pl.when(jnp.logical_not(mine))
            def _():
                out_ref[:, cols] = added[:, cols] + other_ref[0].astype(jnp.float32)

    one = (1, group, group)
    return pl.pallas_call(
        kernel,
        grid_spec=pltpu.PrefetchScalarGridSpec(
            num_scalar_prefetch=1,
            grid=(ring.half, 2),
            in_specs=[pl.BlockSpec(one, lambda c, r, ref, u=u: local_map(c, r, u, ref)) for u in (0, 1)]
            + [pl.BlockSpec(one, lambda c, r, ref, u=u: other_map(c, r, u, ref)) for u in (0, 1)]
            + [
                pl.BlockSpec((examples, group), lambda c, r, ref: (0, 2 * ref[0] + r)),
                pl.BlockSpec((examples, 2 * group), lambda c, r, ref: (0, chip(c, ref))),
            ],
            out_specs=pl.BlockSpec((group, 2 * group), lambda c, r, ref: (r, c)),
        ),
        out_shape=jax.ShapeDtypeStruct((2 * group, 2 * ring.half * group), jnp.float32),
        compiler_params=pltpu.CompilerParams(vmem_limit_bytes=VMEM_BYTES),
        name="finish",
    )(place, blocks, blocks, other, other, vectors, vectors)


def in_order(index, mine, other, axis):
    return jnp.where(
        index == 0,
        jnp.concatenate([mine, other], axis=axis),
        jnp.concatenate([other, mine], axis=axis),
    )


def pair_swap(value, count):
    return lax.ppermute(value, "dp", [(index, index ^ 1) for index in range(count)])


def far_shift(value, step, count):
    return lax.ppermute(value, "dp", [(index, (index + 2 * step) % count) for index in range(count)])


def scatter_pairs(value, pair, count):
    pairs = count // 2
    size = value.shape[0] // pairs

    def slice_of(index):
        return lax.dynamic_slice_in_dim(value, index * size, size, 0)

    total = slice_of(pair)
    for step in range(1, pairs):
        total = total + far_shift(slice_of(lax.rem(pair + step, pairs)), step, count)
    return total


def gather_pairs(value, pair, count):
    pairs = count // 2
    size = value.shape[0]
    whole = jnp.zeros((pairs * size,) + value.shape[1:], value.dtype)
    whole = lax.dynamic_update_slice_in_dim(whole, value, pair * size, 0)
    for step in range(1, pairs):
        came = far_shift(value, step, count)
        whole = lax.dynamic_update_slice_in_dim(whole, came, lax.rem(pair - step + pairs, pairs) * size, 0)
    return whole


def local(ring, activations, out_grads, proj_in, proj_out, stored, counts, query_ids):
    owners = ring.count
    full = stored.shape[1]
    width = full // owners
    group = width // 2
    half = ring.half
    t = lax.axis_index("tensor")
    d = lax.axis_index("dp")
    pair, side = d // 2, lax.rem(d, 2)
    g = 2 * d + t
    place = jnp.stack([d, t]).astype(jnp.int32)

    first_stored = stored[:, :width]
    corner_rows = lead_dot(lax.dynamic_slice_in_dim(first_stored, t * group, group, 1), first_stored)
    corner_rows = scatter_pairs(corner_rows, pair, owners)
    corner_rows = gather_pairs(corner_rows + pair_swap(corner_rows, owners), pair, owners)
    corner = in_order(t, corner_rows, lax.ppermute(corner_rows, "tensor", SWAP), 0)

    sides = jnp.concatenate(
        [
            jnp.dot(activations, proj_in, preferred_element_type=jnp.float32),
            jnp.dot(out_grads, proj_out, preferred_element_type=jnp.float32),
        ],
        axis=1,
    )
    sides = sides + lax.ppermute(sides, "tensor", SWAP)

    examples = counts.shape[0]
    rank = proj_in.shape[1]
    position = jnp.arange(SEQ, dtype=jnp.int32)[None, :]
    weights = jnp.where(
        position < counts[:, None], 1.0 / counts.astype(jnp.float32)[:, None], jnp.float32(0.0)
    )
    act_half = lax.dynamic_slice_in_dim(sides, t * (rank // 2), rank // 2, 1)
    outer = jnp.einsum(
        "es,esi,esj->eij",
        weights,
        act_half.reshape(examples, SEQ, rank // 2),
        sides[:, rank:].reshape(examples, SEQ, rank),
        precision=EXACT,
    )
    own_half = outer.reshape(examples, full // 2).astype(jnp.bfloat16)
    pair_half = in_order(side, own_half, pair_swap(own_half, owners), 0)
    gathered_half = gather_pairs(pair_half, pair, owners)
    vectors = in_order(t, gathered_half, lax.ppermute(gathered_half, "tensor", SWAP), 1)

    split = (len(ring.offsets) + 1) // 2
    far_slots = [(half, None)]
    for offset in ring.offsets[:split]:
        far_slots += [(offset, 0), (offset, 1)]
    near_slots = []
    for offset in ring.offsets[split:] + [0]:
        near_slots += [(offset, 0), (offset, 1)]

    def part(step, slots, arrived, last=False):
        return window_part(ring, place, stored, group, step, slots, arrived, last)

    ahead, back = ring.shift(1), ring.shift(-1)
    far_ahead, far_back, near_ahead, near_back = [], [], [], []
    for step in range(half, 0, -1):
        far_ahead = [lax.ppermute(part(step, far_slots, far_ahead), "dp", ahead)]
        if step < half:
            far_back = [lax.ppermute(part(-step, far_slots, far_back), "dp", back)]
    for step in range(half, 0, -1):
        near_back = [lax.ppermute(part(-step, near_slots, near_back), "dp", back)]
        if step < half:
            near_ahead = [lax.ppermute(part(step, near_slots, near_ahead), "dp", ahead)]

    all_examples = vectors.shape[0]
    first_cols = vectors[:, :width]
    eye = jnp.eye(width, dtype=jnp.float32)
    corner = corner + lead_dot(first_cols, first_cols) + damping * eye
    scale = lax.rsqrt(jnp.sum(corner * eye, axis=1))
    first_cols = first_cols.astype(jnp.float32)
    solved = solve(corner * scale[:, None] * scale[None, :], first_cols.T * scale[:, None]) * scale[:, None]
    first_pairs = exact_dot(first_cols, solved)
    terms = spread_back(place, stored, solved, owners, group)
    terms = scatter_pairs(terms, pair, owners)
    away = lax.dynamic_index_in_dim(terms, 1 - side, 0, keepdims=False)
    terms = lax.dynamic_index_in_dim(terms, side, 0, keepdims=False) + pair_swap(away, owners)
    own_cols = lax.dynamic_slice_in_dim(vectors, g * group, group, 1).astype(jnp.float32)
    damped = lax.dynamic_slice_in_dim(solved.T, lax.rem(g, 2) * group, group, 1)
    damped = jnp.where(g < 2, damping * damped, 0.0)
    rest = own_cols - lead_dot(first_pairs, own_cols, EXACT) - terms - damped
    pairs = trail_dot(rest, rest) + jnp.where(g == 0, first_pairs, 0.0)
    pairs = scatter_pairs(pairs, pair, owners)
    away = lax.dynamic_slice_in_dim(pairs, (1 - side) * examples, examples, 0)
    pairs = lax.dynamic_slice_in_dim(pairs, side * examples, examples, 0) + pair_swap(away, owners)
    pairs = pairs + lax.ppermute(pairs, "tensor", SWAP)
    chosen = (query_ids[:, None] == jnp.arange(all_examples, dtype=jnp.int32)[None, :]).astype(jnp.float32)
    scores = trail_dot(chosen, pairs) / R

    far, far_turned = part(0, far_slots, far_ahead + far_back, last=True)
    near, near_turned = part(0, near_slots, near_ahead + near_back, last=True)
    slots = far_slots + near_slots
    came = []
    for offset in ring.offsets + [half]:
        if offset == half:
            block = far_turned[:1]
        elif (offset, 0) in far_slots:
            block = far_turned[far_slots.index((offset, 0)) :][:2]
        else:
            block = near_turned[near_slots.index((offset, 0)) :][:2]
        came.append(lax.ppermute(block, "dp", ring.shift(offset)))
    blocks = jnp.concatenate([far, near] + came, axis=0)
    table, held, arrived_quarter = source_table(ring, slots)
    send = for_sibling(ring, place, table, held, arrived_quarter, blocks, group)
    other = lax.ppermute(send, "tensor", SWAP)
    return finish(ring, place, table, held, arrived_quarter, blocks, other, vectors, group), scores


def solution(mesh):
    placed = (
        P(("groups", "dp"), "tensor"),
        P(("groups", "dp"), "tensor"),
        P("tensor", None),
        P("tensor", None),
        P(("groups", "dp"), None),
        P(("groups", "dp")),
        P("groups"),
    )
    ring = Ring(mesh)

    def program(*args):
        return local(ring, *args)

    return jax.shard_map(
        program,
        mesh=mesh,
        in_specs=placed,
        out_specs=(P(("groups", "dp"), "tensor"), P("groups", "dp")),
        check_vma=False,
    )
```

time: 995 us -> 308 us (0.31)
  waiting for transfers between devices: 713 us -> 73.1 us
  other arithmetic: 130 us -> 6.56 us
  Pallas kernels: 0 us -> 119 us
  matrix products: 97.9 us -> 10.2 us
  starting transfers between devices: 0.38 us -> 55.3 us
  local copies, waits for them, and re-layouts: 24.4 us -> 41 us
  between operations: 16.9 us -> 1.17 us
    reduce_scatter x1 -> x0, waiting for transfers between devices: 546 us -> none  [local(): lax.psum_scatter(gram_rows(width * lax.axis_size('dp')), 'dp', scatter_di...]
    psum x3 -> x0, waiting for transfers between devices: 167 us -> none  [the longest x1 141 us: local(): panel_block = lax.psum(gram_rows(width), 'dp')]
    pallas_call x0 -> x20, Pallas kernels: none -> 119 us  [the longest x16 68.8 us: window_part(): pl.pallas_call(kernel, grid_spec=pltpu.PrefetchScalarGridSpec(num_scalar_...]
    another operation x17 -> x1, other arithmetic: 118 us -> 0.6 us  [local(): place = jnp.stack([d, t]).astype(jnp.int32)]
    ppermute x0 -> x42, waiting for transfers between devices: none -> 73.1 us  [the longest x15 45.6 us: far_shift(): lax.ppermute(value, 'dp', [(index, (index + 2 * step) % count) for index...]
    dot_general x8 -> x3, matrix products: 62.2 us -> 1.05 us  [lead_dot(): lax.dot_general(left, right, (((0,), (0,)), ((), ())), precision=precisio...]
    ppermute x0 -> x42, starting transfers between devices: none -> 55.3 us  [the longest x15 20 us: far_shift(): lax.ppermute(value, 'dp', [(index, (index + 2 * step) % count) for index...]
    another operation x27 -> x0, matrix products: 27.2 us -> none  [the longest x7 17.9 us: local(): lax.linalg.triangular_solve(corner, panel_block, left_side=True, lower=True)]
  transfers between devices with their start and end apart: 5 -> 42, of which waited for: 4 -> 11; matrix products, arithmetic and copies ran while one was open for 7% -> 14% of each run, Pallas kernels for 0% -> 36%
where the time goes in v2:
time: 308 us; the launch traced here: 306 us
  Pallas kernels  119 us (39%)
  waiting for transfers between devices  73.1 us (24%)
  starting transfers between devices  55.3 us (18%)
  local copies, waits for them, and re-layouts  41 us (13%)
  matrix products  10.2 us (3%)
  other arithmetic  6.56 us (2%)
    pallas_call x16, Pallas kernels, window_part(): pl.pallas_call(kernel, grid_spec=pltpu.PrefetchScalarGridSpec(num_scalar_...  68.8 us
    ppermute x15, waiting for transfers between devices, far_shift(): lax.ppermute(value, 'dp', [(index, (index + 2 * step) % count) for index...  45.6 us
    pallas_call x1, Pallas kernels, solve(): pl.pallas_call(solve_kernel, out_shape=jax.ShapeDtypeStruct((size, column...  27.5 us
    ppermute x4, waiting for transfers between devices, local(): came.append(lax.ppermute(block, 'dp', ring.shift(offset)))  20.2 us
    ppermute x15, starting transfers between devices, far_shift(): lax.ppermute(value, 'dp', [(index, (index + 2 * step) % count) for index...  20 us
    dynamic_update_slice x6, local copies, waits for them, and re-layouts, gather_pairs(): lax.dynamic_update_slice_in_dim(whole, came, lax.rem(pair - step + pairs,...  19.9 us
    ppermute x4, starting transfers between devices, local(): came.append(lax.ppermute(block, 'dp', ring.shift(offset)))  14.6 us
    pallas_call x1, Pallas kernels, spread_back(): pl.pallas_call(kernel, grid_spec=pltpu.PrefetchScalarGridSpec(num_scalar_...  9.35 us
  transfers between devices with their start and end apart: 42, of which 11 were waited for; matrix products, arithmetic and copies ran while one was open for 14% of the time, Pallas kernels for 36%

profile of v2, /device:TPU:0, one launch (start us, length us, event | category | flops | bytes accessed | tf_op | source)
XLA Modules:
  0.0 305.9 jit_solution(5232820930512050333)
XLA Ops:
  0.7 6.1 %fusion.32 = f32[256,64]{0,1:T(8,128)S(1)} fusion(bf16[256,14336]{1,0:T(8,128)(2,1)} %param.7, bf16[14336,64]{0,1:T(8,128)(2,1)} %param.9), kind=kOutput, calls=%fused_computation.76 | convolution fusion | flops 469762048 | bytes 9240576 | tf_op jit(solution)/shard_map/dot_general | solution.py:418
  8.6 3.0 collective-permute-start.25
  11.6 2.1 collective-permute-start.27
  19.7 6.2 %collective-permute-done.26 = f32[64,512]{1,0:T(8,128)S(1)} collective-permute-done((f32[64,512]{1,0:T(8,128)S(1)}, f32[64,512]{1,0:T(8,128)S(1)}, u32[]{:S(2)}, u32[]{:S(2)}) %collective-permute-start.26) | collective-permute-done | bytes 131104 | tf_op jit(solution)/shard_map/ppermute | solution.py:371
  28.1 1.7 collective-permute-start.23
  32.1 1.8 collective-permute-start.30
  33.9 4.3 %window_part.20 = bf16[256,1280]{1,0:T(8,128)(2,1)} custom-call(s32[2]{0:T(128)} %pad_add_fusion.place_ref, bf16[1024,4096]{1,0:T(8,128)(2,1)} %cols_ref.1, bf16[1024,4096]{1,0:T(8,128)(2,1)} %cols_ref.1, bf16[1024,4096]{1,0:T(8,128)(2,1)} %cols_ref.1, bf16[1024,4096]{1,0:T(8,128)(2,1)} %cols_ref.1, bf16[1024,4096]{1,0:T(8,128)(2,1)} %cols_ref.1, ...), custom_call_target="tpu_custom_call" | custom-call | flops 671088640 | bytes 4456448 | tf_op jit(solution)/shard_map/window_part/pallas_call | solution.py:112
  39.3 4.3 %window_part.16 = bf16[256,1280]{1,0:T(8,128)(2,1)} custom-call(s32[2]{0:T(128)} %pad_add_fusion.place_ref, bf16[1024,4096]{1,0:T(8,128)(2,1)} %cols_ref.1, bf16[1024,4096]{1,0:T(8,128)(2,1)} %cols_ref.1, bf16[1024,4096]{1,0:T(8,128)(2,1)} %cols_ref.1, bf16[1024,4096]{1,0:T(8,128)(2,1)} %cols_ref.1, bf16[1024,4096]{1,0:T(8,128)(2,1)} %cols_ref.1, ...), custom_call_target="tpu_custom_call" | custom-call | flops 671088640 | bytes 4456448 | tf_op jit(solution)/shard_map/window_part/pallas_call | solution.py:112
  44.3 3.9 %window_part.24 = bf16[256,1024]{1,0:T(8,128)(2,1)} custom-call(s32[2]{0:T(128)} %pad_add_fusion.place_ref, bf16[1024,4096]{1,0:T(8,128)(2,1)} %cols_ref.1, bf16[1024,4096]{1,0:T(8,128)(2,1)} %cols_ref.1, bf16[1024,4096]{1,0:T(8,128)(2,1)} %cols_ref.1, bf16[1024,4096]{1,0:T(8,128)(2,1)} %cols_ref.1, bf16[1024,4096]{1,0:T(8,128)(2,1)} %cols_ref.1), custom_call_target="tpu_custom_call" | custom-call | flops 536870912 | bytes 3670016 | tf_op jit(solution)/shard_map/window_part/pallas_call | solution.py:112
  48.2 32.4 %collective-permute-done.22 = bf16[32,2048]{0,1:T(8,128)(2,1)S(1)} collective-permute-done((bf16[32,2048]{0,1:T(8,128)(2,1)S(1)}, bf16[32,2048]{0,1:T(8,128)(2,1)S(1)}, u32[]{:S(2)}, u32[]{:S(2)}) %collective-permute-start.22) | collective-permute-done | bytes 131104 | tf_op jit(solution)/shard_map/ppermute | solution.py:371
  80.6 2.1 collective-permute-start.4
  84.4 3.9 %window_part.27 = bf16[256,1024]{1,0:T(8,128)(2,1)} custom-call(s32[2]{0:T(128)} %pad_add_fusion.place_ref, bf16[1024,4096]{1,0:T(8,128)(2,1)} %cols_ref.1, bf16[1024,4096]{1,0:T(8,128)(2,1)} %cols_ref.1, bf16[1024,4096]{1,0:T(8,128)(2,1)} %cols_ref.1, bf16[1024,4096]{1,0:T(8,128)(2,1)} %cols_ref.1, bf16[1024,4096]{1,0:T(8,128)(2,1)} %cols_ref.1), custom_call_target="tpu_custom_call" | custom-call | flops 536870912 | bytes 3670016 | tf_op jit(solution)/shard_map/window_part/pallas_call | solution.py:112
  89.6 2.0 dynamic_update_slice.24
  91.6 5.8 %dynamic_update_slice.25 = bf16[128,2048]{0,1:T(8,128)(2,1)S(1)} dynamic-update-slice(bf16[128,2048]{0,1:T(8,128)(2,1)S(1)} %dynamic_update_slice.24, bf16[32,2048]{0,1:T(8,128)(2,1)} %copy-done.22, s32[]{:T(128)S(6)} %select_n.128, s32[]{:T(128)} %constant.65.clone.1) | dynamic-update-slice | bytes 262148 | tf_op jit(solution)/shard_map/dynamic_update_slice | solution.py:394
  97.4 5.8 %dynamic_update_slice.26 = bf16[128,2048]{0,1:T(8,128)(2,1)S(1)} dynamic-update-slice(bf16[128,2048]{0,1:T(8,128)(2,1)S(1)} %dynamic_update_slice.25, bf16[32,2048]{0,1:T(8,128)(2,1)} %copy-done.21, s32[]{:T(128)S(6)} %select_n.129, s32[]{:T(128)} %constant.65.clone.1) | dynamic-update-slice | bytes 262148 | tf_op jit(solution)/shard_map/dynamic_update_slice | solution.py:394
  103.2 3.6 %dynamic_update_slice.27 = bf16[128,2048]{0,1:T(8,128)(2,1)S(1)} dynamic-update-slice(bf16[128,2048]{0,1:T(8,128)(2,1)S(1)} %dynamic_update_slice.26, bf16[32,2048]{0,1:T(8,128)(2,1)S(1)} %copy-done.20, s32[]{:T(128)S(6)} %select_n.130, s32[]{:T(128)} %constant.65.clone.1) | dynamic-update-slice | bytes 262148 | tf_op jit(solution)/shard_map/dynamic_update_slice | solution.py:394
  112.5 4.1 %window_part.25 = bf16[256,1024]{1,0:T(8,128)(2,1)} custom-call(s32[2]{0:T(128)} %pad_add_fusion.place_ref, bf16[1024,4096]{1,0:T(8,128)(2,1)} %cols_ref.1, bf16[1024,4096]{1,0:T(8,128)(2,1)} %cols_ref.1, bf16[1024,4096]{1,0:T(8,128)(2,1)} %cols_ref.1, bf16[1024,4096]{1,0:T(8,128)(2,1)} %cols_ref.1, bf16[1024,4096]{1,0:T(8,128)(2,1)} %cols_ref.1, ...), custom_call_target="tpu_custom_call" | custom-call | flops 536870912 | bytes 3670016 | tf_op jit(solution)/shard_map/window_part/pallas_call | solution.py:112
  116.6 2.1 collective-permute-start.8
  118.7 4.1 %window_part.28 = bf16[256,1024]{1,0:T(8,128)(2,1)} custom-call(s32[2]{0:T(128)} %pad_add_fusion.place_ref, bf16[1024,4096]{1,0:T(8,128)(2,1)} %cols_ref.1, bf16[1024,4096]{1,0:T(8,128)(2,1)} %cols_ref.1, bf16[1024,4096]{1,0:T(8,128)(2,1)} %cols_ref.1, bf16[1024,4096]{1,0:T(8,128)(2,1)} %cols_ref.1, bf16[1024,4096]{1,0:T(8,128)(2,1)} %cols_ref.1, ...), custom_call_target="tpu_custom_call" | custom-call | flops 536870912 | bytes 3670016 | tf_op jit(solution)/shard_map/window_part/pallas_call | solution.py:112
  123.6 4.5 %window_part.17 = bf16[256,1280]{1,0:T(8,128)(2,1)} custom-call(s32[2]{0:T(128)} %pad_add_fusion.place_ref, bf16[1024,4096]{1,0:T(8,128)(2,1)} %cols_ref.1, bf16[1024,4096]{1,0:T(8,128)(2,1)} %cols_ref.1, bf16[1024,4096]{1,0:T(8,128)(2,1)} %cols_ref.1, bf16[1024,4096]{1,0:T(8,128)(2,1)} %cols_ref.1, bf16[1024,4096]{1,0:T(8,128)(2,1)} %cols_ref.1, ...), custom_call_target="tpu_custom_call" | custom-call | flops 671088640 | bytes 4456448 | tf_op jit(solution)/shard_map/window_part/pallas_call | solution.py:112
  129.3 4.5 %window_part.21 = bf16[256,1280]{1,0:T(8,128)(2,1)} custom-call(s32[2]{0:T(128)} %pad_add_fusion.place_ref, bf16[1024,4096]{1,0:T(8,128)(2,1)} %cols_ref.1, bf16[1024,4096]{1,0:T(8,128)(2,1)} %cols_ref.1, bf16[1024,4096]{1,0:T(8,128)(2,1)} %cols_ref.1, bf16[1024,4096]{1,0:T(8,128)(2,1)} %cols_ref.1, bf16[1024,4096]{1,0:T(8,128)(2,1)} %cols_ref.1, ...), custom_call_target="tpu_custom_call" | custom-call | flops 671088640 | bytes 4456448 | tf_op jit(solution)/shard_map/window_part/pallas_call | solution.py:112
  137.3 27.5 %solve.1 = f32[512,128]{1,0:T(8,128)} custom-call(f32[512,512]{1,0:T(8,128)} %multiply_multiply_fusion.matrix_ref, f32[512,128]{1,0:T(8,128)} %multiply_bitcast_fusion.right_ref), custom_call_target="tpu_custom_call" | custom-call | flops 1610612736 | bytes 1572864 | tf_op jit(solution)/shard_map/solve/pallas_call | solution.py:178
  164.8 1.8 broadcast_multiply_fusion.solved_ref
  167.4 4.5 %window_part.18 = bf16[256,1280]{1,0:T(8,128)(2,1)} custom-call(s32[2]{0:T(128)} %pad_add_fusion.place_ref, bf16[1024,4096]{1,0:T(8,128)(2,1)} %cols_ref.1, bf16[1024,4096]{1,0:T(8,128)(2,1)} %cols_ref.1, bf16[1024,4096]{1,0:T(8,128)(2,1)} %cols_ref.1, bf16[1024,4096]{1,0:T(8,128)(2,1)} %cols_ref.1, bf16[1024,4096]{1,0:T(8,128)(2,1)} %cols_ref.1, ...), custom_call_target="tpu_custom_call" | custom-call | flops 671088640 | bytes 4456448 | tf_op jit(solution)/shard_map/window_part/pallas_call | solution.py:112
  173.9 4.1 %window_part.29 = bf16[256,1024]{1,0:T(8,128)(2,1)} custom-call(s32[2]{0:T(128)} %pad_add_fusion.place_ref, bf16[1024,4096]{1,0:T(8,128)(2,1)} %cols_ref.1, bf16[1024,4096]{1,0:T(8,128)(2,1)} %cols_ref.1, bf16[1024,4096]{1,0:T(8,128)(2,1)} %cols_ref.1, bf16[1024,4096]{1,0:T(8,128)(2,1)} %cols_ref.1, bf16[1024,4096]{1,0:T(8,128)(2,1)} %cols_ref.1, ...), custom_call_target="tpu_custom_call" | custom-call | flops 536870912 | bytes 3670016 | tf_op jit(solution)/shard_map/window_part/pallas_call | solution.py:112
  178.8 9.4 %spread_back.1 = f32[8,128,256]{2,1,0:T(8,128)} custom-call(s32[2]{0:T(128)} %pad_add_fusion.place_ref, bf16[1024,4096]{1,0:T(8,128)(2,1)} %cols_ref.1, f32[512,128]{1,0:T(8,128)} %broadcast_multiply_fusion.solved_ref, bf16[1024,4096]{1,0:T(8,128)(2,1)} %cols_ref.1), custom_call_target="tpu_custom_call" | custom-call | flops 2013265920 | bytes 6291456 | tf_op jit(solution)/shard_map/spread_back/pallas_call | solution.py:216
  190.9 2.7 collective-permute-start.35
  193.6 4.5 %window_part.22 = bf16[256,1280]{1,0:T(8,128)(2,1)} custom-call(s32[2]{0:T(128)} %pad_add_fusion.place_ref, bf16[1024,4096]{1,0:T(8,128)(2,1)} %cols_ref.1, bf16[1024,4096]{1,0:T(8,128)(2,1)} %cols_ref.1, bf16[1024,4096]{1,0:T(8,128)(2,1)} %cols_ref.1, bf16[1024,4096]{1,0:T(8,128)(2,1)} %cols_ref.1, bf16[1024,4096]{1,0:T(8,128)(2,1)} %cols_ref.1, ...), custom_call_target="tpu_custom_call" | custom-call | flops 671088640 | bytes 4456448 | tf_op jit(solution)/shard_map/window_part/pallas_call | solution.py:112
  198.9 4.5 %window_part.19 = bf16[256,1280]{1,0:T(8,128)(2,1)} custom-call(s32[2]{0:T(128)} %pad_add_fusion.place_ref, bf16[1024,4096]{1,0:T(8,128)(2,1)} %cols_ref.1, bf16[1024,4096]{1,0:T(8,128)(2,1)} %cols_ref.1, bf16[1024,4096]{1,0:T(8,128)(2,1)} %cols_ref.1, bf16[1024,4096]{1,0:T(8,128)(2,1)} %cols_ref.1, bf16[1024,4096]{1,0:T(8,128)(2,1)} %cols_ref.1, ...), custom_call_target="tpu_custom_call" | custom-call | flops 671088640 | bytes 4456448 | tf_op jit(solution)/shard_map/window_part/pallas_call | solution.py:112
  203.5 2.0 collective-permute-start.6
  205.8 4.1 %window_part.26 = bf16[256,1024]{1,0:T(8,128)(2,1)} custom-call(s32[2]{0:T(128)} %pad_add_fusion.place_ref, bf16[1024,4096]{1,0:T(8,128)(2,1)} %cols_ref.1, bf16[1024,4096]{1,0:T(8,128)(2,1)} %cols_ref.1, bf16[1024,4096]{1,0:T(8,128)(2,1)} %cols_ref.1, bf16[1024,4096]{1,0:T(8,128)(2,1)} %cols_ref.1, bf16[1024,4096]{1,0:T(8,128)(2,1)} %cols_ref.1, ...), custom_call_target="tpu_custom_call" | custom-call | flops 536870912 | bytes 3670016 | tf_op jit(solution)/shard_map/window_part/pallas_call | solution.py:112
  209.9 4.1 %window_part.30 = bf16[256,1024]{1,0:T(8,128)(2,1)} custom-call(s32[2]{0:T(128)} %pad_add_fusion.place_ref, bf16[1024,4096]{1,0:T(8,128)(2,1)} %cols_ref.1, bf16[1024,4096]{1,0:T(8,128)(2,1)} %cols_ref.1, bf16[1024,4096]{1,0:T(8,128)(2,1)} %cols_ref.1, bf16[1024,4096]{1,0:T(8,128)(2,1)} %cols_ref.1, bf16[1024,4096]{1,0:T(8,128)(2,1)} %cols_ref.1, ...), custom_call_target="tpu_custom_call" | custom-call | flops 536870912 | bytes 3670016 | tf_op jit(solution)/shard_map/window_part/pallas_call | solution.py:112
  219.7 1.7 copy.33
  221.3 1.7 collective-permute-start.36
  223.0 3.3 %collective-permute-done.6.refs_6_ = bf16[256,1280]{1,0:T(8,128)(2,1)S(1)} collective-permute-done((bf16[256,1280]{1,0:T(8,128)(2,1)S(1)}, bf16[256,1280]{1,0:T(8,128)(2,1)S(1)}, u32[]{:S(2)}, u32[]{:S(2)}) %collective-permute-start.6) | collective-permute-done | bytes 655392 | tf_op jit(solution)/shard_map/ppermute | solution.py:460
  228.0 5.0 %window_part.23 = (bf16[5,256,256]{2,1,0:T(8,128)(2,1)}, bf16[5,256,256]{2,1,0:T(8,128)(2,1)}) custom-call(s32[2]{0:T(128)} %pad_add_fusion.place_ref, bf16[1024,4096]{1,0:T(8,128)(2,1)} %cols_ref.1, bf16[1024,4096]{1,0:T(8,128)(2,1)} %cols_ref.1, bf16[1024,4096]{1,0:T(8,128)(2,1)} %cols_ref.1, bf16[1024,4096]{1,0:T(8,128)(2,1)} %cols_ref.1, ...), custom_call_target="tpu_custom_call" | custom-call | flops 671088640 | bytes 4456448 | tf_op jit(solution)/shard_map/window_part/pallas_call | solution.py:112
  234.0 2.5 collective-permute-start.14
  236.5 4.4 %window_part.31 = (bf16[4,256,256]{2,1,0:T(8,128)(2,1)}, bf16[4,256,256]{2,1,0:T(8,128)(2,1)}) custom-call(s32[2]{0:T(128)} %pad_add_fusion.place_ref, bf16[1024,4096]{1,0:T(8,128)(2,1)} %cols_ref.1, bf16[1024,4096]{1,0:T(8,128)(2,1)} %cols_ref.1, bf16[1024,4096]{1,0:T(8,128)(2,1)} %cols_ref.1, bf16[1024,4096]{1,0:T(8,128)(2,1)} %cols_ref.1, ...), custom_call_target="tpu_custom_call" | custom-call | flops 536870912 | bytes 3670016 | tf_op jit(solution)/shard_map/window_part/pallas_call | solution.py:112
  242.0 4.6 %collective-permute-start.16 = (bf16[2,256,256]{2,1,0:T(8,128)(2,1)S(1)}, bf16[2,256,256]{2,1,0:T(8,128)(2,1)S(1)}, u32[]{:S(2)}, u32[]{:S(2)}) collective-permute-start(bf16[2,256,256]{2,1,0:T(8,128)(2,1)S(1)} %slice.25), channel_id=1, source_target_pairs={{0,2},{4,0},{8,4},{12,8},{14,12},{10,14},{6,10},{2,6},{1,3},{5,1},... | collective-permute-start | bytes 786440 | tf_op jit(solution)/shard_map/ppermute | solution.py:501
  247.5 2.3 collective-permute-start.17
  249.8 5.2 %collective-permute-start.15 = (bf16[2,256,256]{2,1,0:T(8,128)(2,1)S(1)}, bf16[2,256,256]{2,1,0:T(8,128)(2,1)S(1)}, u32[]{:S(2)}, u32[]{:S(2)}) collective-permute-start(bf16[2,256,256]{2,1,0:T(8,128)(2,1)S(1)} %get-tuple-element.15), channel_id=1, source_target_pairs={{0,6},{4,2},{8,0},{12,4},{14,8},{10,12},{6,14},{2,10},{1,7},{5,3},... | collective-permute-start | bytes 786440 | tf_op jit(solution)/shard_map/ppermute | solution.py:501
  256.3 19.2 %collective-permute-done.15 = bf16[2,256,256]{2,1,0:T(8,128)(2,1)S(1)} collective-permute-done((bf16[2,256,256]{2,1,0:T(8,128)(2,1)S(1)}, bf16[2,256,256]{2,1,0:T(8,128)(2,1)S(1)}, u32[]{:S(2)}, u32[]{:S(2)}) %collective-permute-start.15) | collective-permute-done | bytes 262176 | tf_op jit(solution)/shard_map/ppermute | solution.py:501
  276.8 4.3 %for_sibling.1 = bf16[8,256,256]{2,1,0:T(8,128)(2,1)} custom-call(s32[2]{0:T(128)} %pad_add_fusion.place_ref, bf16[16,256,256]{2,1,0:T(8,128)(2,1)} %copy-done.2, bf16[16,256,256]{2,1,0:T(8,128)(2,1)} %copy-done.2), custom_call_target="tpu_custom_call" | custom-call | tf_op jit(solution)/shard_map/for_sibling/pallas_call | solution.py:267
  281.6 3.8 %collective-permute-start.39 = (f32[32,128]{1,0:T(8,128)S(1)}, f32[32,128]{1,0:T(8,128)S(1)}, u32[]{:S(2)}, u32[]{:S(2)}) collective-permute-start(f32[32,128]{1,0:T(8,128)S(1)} %get-tuple-element.25), channel_id=1, source_target_pairs={{0,12},{2,14},{4,0},{6,2},{8,4},{10,6},{12,8},{14,10},{1,13},{3,15... | collective-permute-start | bytes 49160 | tf_op jit(solution)/shard_map/ppermute | solution.py:371
  285.4 1.8 collective-permute-done.37
  287.2 2.9 collective-permute-done.38
  290.9 2.9 collective-permute-done.40
  297.0 8.9 %finish.1 = f32[512,2048]{1,0:T(8,128)} custom-call(s32[2]{0:T(128)} %pad_add_fusion.place_ref, bf16[16,256,256]{2,1,0:T(8,128)(2,1)} %copy-done.2, bf16[16,256,256]{2,1,0:T(8,128)(2,1)} %copy-done.2, bf16[8,256,256]{2,1,0:T(8,128)(2,1)} %copy-done.3, bf16[8,256,256]{2,1,0:T(8,128)(2,1)} %copy-done.3, bf16[128,4096]{1,0:T(8,128)(2,1)} %copy.28.rows_ref.cols_ref, ...), custom_call_target="tpu_custom_call" | custom-call | tf_op jit(solution)/shard_map/finish/pallas_call | solution.py:339
  (181 shorter events, 53.1 us)
Async XLA Ops:
  7.5 7.8 %collective-permute-start.19 = (f32[256,128]{0,1:T(8,128)S(1)}, f32[256,128]{0,1:T(8,128)S(1)}, u32[]{:S(2)}, u32[]{:S(2)}) collective-permute-start(f32[256,128]{0,1:T(8,128)S(1)} %pad_maximum_fusion), channel_id=1, source_target_pairs={{0,1},{1,0},{2,3},{3,2},{4,5},{5,4},{6,7},{7,6},{8,9},{9,8},{10,11... | collective-permute-start | bytes 393224 | tf_op jit(solution)/shard_map/ppermute | solution.py:423
  8.6 9.4 %collective-permute-start.25 = (f32[64,512]{1,0:T(8,128)S(1)}, f32[64,512]{1,0:T(8,128)S(1)}, u32[]{:S(2)}, u32[]{:S(2)}) collective-permute-start(f32[64,512]{1,0:T(8,128)S(1)} %get-tuple-element.17), channel_id=1, source_target_pairs={{0,4},{2,6},{4,8},{6,10},{8,12},{10,14},{12,0},{14,2},{1,5},{3,7},... | collective-permute-start | bytes 393224 | tf_op jit(solution)/shard_map/ppermute | solution.py:371
  11.6 8.1 %collective-permute-start.27 = (f32[64,512]{1,0:T(8,128)S(1)}, f32[64,512]{1,0:T(8,128)S(1)}, u32[]{:S(2)}, u32[]{:S(2)}) collective-permute-start(f32[64,512]{1,0:T(8,128)S(1)} %get-tuple-element.18), channel_id=1, source_target_pairs={{0,12},{2,14},{4,0},{6,2},{8,4},{10,6},{12,8},{14,10},{1,13},{3,15... | collective-permute-start | bytes 393224 | tf_op jit(solution)/shard_map/ppermute | solution.py:371
  13.7 12.2 %collective-permute-start.26 = (f32[64,512]{1,0:T(8,128)S(1)}, f32[64,512]{1,0:T(8,128)S(1)}, u32[]{:S(2)}, u32[]{:S(2)}) collective-permute-start(f32[64,512]{1,0:T(8,128)S(1)} %get-tuple-element.19), channel_id=1, source_target_pairs={{0,8},{2,10},{4,12},{6,14},{8,0},{10,2},{12,4},{14,6},{1,9},{3,11}... | collective-permute-start | bytes 393224 | tf_op jit(solution)/shard_map/ppermute | solution.py:371
  16.4 11.0 %collective-permute-start.20 = (bf16[16,2048]{1,0:T(8,128)(2,1)S(1)}, bf16[16,2048]{1,0:T(8,128)(2,1)S(1)}, u32[]{:S(2)}, u32[]{:S(2)}) collective-permute-start(bf16[16,2048]{1,0:T(8,128)(2,1)S(1)} %convert_element_type.21), channel_id=1, source_target_pairs={{0,2},{2,0},{4,6},{6,4},{8,10},{10,8},{12,14},{14,12},{1,3},{3,1},... | collective-permute-start | bytes 196616 | tf_op jit(solution)/shard_map/ppermute | solution.py:367
  25.9 5.5 %collective-permute-start.28 = (f32[64,512]{1,0:T(8,128)S(1)}, f32[64,512]{1,0:T(8,128)S(1)}, u32[]{:S(2)}, u32[]{:S(2)}) collective-permute-start(f32[64,512]{1,0:T(8,128)S(1)} %add_add_fusion.1), channel_id=1, source_target_pairs={{0,2},{2,0},{4,6},{6,4},{8,10},{10,8},{12,14},{14,12},{1,3},{3,1},... | collective-permute-start | bytes 393224 | tf_op jit(solution)/shard_map/ppermute | solution.py:367
  28.1 15.4 %collective-permute-start.23 = (bf16[32,2048]{0,1:T(8,128)(2,1)S(1)}, bf16[32,2048]{0,1:T(8,128)(2,1)S(1)}, u32[]{:S(2)}, u32[]{:S(2)}) collective-permute-start(bf16[32,2048]{0,1:T(8,128)(2,1)S(1)} %broadcast_select_fusion), channel_id=1, source_target_pairs={{0,12},{2,14},{4,0},{6,2},{8,4},{10,6},{12,8},{14,10},{1,13},{3,15... | collective-permute-start | bytes 393224 | tf_op jit(solution)/shard_map/ppermute | solution.py:371
  29.8 50.8 %collective-permute-start.22 = (bf16[32,2048]{0,1:T(8,128)(2,1)S(1)}, bf16[32,2048]{0,1:T(8,128)(2,1)S(1)}, u32[]{:S(2)}, u32[]{:S(2)}) collective-permute-start(bf16[32,2048]{0,1:T(8,128)(2,1)S(1)} %broadcast_select_fusion), channel_id=1, source_target_pairs={{0,8},{2,10},{4,12},{6,14},{8,0},{10,2},{12,4},{14,6},{1,9},{3,11}... | collective-permute-start | bytes 393224 | tf_op jit(solution)/shard_map/ppermute | solution.py:371
  29.8 50.8 %collective-permute-start.21 = (bf16[32,2048]{0,1:T(8,128)(2,1)S(1)}, bf16[32,2048]{0,1:T(8,128)(2,1)S(1)}, u32[]{:S(2)}, u32[]{:S(2)}) collective-permute-start(bf16[32,2048]{0,1:T(8,128)(2,1)S(1)} %broadcast_select_fusion), channel_id=1, source_target_pairs={{0,4},{2,6},{4,8},{6,10},{8,12},{10,14},{12,0},{14,2},{1,5},{3,7},... | collective-permute-start | bytes 393224 | tf_op jit(solution)/shard_map/ppermute | solution.py:371
  32.1 51.3 %collective-permute-start.30 = (f32[64,512]{1,0:T(8,128)}, f32[64,512]{1,0:T(8,128)S(1)}, u32[]{:S(2)}, u32[]{:S(2)}) collective-permute-start(f32[64,512]{1,0:T(8,128)} %get-tuple-element.11), channel_id=1, source_target_pairs={{0,8},{2,10},{4,12},{6,14},{8,0},{10,2},{12,4},{14,6},{1,9},{3,11}... | collective-permute-start | bytes 393224 | tf_op jit(solution)/shard_map/ppermute | solution.py:371
  38.2 50.1 %collective-permute-start.29 = (f32[64,512]{1,0:T(8,128)}, f32[64,512]{1,0:T(8,128)S(1)}, u32[]{:S(2)}, u32[]{:S(2)}) collective-permute-start(f32[64,512]{1,0:T(8,128)} %get-tuple-element.11), channel_id=1, source_target_pairs={{0,4},{2,6},{4,8},{6,10},{8,12},{10,14},{12,0},{14,2},{1,5},{3,7},... | collective-permute-start | bytes 393224 | tf_op jit(solution)/shard_map/ppermute | solution.py:371
  43.6 37.1 %copy-start.6 = (bf16[256,1280]{1,0:T(8,128)(2,1)S(1)}, bf16[256,1280]{1,0:T(8,128)(2,1)}, u32[]{:S(2)}) copy-start(bf16[256,1280]{1,0:T(8,128)(2,1)} %window_part.20) | copy-start | bytes 1966084
  43.6 79.2 %collective-permute-start = (bf16[256,1280]{1,0:T(8,128)(2,1)}, bf16[256,1280]{1,0:T(8,128)(2,1)S(1)}, u32[]{:S(2)}, u32[]{:S(2)}) collective-permute-start(bf16[256,1280]{1,0:T(8,128)(2,1)} %window_part.16), channel_id=1, source_target_pairs={{0,4},{4,8},{8,12},{12,14},{14,10},{10,6},{6,2},{2,0},{1,5},{5,9},... | collective-permute-start | bytes 1966088 | tf_op jit(solution)/shard_map/ppermute | solution.py:458
  80.6 31.0 %collective-permute-start.7 = (bf16[256,1024]{1,0:T(8,128)(2,1)}, bf16[256,1024]{1,0:T(8,128)(2,1)S(1)}, u32[]{:S(2)}, u32[]{:S(2)}) collective-permute-start(bf16[256,1024]{1,0:T(8,128)(2,1)} %window_part.24), channel_id=1, source_target_pairs={{0,4},{4,8},{8,12},{12,14},{14,10},{10,6},{6,2},{2,0},{1,5},{5,9},... | collective-permute-start | bytes 1572872 | tf_op jit(solution)/shard_map/ppermute | solution.py:464
  80.6 47.4 %collective-permute-start.4 = (bf16[256,1280]{1,0:T(8,128)(2,1)S(1)}, bf16[256,1280]{1,0:T(8,128)(2,1)S(1)}, u32[]{:S(2)}, u32[]{:S(2)}) collective-permute-start(bf16[256,1280]{1,0:T(8,128)(2,1)S(1)} %copy-done.6), channel_id=1, source_target_pairs={{0,2},{4,0},{8,4},{12,8},{14,12},{10,14},{6,10},{2,6},{1,3},{5,1},... | collective-permute-start | bytes 1966088 | tf_op jit(solution)/shard_map/ppermute | solution.py:460
  83.4 23.4 %collective-permute-start.31 = (f32[64,512]{1,0:T(8,128)}, f32[64,512]{1,0:T(8,128)}, u32[]{:S(2)}, u32[]{:S(2)}) collective-permute-start(f32[64,512]{1,0:T(8,128)} %get-tuple-element.11), channel_id=1, source_target_pairs={{0,12},{2,14},{4,0},{6,2},{8,4},{10,6},{12,8},{14,10},{1,13},{3,15... | collective-permute-start | bytes 393224 | tf_op jit(solution)/shard_map/ppermute | solution.py:371
  89.0 27.6 %collective-permute-start.10 = (bf16[256,1024]{1,0:T(8,128)(2,1)}, bf16[256,1024]{1,0:T(8,128)(2,1)}, u32[]{:S(2)}, u32[]{:S(2)}) collective-permute-start(bf16[256,1024]{1,0:T(8,128)(2,1)} %window_part.27), channel_id=1, source_target_pairs={{0,2},{4,0},{8,4},{12,8},{14,12},{10,14},{6,10},{2,6},{1,3},{5,1},... | collective-permute-start | bytes 1572872 | tf_op jit(solution)/shard_map/ppermute | solution.py:462
  91.6 11.6 %copy-start.20 = (bf16[32,2048]{0,1:T(8,128)(2,1)S(1)}, bf16[32,2048]{0,1:T(8,128)(2,1)}, u32[]{:S(2)}) copy-start(bf16[32,2048]{0,1:T(8,128)(2,1)} %copy-done.19) | copy-start | bytes 393220
  106.8 27.0 %collective-permute-start.24 = (bf16[128,2048]{0,1:T(8,128)(2,1)S(1)}, bf16[128,2048]{0,1:T(8,128)(2,1)S(1)}, u32[]{:S(2)}, u32[]{:S(2)}) collective-permute-start(bf16[128,2048]{0,1:T(8,128)(2,1)S(1)} %dynamic_update_slice.27), channel_id=1, source_target_pairs={{0,1},{1,0},{2,3},{3,2},{4,5},{5,4},{6,7},{7,6},{8,9},{9,8},{10,11... | collective-permute-start | bytes 1572872 | tf_op jit(solution)/shard_map/ppermute | solution.py:442
  111.6 23.3 %collective-permute-start.32 = (f32[256,512]{1,0:T(8,128)}, f32[256,512]{1,0:T(8,128)S(1)}, u32[]{:S(2)}, u32[]{:S(2)}) collective-permute-start(f32[256,512]{1,0:T(8,128)} %constant_dynamic-update-slice_fusion.6), channel_id=1, source_target_pairs={{0,1},{1,0},{2,3},{3,2},{4,5},{5,4},{6,7},{7,6},{8,9},{9,8},{10,11... | collective-permute-start | bytes 1572872 | tf_op jit(solution)/shard_map/ppermute | solution.py:414
  116.6 86.9 %collective-permute-start.8 = (bf16[256,1024]{1,0:T(8,128)(2,1)}, bf16[256,1024]{1,0:T(8,128)(2,1)S(1)}, u32[]{:S(2)}, u32[]{:S(2)}) collective-permute-start(bf16[256,1024]{1,0:T(8,128)(2,1)} %window_part.25), channel_id=1, source_target_pairs={{0,4},{4,8},{8,12},{12,14},{14,10},{10,6},{6,2},{2,0},{1,5},{5,9},... | collective-permute-start | bytes 1572872 | tf_op jit(solution)/shard_map/ppermute | solution.py:464
  122.8 50.3 %collective-permute-start.11 = (bf16[256,1024]{1,0:T(8,128)(2,1)}, bf16[256,1024]{1,0:T(8,128)(2,1)S(1)}, u32[]{:S(2)}, u32[]{:S(2)}) collective-permute-start(bf16[256,1024]{1,0:T(8,128)(2,1)} %window_part.28), channel_id=1, source_target_pairs={{0,2},{4,0},{8,4},{12,8},{14,12},{10,14},{6,10},{2,6},{1,3},{5,1},... | collective-permute-start | bytes 1572872 | tf_op jit(solution)/shard_map/ppermute | solution.py:462
  128.1 38.5 %collective-permute-start.1 = (bf16[256,1280]{1,0:T(8,128)(2,1)}, bf16[256,1280]{1,0:T(8,128)(2,1)S(1)}, u32[]{:S(2)}, u32[]{:S(2)}) collective-permute-start(bf16[256,1280]{1,0:T(8,128)(2,1)} %window_part.17), channel_id=1, source_target_pairs={{0,4},{4,8},{8,12},{12,14},{14,10},{10,6},{6,2},{2,0},{1,5},{5,9},... | collective-permute-start | bytes 1966088 | tf_op jit(solution)/shard_map/ppermute | solution.py:458
  133.8 57.1 %collective-permute-start.5 = (bf16[256,1280]{1,0:T(8,128)(2,1)}, bf16[256,1280]{1,0:T(8,128)(2,1)S(1)}, u32[]{:S(2)}, u32[]{:S(2)}) collective-permute-start(bf16[256,1280]{1,0:T(8,128)(2,1)} %window_part.21), channel_id=1, source_target_pairs={{0,2},{4,0},{8,4},{12,8},{14,12},{10,14},{6,10},{2,6},{1,3},{5,1},... | collective-permute-start | bytes 1966088 | tf_op jit(solution)/shard_map/ppermute | solution.py:460
  171.9 26.2 %collective-permute-start.2 = (bf16[256,1280]{1,0:T(8,128)(2,1)}, bf16[256,1280]{1,0:T(8,128)(2,1)S(1)}, u32[]{:S(2)}, u32[]{:S(2)}) collective-permute-start(bf16[256,1280]{1,0:T(8,128)(2,1)} %window_part.18), channel_id=1, source_target_pairs={{0,4},{4,8},{8,12},{12,14},{14,10},{10,6},{6,2},{2,0},{1,5},{5,9},... | collective-permute-start | bytes 1966088 | tf_op jit(solution)/shard_map/ppermute | solution.py:458
  177.9 12.6 %copy-start.4 = (f32[512,128]{1,0:T(8,128)S(1)}, f32[512,128]{1,0:T(8,128)}, u32[]{:S(2)}) copy-start(f32[512,128]{1,0:T(8,128)} %broadcast_multiply_fusion.solved_ref) | copy-start | bytes 786436
  177.9 27.6 %collective-permute-start.12 = (bf16[256,1024]{1,0:T(8,128)(2,1)}, bf16[256,1024]{1,0:T(8,128)(2,1)S(1)}, u32[]{:S(2)}, u32[]{:S(2)}) collective-permute-start(bf16[256,1024]{1,0:T(8,128)(2,1)} %window_part.29), channel_id=1, source_target_pairs={{0,2},{4,0},{8,4},{12,8},{14,12},{10,14},{6,10},{2,6},{1,3},{5,1},... | collective-permute-start | bytes 1572872 | tf_op jit(solution)/shard_map/ppermute | solution.py:462
  189.3 24.6 %collective-permute-start.33 = (f32[2,128,256]{2,1,0:T(8,128)S(1)}, f32[2,128,256]{2,1,0:T(8,128)S(1)}, u32[]{:S(2)}, u32[]{:S(2)}) collective-permute-start(f32[2,128,256]{2,1,0:T(8,128)S(1)} %get-tuple-element.12), channel_id=1, source_target_pairs={{0,4},{2,6},{4,8},{6,10},{8,12},{10,14},{12,0},{14,2},{1,5},{3,7},... | collective-permute-start | bytes 786440 | tf_op jit(solution)/shard_map/ppermute | solution.py:371
  190.9 23.8 %collective-permute-start.35 = (f32[2,128,256]{2,1,0:T(8,128)S(1)}, f32[2,128,256]{2,1,0:T(8,128)S(1)}, u32[]{:S(2)}, u32[]{:S(2)}) collective-permute-start(f32[2,128,256]{2,1,0:T(8,128)S(1)} %get-tuple-element.13), channel_id=1, source_target_pairs={{0,12},{2,14},{4,0},{6,2},{8,4},{10,6},{12,8},{14,10},{1,13},{3,15... | collective-permute-start | bytes 786440 | tf_op jit(solution)/shard_map/ppermute | solution.py:371
  198.1 18.2 %collective-permute-start.34 = (f32[2,128,256]{2,1,0:T(8,128)S(1)}, f32[2,128,256]{2,1,0:T(8,128)S(1)}, u32[]{:S(2)}, u32[]{:S(2)}) collective-permute-start(f32[2,128,256]{2,1,0:T(8,128)S(1)} %get-tuple-element.14), channel_id=1, source_target_pairs={{0,8},{2,10},{4,12},{6,14},{8,0},{10,2},{12,4},{14,6},{1,9},{3,11}... | collective-permute-start | bytes 786440 | tf_op jit(solution)/shard_map/ppermute | solution.py:371
  203.5 22.9 %collective-permute-start.6 = (bf16[256,1280]{1,0:T(8,128)(2,1)S(1)}, bf16[256,1280]{1,0:T(8,128)(2,1)S(1)}, u32[]{:S(2)}, u32[]{:S(2)}) collective-permute-start(bf16[256,1280]{1,0:T(8,128)(2,1)S(1)} %copy-done.9), channel_id=1, source_target_pairs={{0,2},{4,0},{8,4},{12,8},{14,12},{10,14},{6,10},{2,6},{1,3},{5,1},... | collective-permute-start | bytes 1966088 | tf_op jit(solution)/shard_map/ppermute | solution.py:460
  205.5 20.8 %collective-permute-start.3 = (bf16[256,1280]{1,0:T(8,128)(2,1)}, bf16[256,1280]{1,0:T(8,128)(2,1)S(1)}, u32[]{:S(2)}, u32[]{:S(2)}) collective-permute-start(bf16[256,1280]{1,0:T(8,128)(2,1)} %window_part.19), channel_id=1, source_target_pairs={{0,4},{4,8},{8,12},{12,14},{14,10},{10,6},{6,2},{2,0},{1,5},{5,9},... | collective-permute-start | bytes 1966088 | tf_op jit(solution)/shard_map/ppermute | solution.py:458
  213.9 22.6 %collective-permute-start.9 = (bf16[256,1024]{1,0:T(8,128)(2,1)}, bf16[256,1024]{1,0:T(8,128)(2,1)}, u32[]{:S(2)}, u32[]{:S(2)}) collective-permute-start(bf16[256,1024]{1,0:T(8,128)(2,1)} %window_part.26), channel_id=1, source_target_pairs={{0,4},{4,8},{8,12},{12,14},{14,10},{10,6},{6,2},{2,0},{1,5},{5,9},... | collective-permute-start | bytes 1572872 | tf_op jit(solution)/shard_map/ppermute | solution.py:464
  214.7 21.8 %collective-permute-start.13 = (bf16[256,1024]{1,0:T(8,128)(2,1)}, bf16[256,1024]{1,0:T(8,128)(2,1)}, u32[]{:S(2)}, u32[]{:S(2)}) collective-permute-start(bf16[256,1024]{1,0:T(8,128)(2,1)} %window_part.30), channel_id=1, source_target_pairs={{0,2},{4,0},{8,4},{12,8},{14,12},{10,14},{6,10},{2,6},{1,3},{5,1},... | collective-permute-start | bytes 1572872 | tf_op jit(solution)/shard_map/ppermute | solution.py:462
  221.3 59.8 %collective-permute-start.36 = (f32[128,256]{0,1:T(8,128)}, f32[128,256]{0,1:T(8,128)S(1)}, u32[]{:S(2)}, u32[]{:S(2)}) collective-permute-start(f32[128,256]{0,1:T(8,128)} %bitcast.27), channel_id=1, source_target_pairs={{0,2},{2,0},{4,6},{6,4},{8,10},{10,8},{12,14},{14,12},{1,3},{3,1},... | collective-permute-start | bytes 393224 | tf_op jit(solution)/shard_map/ppermute | solution.py:367
  234.0 21.0 %copy-start.5 = (bf16[5,256,256]{2,1,0:T(8,128)(2,1)S(1)}, bf16[5,256,256]{2,1,0:T(8,128)(2,1)}, u32[]{:S(2)}) copy-start(bf16[5,256,256]{2,1,0:T(8,128)(2,1)} %get-tuple-element.6) | copy-start | bytes 1966084
  234.0 22.2 %collective-permute-start.14 = (bf16[2,256,256]{2,1,0:T(8,128)(2,1)S(1)}, bf16[2,256,256]{2,1,0:T(8,128)(2,1)S(1)}, u32[]{:S(2)}, u32[]{:S(2)}) collective-permute-start(bf16[2,256,256]{2,1,0:T(8,128)(2,1)S(1)} %get-tuple-element.16), channel_id=1, source_target_pairs={{0,12},{4,14},{8,10},{12,6},{14,2},{10,0},{6,4},{2,8},{1,13},{5,15... | collective-permute-start | bytes 786440 | tf_op jit(solution)/shard_map/ppermute | solution.py:501
  241.0 14.2 %copy-start.25 = (bf16[4,256,256]{2,1,0:T(8,128)(2,1)S(1)}, bf16[4,256,256]{2,1,0:T(8,128)(2,1)}, u32[]{:S(2)}) copy-start(bf16[4,256,256]{2,1,0:T(8,128)(2,1)} %get-tuple-element.7) | copy-start | bytes 1572868
  242.0 33.5 %collective-permute-start.16 = (bf16[2,256,256]{2,1,0:T(8,128)(2,1)S(1)}, bf16[2,256,256]{2,1,0:T(8,128)(2,1)S(1)}, u32[]{:S(2)}, u32[]{:S(2)}) collective-permute-start(bf16[2,256,256]{2,1,0:T(8,128)(2,1)S(1)} %slice.25), channel_id=1, source_target_pairs={{0,2},{4,0},{8,4},{12,8},{14,12},{10,14},{6,10},{2,6},{1,3},{5,1},... | collective-permute-start | bytes 786440 | tf_op jit(solution)/shard_map/ppermute | solution.py:501
  247.5 28.0 %collective-permute-start.17 = (bf16[1,256,256]{2,1,0:T(8,128)(2,1)S(1)}, bf16[1,256,256]{2,1,0:T(8,128)(2,1)S(1)}, u32[]{:S(2)}, u32[]{:S(2)}) collective-permute-start(bf16[1,256,256]{2,1,0:T(8,128)(2,1)S(1)} %slice.26), channel_id=1, source_target_pairs={{0,14},{4,10},{8,6},{12,2},{14,0},{10,4},{6,8},{2,12},{1,15},{5,11... | collective-permute-start | bytes 393224 | tf_op jit(solution)/shard_map/ppermute | solution.py:501
  249.8 25.6 %collective-permute-start.15 = (bf16[2,256,256]{2,1,0:T(8,128)(2,1)S(1)}, bf16[2,256,256]{2,1,0:T(8,128)(2,1)S(1)}, u32[]{:S(2)}, u32[]{:S(2)}) collective-permute-start(bf16[2,256,256]{2,1,0:T(8,128)(2,1)S(1)} %get-tuple-element.15), channel_id=1, source_target_pairs={{0,6},{4,2},{8,0},{12,4},{14,8},{10,12},{6,14},{2,10},{1,7},{5,3},... | collective-permute-start | bytes 786440 | tf_op jit(solution)/shard_map/ppermute | solution.py:501
  281.1 14.1 %copy-start.31 = (s32[256]{0:T(256)S(1)}, s32[256]{0:T(256)}, u32[]{:S(2)}) copy-start(s32[256]{0:T(256)} %param.13) | copy-start | bytes 3076
  281.1 14.9 %collective-permute-start.18 = (bf16[8,256,256]{2,1,0:T(8,128)(2,1)}, bf16[8,256,256]{2,1,0:T(8,128)(2,1)S(1)}, u32[]{:S(2)}, u32[]{:S(2)}) collective-permute-start(bf16[8,256,256]{2,1,0:T(8,128)(2,1)} %for_sibling.1), channel_id=1, source_target_pairs={{0,1},{1,0},{2,3},{3,2},{4,5},{5,4},{6,7},{7,6},{8,9},{9,8},{10,11... | collective-permute-start | bytes 3145736 | tf_op jit(solution)/shard_map/ppermute | solution.py:505
  281.6 5.6 %collective-permute-start.37 = (f32[32,128]{1,0:T(8,128)S(1)}, f32[32,128]{1,0:T(8,128)S(1)}, u32[]{:S(2)}, u32[]{:S(2)}) collective-permute-start(f32[32,128]{1,0:T(8,128)S(1)} %get-tuple-element.24), channel_id=1, source_target_pairs={{0,4},{2,6},{4,8},{6,10},{8,12},{10,14},{12,0},{14,2},{1,5},{3,7},... | collective-permute-start | bytes 49160 | tf_op jit(solution)/shard_map/ppermute | solution.py:371
  281.6 5.6 %collective-permute-start.39 = (f32[32,128]{1,0:T(8,128)S(1)}, f32[32,128]{1,0:T(8,128)S(1)}, u32[]{:S(2)}, u32[]{:S(2)}) collective-permute-start(f32[32,128]{1,0:T(8,128)S(1)} %get-tuple-element.25), channel_id=1, source_target_pairs={{0,12},{2,14},{4,0},{6,2},{8,4},{10,6},{12,8},{14,10},{1,13},{3,15... | collective-permute-start | bytes 49160 | tf_op jit(solution)/shard_map/ppermute | solution.py:371
  285.4 4.6 %collective-permute-start.38 = (f32[32,128]{1,0:T(8,128)S(1)}, f32[32,128]{1,0:T(8,128)S(1)}, u32[]{:S(2)}, u32[]{:S(2)}) collective-permute-start(f32[32,128]{1,0:T(8,128)S(1)} %get-tuple-element.26), channel_id=1, source_target_pairs={{0,8},{2,10},{4,12},{6,14},{8,0},{10,2},{12,4},{14,6},{1,9},{3,11}... | collective-permute-start | bytes 49160 | tf_op jit(solution)/shard_map/ppermute | solution.py:371
  290.1 3.7 %collective-permute-start.40 = (f32[16,128]{1,0:T(8,128)S(1)}, f32[16,128]{1,0:T(8,128)S(1)}, u32[]{:S(2)}, u32[]{:S(2)}) collective-permute-start(f32[16,128]{1,0:T(8,128)S(1)} %constant_dynamic-slice_fusion), channel_id=1, source_target_pairs={{0,2},{2,0},{4,6},{6,4},{8,10},{10,8},{12,14},{14,12},{1,3},{3,1},... | collective-permute-start | bytes 24584 | tf_op jit(solution)/shard_map/ppermute | solution.py:367
  293.8 1.3 collective-permute-start.41
  (27 other events, 90.1 us)

commit v3 on v2

v3 whole, which is shorter than its diff:
```python
import jax
import jax.numpy as jnp
from jax import lax
from jax.experimental import pallas as pl
from jax.experimental.pallas import tpu as pltpu
from jax.sharding import PartitionSpec as P

R = 64
SEQ = 16
damping = 1.0
EXACT = lax.Precision.HIGHEST
SWAP = [(0, 1), (1, 0)]
VMEM_BYTES = 56 * 1024 * 1024


class Ring:
    def __init__(self, mesh):
        self.count = mesh.shape["dp"]
        self.half = self.count // 2
        coords = [getattr(device, "coords", None) for device in mesh.devices[0, :, 0]]
        self.folded = False
        if None not in coords:
            moving = [axis for axis in range(3) if len({place[axis] for place in coords}) > 1]
            fast = [axis for axis in moving if coords[0][axis] != coords[1][axis]]
            self.folded = len(moving) == 2 and len(fast) == 1 and len({place[fast[0]] for place in coords}) == 2
        reach = [0, 0]
        self.offsets = []
        for distance in range(self.half - 1, 0, -1):
            side = 0 if reach[0] <= reach[1] else 1
            reach[side] += distance
            self.offsets.append(distance if side == 0 else -distance)

    def index_at(self, position):
        if isinstance(position, int):
            position = position % self.count
            if not self.folded:
                return position
            return 2 * position if position < self.half else 2 * (self.count - 1 - position) + 1
        position = lax.rem(position + 2 * self.count, self.count)
        if not self.folded:
            return position
        return jnp.where(position < self.half, 2 * position, 2 * (self.count - 1 - position) + 1)

    def position_of(self, index):
        if not self.folded:
            return index
        return jnp.where(lax.rem(index, 2) == 0, index // 2, self.count - 1 - index // 2)

    def shift(self, step):
        return [(self.index_at(p), self.index_at(p + step)) for p in range(self.count)]


def lead_dot(left, right, precision=None):
    return lax.dot_general(
        left, right, (((0,), (0,)), ((), ())), precision=precision, preferred_element_type=jnp.float32
    )


def exact_dot(left, right):
    return jnp.dot(left, right, precision=EXACT, preferred_element_type=jnp.float32)


def pairs_of(slots):
    found = []
    for index, (offset, core) in enumerate(slots):
        if core is None:
            found.append((offset, 1, index))
        elif core == 0:
            found.append((offset, 2, index))
    return found


def window_terms(ring, place, stored, vectors, group, steps, far_slots, near_slots):
    rows, full = stored.shape
    new_rows = vectors.shape[0]
    taps = jnp.array(steps, jnp.int32)

    def kernel(place_ref, step_ref, stored_ref, vectors_ref, far_ref, near_ref):
        owner = ring.position_of(place_ref[0]) + step_ref[pl.program_id(0)] + ring.count
        owner = lax.rem(owner, ring.count)
        core = place_ref[1]
        left = pl.ds(pl.multiple_of((2 * ring.index_at(owner) + core) * group, group), group)
        turned = stored_ref[:, left].T
        turned_new = vectors_ref[:, left].T
        for slots, out_ref in ((far_slots, far_ref), (near_slots, near_ref)):
            for offset, blocks, first in pairs_of(slots):
                column = 2 * ring.index_at(owner + offset)
                if blocks == 1:
                    column = column + jnp.where(owner < ring.half, core, 1 - core)
                right = pl.ds(pl.multiple_of(column * group, blocks * group), blocks * group)
                total = jnp.dot(turned, stored_ref[:, right], preferred_element_type=jnp.float32)
                total = total + jnp.dot(turned_new, vectors_ref[:, right], preferred_element_type=jnp.float32)
                out_ref[0, :, first * group : (first + blocks) * group] = total.astype(jnp.bfloat16)

    def out(slots):
        return pl.BlockSpec((1, group, len(slots) * group), lambda i, a, b: (i, 0, 0))

    def shape(slots):
        return jax.ShapeDtypeStruct((len(steps), group, len(slots) * group), jnp.bfloat16)

    blocks = len(far_slots) + len(near_slots)
    return pl.pallas_call(
        kernel,
        grid_spec=pltpu.PrefetchScalarGridSpec(
            num_scalar_prefetch=2,
            grid=(len(steps),),
            in_specs=[
                pl.BlockSpec((rows, full), lambda i, a, b: (0, 0), pipeline_mode=pl.Buffered(1)),
                pl.BlockSpec((new_rows, full), lambda i, a, b: (0, 0), pipeline_mode=pl.Buffered(1)),
            ],
            out_specs=[out(far_slots), out(near_slots)],
        ),
        out_shape=[shape(far_slots), shape(near_slots)],
        compiler_params=pltpu.CompilerParams(vmem_limit_bytes=VMEM_BYTES),
        cost_estimate=pl.CostEstimate(
            flops=4 * rows * len(steps) * blocks * group * group,
            bytes_accessed=2 * rows * full + 2 * len(steps) * blocks * group * group,
            transcendentals=0,
        ),
        name="window_terms",
    )(place, taps, stored, vectors)


def close_window(own, ahead, back, slots, group):
    count = len(slots)
    chips = [chip for chip in pairs_of(slots) if chip[0] != 0]

    def kernel(own_ref, ahead_ref, back_ref, blocks_ref, *turned_refs):
        for k in range(count):
            cols = slice(k * group, (k + 1) * group)
            total = own_ref[0, :, cols].astype(jnp.float32)
            total = total + ahead_ref[:, cols].astype(jnp.float32) + back_ref[:, cols].astype(jnp.float32)
            total = total.astype(jnp.bfloat16)
            blocks_ref[k] = total
            for (_, blocks, first), turned_ref in zip(chips, turned_refs):
                if first <= k < first + blocks:
                    turned_ref[k - first] = total.T

    index = own.shape[0] - 1
    flat = pl.BlockSpec((group, count * group), lambda i: (0, 0))
    sizes = [count] + [blocks for _, blocks, _ in chips]
    return pl.pallas_call(
        kernel,
        grid=(1,),
        in_specs=[pl.BlockSpec((1, group, count * group), lambda i: (index, 0, 0)), flat, flat],
        out_specs=[pl.BlockSpec((size, group, group), lambda i: (0, 0, 0)) for size in sizes],
        out_shape=[jax.ShapeDtypeStruct((size, group, group), jnp.bfloat16) for size in sizes],
        compiler_params=pltpu.CompilerParams(vmem_limit_bytes=VMEM_BYTES),
        cost_estimate=pl.CostEstimate(flops=4 * count * group**2, bytes_accessed=10 * count * group**2, transcendentals=0),
        name="close_window",
    )(own, ahead, back)


def rough_dot(left, right):
    return jnp.dot(left.astype(jnp.bfloat16), right.astype(jnp.bfloat16), preferred_element_type=jnp.float32)


def solve_kernel(matrix_ref, right_ref, out_ref, work, inverse, residual):
    size = matrix_ref.shape[0]
    block = inverse.shape[0]
    work[...] = matrix_ref[...]
    out_ref[...] = right_ref[...]
    row_ids = lax.broadcasted_iota(jnp.int32, (block, block), 0)
    col_ids = lax.broadcasted_iota(jnp.int32, (block, block), 1)
    eye = (row_ids == col_ids).astype(jnp.float32)
    for start in range(0, size, block):
        here = slice(start, start + block)
        rest = slice(start + block, size)
        corner = work[here, here]
        norm = jnp.max(jnp.sum(jnp.abs(corner), axis=0))
        inverse[...] = eye / norm
        residual[...] = eye - corner / norm

        def improve(dot):
            def step_of(state):
                step, _ = state
                better = inverse[...] + dot(inverse[...], residual[...])
                left_over = eye - dot(work[here, here], better)
                inverse[...] = better
                residual[...] = left_over
                return step + 1, jnp.max(jnp.abs(left_over))

            return step_of

        def until(steps, bound):
            return lambda state: jnp.logical_and(state[0] < steps, state[1] > bound)

        begin = (jnp.int32(0), jnp.float32(1.0))
        lax.while_loop(until(10, 0.02), improve(rough_dot), begin)
        left_over = eye - exact_dot(work[here, here], inverse[...])
        good = jnp.max(jnp.sum(jnp.abs(left_over), axis=0)) < 0.7
        inverse[...] = jnp.where(good, inverse[...], eye / norm)
        residual[...] = jnp.where(good, left_over, eye - work[here, here] / norm)
        lax.while_loop(until(40, 5e-5), improve(exact_dot), begin)
        found = inverse[...] + exact_dot(inverse[...], residual[...])
        solved = exact_dot(found, out_ref[here, :])
        out_ref[here, :] = solved
        if start + block < size:
            across = exact_dot(found, work[here, rest])
            down = work[rest, here]
            work[rest, rest] = work[rest, rest] - exact_dot(down, across)
            out_ref[rest, :] = out_ref[rest, :] - exact_dot(down, solved)
            work[here, rest] = across
    for start in range(size - 2 * block, -1, -block):
        here = slice(start, start + block)
        rest = slice(start + block, size)
        out_ref[here, :] = out_ref[here, :] - exact_dot(work[here, rest], out_ref[rest, :])


def solve(matrix, right):
    size, columns = right.shape
    block = 128
    return pl.pallas_call(
        solve_kernel,
        out_shape=jax.ShapeDtypeStruct((size, columns), jnp.float32),
        scratch_shapes=[
            pltpu.VMEM((size, size), jnp.float32),
            pltpu.VMEM((block, block), jnp.float32),
            pltpu.VMEM((block, block), jnp.float32),
        ],
        compiler_params=pltpu.CompilerParams(vmem_limit_bytes=VMEM_BYTES),
        cost_estimate=pl.CostEstimate(flops=12 * size**3, bytes_accessed=4 * size * (size + 2 * columns), transcendentals=0),
        name="solve",
    )(matrix, right)


def split_terms(value):
    high = value.astype(jnp.bfloat16)
    value = value - high.astype(jnp.float32)
    middle = value.astype(jnp.bfloat16)
    value = value - middle.astype(jnp.float32)
    return high, middle, value.astype(jnp.bfloat16)


def spread_back(place, stored, solved, owners, group):
    rows = stored.shape[0]
    width, examples = solved.shape

    def kernel(place_ref, first_ref, solved_ref, cols_ref, out_ref, terms):
        @pl.when(pl.program_id(0) == 0)
        def _():
            total = jnp.zeros((rows, examples), jnp.float32)
            for term in split_terms(solved_ref[...]):
                total = total + jnp.dot(first_ref[...], term, preferred_element_type=jnp.float32)
            for index, term in enumerate(split_terms(total.T)[:2]):
                terms[index * examples : (index + 1) * examples, :] = term

        product = jnp.dot(terms[...], cols_ref[...], preferred_element_type=jnp.float32)
        out_ref[0] = (product[:examples] + product[examples:]).astype(jnp.bfloat16)

    return pl.pallas_call(
        kernel,
        grid_spec=pltpu.PrefetchScalarGridSpec(
            num_scalar_prefetch=1,
            grid=(owners,),
            in_specs=[
                pl.BlockSpec((rows, width), lambda o, ref: (0, 0)),
                pl.BlockSpec((width, examples), lambda o, ref: (0, 0)),
                pl.BlockSpec((rows, group), lambda o, ref: (0, 2 * o + ref[1])),
            ],
            out_specs=pl.BlockSpec((1, examples, group), lambda o, ref: (o, 0, 0)),
            scratch_shapes=[pltpu.VMEM((2 * examples, rows), jnp.bfloat16)],
        ),
        out_shape=jax.ShapeDtypeStruct((owners, examples, group), jnp.bfloat16),
        compiler_params=pltpu.CompilerParams(vmem_limit_bytes=VMEM_BYTES),
        cost_estimate=pl.CostEstimate(
            flops=6 * rows * examples * (width + owners * group),
            bytes_accessed=2 * rows * (width + owners * group) + 2 * owners * examples * group,
            transcendentals=0,
        ),
        name="spread_back",
    )(place, stored, solved, stored)


def assembly_tables(ring, slots, d, t):
    start = [0] * ring.count
    arrived = [0] * ring.count
    for offset, _, first in pairs_of(slots):
        start[offset % ring.count] = first
    place = len(slots)
    for offset in ring.offsets:
        start[-offset % ring.count] = place
        arrived[-offset % ring.count] = 1
        place += 2
    here = ring.position_of(d)
    early = here < ring.half

    def look_up(values, offset):
        found = jnp.zeros_like(offset)
        for index, value in enumerate(values):
            if value:
                found = jnp.where(offset == index, value, found)
        return found

    def offsets_of(chips):
        return lax.rem(ring.position_of(chips) - here + 2 * ring.count, ring.count)

    def fetch(offset, j):
        own = (j == t) == early
        quarter = jnp.where(own, start[ring.half], place)
        return jnp.where(offset == ring.half, quarter, look_up(start, offset) + j)

    chips = jnp.arange(ring.half, dtype=jnp.int32)
    j = jnp.arange(2, dtype=jnp.int32)[None, :]
    send = fetch(offsets_of((1 - t) * ring.half + chips)[:, None], j)
    offset = offsets_of(t * ring.half + chips)[:, None, None]
    r = jnp.arange(2, dtype=jnp.int32)[None, :, None]
    u = jnp.arange(2, dtype=jnp.int32)[None, None, :]
    by_columns = jnp.where(offset == ring.half, early.astype(jnp.int32), look_up(arrived, offset)) == 1
    j = jnp.where(by_columns, r, u)
    local = fetch(offset, j)
    other = 2 * chips[:, None, None] + j
    mine = (jnp.where(by_columns, u, r) == t).astype(jnp.int32)
    final = jnp.stack([local, other, mine]).reshape(-1)
    return send.reshape(-1).astype(jnp.int32), final.astype(jnp.int32)


def for_sibling(table, blocks, group):
    total = table.shape[0]
    wide = min(4, total)

    def kernel(table_ref, *refs):
        for k in range(wide):
            refs[-1][k] = refs[k][0]

    return pl.pallas_call(
        kernel,
        grid_spec=pltpu.PrefetchScalarGridSpec(
            num_scalar_prefetch=1,
            grid=(total // wide,),
            in_specs=[
                pl.BlockSpec((1, group, group), lambda c, ref, k=k: (ref[wide * c + k], 0, 0)) for k in range(wide)
            ],
            out_specs=pl.BlockSpec((wide, group, group), lambda c, ref: (c, 0, 0)),
        ),
        out_shape=jax.ShapeDtypeStruct((total, group, group), jnp.bfloat16),
        compiler_params=pltpu.CompilerParams(vmem_limit_bytes=VMEM_BYTES),
        name="for_sibling",
    )(table, *([blocks] * wide))


def finish(place, table, blocks, other, half, group):
    wide = half // 2
    total = 4 * half

    def at(kind, r, c, k, u, ref):
        return ref[kind * total + 4 * (wide * c + k) + 2 * r + u]

    def spec(kind, k, u):
        return pl.BlockSpec((1, group, group), lambda r, c, ref, place: (at(kind, r, c, k, u, ref), 0, 0))

    order = [(k, u) for k in range(wide) for u in (0, 1)]

    def kernel(table_ref, place_ref, *refs):
        r, c = pl.program_id(0), pl.program_id(1)
        out_ref = refs[-1]
        shape = (group, group)
        gap = lax.broadcasted_iota(jnp.int32, shape, 1) - lax.broadcasted_iota(jnp.int32, shape, 0)
        for index, (k, u) in enumerate(order):
            cols = slice(index * group, (index + 1) * group)
            chip = place_ref[1] * half + wide * c + k
            apart = (2 * place_ref[0] + r - 2 * chip - u) * group
            added = jnp.where(gap == apart, jnp.float32(damping), jnp.float32(0.0))
            mine = at(2, r, c, k, u, table_ref) == 1

            @pl.when(mine)
            def _():
                out_ref[:, cols] = added + refs[index][0].astype(jnp.float32)

            @pl.when(jnp.logical_not(mine))
            def _():
                out_ref[:, cols] = added + refs[len(order) + index][0].astype(jnp.float32)

    return pl.pallas_call(
        kernel,
        grid_spec=pltpu.PrefetchScalarGridSpec(
            num_scalar_prefetch=2,
            grid=(2, 2),
            in_specs=[spec(0, k, u) for k, u in order] + [spec(1, k, u) for k, u in order],
            out_specs=pl.BlockSpec((group, 2 * wide * group), lambda r, c, ref, place: (r, c)),
        ),
        out_shape=jax.ShapeDtypeStruct((2 * group, 2 * half * group), jnp.float32),
        compiler_params=pltpu.CompilerParams(vmem_limit_bytes=VMEM_BYTES),
        name="finish",
    )(table, place, *([blocks] * len(order)), *([other] * len(order)))


def in_order(index, mine, other, axis):
    return jnp.where(
        index == 0,
        jnp.concatenate([mine, other], axis=axis),
        jnp.concatenate([other, mine], axis=axis),
    )


def pair_swap(value, count):
    return lax.ppermute(value, "dp", [(index, index ^ 1) for index in range(count)])


def far_shift(value, step, count):
    return lax.ppermute(value, "dp", [(index, (index + 2 * step) % count) for index in range(count)])


def exchange_pairs(slice_of, pair, count):
    pairs = count // 2
    came = [slice_of(pair)]
    for step in range(1, pairs):
        came.append(far_shift(slice_of(lax.rem(pair + step, pairs)), step, count))
    return came


def natural(came, pair):
    pairs = len(came)
    pieces = []
    for index in range(pairs):
        behind = lax.rem(pair - index + pairs, pairs)
        piece = came[0]
        for step in range(1, pairs):
            piece = jnp.where(behind == step, came[step], piece)
        pieces.append(piece)
    return pieces


def scatter_pairs(value, pair, count):
    size = value.shape[0] // (count // 2)

    def slice_of(index):
        return lax.dynamic_slice_in_dim(value, index * size, size, 0)

    return sum(piece.astype(jnp.float32) for piece in exchange_pairs(slice_of, pair, count))


def local(ring, activations, out_grads, proj_in, proj_out, stored, counts, query_ids):
    owners = ring.count
    full = stored.shape[1]
    width = full // owners
    group = width // 2
    half = ring.half
    t = lax.axis_index("tensor")
    d = lax.axis_index("dp")
    pair, side = d // 2, lax.rem(d, 2)
    g = 2 * d + t
    place = jnp.stack([d, t]).astype(jnp.int32)

    first_stored = stored[:, :width]
    corner_rows = lead_dot(lax.dynamic_slice_in_dim(first_stored, t * group, group, 1), first_stored)
    corner_rows = scatter_pairs(corner_rows, pair, owners)
    corner_rows = corner_rows + pair_swap(corner_rows, owners)
    corner_rows = exchange_pairs(lambda index: corner_rows, pair, owners)
    corner_rows = jnp.concatenate(natural(corner_rows, pair), axis=0)
    corner = in_order(t, corner_rows, lax.ppermute(corner_rows, "tensor", SWAP), 0)

    sides = jnp.concatenate(
        [
            jnp.dot(activations, proj_in, preferred_element_type=jnp.float32),
            jnp.dot(out_grads, proj_out, preferred_element_type=jnp.float32),
        ],
        axis=1,
    )
    sides = sides + lax.ppermute(sides, "tensor", SWAP)

    examples = counts.shape[0]
    all_examples = examples * owners
    rank = proj_in.shape[1]
    position = jnp.arange(SEQ, dtype=jnp.int32)[None, :]
    weights = jnp.where(
        position < counts[:, None], 1.0 / counts.astype(jnp.float32)[:, None], jnp.float32(0.0)
    )
    outer = jnp.einsum(
        "es,esi,esj->eij",
        weights,
        sides[:, :rank].reshape(examples, SEQ, rank),
        sides[:, rank:].reshape(examples, SEQ, rank),
        precision=EXACT,
    )
    vectors = outer.reshape(examples, full).astype(jnp.bfloat16)

    def columns_for(index):
        groups = [lax.dynamic_slice_in_dim(vectors, (4 * index + 2 * s + t) * group, group, 1) for s in (0, 1)]
        return jnp.concatenate([vectors[:, :width]] + groups, axis=1)

    came = natural(exchange_pairs(columns_for, pair, owners), pair)
    came = jnp.concatenate(came, axis=0)
    kept = jnp.where(side == 0, came[:, : width + group], jnp.concatenate([came[:, :width], came[:, width + group :]], axis=1))
    away = jnp.where(side == 0, jnp.concatenate([came[:, :width], came[:, width + group :]], axis=1), came[:, : width + group])
    shape = (owners // 2, 1, examples, width + group)
    known = in_order(side, kept.reshape(shape), pair_swap(away, owners).reshape(shape), 1)
    known = known.reshape(all_examples, width + group)
    first_cols, own_cols = known[:, :width], known[:, width:].astype(jnp.float32)

    split = (len(ring.offsets) + 1) // 2
    far_slots = [(half, None)]
    for offset in ring.offsets[:split]:
        far_slots += [(offset, 0), (offset, 1)]
    near_slots = []
    for offset in ring.offsets[split:] + [0]:
        near_slots += [(offset, 0), (offset, 1)]

    def terms_of(steps):
        return window_terms(ring, place, stored, vectors, group, steps, far_slots, near_slots)

    outermost = terms_of([half])
    second = terms_of([half - 1, 1 - half])
    later_steps = [s for step in range(half - 2, 0, -1) for s in (step, -step)] + [0]
    later = terms_of(later_steps)

    def term(kind, step):
        if abs(step) == half:
            return outermost[kind][0]
        if abs(step) == half - 1:
            return second[kind][0 if step > 0 else 1]
        return later[kind][later_steps.index(step)]

    ahead, back = ring.shift(1), ring.shift(-1)

    def passed_on(kind, step, arrived):
        value = term(kind, step)
        if arrived is not None:
            value = (value.astype(jnp.float32) + arrived.astype(jnp.float32)).astype(jnp.bfloat16)
        return lax.ppermute(value, "dp", ahead if step > 0 else back)

    far_ahead = far_back = near_ahead = near_back = None
    for step in range(half, 0, -1):
        far_ahead = passed_on(0, step, far_ahead)
        near_back = passed_on(1, -step, near_back)
        if step < half:
            far_back = passed_on(0, -step, far_back)
            near_ahead = passed_on(1, step, near_ahead)

    eye = jnp.eye(width, dtype=jnp.float32)
    corner = corner + lead_dot(first_cols, first_cols) + damping * eye
    scale = lax.rsqrt(jnp.sum(corner * eye, axis=1))
    first_cols = first_cols.astype(jnp.float32)
    solved = solve(corner * scale[:, None] * scale[None, :], first_cols.T * scale[:, None]) * scale[:, None]
    first_pairs = exact_dot(first_cols, solved)
    terms = spread_back(place, stored, solved, owners, group)
    terms = scatter_pairs(terms, pair, owners)
    away = jnp.where(side == 0, terms[1], terms[0]).astype(jnp.bfloat16)
    terms = jnp.where(side == 0, terms[0], terms[1]) + pair_swap(away, owners).astype(jnp.float32)
    damped = lax.dynamic_slice_in_dim(solved.T, lax.rem(g, 2) * group, group, 1)
    damped = jnp.where(g < 2, damping * damped, 0.0)
    rest = own_cols - lead_dot(first_pairs, own_cols, EXACT) - terms - damped
    pairs = lax.dot_general(rest, rest, (((1,), (1,)), ((), ())), precision=EXACT, preferred_element_type=jnp.float32)
    pairs = pairs + jnp.where(g == 0, first_pairs, 0.0)
    pairs = scatter_pairs(pairs, pair, owners)
    away = lax.dynamic_slice_in_dim(pairs, (1 - side) * examples, examples, 0)
    pairs = lax.dynamic_slice_in_dim(pairs, side * examples, examples, 0) + pair_swap(away, owners)
    pairs = pairs + lax.ppermute(pairs, "tensor", SWAP)
    chosen = (query_ids[:, None] == jnp.arange(all_examples, dtype=jnp.int32)[None, :]).astype(jnp.float32)
    scores = lax.dot_general(chosen, pairs, (((1,), (1,)), ((), ())), precision=EXACT, preferred_element_type=jnp.float32) / R

    far = close_window(later[0], far_ahead, far_back, far_slots, group)
    near = close_window(later[1], near_ahead, near_back, near_slots, group)
    turned = {}
    for (found, slots) in ((far, far_slots), (near, near_slots)):
        chips = [chip for chip in pairs_of(slots) if chip[0] != 0]
        for (offset, _, _), block in zip(chips, found[1:]):
            turned[offset] = block
    came = [lax.ppermute(turned[offset], "dp", ring.shift(offset)) for offset in ring.offsets + [half]]
    blocks = jnp.concatenate([far[0], near[0]] + came, axis=0)
    send_table, final_table = assembly_tables(ring, far_slots + near_slots, d, t)
    other = lax.ppermute(for_sibling(send_table, blocks, group), "tensor", SWAP)
    return finish(place, final_table, blocks, other, half, group), scores


def solution(mesh):
    placed = (
        P(("groups", "dp"), "tensor"),
        P(("groups", "dp"), "tensor"),
        P("tensor", None),
        P("tensor", None),
        P(("groups", "dp"), None),
        P(("groups", "dp")),
        P("groups"),
    )
    ring = Ring(mesh)

    def program(*args):
        return local(ring, *args)

    return jax.shard_map(
        program,
        mesh=mesh,
        in_specs=placed,
        out_specs=(P(("groups", "dp"), "tensor"), P("groups", "dp")),
        check_vma=False,
    )
```

time: 308 us -> 256 us (0.83)
  Pallas kernels: 119 us -> 74 us
  local copies, waits for them, and re-layouts: 41 us -> 19 us
  starting transfers between devices: 55.3 us -> 65.9 us
  other arithmetic: 6.56 us -> 16.3 us
  waiting for transfers between devices: 73.1 us -> 64.2 us
    ppermute x15, waiting for transfers between devices: 45.6 us -> 9.29 us  [far_shift(): lax.ppermute(value, 'dp', [(index, (index + 2 * step) % count) for index...]
    pallas_call x16 -> x5, Pallas kernels: 68.8 us -> 34.3 us  [the longest x3 29.1 us: window_terms(): pl.pallas_call(kernel, grid_spec=pltpu.PrefetchScalarGridSpec(num_scalar_...]
    ppermute x20 -> x19, waiting for transfers between devices: 23.6 us -> 50.8 us  [the longest x14 37.9 us: passed_on(): return lax.ppermute(value, 'dp', ahead if step > 0 else back)]
    dynamic_update_slice x7 -> x0, local copies, waits for them, and re-layouts: 21.9 us -> none  [the longest x6 19.9 us: gather_pairs(): lax.dynamic_update_slice_in_dim(whole, came, lax.rem(pair - step + pairs,...]
    convert_element_type x0 -> x10, other arithmetic: none -> 11 us  [the longest x8 10.9 us: passed_on(): (value.astype(jnp.float32) + arrived.astype(jnp.float32)).astype(jnp.bflo...]
    ppermute x15, starting transfers between devices: 20 us -> 26.6 us  [far_shift(): lax.ppermute(value, 'dp', [(index, (index + 2 * step) % count) for index...]
    ppermute x20 -> x19, starting transfers between devices: 28.6 us -> 35.1 us  [the longest x14 20.2 us: passed_on(): return lax.ppermute(value, 'dp', ahead if step > 0 else back)]
    pallas_call x1, Pallas kernels: 27.5 us -> 21.9 us  [solve(): pl.pallas_call(solve_kernel, out_shape=jax.ShapeDtypeStruct((size, column...]
  transfers between devices with their start and end apart: 42 -> 41, of which waited for: 11 -> 12; matrix products, arithmetic and copies ran while one was open for 14% -> 15% of each run, Pallas kernels for 36% -> 27%
where the time goes in v3:
time: 256 us; the launch traced here: 253 us
  Pallas kernels  74 us (29%)
  starting transfers between devices  65.9 us (26%)
  waiting for transfers between devices  64.2 us (25%)
  local copies, waits for them, and re-layouts  19 us (7%)
  other arithmetic  16.3 us (6%)
  matrix products  12.4 us (5%)
    ppermute x14, waiting for transfers between devices, passed_on(): return lax.ppermute(value, 'dp', ahead if step > 0 else back)  37.9 us
    pallas_call x3, Pallas kernels, window_terms(): pl.pallas_call(kernel, grid_spec=pltpu.PrefetchScalarGridSpec(num_scalar_...  29.1 us
    ppermute x15, starting transfers between devices, far_shift(): lax.ppermute(value, 'dp', [(index, (index + 2 * step) % count) for index...  26.6 us
    pallas_call x1, Pallas kernels, solve(): pl.pallas_call(solve_kernel, out_shape=jax.ShapeDtypeStruct((size, column...  21.9 us
    ppermute x14, starting transfers between devices, passed_on(): return lax.ppermute(value, 'dp', ahead if step > 0 else back)  20.2 us
    ppermute x4, starting transfers between devices, local(): lax.ppermute(turned[offset], 'dp', ring.shift(offset))  14.9 us
    unnamed x67, local copies, waits for them, and re-layouts  13.4 us
    ppermute x4, waiting for transfers between devices, local(): lax.ppermute(turned[offset], 'dp', ring.shift(offset))  13 us
  transfers between devices with their start and end apart: 41, of which 12 were waited for; matrix products, arithmetic and copies ran while one was open for 15% of the time, Pallas kernels for 27%

profile of v3, /device:TPU:0, one launch (start us, length us, event | category | flops | bytes accessed | tf_op | source)
XLA Modules:
  0.0 253.2 jit_solution(17723320771670325852)
XLA Ops:
  0.7 6.1 %fusion.60 = f32[256,64]{0,1:T(8,128)S(1)} fusion(bf16[256,14336]{1,0:T(8,128)(2,1)} %param.10, bf16[14336,64]{0,1:T(8,128)(2,1)} %param.12), kind=kOutput, calls=%fused_computation.183 | convolution fusion | flops 469762048 | bytes 9240576 | tf_op jit(solution)/shard_map/dot_general | solution.py:455
  8.6 3.0 %collective-permute-start.24 = (f32[64,512]{1,0:T(8,128)S(1)}, f32[64,512]{1,0:T(8,128)S(1)}, u32[]{:S(2)}, u32[]{:S(2)}) collective-permute-start(f32[64,512]{1,0:T(8,128)S(1)} %get-tuple-element.46), channel_id=1, source_target_pairs={{0,4},{2,6},{4,8},{6,10},{8,12},{10,14},{12,0},{14,2},{1,5},{3,7},... | collective-permute-start | bytes 393224 | tf_op jit(solution)/shard_map/ppermute | solution.py:401
  11.6 2.1 collective-permute-start.26
  17.9 1.6 collective-permute-start.22
  20.0 2.8 %collective-permute-start.20 = (bf16[16,1024]{1,0:T(8,128)(2,1)S(1)}, bf16[16,1024]{1,0:T(8,128)(2,1)S(1)}, u32[]{:S(2)}, u32[]{:S(2)}) collective-permute-start(bf16[16,1024]{1,0:T(8,128)(2,1)S(1)} %get-tuple-element.68), channel_id=1, source_target_pairs={{0,12},{2,14},{4,0},{6,2},{8,4},{10,6},{12,8},{14,10},{1,13},{3,15... | collective-permute-start | bytes 98312 | tf_op jit(solution)/shard_map/ppermute | solution.py:401
  22.9 4.5 %collective-permute-done.25 = f32[64,512]{1,0:T(8,128)S(1)} collective-permute-done((f32[64,512]{1,0:T(8,128)S(1)}, f32[64,512]{1,0:T(8,128)S(1)}, u32[]{:S(2)}, u32[]{:S(2)}) %collective-permute-start.25) | collective-permute-done | bytes 131104 | tf_op jit(solution)/shard_map/ppermute | solution.py:401
  27.4 1.6 collective-permute-start.27
  29.0 6.7 %window_terms.5 = (bf16[1,256,1280]{2,1,0:T(8,128)(2,1)}, bf16[1,256,1024]{2,1,0:T(8,128)(2,1)}) custom-call(s32[2]{0:T(128)} %get-tuple-element.76.place_ref, s32[1]{0:T(128)} %constant.143.clone.step_ref, bf16[1024,4096]{1,0:T(8,128)(2,1)} %cols_ref.1, bf16[16,4096]{1,0:T(8,128)(2,1)} %copy-done.19), custom_call_target="tpu_custom_call" | custom-call | flops 2415919104 | bytes 9568256 | tf_op jit(solution)/shard_map/window_terms/pallas_call | solution.py:102
  36.1 8.5 %window_terms.4 = (bf16[2,256,1280]{2,1,0:T(8,128)(2,1)}, bf16[2,256,1024]{2,1,0:T(8,128)(2,1)}) custom-call(s32[2]{0:T(128)} %get-tuple-element.76.place_ref, s32[2]{0:T(128)} %constant.144.clone.step_ref, bf16[1024,4096]{1,0:T(8,128)(2,1)} %cols_ref.1, bf16[16,4096]{1,0:T(8,128)(2,1)} %copy-done.19), custom_call_target="tpu_custom_call" | custom-call | flops 4831838208 | bytes 10747904 | tf_op jit(solution)/shard_map/window_terms/pallas_call | solution.py:102
  44.6 14.0 %window_terms.3 = (bf16[5,256,1280]{2,1,0:T(8,128)(2,1)}, bf16[5,256,1024]{2,1,0:T(8,128)(2,1)}) custom-call(s32[2]{0:T(128)} %get-tuple-element.76.place_ref, s32[5]{0:T(128)} %constant.145.clone.step_ref, bf16[1024,4096]{1,0:T(8,128)(2,1)} %cols_ref.1, bf16[16,4096]{1,0:T(8,128)(2,1)} %copy-done.19), custom_call_target="tpu_custom_call" | custom-call | flops 12079595520 | bytes 14286848 | tf_op jit(solution)/shard_map/window_terms/pallas_call | solution.py:102
  61.4 2.6 %collective-permute-start.29 = (f32[64,512]{1,0:T(8,128)S(1)}, f32[64,512]{1,0:T(8,128)S(1)}, u32[]{:S(2)}, u32[]{:S(2)}) collective-permute-start(f32[64,512]{1,0:T(8,128)S(1)} %add.402), channel_id=1, source_target_pairs={{0,8},{2,10},{4,12},{6,14},{8,0},{10,2},{12,4},{14,6},{1,9},{3,11}... | collective-permute-start | bytes 393224 | tf_op jit(solution)/shard_map/ppermute | solution.py:401
  68.4 3.0 %collective-permute-start.8 = (bf16[256,1024]{1,0:T(8,128)(2,1)}, bf16[256,1024]{1,0:T(8,128)(2,1)}, u32[]{:S(2)}, u32[]{:S(2)}) collective-permute-start(bf16[256,1024]{1,0:T(8,128)(2,1)} %slice_bitcast_fusion.1), channel_id=1, source_target_pairs={{0,4},{4,8},{8,12},{12,14},{14,10},{10,6},{6,2},{2,0},{1,5},{5,9},... | collective-permute-start | bytes 1572872 | tf_op jit(solution)/shard_map/ppermute | solution.py:520
  72.1 1.8 collective-permute-start.5
  74.2 2.2 fusion.5
  77.2 8.0 %collective-permute-done.1 = bf16[256,1280]{1,0:T(8,128)(2,1)} collective-permute-done((bf16[256,1280]{1,0:T(8,128)(2,1)}, bf16[256,1280]{1,0:T(8,128)(2,1)}, u32[]{:S(2)}, u32[]{:S(2)}) %collective-permute-start.1) | collective-permute-done | bytes 655392 | tf_op jit(solution)/shard_map/ppermute | solution.py:520
  85.1 2.1 fusion.2
  87.2 4.0 %collective-permute-start.2 = (bf16[256,1280]{1,0:T(8,128)(2,1)}, bf16[256,1280]{1,0:T(8,128)(2,1)}, u32[]{:S(2)}, u32[]{:S(2)}) collective-permute-start(bf16[256,1280]{1,0:T(8,128)(2,1)} %fusion.2), channel_id=1, source_target_pairs={{0,4},{4,8},{8,12},{12,14},{14,10},{10,6},{6,2},{2,0},{1,5},{5,9},... | collective-permute-start | bytes 1966088 | tf_op jit(solution)/shard_map/ppermute | solution.py:520
  95.4 21.9 %solve.1 = f32[512,128]{1,0:T(8,128)} custom-call(f32[512,512]{1,0:T(8,128)} %multiply_multiply_fusion.matrix_ref, f32[512,128]{1,0:T(8,128)} %multiply_bitcast_fusion.right_ref), custom_call_target="tpu_custom_call" | custom-call | flops 1610612736 | bytes 1572864 | tf_op jit(solution)/shard_map/solve/pallas_call | solution.py:213
  117.3 1.8 broadcast_multiply_fusion.solved_ref
  119.1 9.0 %spread_back.1 = bf16[8,128,256]{2,1,0:T(8,128)(2,1)} custom-call(s32[2]{0:T(128)} %get-tuple-element.76.place_ref, bf16[1024,4096]{1,0:T(8,128)(2,1)} %cols_ref.1, f32[512,128]{1,0:T(8,128)} %broadcast_multiply_fusion.solved_ref, bf16[1024,4096]{1,0:T(8,128)(2,1)} %cols_ref.1), custom_call_target="tpu_custom_call" | custom-call | flops 2013265920 | bytes 5767168 | tf_op jit(solution)/shard_map/spread_back/pallas_call | solution.py:251
  128.1 1.9 constant_dynamic-slice_fusion.7
  130.0 1.7 copy.39
  131.6 1.7 copy.41
  133.3 1.7 copy.40
  135.0 1.6 copy.42
  136.6 4.0 %collective-permute-start.34 = (bf16[2,128,256]{1,2,0:T(8,128)(2,1)}, bf16[2,128,256]{1,2,0:T(8,128)(2,1)S(1)}, u32[]{:S(2)}, u32[]{:S(2)}) collective-permute-start(bf16[2,128,256]{1,2,0:T(8,128)(2,1)} %copy.42), channel_id=1, source_target_pairs={{0,12},{2,14},{4,0},{6,2},{8,4},{10,6},{12,8},{14,10},{1,13},{3,15... | collective-permute-start | bytes 393224 | tf_op jit(solution)/shard_map/ppermute | solution.py:401
  145.9 1.6 fusion.1
  147.5 1.8 collective-permute-start.3
  150.3 3.1 %collective-permute-done.33 = bf16[2,128,256]{1,2,0:T(8,128)(2,1)S(1)} collective-permute-done((bf16[2,128,256]{1,2,0:T(8,128)(2,1)}, bf16[2,128,256]{1,2,0:T(8,128)(2,1)S(1)}, u32[]{:S(2)}, u32[]{:S(2)}) %collective-permute-start.33) | collective-permute-done | bytes 131104 | tf_op jit(solution)/shard_map/ppermute | solution.py:401
  153.5 1.9 collective-permute-start.35
  155.6 6.6 %collective-permute-done.13 = bf16[256,1024]{1,0:T(8,128)(2,1)S(1)} collective-permute-done((bf16[256,1024]{1,0:T(8,128)(2,1)S(1)}, bf16[256,1024]{1,0:T(8,128)(2,1)S(1)}, u32[]{:S(2)}, u32[]{:S(2)}) %collective-permute-start.13) | collective-permute-done | bytes 524320 | tf_op jit(solution)/shard_map/ppermute | solution.py:520
  162.2 2.3 fusion.7
  165.7 1.8 collective-permute-start.9
  167.6 2.1 collective-permute-start.4
  169.7 11.8 %collective-permute-done.9 = bf16[256,1024]{1,0:T(8,128)(2,1)S(1)} collective-permute-done((bf16[256,1024]{1,0:T(8,128)(2,1)S(1)}, bf16[256,1024]{1,0:T(8,128)(2,1)S(1)}, u32[]{:S(2)}, u32[]{:S(2)}) %collective-permute-start.9) | collective-permute-done | bytes 524320 | tf_op jit(solution)/shard_map/ppermute | solution.py:520
  184.1 11.5 %collective-permute-done.4.ahead_ref = bf16[256,1280]{1,0:T(8,128)(2,1)S(1)} collective-permute-done((bf16[256,1280]{1,0:T(8,128)(2,1)S(1)}, bf16[256,1280]{1,0:T(8,128)(2,1)S(1)}, u32[]{:S(2)}, u32[]{:S(2)}) %collective-permute-start.4) | collective-permute-done | bytes 655392 | tf_op jit(solution)/shard_map/ppermute | solution.py:520
  196.5 2.7 %close_window.2 = (bf16[5,256,256]{2,1,0:T(8,128)(2,1)}, bf16[1,256,256]{2,1,0:T(8,128)(2,1)}, bf16[2,256,256]{2,1,0:T(8,128)(2,1)}, bf16[2,256,256]{2,1,0:T(8,128)(2,1)}) custom-call(bf16[5,256,1280]{2,1,0:T(8,128)(2,1)} %get-tuple-element.14.own_ref, bf16[256,1280]{1,0:T(8,128)(2,1)} %copy-done.13, bf16[256,1280]{1,0:T(8,128)(2,1)} %copy-done.12), custom_call_target="tpu_custom_call" | custom-call | flops 1310720 | bytes 3276800 | tf_op jit(solution)/shard_map/close_window/pallas_call | solution.py:142
  199.2 1.9 collective-permute-start.15
  202.1 3.4 %collective-permute-start.38 = (f32[32,128]{1,0:T(8,128)S(1)}, f32[32,128]{1,0:T(8,128)S(1)}, u32[]{:S(2)}, u32[]{:S(2)}) collective-permute-start(f32[32,128]{1,0:T(8,128)S(1)} %get-tuple-element.64), channel_id=1, source_target_pairs={{0,12},{2,14},{4,0},{6,2},{8,4},{10,6},{12,8},{14,10},{1,13},{3,15... | collective-permute-start | bytes 49160 | tf_op jit(solution)/shard_map/ppermute | solution.py:401
  206.4 2.4 close_window.3
  208.8 6.0 %collective-permute-start.17 = (bf16[2,256,256]{2,1,0:T(8,128)(2,1)}, bf16[2,256,256]{2,1,0:T(8,128)(2,1)S(1)}, u32[]{:S(2)}, u32[]{:S(2)}) collective-permute-start(bf16[2,256,256]{2,1,0:T(8,128)(2,1)} %get-tuple-element.24), channel_id=1, source_target_pairs={{0,2},{4,0},{8,4},{12,8},{14,12},{10,14},{6,10},{2,6},{1,3},{5,1},... | collective-permute-start | bytes 786440 | tf_op jit(solution)/shard_map/ppermute | solution.py:559
  214.9 3.7 %collective-permute-start.16 = (bf16[2,256,256]{2,1,0:T(8,128)(2,1)S(1)}, bf16[2,256,256]{2,1,0:T(8,128)(2,1)S(1)}, u32[]{:S(2)}, u32[]{:S(2)}) collective-permute-start(bf16[2,256,256]{2,1,0:T(8,128)(2,1)S(1)} %copy-done.22), channel_id=1, source_target_pairs={{0,6},{4,2},{8,0},{12,4},{14,8},{10,12},{6,14},{2,10},{1,7},{5,3},... | collective-permute-start | bytes 786440 | tf_op jit(solution)/shard_map/ppermute | solution.py:559
  219.8 8.6 %collective-permute-done.16 = bf16[2,256,256]{2,1,0:T(8,128)(2,1)S(1)} collective-permute-done((bf16[2,256,256]{2,1,0:T(8,128)(2,1)S(1)}, bf16[2,256,256]{2,1,0:T(8,128)(2,1)S(1)}, u32[]{:S(2)}, u32[]{:S(2)}) %collective-permute-start.16) | collective-permute-done | bytes 262176 | tf_op jit(solution)/shard_map/ppermute | solution.py:559
  228.4 3.2 %collective-permute-start.18 = (bf16[1,256,256]{2,1,0:T(8,128)(2,1)S(1)}, bf16[1,256,256]{2,1,0:T(8,128)(2,1)S(1)}, u32[]{:S(2)}, u32[]{:S(2)}) collective-permute-start(bf16[1,256,256]{2,1,0:T(8,128)(2,1)S(1)} %copy-done.23), channel_id=1, source_target_pairs={{0,14},{4,10},{8,6},{12,2},{14,0},{10,4},{6,8},{2,12},{1,15},{5,11... | collective-permute-start | bytes 393224 | tf_op jit(solution)/shard_map/ppermute | solution.py:559
  231.6 4.4 %collective-permute-done.18 = bf16[1,256,256]{2,1,0:T(8,128)(2,1)S(1)} collective-permute-done((bf16[1,256,256]{2,1,0:T(8,128)(2,1)S(1)}, bf16[1,256,256]{2,1,0:T(8,128)(2,1)S(1)}, u32[]{:S(2)}, u32[]{:S(2)}) %collective-permute-start.18) | collective-permute-done | bytes 131104 | tf_op jit(solution)/shard_map/ppermute | solution.py:559
  237.4 2.9 %for_sibling.1 = bf16[8,256,256]{2,1,0:T(8,128)(2,1)} custom-call(s32[8]{0:T(128)} %select_n.594.table_ref, bf16[16,256,256]{2,1,0:T(8,128)(2,1)} %copy-done.2, bf16[16,256,256]{2,1,0:T(8,128)(2,1)} %copy-done.2, bf16[16,256,256]{2,1,0:T(8,128)(2,1)} %copy-done.2, bf16[16,256,256]{2,1,0:T(8,128)(2,1)} %copy-done.2), custom_call_target="tpu_custom_call" | custom-call | tf_op jit(solution)/shard_map/for_sibling/pallas_call | solution.py:326
  240.5 3.6 %collective-permute-done.39 = f32[16,128]{1,0:T(8,128)S(1)} collective-permute-done((f32[16,128]{1,0:T(8,128)S(1)}, f32[16,128]{1,0:T(8,128)S(1)}, u32[]{:S(2)}, u32[]{:S(2)}) %collective-permute-start.39) | collective-permute-done | bytes 8224 | tf_op jit(solution)/shard_map/ppermute | solution.py:397
  247.1 5.9 %finish.1 = f32[512,2048]{1,0:T(8,128)} custom-call(s32[48]{0:T(128)} %reshape.260.table_ref, s32[2]{0:T(128)} %get-tuple-element.76.place_ref, bf16[16,256,256]{2,1,0:T(8,128)(2,1)} %copy-done.2, bf16[16,256,256]{2,1,0:T(8,128)(2,1)} %copy-done.2, bf16[16,256,256]{2,1,0:T(8,128)(2,1)} %copy-done.2, bf16[16,256,256]{2,1,0:T(8,128)(2,1)} %copy-done.2, ...), custom_call_target="tpu_custom_call" | custom-call | tf_op jit(solution)/shard_map/finish/pallas_call | solution.py:374
  (181 shorter events, 38.9 us)
Async XLA Ops:
  7.5 8.7 %collective-permute-start = (f32[256,128]{0,1:T(8,128)S(1)}, f32[256,128]{0,1:T(8,128)S(1)}, u32[]{:S(2)}, u32[]{:S(2)}) collective-permute-start(f32[256,128]{0,1:T(8,128)S(1)} %pad_maximum_fusion.1), channel_id=1, source_target_pairs={{0,1},{1,0},{2,3},{3,2},{4,5},{5,4},{6,7},{7,6},{8,9},{9,8},{10,11... | collective-permute-start | bytes 393224 | tf_op jit(solution)/shard_map/ppermute | solution.py:460
  8.6 11.4 %collective-permute-start.24 = (f32[64,512]{1,0:T(8,128)S(1)}, f32[64,512]{1,0:T(8,128)S(1)}, u32[]{:S(2)}, u32[]{:S(2)}) collective-permute-start(f32[64,512]{1,0:T(8,128)S(1)} %get-tuple-element.46), channel_id=1, source_target_pairs={{0,4},{2,6},{4,8},{6,10},{8,12},{10,14},{12,0},{14,2},{1,5},{3,7},... | collective-permute-start | bytes 393224 | tf_op jit(solution)/shard_map/ppermute | solution.py:401
  11.6 11.3 %collective-permute-start.26 = (f32[64,512]{1,0:T(8,128)S(1)}, f32[64,512]{1,0:T(8,128)S(1)}, u32[]{:S(2)}, u32[]{:S(2)}) collective-permute-start(f32[64,512]{1,0:T(8,128)S(1)} %get-tuple-element.47), channel_id=1, source_target_pairs={{0,12},{2,14},{4,0},{6,2},{8,4},{10,6},{12,8},{14,10},{1,13},{3,15... | collective-permute-start | bytes 393224 | tf_op jit(solution)/shard_map/ppermute | solution.py:401
  13.7 13.7 %collective-permute-start.25 = (f32[64,512]{1,0:T(8,128)S(1)}, f32[64,512]{1,0:T(8,128)S(1)}, u32[]{:S(2)}, u32[]{:S(2)}) collective-permute-start(f32[64,512]{1,0:T(8,128)S(1)} %get-tuple-element.48), channel_id=1, source_target_pairs={{0,8},{2,10},{4,12},{6,14},{8,0},{10,2},{12,4},{14,6},{1,9},{3,11}... | collective-permute-start | bytes 393224 | tf_op jit(solution)/shard_map/ppermute | solution.py:401
  17.9 41.6 %collective-permute-start.22 = (bf16[16,1024]{1,0:T(8,128)(2,1)S(1)}, bf16[16,1024]{1,0:T(8,128)(2,1)S(1)}, u32[]{:S(2)}, u32[]{:S(2)}) collective-permute-start(bf16[16,1024]{1,0:T(8,128)(2,1)S(1)} %get-tuple-element.66), channel_id=1, source_target_pairs={{0,4},{2,6},{4,8},{6,10},{8,12},{10,14},{12,0},{14,2},{1,5},{3,7},... | collective-permute-start | bytes 98312 | tf_op jit(solution)/shard_map/ppermute | solution.py:401
  19.5 40.0 %collective-permute-start.21 = (bf16[16,1024]{1,0:T(8,128)(2,1)S(1)}, bf16[16,1024]{1,0:T(8,128)(2,1)S(1)}, u32[]{:S(2)}, u32[]{:S(2)}) collective-permute-start(bf16[16,1024]{1,0:T(8,128)(2,1)S(1)} %get-tuple-element.67), channel_id=1, source_target_pairs={{0,8},{2,10},{4,12},{6,14},{8,0},{10,2},{12,4},{14,6},{1,9},{3,11}... | collective-permute-start | bytes 98312 | tf_op jit(solution)/shard_map/ppermute | solution.py:401
  20.0 39.5 %collective-permute-start.20 = (bf16[16,1024]{1,0:T(8,128)(2,1)S(1)}, bf16[16,1024]{1,0:T(8,128)(2,1)S(1)}, u32[]{:S(2)}, u32[]{:S(2)}) collective-permute-start(bf16[16,1024]{1,0:T(8,128)(2,1)S(1)} %get-tuple-element.68), channel_id=1, source_target_pairs={{0,12},{2,14},{4,0},{6,2},{8,4},{10,6},{12,8},{14,10},{1,13},{3,15... | collective-permute-start | bytes 98312 | tf_op jit(solution)/shard_map/ppermute | solution.py:401
  27.4 32.4 %collective-permute-start.27 = (f32[64,512]{1,0:T(8,128)S(1)}, f32[64,512]{1,0:T(8,128)S(1)}, u32[]{:S(2)}, u32[]{:S(2)}) collective-permute-start(f32[64,512]{1,0:T(8,128)S(1)} %add_add_fusion), channel_id=1, source_target_pairs={{0,2},{2,0},{4,6},{6,4},{8,10},{10,8},{12,14},{14,12},{1,3},{3,1},... | collective-permute-start | bytes 393224 | tf_op jit(solution)/shard_map/ppermute | solution.py:397
  35.6 38.6 %collective-permute-start.11 = (bf16[256,1024]{1,0:T(8,128)(2,1)}, bf16[256,1024]{1,0:T(8,128)(2,1)}, u32[]{:S(2)}, u32[]{:S(2)}) collective-permute-start(bf16[256,1024]{1,0:T(8,128)(2,1)} %bitcast.80), channel_id=1, source_target_pairs={{0,2},{4,0},{8,4},{12,8},{14,12},{10,14},{6,10},{2,6},{1,3},{5,1},... | collective-permute-start | bytes 1572872 | tf_op jit(solution)/shard_map/ppermute | solution.py:520
  59.7 6.5 %collective-permute-start.23 = (bf16[64,768]{1,0:T(8,128)(2,1)S(1)}, bf16[64,768]{1,0:T(8,128)(2,1)S(1)}, u32[]{:S(2)}, u32[]{:S(2)}) collective-permute-start(bf16[64,768]{1,0:T(8,128)(2,1)S(1)} %broadcast_select_fusion), channel_id=1, source_target_pairs={{0,2},{2,0},{4,6},{6,4},{8,10},{10,8},{12,14},{14,12},{1,3},{3,1},... | collective-permute-start | bytes 294920 | tf_op jit(solution)/shard_map/ppermute | solution.py:397
  59.8 8.6 %collective-permute-start.30 = (f32[64,512]{1,0:T(8,128)S(1)}, f32[64,512]{1,0:T(8,128)S(1)}, u32[]{:S(2)}, u32[]{:S(2)}) collective-permute-start(f32[64,512]{1,0:T(8,128)S(1)} %add.402), channel_id=1, source_target_pairs={{0,4},{2,6},{4,8},{6,10},{8,12},{10,14},{12,0},{14,2},{1,5},{3,7},... | collective-permute-start | bytes 393224 | tf_op jit(solution)/shard_map/ppermute | solution.py:401
  61.4 10.7 %collective-permute-start.29 = (f32[64,512]{1,0:T(8,128)S(1)}, f32[64,512]{1,0:T(8,128)S(1)}, u32[]{:S(2)}, u32[]{:S(2)}) collective-permute-start(f32[64,512]{1,0:T(8,128)S(1)} %add.402), channel_id=1, source_target_pairs={{0,8},{2,10},{4,12},{6,14},{8,0},{10,2},{12,4},{14,6},{1,9},{3,11}... | collective-permute-start | bytes 393224 | tf_op jit(solution)/shard_map/ppermute | solution.py:401
  64.0 9.9 %collective-permute-start.28 = (f32[64,512]{1,0:T(8,128)S(1)}, f32[64,512]{1,0:T(8,128)S(1)}, u32[]{:S(2)}, u32[]{:S(2)}) collective-permute-start(f32[64,512]{1,0:T(8,128)S(1)} %add.402), channel_id=1, source_target_pairs={{0,12},{2,14},{4,0},{6,2},{8,4},{10,6},{12,8},{14,10},{1,13},{3,15... | collective-permute-start | bytes 393224 | tf_op jit(solution)/shard_map/ppermute | solution.py:401
  66.2 18.9 %collective-permute-start.1 = (bf16[256,1280]{1,0:T(8,128)(2,1)}, bf16[256,1280]{1,0:T(8,128)(2,1)}, u32[]{:S(2)}, u32[]{:S(2)}) collective-permute-start(bf16[256,1280]{1,0:T(8,128)(2,1)} %bitcast.7), channel_id=1, source_target_pairs={{0,4},{4,8},{8,12},{12,14},{14,10},{10,6},{6,2},{2,0},{1,5},{5,9},... | collective-permute-start | bytes 1966088 | tf_op jit(solution)/shard_map/ppermute | solution.py:520
  66.9 26.1 %copy-start.7 = (bf16[4,2,16,768]{3,2,1,0:T(8,128)(2,1)}, bf16[4,2,16,768]{3,2,1,0:T(8,128)(2,1)S(1)}, u32[]{:S(2)}) copy-start(bf16[4,2,16,768]{3,2,1,0:T(8,128)(2,1)S(1)} %maximum_select_fusion) | copy-start | bytes 589828
  68.4 87.2 %collective-permute-start.8 = (bf16[256,1024]{1,0:T(8,128)(2,1)}, bf16[256,1024]{1,0:T(8,128)(2,1)}, u32[]{:S(2)}, u32[]{:S(2)}) collective-permute-start(bf16[256,1024]{1,0:T(8,128)(2,1)} %slice_bitcast_fusion.1), channel_id=1, source_target_pairs={{0,4},{4,8},{8,12},{12,14},{14,10},{10,6},{6,2},{2,0},{1,5},{5,9},... | collective-permute-start | bytes 1572872 | tf_op jit(solution)/shard_map/ppermute | solution.py:520
  72.1 19.1 %collective-permute-start.5 = (bf16[256,1280]{1,0:T(8,128)(2,1)}, bf16[256,1280]{1,0:T(8,128)(2,1)S(1)}, u32[]{:S(2)}, u32[]{:S(2)}) collective-permute-start(bf16[256,1280]{1,0:T(8,128)(2,1)} %slice_bitcast_fusion), channel_id=1, source_target_pairs={{0,2},{4,0},{8,4},{12,8},{14,12},{10,14},{6,10},{2,6},{1,3},{5,1},... | collective-permute-start | bytes 1966088 | tf_op jit(solution)/shard_map/ppermute | solution.py:520
  74.1 17.1 %copy-start.4 = (bf16[5,256,1280]{2,1,0:T(8,128)(2,1)S(1)}, bf16[5,256,1280]{2,1,0:T(8,128)(2,1)}, u32[]{:S(2)}) copy-start(bf16[5,256,1280]{2,1,0:T(8,128)(2,1)} %get-tuple-element.14.own_ref) | copy-start | bytes 9830404
  74.1 18.6 %collective-permute-start.31 = (f32[256,512]{1,0:T(8,128)S(1)}, f32[256,512]{1,0:T(8,128)S(1)}, u32[]{:S(2)}, u32[]{:S(2)}) collective-permute-start(f32[256,512]{1,0:T(8,128)S(1)} %pad_maximum_fusion), channel_id=1, source_target_pairs={{0,1},{1,0},{2,3},{3,2},{4,5},{5,4},{6,7},{7,6},{8,9},{9,8},{10,11... | collective-permute-start | bytes 1572872 | tf_op jit(solution)/shard_map/ppermute | solution.py:451
  76.5 65.3 %collective-permute-start.12 = (bf16[256,1024]{1,0:T(8,128)(2,1)}, bf16[256,1024]{1,0:T(8,128)(2,1)}, u32[]{:S(2)}, u32[]{:S(2)}) collective-permute-start(bf16[256,1024]{1,0:T(8,128)(2,1)} %fusion.5), channel_id=1, source_target_pairs={{0,2},{4,0},{8,4},{12,8},{14,12},{10,14},{6,10},{2,6},{1,3},{5,1},... | collective-permute-start | bytes 1572872 | tf_op jit(solution)/shard_map/ppermute | solution.py:520
  87.2 56.1 %collective-permute-start.2 = (bf16[256,1280]{1,0:T(8,128)(2,1)}, bf16[256,1280]{1,0:T(8,128)(2,1)}, u32[]{:S(2)}, u32[]{:S(2)}) collective-permute-start(bf16[256,1280]{1,0:T(8,128)(2,1)} %fusion.2), channel_id=1, source_target_pairs={{0,4},{4,8},{8,12},{12,14},{14,10},{10,6},{6,2},{2,0},{1,5},{5,9},... | collective-permute-start | bytes 1966088 | tf_op jit(solution)/shard_map/ppermute | solution.py:520
  92.2 52.6 %collective-permute-start.6 = (bf16[256,1280]{1,0:T(8,128)(2,1)}, bf16[256,1280]{1,0:T(8,128)(2,1)}, u32[]{:S(2)}, u32[]{:S(2)}) collective-permute-start(bf16[256,1280]{1,0:T(8,128)(2,1)} %fusion), channel_id=1, source_target_pairs={{0,2},{4,0},{8,4},{12,8},{14,12},{10,14},{6,10},{2,6},{1,3},{5,1},... | collective-permute-start | bytes 1966088 | tf_op jit(solution)/shard_map/ppermute | solution.py:520
  136.6 10.9 %collective-permute-start.34 = (bf16[2,128,256]{1,2,0:T(8,128)(2,1)}, bf16[2,128,256]{1,2,0:T(8,128)(2,1)S(1)}, u32[]{:S(2)}, u32[]{:S(2)}) collective-permute-start(bf16[2,128,256]{1,2,0:T(8,128)(2,1)} %copy.42), channel_id=1, source_target_pairs={{0,12},{2,14},{4,0},{6,2},{8,4},{10,6},{12,8},{14,10},{1,13},{3,15... | collective-permute-start | bytes 393224 | tf_op jit(solution)/shard_map/ppermute | solution.py:401
  141.8 8.5 %collective-permute-start.32 = (bf16[2,128,256]{1,2,0:T(8,128)(2,1)}, bf16[2,128,256]{1,2,0:T(8,128)(2,1)S(1)}, u32[]{:S(2)}, u32[]{:S(2)}) collective-permute-start(bf16[2,128,256]{1,2,0:T(8,128)(2,1)} %copy.40), channel_id=1, source_target_pairs={{0,4},{2,6},{4,8},{6,10},{8,12},{10,14},{12,0},{14,2},{1,5},{3,7},... | collective-permute-start | bytes 393224 | tf_op jit(solution)/shard_map/ppermute | solution.py:401
  143.3 18.9 %copy-start.5 = (bf16[5,256,1024]{2,1,0:T(8,128)(2,1)S(1)}, bf16[5,256,1024]{2,1,0:T(8,128)(2,1)}, u32[]{:S(2)}) copy-start(bf16[5,256,1024]{2,1,0:T(8,128)(2,1)} %get-tuple-element.18.own_ref) | copy-start | bytes 7864324
  143.3 10.2 %collective-permute-start.33 = (bf16[2,128,256]{1,2,0:T(8,128)(2,1)}, bf16[2,128,256]{1,2,0:T(8,128)(2,1)S(1)}, u32[]{:S(2)}, u32[]{:S(2)}) collective-permute-start(bf16[2,128,256]{1,2,0:T(8,128)(2,1)} %copy.41), channel_id=1, source_target_pairs={{0,8},{2,10},{4,12},{6,14},{8,0},{10,2},{12,4},{14,6},{1,9},{3,11}... | collective-permute-start | bytes 393224 | tf_op jit(solution)/shard_map/ppermute | solution.py:401
  144.8 17.4 %collective-permute-start.13 = (bf16[256,1024]{1,0:T(8,128)(2,1)S(1)}, bf16[256,1024]{1,0:T(8,128)(2,1)S(1)}, u32[]{:S(2)}, u32[]{:S(2)}) collective-permute-start(bf16[256,1024]{1,0:T(8,128)(2,1)S(1)} %fusion.6), channel_id=1, source_target_pairs={{0,2},{4,0},{8,4},{12,8},{14,12},{10,14},{6,10},{2,6},{1,3},{5,1},... | collective-permute-start | bytes 1572872 | tf_op jit(solution)/shard_map/ppermute | solution.py:520
  147.5 20.0 %collective-permute-start.3 = (bf16[256,1280]{1,0:T(8,128)(2,1)S(1)}, bf16[256,1280]{1,0:T(8,128)(2,1)S(1)}, u32[]{:S(2)}, u32[]{:S(2)}) collective-permute-start(bf16[256,1280]{1,0:T(8,128)(2,1)S(1)} %get-tuple-element.37), channel_id=1, source_target_pairs={{0,4},{4,8},{8,12},{12,14},{14,10},{10,6},{6,2},{2,0},{1,5},{5,9},... | collective-permute-start | bytes 1966088 | tf_op jit(solution)/shard_map/ppermute | solution.py:520
  153.5 30.2 %collective-permute-start.35 = (bf16[128,256]{0,1:T(8,128)(2,1)S(1)}, bf16[128,256]{0,1:T(8,128)(2,1)S(1)}, u32[]{:S(2)}, u32[]{:S(2)}) collective-permute-start(bf16[128,256]{0,1:T(8,128)(2,1)S(1)} %fusion.29), channel_id=1, source_target_pairs={{0,2},{2,0},{4,6},{6,4},{8,10},{10,8},{12,14},{14,12},{1,3},{3,1},... | collective-permute-start | bytes 196616 | tf_op jit(solution)/shard_map/ppermute | solution.py:397
  155.4 28.8 %collective-permute-start.7 = (bf16[256,1280]{1,0:T(8,128)(2,1)S(1)}, bf16[256,1280]{1,0:T(8,128)(2,1)S(1)}, u32[]{:S(2)}, u32[]{:S(2)}) collective-permute-start(bf16[256,1280]{1,0:T(8,128)(2,1)S(1)} %get-tuple-element.36), channel_id=1, source_target_pairs={{0,2},{4,0},{8,4},{12,8},{14,12},{10,14},{6,10},{2,6},{1,3},{5,1},... | collective-permute-start | bytes 1966088 | tf_op jit(solution)/shard_map/ppermute | solution.py:520
  164.5 18.1 %copy-start.20 = (bf16[128,256]{0,1:T(8,128)(2,1)S(1)}, bf16[128,256]{0,1:T(8,128)(2,1)}, u32[]{:S(2)}) copy-start(bf16[128,256]{0,1:T(8,128)(2,1)} %copy.37) | copy-start | bytes 196612
  164.5 41.1 %collective-permute-start.14 = (bf16[256,1024]{1,0:T(8,128)(2,1)}, bf16[256,1024]{1,0:T(8,128)(2,1)}, u32[]{:S(2)}, u32[]{:S(2)}) collective-permute-start(bf16[256,1024]{1,0:T(8,128)(2,1)} %get-tuple-element.38), channel_id=1, source_target_pairs={{0,2},{4,0},{8,4},{12,8},{14,12},{10,14},{6,10},{2,6},{1,3},{5,1},... | collective-permute-start | bytes 1572872 | tf_op jit(solution)/shard_map/ppermute | solution.py:520
  165.7 15.8 %collective-permute-start.9 = (bf16[256,1024]{1,0:T(8,128)(2,1)S(1)}, bf16[256,1024]{1,0:T(8,128)(2,1)S(1)}, u32[]{:S(2)}, u32[]{:S(2)}) collective-permute-start(bf16[256,1024]{1,0:T(8,128)(2,1)S(1)} %get-tuple-element.39), channel_id=1, source_target_pairs={{0,4},{4,8},{8,12},{12,14},{14,10},{10,6},{6,2},{2,0},{1,5},{5,9},... | collective-permute-start | bytes 1572872 | tf_op jit(solution)/shard_map/ppermute | solution.py:520
  167.6 28.0 %collective-permute-start.4 = (bf16[256,1280]{1,0:T(8,128)(2,1)S(1)}, bf16[256,1280]{1,0:T(8,128)(2,1)S(1)}, u32[]{:S(2)}, u32[]{:S(2)}) collective-permute-start(bf16[256,1280]{1,0:T(8,128)(2,1)S(1)} %fusion.4), channel_id=1, source_target_pairs={{0,4},{4,8},{8,12},{12,14},{14,10},{10,6},{6,2},{2,0},{1,5},{5,9},... | collective-permute-start | bytes 1966088 | tf_op jit(solution)/shard_map/ppermute | solution.py:520
  181.8 23.8 %collective-permute-start.10 = (bf16[256,1024]{1,0:T(8,128)(2,1)S(1)}, bf16[256,1024]{1,0:T(8,128)(2,1)S(1)}, u32[]{:S(2)}, u32[]{:S(2)}) collective-permute-start(bf16[256,1024]{1,0:T(8,128)(2,1)S(1)} %fusion.9), channel_id=1, source_target_pairs={{0,4},{4,8},{8,12},{12,14},{14,10},{10,6},{6,2},{2,0},{1,5},{5,9},... | collective-permute-start | bytes 1572872 | tf_op jit(solution)/shard_map/ppermute | solution.py:520
  199.2 15.7 %copy-start.22 = (bf16[2,256,256]{2,1,0:T(8,128)(2,1)S(1)}, bf16[2,256,256]{2,1,0:T(8,128)(2,1)}, u32[]{:S(2)}) copy-start(bf16[2,256,256]{2,1,0:T(8,128)(2,1)} %get-tuple-element.23) | copy-start | bytes 786436
  199.2 19.4 %copy-start.14 = (bf16[5,256,256]{2,1,0:T(8,128)(2,1)S(1)}, bf16[5,256,256]{2,1,0:T(8,128)(2,1)}, u32[]{:S(2)}) copy-start(bf16[5,256,256]{2,1,0:T(8,128)(2,1)} %get-tuple-element.17) | copy-start | bytes 1966084
  199.2 20.5 %collective-permute-start.15 = (bf16[2,256,256]{2,1,0:T(8,128)(2,1)}, bf16[2,256,256]{2,1,0:T(8,128)(2,1)S(1)}, u32[]{:S(2)}, u32[]{:S(2)}) collective-permute-start(bf16[2,256,256]{2,1,0:T(8,128)(2,1)} %get-tuple-element.22), channel_id=1, source_target_pairs={{0,12},{4,14},{8,10},{12,6},{14,2},{10,0},{6,4},{2,8},{1,13},{5,15... | collective-permute-start | bytes 786440 | tf_op jit(solution)/shard_map/ppermute | solution.py:559
  201.1 39.2 %collective-permute-start.36 = (f32[32,128]{1,0:T(8,128)S(1)}, f32[32,128]{1,0:T(8,128)S(1)}, u32[]{:S(2)}, u32[]{:S(2)}) collective-permute-start(f32[32,128]{1,0:T(8,128)S(1)} %get-tuple-element.63), channel_id=1, source_target_pairs={{0,4},{2,6},{4,8},{6,10},{8,12},{10,14},{12,0},{14,2},{1,5},{3,7},... | collective-permute-start | bytes 49160 | tf_op jit(solution)/shard_map/ppermute | solution.py:401
  202.1 38.2 %collective-permute-start.38 = (f32[32,128]{1,0:T(8,128)S(1)}, f32[32,128]{1,0:T(8,128)S(1)}, u32[]{:S(2)}, u32[]{:S(2)}) collective-permute-start(f32[32,128]{1,0:T(8,128)S(1)} %get-tuple-element.64), channel_id=1, source_target_pairs={{0,12},{2,14},{4,0},{6,2},{8,4},{10,6},{12,8},{14,10},{1,13},{3,15... | collective-permute-start | bytes 49160 | tf_op jit(solution)/shard_map/ppermute | solution.py:401
  208.8 19.6 %copy-start.23 = (bf16[1,256,256]{2,1,0:T(8,128)(2,1)S(1)}, bf16[1,256,256]{2,1,0:T(8,128)(2,1)}, u32[]{:S(2)}) copy-start(bf16[1,256,256]{2,1,0:T(8,128)(2,1)} %get-tuple-element.25) | copy-start | bytes 393220
  208.8 22.8 %collective-permute-start.17 = (bf16[2,256,256]{2,1,0:T(8,128)(2,1)}, bf16[2,256,256]{2,1,0:T(8,128)(2,1)S(1)}, u32[]{:S(2)}, u32[]{:S(2)}) collective-permute-start(bf16[2,256,256]{2,1,0:T(8,128)(2,1)} %get-tuple-element.24), channel_id=1, source_target_pairs={{0,2},{4,0},{8,4},{12,8},{14,12},{10,14},{6,10},{2,6},{1,3},{5,1},... | collective-permute-start | bytes 786440 | tf_op jit(solution)/shard_map/ppermute | solution.py:559
  214.9 13.5 %collective-permute-start.16 = (bf16[2,256,256]{2,1,0:T(8,128)(2,1)S(1)}, bf16[2,256,256]{2,1,0:T(8,128)(2,1)S(1)}, u32[]{:S(2)}, u32[]{:S(2)}) collective-permute-start(bf16[2,256,256]{2,1,0:T(8,128)(2,1)S(1)} %copy-done.22), channel_id=1, source_target_pairs={{0,6},{4,2},{8,0},{12,4},{14,8},{10,12},{6,14},{2,10},{1,7},{5,3},... | collective-permute-start | bytes 786440 | tf_op jit(solution)/shard_map/ppermute | solution.py:559
  219.7 20.6 %collective-permute-start.37 = (f32[32,128]{1,0:T(8,128)S(1)}, f32[32,128]{1,0:T(8,128)S(1)}, u32[]{:S(2)}, u32[]{:S(2)}) collective-permute-start(f32[32,128]{1,0:T(8,128)S(1)} %get-tuple-element.65), channel_id=1, source_target_pairs={{0,8},{2,10},{4,12},{6,14},{8,0},{10,2},{12,4},{14,6},{1,9},{3,11}... | collective-permute-start | bytes 49160 | tf_op jit(solution)/shard_map/ppermute | solution.py:401
  228.4 7.7 %collective-permute-start.18 = (bf16[1,256,256]{2,1,0:T(8,128)(2,1)S(1)}, bf16[1,256,256]{2,1,0:T(8,128)(2,1)S(1)}, u32[]{:S(2)}, u32[]{:S(2)}) collective-permute-start(bf16[1,256,256]{2,1,0:T(8,128)(2,1)S(1)} %copy-done.23), channel_id=1, source_target_pairs={{0,14},{4,10},{8,6},{12,2},{14,0},{10,4},{6,8},{2,12},{1,15},{5,11... | collective-permute-start | bytes 393224 | tf_op jit(solution)/shard_map/ppermute | solution.py:559
  240.3 5.8 %collective-permute-start.19 = (bf16[8,256,256]{2,1,0:T(8,128)(2,1)}, bf16[8,256,256]{2,1,0:T(8,128)(2,1)S(1)}, u32[]{:S(2)}, u32[]{:S(2)}) collective-permute-start(bf16[8,256,256]{2,1,0:T(8,128)(2,1)} %for_sibling.1), channel_id=1, source_target_pairs={{0,1},{1,0},{2,3},{3,2},{4,5},{5,4},{6,7},{7,6},{8,9},{9,8},{10,11... | collective-permute-start | bytes 3145736 | tf_op jit(solution)/shard_map/ppermute | solution.py:562
  240.4 3.7 %collective-permute-start.39 = (f32[16,128]{1,0:T(8,128)S(1)}, f32[16,128]{1,0:T(8,128)S(1)}, u32[]{:S(2)}, u32[]{:S(2)}) collective-permute-start(f32[16,128]{1,0:T(8,128)S(1)} %constant_dynamic-slice_fusion), channel_id=1, source_target_pairs={{0,2},{2,0},{4,6},{6,4},{8,10},{10,8},{12,14},{14,12},{1,3},{3,1},... | collective-permute-start | bytes 24584 | tf_op jit(solution)/shard_map/ppermute | solution.py:397
  244.1 1.2 collective-permute-start.40
  (19 other events, 122.5 us)

commit v4 on v3

--- a/solution.py
+++ b/solution.py
@@ -11,6 +11,8 @@
 EXACT = lax.Precision.HIGHEST
 SWAP = [(0, 1), (1, 0)]
 VMEM_BYTES = 56 * 1024 * 1024
+LIGHT = pl.CostEstimate(flops=10**6, bytes_accessed=10**5, transcendentals=0)
+ANYWHERE = pl.BlockSpec(memory_space=pl.ANY)
 
 
 class Ring:
@@ -70,19 +72,19 @@
     return found
 
 
-def window_terms(ring, place, stored, vectors, group, steps, far_slots, near_slots):
+def window_terms(ring, place, stored, vectors, group, steps, parts, after=()):
     rows, full = stored.shape
     new_rows = vectors.shape[0]
     taps = jnp.array(steps, jnp.int32)
 
-    def kernel(place_ref, step_ref, stored_ref, vectors_ref, far_ref, near_ref):
+    def kernel(place_ref, step_ref, stored_ref, vectors_ref, *refs):
         owner = ring.position_of(place_ref[0]) + step_ref[pl.program_id(0)] + ring.count
         owner = lax.rem(owner, ring.count)
         core = place_ref[1]
         left = pl.ds(pl.multiple_of((2 * ring.index_at(owner) + core) * group, group), group)
         turned = stored_ref[:, left].T
         turned_new = vectors_ref[:, left].T
-        for slots, out_ref in ((far_slots, far_ref), (near_slots, near_ref)):
+        for slots, out_ref in zip(parts, refs[len(after) :]):
             for offset, blocks, first in pairs_of(slots):
                 column = 2 * ring.index_at(owner + offset)
                 if blocks == 1:
@@ -98,7 +100,6 @@
     def shape(slots):
         return jax.ShapeDtypeStruct((len(steps), group, len(slots) * group), jnp.bfloat16)
 
-    blocks = len(far_slots) + len(near_slots)
     return pl.pallas_call(
         kernel,
         grid_spec=pltpu.PrefetchScalarGridSpec(
@@ -107,28 +108,58 @@
             in_specs=[
                 pl.BlockSpec((rows, full), lambda i, a, b: (0, 0), pipeline_mode=pl.Buffered(1)),
                 pl.BlockSpec((new_rows, full), lambda i, a, b: (0, 0), pipeline_mode=pl.Buffered(1)),
-            ],
-            out_specs=[out(far_slots), out(near_slots)],
+            ]
+            + [ANYWHERE] * len(after),
+            out_specs=[out(slots) for slots in parts],
         ),
-        out_shape=[shape(far_slots), shape(near_slots)],
+        out_shape=[shape(slots) for slots in parts],
         compiler_params=pltpu.CompilerParams(vmem_limit_bytes=VMEM_BYTES),
-        cost_estimate=pl.CostEstimate(
-            flops=4 * rows * len(steps) * blocks * group * group,
-            bytes_accessed=2 * rows * full + 2 * len(steps) * blocks * group * group,
-            transcendentals=0,
-        ),
+        cost_estimate=LIGHT,
         name="window_terms",
-    )(place, taps, stored, vectors)
-
-
-def close_window(own, ahead, back, slots, group):
+    )(place, taps, stored, vectors, *after)
+
+
+def add_terms(terms, index, arrived, sizes, group, after=()):
+    count = terms.shape[2] // group
+
+    def kernel(terms_ref, *refs):
+        outs = refs[len(arrived) + len(after) :]
+        for k in range(count):
+            total = terms_ref[0, :, k * group : (k + 1) * group].astype(jnp.float32)
+            for ref, (array, first) in zip(refs, arrived):
+                if first <= k < first + array.shape[1] // group:
+                    total = total + ref[:, (k - first) * group : (k - first + 1) * group].astype(jnp.float32)
+            place, start = 0, 0
+            while k - start >= sizes[place]:
+                start += sizes[place]
+                place += 1
+            outs[place][:, (k - start) * group : (k - start + 1) * group] = total.astype(jnp.bfloat16)
+
+    def flat(columns):
+        return pl.BlockSpec((group, columns), lambda i: (0, 0))
+
+    return pl.pallas_call(
+        kernel,
+        grid=(1,),
+        in_specs=[pl.BlockSpec((1, group, count * group), lambda i: (index, 0, 0))]
+        + [flat(array.shape[1]) for array, _ in arrived]
+        + [ANYWHERE] * len(after),
+        out_specs=[flat(size * group) for size in sizes],
+        out_shape=[jax.ShapeDtypeStruct((group, size * group), jnp.bfloat16) for size in sizes],
+        compiler_params=pltpu.CompilerParams(vmem_limit_bytes=VMEM_BYTES),
+        cost_estimate=LIGHT,
+        name="add_terms",
+    )(terms, *[array for array, _ in arrived], *after)
+
+
+def close_window(terms, base, ahead, back, slots, group):
     count = len(slots)
     chips = [chip for chip in pairs_of(slots) if chip[0] != 0]
 
     def kernel(own_ref, ahead_ref, back_ref, blocks_ref, *turned_refs):
         for k in range(count):
             cols = slice(k * group, (k + 1) * group)
-            total = own_ref[0, :, cols].astype(jnp.float32)
+            total = own_ref[0, :, (base + k) * group : (base + k + 1) * group].astype(jnp.float32)
             total = total + ahead_ref[:, cols].astype(jnp.float32) + back_ref[:, cols].astype(jnp.float32)
             total = total.astype(jnp.bfloat16)
             blocks_ref[k] = total
@@ -136,63 +167,61 @@
                 if first <= k < first + blocks:
                     turned_ref[k - first] = total.T
 
-    index = own.shape[0] - 1
+    index = terms.shape[0] - 1
     flat = pl.BlockSpec((group, count * group), lambda i: (0, 0))
     sizes = [count] + [blocks for _, blocks, _ in chips]
     return pl.pallas_call(
         kernel,
         grid=(1,),
-        in_specs=[pl.BlockSpec((1, group, count * group), lambda i: (index, 0, 0)), flat, flat],
+        in_specs=[pl.BlockSpec((1,) + terms.shape[1:], lambda i: (index, 0, 0)), flat, flat],
         out_specs=[pl.BlockSpec((size, group, group), lambda i: (0, 0, 0)) for size in sizes],
         out_shape=[jax.ShapeDtypeStruct((size, group, group), jnp.bfloat16) for size in sizes],
         compiler_params=pltpu.CompilerParams(vmem_limit_bytes=VMEM_BYTES),
-        cost_estimate=pl.CostEstimate(flops=4 * count * group**2, bytes_accessed=10 * count * group**2, transcendentals=0),
+        cost_estimate=LIGHT,
         name="close_window",
-    )(own, ahead, back)
+    )(terms, ahead, back)
 
 
 def rough_dot(left, right):
     return jnp.dot(left.astype(jnp.bfloat16), right.astype(jnp.bfloat16), preferred_element_type=jnp.float32)
 
 
-def solve_kernel(matrix_ref, right_ref, out_ref, work, inverse, residual):
+def split_terms(value):
+    high = value.astype(jnp.bfloat16)
+    value = value - high.astype(jnp.float32)
+    middle = value.astype(jnp.bfloat16)
+    value = value - middle.astype(jnp.float32)
+    return high, middle, value.astype(jnp.bfloat16)
+
+
+def identity(size):
+    rows = lax.broadcasted_iota(jnp.int32, (size, size), 0)
+    cols = lax.broadcasted_iota(jnp.int32, (size, size), 1)
+    return (rows == cols).astype(jnp.float32)
+
+
+def eliminate(matrix_ref, right_ref, out_ref, work, block):
     size = matrix_ref.shape[0]
-    block = inverse.shape[0]
     work[...] = matrix_ref[...]
     out_ref[...] = right_ref[...]
-    row_ids = lax.broadcasted_iota(jnp.int32, (block, block), 0)
-    col_ids = lax.broadcasted_iota(jnp.int32, (block, block), 1)
-    eye = (row_ids == col_ids).astype(jnp.float32)
+    eye = identity(block)
     for start in range(0, size, block):
         here = slice(start, start + block)
         rest = slice(start + block, size)
         corner = work[here, here]
         norm = jnp.max(jnp.sum(jnp.abs(corner), axis=0))
-        inverse[...] = eye / norm
-        residual[...] = eye - corner / norm
-
-        def improve(dot):
-            def step_of(state):
-                step, _ = state
-                better = inverse[...] + dot(inverse[...], residual[...])
-                left_over = eye - dot(work[here, here], better)
-                inverse[...] = better
-                residual[...] = left_over
-                return step + 1, jnp.max(jnp.abs(left_over))
-
-            return step_of
-
-        def until(steps, bound):
-            return lambda state: jnp.logical_and(state[0] < steps, state[1] > bound)
-
-        begin = (jnp.int32(0), jnp.float32(1.0))
-        lax.while_loop(until(10, 0.02), improve(rough_dot), begin)
-        left_over = eye - exact_dot(work[here, here], inverse[...])
-        good = jnp.max(jnp.sum(jnp.abs(left_over), axis=0)) < 0.7
-        inverse[...] = jnp.where(good, inverse[...], eye / norm)
-        residual[...] = jnp.where(good, left_over, eye - work[here, here] / norm)
-        lax.while_loop(until(40, 5e-5), improve(exact_dot), begin)
-        found = inverse[...] + exact_dot(inverse[...], residual[...])
+
+        def unfinished(state):
+            return jnp.logical_and(state[0] < 40, state[1] > 5e-5)
+
+        def improve(state):
+            step, _, inverse = state
+            better = inverse + exact_dot(inverse, eye - exact_dot(work[here, here], inverse))
+            left_over = eye - exact_dot(work[here, here], better)
+            return step + 1, jnp.max(jnp.abs(left_over)), better
+
+        found = lax.while_loop(unfinished, improve, (jnp.int32(0), jnp.float32(1.0), eye / norm))[2]
+        found = found + exact_dot(found, eye - exact_dot(work[here, here], found))
         solved = exact_dot(found, out_ref[here, :])
         out_ref[here, :] = solved
         if start + block < size:
@@ -207,69 +236,122 @@
         out_ref[here, :] = out_ref[here, :] - exact_dot(work[here, rest], out_ref[rest, :])
 
 
-def solve(matrix, right):
-    size, columns = right.shape
-    block = 128
+def solve(place, mine, other, first_cols, after=()):
+    group, width = mine.shape
+    examples = first_cols.shape[0]
+
+    def kernel(place_ref, mine_ref, other_ref, first_ref, *refs):
+        out_ref, pairs_ref, matrix, right, power, inverse = refs[len(after) :]
+        eye = identity(width)
+        t = place_ref[1]
+        matrix[pl.ds(pl.multiple_of(t * group, group), group), :] = mine_ref[...]
+        matrix[pl.ds(pl.multiple_of((1 - t) * group, group), group), :] = other_ref[...]
+        turned = first_ref[...].T
+        full = matrix[...] + jnp.dot(turned, first_ref[...], preferred_element_type=jnp.float32) + damping * eye
+        diagonal = full * eye
+        rows_scale = lax.rsqrt(jnp.sum(diagonal, axis=1, keepdims=True))
+        cols_scale = lax.rsqrt(jnp.sum(diagonal, axis=0, keepdims=True))
+        full = full * rows_scale * cols_scale
+        matrix[...] = full
+        right[...] = turned.astype(jnp.float32) * rows_scale
+
+        sums = jnp.max(jnp.sum(jnp.abs(full), axis=0))
+        squared = rough_dot(full, full)
+        norm = jnp.sqrt(jnp.max(jnp.sum(jnp.abs(squared), axis=0)) + sums * sums / 128)
+        start = eye - full / norm
+        inverse[...] = eye + start
+        power[...] = start.astype(jnp.bfloat16)
+        for _ in range(7):
+            raised = jnp.dot(power[...], power[...], preferred_element_type=jnp.float32).astype(jnp.bfloat16)
+            power[...] = raised
+            held = inverse[...]
+            inverse[...] = held + jnp.dot(held.astype(jnp.bfloat16), raised, preferred_element_type=jnp.float32)
+        power[...] = (inverse[...] / norm).astype(jnp.bfloat16)
+
+        largest = jnp.max(jnp.abs(right[...]))
+        out_ref[...] = jnp.dot(power[...], right[...].astype(jnp.bfloat16), preferred_element_type=jnp.float32)
+
+        def unfinished(state):
+            return jnp.logical_and(state[0] < 12, jnp.logical_not(state[1] <= 5e-5 * largest))
+
+        def refine(state):
+            left_over = right[...] - exact_dot(matrix[...], out_ref[...])
+            change = jnp.dot(power[...], left_over.astype(jnp.bfloat16), preferred_element_type=jnp.float32)
+            out_ref[...] = out_ref[...] + change
+            return state[0] + 1, jnp.max(jnp.abs(left_over))
+
+        worst = lax.while_loop(unfinished, refine, (jnp.int32(0), 1.0 + largest))[1]
+
+        @pl.when(jnp.logical_not(worst <= 5e-5 * largest))
+        def _():
+            eliminate(matrix, right, out_ref, inverse, 128)
+
+        solved = out_ref[...] * rows_scale
+        out_ref[...] = solved
+        pairs = jnp.zeros((examples, examples), jnp.float32)
+        for term in split_terms(solved):
+            pairs = pairs + jnp.dot(first_ref[...], term, preferred_element_type=jnp.float32)
+        pairs_ref[...] = pairs
+
+    whole = pl.BlockSpec(memory_space=pltpu.VMEM)
     return pl.pallas_call(
-        solve_kernel,
-        out_shape=jax.ShapeDtypeStruct((size, columns), jnp.float32),
+        kernel,
+        in_specs=[pl.BlockSpec(memory_space=pltpu.SMEM)] + [whole] * 3 + [ANYWHERE] * len(after),
+        out_shape=[
+            jax.ShapeDtypeStruct((width, examples), jnp.float32),
+            jax.ShapeDtypeStruct((examples, examples), jnp.float32),
+        ],
         scratch_shapes=[
-            pltpu.VMEM((size, size), jnp.float32),
-            pltpu.VMEM((block, block), jnp.float32),
-            pltpu.VMEM((block, block), jnp.float32),
+            pltpu.VMEM((width, width), jnp.float32),
+            pltpu.VMEM((width, examples), jnp.float32),
+            pltpu.VMEM((width, width), jnp.bfloat16),
+            pltpu.VMEM((width, width), jnp.float32),
         ],
         compiler_params=pltpu.CompilerParams(vmem_limit_bytes=VMEM_BYTES),
-        cost_estimate=pl.CostEstimate(flops=12 * size**3, bytes_accessed=4 * size * (size + 2 * columns), transcendentals=0),
+        cost_estimate=LIGHT,
         name="solve",
-    )(matrix, right)
-
-
-def split_terms(value):
-    high = value.astype(jnp.bfloat16)
-    value = value - high.astype(jnp.float32)
-    middle = value.astype(jnp.bfloat16)
-    value = value - middle.astype(jnp.float32)
-    return high, middle, value.astype(jnp.bfloat16)
-
-
-def spread_back(place, stored, solved, owners, group):
+    )(place, mine, other, first_cols, *after)
+
+
+def spread_back(place, stored, solved, owners, group, after=()):
     rows = stored.shape[0]
     width, examples = solved.shape
-
-    def kernel(place_ref, first_ref, solved_ref, cols_ref, out_ref, terms):
-        @pl.when(pl.program_id(0) == 0)
-        def _():
-            total = jnp.zeros((rows, examples), jnp.float32)
-            for term in split_terms(solved_ref[...]):
-                total = total + jnp.dot(first_ref[...], term, preferred_element_type=jnp.float32)
-            for index, term in enumerate(split_terms(total.T)[:2]):
-                terms[index * examples : (index + 1) * examples, :] = term
-
-        product = jnp.dot(terms[...], cols_ref[...], preferred_element_type=jnp.float32)
-        out_ref[0] = (product[:examples] + product[examples:]).astype(jnp.bfloat16)
+    pairs = owners // 2
+
+    def kernel(place_ref, first_ref, solved_ref, *refs):
+        cols, outs = refs[:owners], refs[owners + len(after) :]
+        total = jnp.zeros((rows, examples), jnp.float32)
+        for term in split_terms(solved_ref[...]):
+            total = total + jnp.dot(first_ref[...], term, preferred_element_type=jnp.float32)
+        terms = jnp.concatenate(split_terms(total.T)[:2], axis=0)
+        for index in range(owners):
+            product = jnp.dot(terms, cols[index][...], preferred_element_type=jnp.float32)
+            outs[index // 2][index % 2] = (product[:examples] + product[examples:]).astype(jnp.bfloat16)
+
+    def owner(index, ref):
+        return 2 * lax.rem(ref[0] // 2 + index // 2, pairs) + index % 2
 
     return pl.pallas_call(
         kernel,
         grid_spec=pltpu.PrefetchScalarGridSpec(
             num_scalar_prefetch=1,
-            grid=(owners,),
+            grid=(1,),
             in_specs=[
-                pl.BlockSpec((rows, width), lambda o, ref: (0, 0)),
-                pl.BlockSpec((width, examples), lambda o, ref: (0, 0)),
-                pl.BlockSpec((rows, group), lambda o, ref: (0, 2 * o + ref[1])),
-            ],
-            out_specs=pl.BlockSpec((1, examples, group), lambda o, ref: (o, 0, 0)),
-            scratch_shapes=[pltpu.VMEM((2 * examples, rows), jnp.bfloat16)],
+                pl.BlockSpec((rows, width), lambda i, ref: (0, 0)),
+                pl.BlockSpec((width, examples), lambda i, ref: (0, 0)),
+            ]
+            + [
+                pl.BlockSpec((rows, group), lambda i, ref, index=index: (0, 2 * owner(index, ref) + ref[1]))
+                for index in range(owners)
+            ]
+            + [ANYWHERE] * len(after),
+            out_specs=[pl.BlockSpec((2, examples, group), lambda i, ref: (0, 0, 0))] * pairs,
         ),
-        out_shape=jax.ShapeDtypeStruct((owners, examples, group), jnp.bfloat16),
+        out_shape=[jax.ShapeDtypeStruct((2, examples, group), jnp.bfloat16)] * pairs,
         compiler_params=pltpu.CompilerParams(vmem_limit_bytes=VMEM_BYTES),
-        cost_estimate=pl.CostEstimate(
-            flops=6 * rows * examples * (width + owners * group),
-            bytes_accessed=2 * rows * (width + owners * group) + 2 * owners * examples * group,
-            transcendentals=0,
-        ),
+        cost_estimate=LIGHT,
         name="spread_back",
-    )(place, stored, solved, stored)
+    )(place, stored, solved, *([stored] * owners), *after)
 
 
 def assembly_tables(ring, slots, d, t):
@@ -335,6 +417,7 @@
         ),
         out_shape=jax.ShapeDtypeStruct((total, group, group), jnp.bfloat16),
         compiler_params=pltpu.CompilerParams(vmem_limit_bytes=VMEM_BYTES),
+        cost_estimate=LIGHT,
         name="for_sibling",
     )(table, *([blocks] * wide))
 
@@ -381,6 +464,7 @@
         ),
         out_shape=jax.ShapeDtypeStruct((2 * group, 2 * half * group), jnp.float32),
         compiler_params=pltpu.CompilerParams(vmem_limit_bytes=VMEM_BYTES),
+        cost_estimate=LIGHT,
         name="finish",
     )(table, place, *([blocks] * len(order)), *([other] * len(order)))
 
@@ -448,7 +532,7 @@
     corner_rows = corner_rows + pair_swap(corner_rows, owners)
     corner_rows = exchange_pairs(lambda index: corner_rows, pair, owners)
     corner_rows = jnp.concatenate(natural(corner_rows, pair), axis=0)
-    corner = in_order(t, corner_rows, lax.ppermute(corner_rows, "tensor", SWAP), 0)
+    corner_other = lax.ppermute(corner_rows, "tensor", SWAP)
 
     sides = jnp.concatenate(
         [
@@ -496,45 +580,42 @@
     for offset in ring.offsets[split:] + [0]:
         near_slots += [(offset, 0), (offset, 1)]
 
-    def terms_of(steps):
-        return window_terms(ring, place, stored, vectors, group, steps, far_slots, near_slots)
-
-    outermost = terms_of([half])
-    second = terms_of([half - 1, 1 - half])
+    slots = far_slots + near_slots
+    far_count, near_count = len(far_slots), len(near_slots)
+    ahead, back = ring.shift(1), ring.shift(-1)
+
+    def terms_of(steps, parts, after=()):
+        return window_terms(ring, place, stored, vectors, group, steps, parts, after)
+
+    far, near = terms_of([half], [far_slots, near_slots])
+    far, near = far[0], near[0]
+    second = terms_of([half - 1, 1 - half], [slots], [far])[0]
+    far_ahead = lax.ppermute(far, "dp", ahead)
+    near_back = lax.ppermute(near, "dp", back)
+    last = [far_count, near_count] if half == 2 else [far_count + near_count]
+    going = add_terms(second, 0, [(far_ahead, 0)], last, group)
+    coming = add_terms(second, 1, [(near_back, far_count)], last, group)
+
     later_steps = [s for step in range(half - 2, 0, -1) for s in (step, -step)] + [0]
-    later = terms_of(later_steps)
-
-    def term(kind, step):
-        if abs(step) == half:
-            return outermost[kind][0]
-        if abs(step) == half - 1:
-            return second[kind][0 if step > 0 else 1]
-        return later[kind][later_steps.index(step)]
-
-    ahead, back = ring.shift(1), ring.shift(-1)
-
-    def passed_on(kind, step, arrived):
-        value = term(kind, step)
-        if arrived is not None:
-            value = (value.astype(jnp.float32) + arrived.astype(jnp.float32)).astype(jnp.bfloat16)
-        return lax.ppermute(value, "dp", ahead if step > 0 else back)
-
-    far_ahead = far_back = near_ahead = near_back = None
-    for step in range(half, 0, -1):
-        far_ahead = passed_on(0, step, far_ahead)
-        near_back = passed_on(1, -step, near_back)
-        if step < half:
-            far_back = passed_on(0, -step, far_back)
-            near_ahead = passed_on(1, step, near_ahead)
-
-    eye = jnp.eye(width, dtype=jnp.float32)
-    corner = corner + lead_dot(first_cols, first_cols) + damping * eye
-    scale = lax.rsqrt(jnp.sum(corner * eye, axis=1))
-    first_cols = first_cols.astype(jnp.float32)
-    solved = solve(corner * scale[:, None] * scale[None, :], first_cols.T * scale[:, None]) * scale[:, None]
-    first_pairs = exact_dot(first_cols, solved)
-    terms = spread_back(place, stored, solved, owners, group)
-    terms = scatter_pairs(terms, pair, owners)
+    later = terms_of(later_steps, [slots], [going[0], coming[0]])[0]
+    solved, first_pairs = solve(place, corner_rows, corner_other, first_cols, [later])
+    token = solved
+    for step in range(half - 2, 0, -1):
+        last = [far_count, near_count] if step == 1 else [far_count + near_count]
+        going = [lax.ppermute(value, "dp", ahead) for value in going]
+        coming = [lax.ppermute(value, "dp", back) for value in coming]
+        index = later_steps.index(step)
+        going = add_terms(later, index, [(going[0], 0)], last, group, [token])
+        coming = add_terms(later, index + 1, [(coming[0], 0)], last, group, [token])
+        if step == half - 2:
+            pieces = spread_back(place, stored, solved, owners, group, [going[0], coming[0]])
+            token = pieces[0]
+    going = [lax.ppermute(value, "dp", ahead) for value in going]
+    coming = [lax.ppermute(value, "dp", back) for value in coming]
+
+    terms = pieces[0].astype(jnp.float32)
+    for step in range(1, owners // 2):
+        terms = terms + far_shift(pieces[step], step, owners).astype(jnp.float32)
     away = jnp.where(side == 0, terms[1], terms[0]).astype(jnp.bfloat16)
     terms = jnp.where(side == 0, terms[0], terms[1]) + pair_swap(away, owners).astype(jnp.float32)
     damped = lax.dynamic_slice_in_dim(solved.T, lax.rem(g, 2) * group, group, 1)
@@ -549,8 +630,8 @@
     chosen = (query_ids[:, None] == jnp.arange(all_examples, dtype=jnp.int32)[None, :]).astype(jnp.float32)
     scores = lax.dot_general(chosen, pairs, (((1,), (1,)), ((), ())), precision=EXACT, preferred_element_type=jnp.float32) / R
 
-    far = close_window(later[0], far_ahead, far_back, far_slots, group)
-    near = close_window(later[1], near_ahead, near_back, near_slots, group)
+    far = close_window(later, 0, going[0], coming[0], far_slots, group)
+    near = close_window(later, far_count, going[1], coming[1], near_slots, group)
     turned = {}
     for (found, slots) in ((far, far_slots), (near, near_slots)):
         chips = [chip for chip in pairs_of(slots) if chip[0] != 0]

time: 256 us -> 246 us (0.961)
  starting transfers between devices: 65.9 us -> 50.7 us
  Pallas kernels: 74 us -> 86.5 us
  other arithmetic: 16.3 us -> 3.92 us
  waiting for transfers between devices: 64.2 us -> 73 us
    ppermute x15 -> x11, waiting for transfers between devices: 37.9 us -> 8.87 us  [the longest x4 6.27 us: local(): going = [lax.ppermute(value, 'dp', ahead) for value in going]]
    ppermute x4, waiting for transfers between devices: 3.57 us -> 30 us  [pair_swap(): lax.ppermute(value, 'dp', [(index, index ^ 1) for index in range(count)])]
    pallas_call x3 -> x9, Pallas kernels: 27 us -> 40.9 us  [the longest x1 18.6 us: solve(): pl.pallas_call(kernel, in_specs=[pl.BlockSpec(memory_space=pltpu.SMEM)] +...]
    convert_element_type x8 -> x0, other arithmetic: 10.9 us -> none  [passed_on(): (value.astype(jnp.float32) + arrived.astype(jnp.float32)).astype(jnp.bflo...]
    ppermute x15, waiting for transfers between devices: 9.29 us -> 19.5 us  [far_shift(): lax.ppermute(value, 'dp', [(index, (index + 2 * step) % count) for index...]
    ppermute x15 -> x11, starting transfers between devices: 20.3 us -> 10.2 us  [the longest x4 6.04 us: local(): going = [lax.ppermute(value, 'dp', ahead) for value in going]]
    ppermute x15, starting transfers between devices: 26.6 us -> 21.9 us  [far_shift(): lax.ppermute(value, 'dp', [(index, (index + 2 * step) % count) for index...]
    ppermute x4, starting transfers between devices: 14.9 us -> 10.5 us  [local(): lax.ppermute(turned[offset], 'dp', ring.shift(offset))]
  transfers between devices with their start and end apart: 41 -> 37, of which waited for: 12 -> 13; matrix products, arithmetic and copies ran while one was open for 15% -> 6% of each run, Pallas kernels for 27% -> 33%
where the time goes in v4:
time: 246 us; the launch traced here: 244 us
  Pallas kernels  86.5 us (35%)
  waiting for transfers between devices  73 us (30%)
  starting transfers between devices  50.7 us (21%)
  local copies, waits for them, and re-layouts  17.1 us (7%)
  matrix products  11.7 us (5%)
  other arithmetic  3.92 us (2%)
    ppermute x4, waiting for transfers between devices, pair_swap(): lax.ppermute(value, 'dp', [(index, index ^ 1) for index in range(count)])  30 us
    pallas_call x3, Pallas kernels, window_terms(): pl.pallas_call(kernel, grid_spec=pltpu.PrefetchScalarGridSpec(num_scalar_...  29.4 us
    ppermute x15, starting transfers between devices, far_shift(): lax.ppermute(value, 'dp', [(index, (index + 2 * step) % count) for index...  21.9 us
    ppermute x15, waiting for transfers between devices, far_shift(): lax.ppermute(value, 'dp', [(index, (index + 2 * step) % count) for index...  19.5 us
    pallas_call x1, Pallas kernels, solve(): pl.pallas_call(kernel, in_specs=[pl.BlockSpec(memory_space=pltpu.SMEM)] +...  18.6 us
    pallas_call x6, Pallas kernels, add_terms(): pl.pallas_call(kernel, grid=(1,), in_specs=[pl.BlockSpec((1, group, count...  16.8 us
    ppermute x4, waiting for transfers between devices, local(): lax.ppermute(turned[offset], 'dp', ring.shift(offset))  14.1 us
    unnamed x53, local copies, waits for them, and re-layouts  12.9 us
  transfers between devices with their start and end apart: 37, of which 13 were waited for; matrix products, arithmetic and copies ran while one was open for 6% of the time, Pallas kernels for 33%

profile of v4, /device:TPU:0, one launch (start us, length us, event | category | flops | bytes accessed | tf_op | source)
XLA Modules:
  0.0 244.1 jit_solution(7755458766635958216)
XLA Ops:
  0.7 6.1 %fusion.33 = f32[256,64]{0,1:T(8,128)S(1)} fusion(bf16[256,14336]{1,0:T(8,128)(2,1)} %param.10, bf16[14336,64]{0,1:T(8,128)(2,1)} %param.12), kind=kOutput, calls=%fused_computation.126 | convolution fusion | flops 469762048 | bytes 9240576 | tf_op jit(solution)/shard_map/dot_general | solution.py:539
  10.1 2.9 %collective-permute-start.4 = (f32[64,512]{1,0:T(8,128)}, f32[64,512]{1,0:T(8,128)S(1)}, u32[]{:S(2)}, u32[]{:S(2)}) collective-permute-start(f32[64,512]{1,0:T(8,128)} %get-tuple-element.44), channel_id=1, source_target_pairs={{0,4},{2,6},{4,8},{6,10},{8,12},{10,14},{12,0},{14,2},{1,5},{3,7},... | collective-permute-start | bytes 393224 | tf_op jit(solution)/shard_map/ppermute | solution.py:485
  13.0 2.6 %collective-permute-start.5 = (f32[64,512]{1,0:T(8,128)}, f32[64,512]{1,0:T(8,128)S(1)}, u32[]{:S(2)}, u32[]{:S(2)}) collective-permute-start(f32[64,512]{1,0:T(8,128)} %get-tuple-element.46), channel_id=1, source_target_pairs={{0,8},{2,10},{4,12},{6,14},{8,0},{10,2},{12,4},{14,6},{1,9},{3,11}... | collective-permute-start | bytes 393224 | tf_op jit(solution)/shard_map/ppermute | solution.py:485
  15.6 1.3 collective-permute-start.6
  20.0 6.6 %window_terms.3 = (bf16[1,256,1280]{2,1,0:T(8,128)(2,1)}, bf16[1,256,1024]{2,1,0:T(8,128)(2,1)}) custom-call(s32[2]{0:T(128)} %pad_add_fusion.1.place_ref, s32[1]{0:T(128)} %constant.140.clone.step_ref, bf16[1024,4096]{1,0:T(8,128)(2,1)} %refs_7_.1, bf16[16,4096]{1,0:T(8,128)(2,1)} %copy-done.4), custom_call_target="tpu_custom_call" | custom-call | flops 1000000 | bytes 100000 | tf_op jit(solution)/shard_map/window_terms/pallas_call | solution.py:103
  27.3 1.3 collective-permute-start.2
  30.0 1.7 collective-permute-start.13
  32.6 8.7 %window_terms.4.terms_ref = bf16[2,256,2304]{2,1,0:T(8,128)(2,1)} custom-call(s32[2]{0:T(128)} %pad_add_fusion.1.place_ref, s32[2]{0:T(128)} %constant.141.clone.step_ref, bf16[1024,4096]{1,0:T(8,128)(2,1)} %refs_7_.1, bf16[16,4096]{1,0:T(8,128)(2,1)} %copy-done.4, bf16[256,1280]{1,0:T(8,128)(2,1)} %bitcast.35), custom_call_target="tpu_custom_call" | custom-call | flops 1000000 | bytes 100000 | tf_op jit(solution)/shard_map/window_terms/pallas_call | solution.py:103
  42.3 3.3 %collective-permute-start.7 = (f32[64,512]{1,0:T(8,128)S(1)}, f32[64,512]{1,0:T(8,128)S(1)}, u32[]{:S(2)}, u32[]{:S(2)}) collective-permute-start(f32[64,512]{1,0:T(8,128)S(1)} %add_add_fusion), channel_id=1, source_target_pairs={{0,2},{2,0},{4,6},{6,4},{8,10},{10,8},{12,14},{14,12},{1,3},{3,1},... | collective-permute-start | bytes 393224 | tf_op jit(solution)/shard_map/ppermute | solution.py:481
  45.7 2.9 %collective-permute-done.7 = f32[64,512]{1,0:T(8,128)S(1)} collective-permute-done((f32[64,512]{1,0:T(8,128)S(1)}, f32[64,512]{1,0:T(8,128)S(1)}, u32[]{:S(2)}, u32[]{:S(2)}) %collective-permute-start.7) | collective-permute-done | bytes 131104 | tf_op jit(solution)/shard_map/ppermute | solution.py:481
  48.6 1.8 collective-permute-start.10
  50.4 2.1 collective-permute-start.8
  53.3 2.6 %add_terms.7.refs_1_ = bf16[256,2304]{1,0:T(8,128)(2,1)} custom-call(bf16[2,256,2304]{2,1,0:T(8,128)(2,1)} %window_terms.4.terms_ref, bf16[256,1024]{1,0:T(8,128)(2,1)} %copy-done.17), custom_call_target="tpu_custom_call" | custom-call | flops 1000000 | bytes 100000 | tf_op jit(solution)/shard_map/add_terms/pallas_call | solution.py:141
  55.9 2.0 collective-permute-start.17
  58.8 2.7 %add_terms.6.refs_0_ = bf16[256,2304]{1,0:T(8,128)(2,1)} custom-call(bf16[2,256,2304]{2,1,0:T(8,128)(2,1)} %window_terms.4.terms_ref, bf16[256,1280]{1,0:T(8,128)(2,1)} %copy-done.13), custom_call_target="tpu_custom_call" | custom-call | flops 1000000 | bytes 100000 | tf_op jit(solution)/shard_map/add_terms/pallas_call | solution.py:141
  61.6 1.2 collective-permute-done.9
  64.0 23.5 %collective-permute-done.15 = bf16[64,768]{1,0:T(8,128)(2,1)S(1)} collective-permute-done((bf16[64,768]{1,0:T(8,128)(2,1)S(1)}, bf16[64,768]{1,0:T(8,128)(2,1)S(1)}, u32[]{:S(2)}, u32[]{:S(2)}) %collective-permute-start.15) | collective-permute-done | bytes 98336 | tf_op jit(solution)/shard_map/ppermute | solution.py:481
  88.3 14.1 %window_terms.5.refs_0_.terms_ref.own_ref = bf16[5,256,2304]{2,1,0:T(8,128)(2,1)} custom-call(s32[2]{0:T(128)} %pad_add_fusion.1.place_ref, s32[5]{0:T(128)} %constant.142.clone.step_ref, bf16[1024,4096]{1,0:T(8,128)(2,1)} %refs_7_.1, bf16[16,4096]{1,0:T(8,128)(2,1)} %copy-done.4, bf16[256,2304]{1,0:T(8,128)(2,1)} %add_terms.6.refs_0_, ...), custom_call_target="tpu_custom_call" | custom-call | flops 1000000 | bytes 100000 | tf_op jit(solution)/shard_map/window_terms/pallas_call | solution.py:103
  103.2 18.6 %solve.1 = (f32[512,128]{1,0:T(8,128)}, f32[128,128]{1,0:T(8,128)}) custom-call(s32[2]{0:T(128)} %pad_add_fusion.1.place_ref, f32[256,512]{1,0:T(8,128)} %copy-done.5, f32[256,512]{1,0:T(8,128)} %copy-done.14, bf16[128,512]{1,0:T(8,128)(2,1)} %slice.57.first_ref, bf16[5,256,2304]{2,1,0:T(8,128)(2,1)} %window_terms.5.refs_0_.terms_ref.own_ref), custom_call_target="tpu_custom_call" | custom-call | flops 1000000 | bytes 100000 | tf_op jit(solution)/shard_map/solve/pallas_call | solution.py:297
  122.7 2.9 %add_terms.9.refs_9_ = bf16[256,2304]{1,0:T(8,128)(2,1)} custom-call(bf16[5,256,2304]{2,1,0:T(8,128)(2,1)} %window_terms.5.refs_0_.terms_ref.own_ref, bf16[256,2304]{1,0:T(8,128)(2,1)} %copy-done.7, f32[512,128]{1,0:T(8,128)} %get-tuple-element.22.refs_1_.solved_ref), custom_call_target="tpu_custom_call" | custom-call | flops 1000000 | bytes 100000 | tf_op jit(solution)/shard_map/add_terms/pallas_call | solution.py:141
  126.7 2.9 %add_terms.8.refs_8_ = bf16[256,2304]{1,0:T(8,128)(2,1)} custom-call(bf16[5,256,2304]{2,1,0:T(8,128)(2,1)} %window_terms.5.refs_0_.terms_ref.own_ref, bf16[256,2304]{1,0:T(8,128)(2,1)} %copy-done.8, f32[512,128]{1,0:T(8,128)} %get-tuple-element.22.refs_1_.solved_ref), custom_call_target="tpu_custom_call" | custom-call | flops 1000000 | bytes 100000 | tf_op jit(solution)/shard_map/add_terms/pallas_call | solution.py:141
  129.6 2.0 collective-permute-start.16
  131.7 7.6 %spread_back.1 = (bf16[2,128,256]{2,1,0:T(8,128)(2,1)}, bf16[2,128,256]{2,1,0:T(8,128)(2,1)}, bf16[2,128,256]{2,1,0:T(8,128)(2,1)}, bf16[2,128,256]{2,1,0:T(8,128)(2,1)}) custom-call(s32[2]{0:T(128)} %pad_add_fusion.1.place_ref, bf16[1024,4096]{1,0:T(8,128)(2,1)} %refs_7_.1, f32[512,128]{1,0:T(8,128)} %get-tuple-element.22.refs_1_.solved_ref, ...), custom_call_target="tpu_custom_call" | custom-call | flops 1000000 | bytes 100000 | tf_op jit(solution)/shard_map/spread_back/pallas_call | solution.py:334
  140.3 2.8 %collective-permute-start.30 = (bf16[2,128,256]{2,1,0:T(8,128)(2,1)}, bf16[2,128,256]{2,1,0:T(8,128)(2,1)S(1)}, u32[]{:S(2)}, u32[]{:S(2)}) collective-permute-start(bf16[2,128,256]{2,1,0:T(8,128)(2,1)} %get-tuple-element.37), channel_id=1, source_target_pairs={{0,12},{2,14},{4,0},{6,2},{8,4},{10,6},{12,8},{14,10},{1,13},{3,15... | collective-permute-start | bytes 393224 | tf_op jit(solution)/shard_map/ppermute | solution.py:485
  143.2 14.4 %collective-permute-done.28 = bf16[2,128,256]{2,1,0:T(8,128)(2,1)S(1)} collective-permute-done((bf16[2,128,256]{2,1,0:T(8,128)(2,1)}, bf16[2,128,256]{2,1,0:T(8,128)(2,1)S(1)}, u32[]{:S(2)}, u32[]{:S(2)}) %collective-permute-start.28) | collective-permute-done | bytes 131104 | tf_op jit(solution)/shard_map/ppermute | solution.py:485
  157.6 1.5 collective-permute-done.29
  159.0 1.4 collective-permute-done.30
  162.1 3.2 %collective-permute-start.31 = (bf16[128,256]{1,0:T(8,128)(2,1)}, bf16[128,256]{1,0:T(8,128)(2,1)}, u32[]{:S(2)}, u32[]{:S(2)}) collective-permute-start(bf16[128,256]{1,0:T(8,128)(2,1)} %fusion.13), channel_id=1, source_target_pairs={{0,2},{2,0},{4,6},{6,4},{8,10},{10,8},{12,14},{14,12},{1,3},{3,1},... | collective-permute-start | bytes 196616 | tf_op jit(solution)/shard_map/ppermute | solution.py:481
  165.3 2.9 %add_terms.11 = (bf16[256,1280]{1,0:T(8,128)(2,1)}, bf16[256,1024]{1,0:T(8,128)(2,1)}) custom-call(bf16[5,256,2304]{2,1,0:T(8,128)(2,1)} %window_terms.5.refs_0_.terms_ref.own_ref, bf16[256,2304]{1,0:T(8,128)(2,1)} %collective-permute-done.19.refs_0_, bf16[2,128,256]{2,1,0:T(8,128)(2,1)} %get-tuple-element.23.refs_1_), custom_call_target="tpu_custom_call" | custom-call | flops 1000000 | bytes 100000 | tf_op jit(solution)/shard_map/add_terms/pallas_call | solution.py:141
  169.2 2.8 %add_terms.10 = (bf16[256,1280]{1,0:T(8,128)(2,1)}, bf16[256,1024]{1,0:T(8,128)(2,1)}) custom-call(bf16[5,256,2304]{2,1,0:T(8,128)(2,1)} %window_terms.5.refs_0_.terms_ref.own_ref, bf16[256,2304]{1,0:T(8,128)(2,1)} %copy-done.6, bf16[2,128,256]{2,1,0:T(8,128)(2,1)} %get-tuple-element.23.refs_1_), custom_call_target="tpu_custom_call" | custom-call | flops 1000000 | bytes 100000 | tf_op jit(solution)/shard_map/add_terms/pallas_call | solution.py:141
  172.0 2.0 collective-permute-start.18
  174.9 2.0 collective-permute-start.21
  176.9 1.3 fusion.1
  179.4 2.6 %collective-permute-done.20.back_ref = bf16[256,1280]{1,0:T(8,128)(2,1)} collective-permute-done((bf16[256,1280]{1,0:T(8,128)(2,1)}, bf16[256,1280]{1,0:T(8,128)(2,1)}, u32[]{:S(2)}, u32[]{:S(2)}) %collective-permute-start.20) | collective-permute-done | bytes 655392 | tf_op jit(solution)/shard_map/ppermute | solution.py:614
  182.0 6.3 %collective-permute-done.18.ahead_ref = bf16[256,1280]{1,0:T(8,128)(2,1)S(1)} collective-permute-done((bf16[256,1280]{1,0:T(8,128)(2,1)}, bf16[256,1280]{1,0:T(8,128)(2,1)S(1)}, u32[]{:S(2)}, u32[]{:S(2)}) %collective-permute-start.18) | collective-permute-done | bytes 655392 | tf_op jit(solution)/shard_map/ppermute | solution.py:613
  189.1 2.9 %close_window.2 = (bf16[5,256,256]{2,1,0:T(8,128)(2,1)}, bf16[1,256,256]{2,1,0:T(8,128)(2,1)}, bf16[2,256,256]{2,1,0:T(8,128)(2,1)}, bf16[2,256,256]{2,1,0:T(8,128)(2,1)}) custom-call(bf16[5,256,2304]{2,1,0:T(8,128)(2,1)} %window_terms.5.refs_0_.terms_ref.own_ref, bf16[256,1280]{1,0:T(8,128)(2,1)} %copy-done.11, ...), custom_call_target="tpu_custom_call" | custom-call | flops 1000000 | bytes 100000 | tf_op jit(solution)/shard_map/close_window/pallas_call | solution.py:173
  192.0 7.2 %collective-permute-start.23 = (bf16[2,256,256]{2,1,0:T(8,128)(2,1)}, bf16[2,256,256]{2,1,0:T(8,128)(2,1)S(1)}, u32[]{:S(2)}, u32[]{:S(2)}) collective-permute-start(bf16[2,256,256]{2,1,0:T(8,128)(2,1)} %get-tuple-element.30), channel_id=1, source_target_pairs={{0,12},{4,14},{8,10},{12,6},{14,2},{10,0},{6,4},{2,8},{1,13},{5,15... | collective-permute-start | bytes 786440 | tf_op jit(solution)/shard_map/ppermute | solution.py:640
  199.2 2.7 %collective-permute-start.33 = (f32[32,128]{1,0:T(8,128)S(1)}, f32[32,128]{1,0:T(8,128)S(1)}, u32[]{:S(2)}, u32[]{:S(2)}) collective-permute-start(f32[32,128]{1,0:T(8,128)S(1)} %get-tuple-element.63), channel_id=1, source_target_pairs={{0,8},{2,10},{4,12},{6,14},{8,0},{10,2},{12,4},{14,6},{1,9},{3,11}... | collective-permute-start | bytes 49160 | tf_op jit(solution)/shard_map/ppermute | solution.py:485
  203.5 2.6 %close_window.3 = (bf16[4,256,256]{2,1,0:T(8,128)(2,1)}, bf16[2,256,256]{2,1,0:T(8,128)(2,1)}) custom-call(bf16[5,256,2304]{2,1,0:T(8,128)(2,1)} %window_terms.5.refs_0_.terms_ref.own_ref, bf16[256,1024]{1,0:T(8,128)(2,1)} %copy-done.19, bf16[256,1024]{1,0:T(8,128)(2,1)} %copy-done.18), custom_call_target="tpu_custom_call" | custom-call | flops 1000000 | bytes 100000 | tf_op jit(solution)/shard_map/close_window/pallas_call | solution.py:173
  206.2 1.9 collective-permute-start.24
  209.3 2.5 %collective-permute-start.34 = (f32[32,128]{1,0:T(8,128)S(1)}, f32[32,128]{1,0:T(8,128)S(1)}, u32[]{:S(2)}, u32[]{:S(2)}) collective-permute-start(f32[32,128]{1,0:T(8,128)S(1)} %get-tuple-element.62), channel_id=1, source_target_pairs={{0,12},{2,14},{4,0},{6,2},{8,4},{10,6},{12,8},{14,10},{1,13},{3,15... | collective-permute-start | bytes 49160 | tf_op jit(solution)/shard_map/ppermute | solution.py:485
  211.8 7.7 %collective-permute-done.24 = bf16[2,256,256]{2,1,0:T(8,128)(2,1)S(1)} collective-permute-done((bf16[2,256,256]{2,1,0:T(8,128)(2,1)S(1)}, bf16[2,256,256]{2,1,0:T(8,128)(2,1)S(1)}, u32[]{:S(2)}, u32[]{:S(2)}) %collective-permute-start.24) | collective-permute-done | bytes 262176 | tf_op jit(solution)/shard_map/ppermute | solution.py:640
  219.5 1.3 collective-permute-start.26
  220.9 6.3 %collective-permute-done.26 = bf16[1,256,256]{2,1,0:T(8,128)(2,1)S(1)} collective-permute-done((bf16[1,256,256]{2,1,0:T(8,128)(2,1)S(1)}, bf16[1,256,256]{2,1,0:T(8,128)(2,1)S(1)}, u32[]{:S(2)}, u32[]{:S(2)}) %collective-permute-start.26) | collective-permute-done | bytes 131104 | tf_op jit(solution)/shard_map/ppermute | solution.py:640
  227.2 1.3 copy-done.1
  228.5 2.9 %for_sibling.1 = bf16[8,256,256]{2,1,0:T(8,128)(2,1)} custom-call(s32[8]{0:T(128)} %select_n.641.table_ref, bf16[16,256,256]{2,1,0:T(8,128)(2,1)} %copy-done.1, bf16[16,256,256]{2,1,0:T(8,128)(2,1)} %copy-done.1, bf16[16,256,256]{2,1,0:T(8,128)(2,1)} %copy-done.1, bf16[16,256,256]{2,1,0:T(8,128)(2,1)} %copy-done.1), custom_call_target="tpu_custom_call" | custom-call | flops 1000000 | bytes 100000 | tf_op jit(solution)/shard_map/for_sibling/pallas_call | solution.py:408
  231.7 3.6 %collective-permute-done.35 = f32[16,128]{1,0:T(8,128)S(1)} collective-permute-done((f32[16,128]{1,0:T(8,128)S(1)}, f32[16,128]{1,0:T(8,128)S(1)}, u32[]{:S(2)}, u32[]{:S(2)}) %collective-permute-start.35) | collective-permute-done | bytes 8224 | tf_op jit(solution)/shard_map/ppermute | solution.py:481
  238.3 5.8 %finish.1 = f32[512,2048]{1,0:T(8,128)} custom-call(s32[48]{0:T(128)} %reshape.234.table_ref, s32[2]{0:T(128)} %pad_add_fusion.1.place_ref, bf16[16,256,256]{2,1,0:T(8,128)(2,1)} %copy-done.1, bf16[16,256,256]{2,1,0:T(8,128)(2,1)} %copy-done.1, bf16[16,256,256]{2,1,0:T(8,128)(2,1)} %copy-done.1, bf16[16,256,256]{2,1,0:T(8,128)(2,1)} %copy-done.1, ...), custom_call_target="tpu_custom_call" | custom-call | flops 1000000 | bytes 100000 | tf_op jit(solution)/shard_map/finish/pallas_call | solution.py:457
  (147 shorter events, 29.6 us)
Async XLA Ops:
  0.6 6.1 %copy-start = (bf16[256,4096]{1,0:T(8,128)(2,1)S(1)}, bf16[256,4096]{1,0:T(8,128)(2,1)}, u32[]{:S(2)}) copy-start(bf16[256,4096]{1,0:T(8,128)(2,1)} %param.11) | copy-start | bytes 6291460
  0.6 6.1 %copy-start.16 = (bf16[4096,64]{0,1:T(8,128)(2,1)S(1)}, bf16[4096,64]{0,1:T(8,128)(2,1)}, u32[]{:S(2)}) copy-start(bf16[4096,64]{0,1:T(8,128)(2,1)} %param.13) | copy-start | bytes 1572868
  7.5 10.1 %collective-permute-start = (f32[256,128]{0,1:T(8,128)S(1)}, f32[256,128]{0,1:T(8,128)S(1)}, u32[]{:S(2)}, u32[]{:S(2)}) collective-permute-start(f32[256,128]{0,1:T(8,128)S(1)} %pad_maximum_fusion.1), channel_id=1, source_target_pairs={{0,1},{1,0},{2,3},{3,2},{4,5},{5,4},{6,7},{7,6},{8,9},{9,8},{10,11... | collective-permute-start | bytes 393224 | tf_op jit(solution)/shard_map/ppermute | solution.py:544
  8.1 8.9 %copy-start.20 = (s32[16]{0:T(128)S(1)}, s32[16]{0:T(128)}, u32[]{:S(2)}) copy-start(s32[16]{0:T(128)} %param.15) | copy-start | bytes 196
  10.1 19.4 %collective-permute-start.4 = (f32[64,512]{1,0:T(8,128)}, f32[64,512]{1,0:T(8,128)S(1)}, u32[]{:S(2)}, u32[]{:S(2)}) collective-permute-start(f32[64,512]{1,0:T(8,128)} %get-tuple-element.44), channel_id=1, source_target_pairs={{0,4},{2,6},{4,8},{6,10},{8,12},{10,14},{12,0},{14,2},{1,5},{3,7},... | collective-permute-start | bytes 393224 | tf_op jit(solution)/shard_map/ppermute | solution.py:485
  13.0 16.9 %collective-permute-start.5 = (f32[64,512]{1,0:T(8,128)}, f32[64,512]{1,0:T(8,128)S(1)}, u32[]{:S(2)}, u32[]{:S(2)}) collective-permute-start(f32[64,512]{1,0:T(8,128)} %get-tuple-element.46), channel_id=1, source_target_pairs={{0,8},{2,10},{4,12},{6,14},{8,0},{10,2},{12,4},{14,6},{1,9},{3,11}... | collective-permute-start | bytes 393224 | tf_op jit(solution)/shard_map/ppermute | solution.py:485
  15.6 16.0 %collective-permute-start.6 = (f32[64,512]{1,0:T(8,128)S(1)}, f32[64,512]{1,0:T(8,128)S(1)}, u32[]{:S(2)}, u32[]{:S(2)}) collective-permute-start(f32[64,512]{1,0:T(8,128)S(1)} %get-tuple-element.45), channel_id=1, source_target_pairs={{0,12},{2,14},{4,0},{6,2},{8,4},{10,6},{12,8},{14,10},{1,13},{3,15... | collective-permute-start | bytes 393224 | tf_op jit(solution)/shard_map/ppermute | solution.py:485
  26.6 31.3 %collective-permute-start.1 = (bf16[256,1280]{1,0:T(8,128)(2,1)}, bf16[256,1280]{1,0:T(8,128)(2,1)S(1)}, u32[]{:S(2)}, u32[]{:S(2)}) collective-permute-start(bf16[256,1280]{1,0:T(8,128)(2,1)} %bitcast.34), channel_id=1, source_target_pairs={{0,4},{4,8},{8,12},{12,14},{14,10},{10,6},{6,2},{2,0},{1,5},{5,9},... | collective-permute-start | bytes 1966088 | tf_op jit(solution)/shard_map/ppermute | solution.py:593
  27.3 25.3 %collective-permute-start.2 = (bf16[256,1024]{1,0:T(8,128)(2,1)}, bf16[256,1024]{1,0:T(8,128)(2,1)S(1)}, u32[]{:S(2)}, u32[]{:S(2)}) collective-permute-start(bf16[256,1024]{1,0:T(8,128)(2,1)} %bitcast.40), channel_id=1, source_target_pairs={{0,2},{4,0},{8,4},{12,8},{14,12},{10,14},{6,10},{2,6},{1,3},{5,1},... | collective-permute-start | bytes 1572872 | tf_op jit(solution)/shard_map/ppermute | solution.py:594
  29.4 12.9 %collective-permute-start.12 = (bf16[16,1024]{1,0:T(8,128)(2,1)S(1)}, bf16[16,1024]{1,0:T(8,128)(2,1)S(1)}, u32[]{:S(2)}, u32[]{:S(2)}) collective-permute-start(bf16[16,1024]{1,0:T(8,128)(2,1)S(1)} %get-tuple-element.66), channel_id=1, source_target_pairs={{0,12},{2,14},{4,0},{6,2},{8,4},{10,6},{12,8},{14,10},{1,13},{3,15... | collective-permute-start | bytes 98312 | tf_op jit(solution)/shard_map/ppermute | solution.py:485
  30.0 15.7 %collective-permute-start.13 = (bf16[16,1024]{1,0:T(8,128)(2,1)S(1)}, bf16[16,1024]{1,0:T(8,128)(2,1)S(1)}, u32[]{:S(2)}, u32[]{:S(2)}) collective-permute-start(bf16[16,1024]{1,0:T(8,128)(2,1)S(1)} %get-tuple-element.65), channel_id=1, source_target_pairs={{0,8},{2,10},{4,12},{6,14},{8,0},{10,2},{12,4},{14,6},{1,9},{3,11}... | collective-permute-start | bytes 98312 | tf_op jit(solution)/shard_map/ppermute | solution.py:485
  31.6 14.0 %collective-permute-start.14 = (bf16[16,1024]{1,0:T(8,128)(2,1)S(1)}, bf16[16,1024]{1,0:T(8,128)(2,1)S(1)}, u32[]{:S(2)}, u32[]{:S(2)}) collective-permute-start(bf16[16,1024]{1,0:T(8,128)(2,1)S(1)} %get-tuple-element.64), channel_id=1, source_target_pairs={{0,4},{2,6},{4,8},{6,10},{8,12},{10,14},{12,0},{14,2},{1,5},{3,7},... | collective-permute-start | bytes 98312 | tf_op jit(solution)/shard_map/ppermute | solution.py:485
  42.3 6.3 %collective-permute-start.7 = (f32[64,512]{1,0:T(8,128)S(1)}, f32[64,512]{1,0:T(8,128)S(1)}, u32[]{:S(2)}, u32[]{:S(2)}) collective-permute-start(f32[64,512]{1,0:T(8,128)S(1)} %add_add_fusion), channel_id=1, source_target_pairs={{0,2},{2,0},{4,6},{6,4},{8,10},{10,8},{12,14},{14,12},{1,3},{3,1},... | collective-permute-start | bytes 393224 | tf_op jit(solution)/shard_map/ppermute | solution.py:481
  48.6 13.0 %collective-permute-start.10 = (f32[64,512]{1,0:T(8,128)S(1)}, f32[64,512]{1,0:T(8,128)S(1)}, u32[]{:S(2)}, u32[]{:S(2)}) collective-permute-start(f32[64,512]{1,0:T(8,128)S(1)} %add.315), channel_id=1, source_target_pairs={{0,4},{2,6},{4,8},{6,10},{8,12},{10,14},{12,0},{14,2},{1,5},{3,7},... | collective-permute-start | bytes 393224 | tf_op jit(solution)/shard_map/ppermute | solution.py:485
  50.4 11.2 %collective-permute-start.8 = (f32[64,512]{1,0:T(8,128)S(1)}, f32[64,512]{1,0:T(8,128)S(1)}, u32[]{:S(2)}, u32[]{:S(2)}) collective-permute-start(f32[64,512]{1,0:T(8,128)S(1)} %add.315), channel_id=1, source_target_pairs={{0,12},{2,14},{4,0},{6,2},{8,4},{10,6},{12,8},{14,10},{1,13},{3,15... | collective-permute-start | bytes 393224 | tf_op jit(solution)/shard_map/ppermute | solution.py:485
  52.5 10.3 %collective-permute-start.9 = (f32[64,512]{1,0:T(8,128)S(1)}, f32[64,512]{1,0:T(8,128)S(1)}, u32[]{:S(2)}, u32[]{:S(2)}) collective-permute-start(f32[64,512]{1,0:T(8,128)S(1)} %add.315), channel_id=1, source_target_pairs={{0,8},{2,10},{4,12},{6,14},{8,0},{10,2},{12,4},{14,6},{1,9},{3,11}... | collective-permute-start | bytes 393224 | tf_op jit(solution)/shard_map/ppermute | solution.py:485
  55.9 65.8 %collective-permute-start.17 = (bf16[256,2304]{1,0:T(8,128)(2,1)}, bf16[256,2304]{1,0:T(8,128)(2,1)S(1)}, u32[]{:S(2)}, u32[]{:S(2)}) collective-permute-start(bf16[256,2304]{1,0:T(8,128)(2,1)} %add_terms.7.refs_1_), channel_id=1, source_target_pairs={{0,2},{4,0},{8,4},{12,8},{14,12},{10,14},{6,10},{2,6},{1,3},{5,1},... | collective-permute-start | bytes 3538952 | tf_op jit(solution)/shard_map/ppermute | solution.py:606
  61.5 64.2 %collective-permute-start.3 = (bf16[256,2304]{1,0:T(8,128)(2,1)}, bf16[256,2304]{1,0:T(8,128)(2,1)S(1)}, u32[]{:S(2)}, u32[]{:S(2)}) collective-permute-start(bf16[256,2304]{1,0:T(8,128)(2,1)} %add_terms.6.refs_0_), channel_id=1, source_target_pairs={{0,4},{4,8},{8,12},{12,14},{14,10},{10,6},{6,2},{2,0},{1,5},{5,9},... | collective-permute-start | bytes 3538952 | tf_op jit(solution)/shard_map/ppermute | solution.py:605
  62.9 39.4 %copy-start.5 = (f32[256,512]{1,0:T(8,128)}, f32[256,512]{1,0:T(8,128)S(1)}, u32[]{:S(2)}) copy-start(f32[256,512]{1,0:T(8,128)S(1)} %pad_maximum_fusion.mine_ref) | copy-start | bytes 1572868
  62.9 39.4 %collective-permute-start.11 = (f32[256,512]{1,0:T(8,128)S(1)}, f32[256,512]{1,0:T(8,128)S(1)}, u32[]{:S(2)}, u32[]{:S(2)}) collective-permute-start(f32[256,512]{1,0:T(8,128)S(1)} %pad_maximum_fusion.mine_ref), channel_id=1, source_target_pairs={{0,1},{1,0},{2,3},{3,2},{4,5},{5,4},{6,7},{7,6},{8,9},{9,8},{10,11... | collective-permute-start | bytes 1572872 | tf_op jit(solution)/shard_map/ppermute | solution.py:535
  63.1 24.5 %collective-permute-start.15 = (bf16[64,768]{1,0:T(8,128)(2,1)S(1)}, bf16[64,768]{1,0:T(8,128)(2,1)S(1)}, u32[]{:S(2)}, u32[]{:S(2)}) collective-permute-start(bf16[64,768]{1,0:T(8,128)(2,1)S(1)} %broadcast_select_fusion), channel_id=1, source_target_pairs={{0,2},{2,0},{4,6},{6,4},{8,10},{10,8},{12,14},{14,12},{1,3},{3,1},... | collective-permute-start | bytes 294920 | tf_op jit(solution)/shard_map/ppermute | solution.py:481
  87.5 14.8 %copy-start.10 = (bf16[4,2,16,768]{3,2,1,0:T(8,128)(2,1)}, bf16[4,2,16,768]{3,2,1,0:T(8,128)(2,1)S(1)}, u32[]{:S(2)}) copy-start(bf16[4,2,16,768]{3,2,1,0:T(8,128)(2,1)S(1)} %maximum_select_fusion) | copy-start | bytes 589828
  125.7 39.6 %collective-permute-start.19 = (bf16[256,2304]{1,0:T(8,128)(2,1)}, bf16[256,2304]{1,0:T(8,128)(2,1)}, u32[]{:S(2)}, u32[]{:S(2)}) collective-permute-start(bf16[256,2304]{1,0:T(8,128)(2,1)} %add_terms.9.refs_9_), channel_id=1, source_target_pairs={{0,2},{4,0},{8,4},{12,8},{14,12},{10,14},{6,10},{2,6},{1,3},{5,1},... | collective-permute-start | bytes 3538952 | tf_op jit(solution)/shard_map/ppermute | solution.py:606
  129.6 38.6 %collective-permute-start.16 = (bf16[256,2304]{1,0:T(8,128)(2,1)}, bf16[256,2304]{1,0:T(8,128)(2,1)S(1)}, u32[]{:S(2)}, u32[]{:S(2)}) collective-permute-start(bf16[256,2304]{1,0:T(8,128)(2,1)} %add_terms.8.refs_8_), channel_id=1, source_target_pairs={{0,4},{4,8},{8,12},{12,14},{14,10},{10,6},{6,2},{2,0},{1,5},{5,9},... | collective-permute-start | bytes 3538952 | tf_op jit(solution)/shard_map/ppermute | solution.py:605
  139.3 18.3 %collective-permute-start.28 = (bf16[2,128,256]{2,1,0:T(8,128)(2,1)}, bf16[2,128,256]{2,1,0:T(8,128)(2,1)S(1)}, u32[]{:S(2)}, u32[]{:S(2)}) collective-permute-start(bf16[2,128,256]{2,1,0:T(8,128)(2,1)} %get-tuple-element.35), channel_id=1, source_target_pairs={{0,4},{2,6},{4,8},{6,10},{8,12},{10,14},{12,0},{14,2},{1,5},{3,7},... | collective-permute-start | bytes 393224 | tf_op jit(solution)/shard_map/ppermute | solution.py:485
  139.3 19.7 %collective-permute-start.29 = (bf16[2,128,256]{2,1,0:T(8,128)(2,1)}, bf16[2,128,256]{2,1,0:T(8,128)(2,1)S(1)}, u32[]{:S(2)}, u32[]{:S(2)}) collective-permute-start(bf16[2,128,256]{2,1,0:T(8,128)(2,1)} %get-tuple-element.36), channel_id=1, source_target_pairs={{0,8},{2,10},{4,12},{6,14},{8,0},{10,2},{12,4},{14,6},{1,9},{3,11}... | collective-permute-start | bytes 393224 | tf_op jit(solution)/shard_map/ppermute | solution.py:485
  140.3 20.1 %collective-permute-start.30 = (bf16[2,128,256]{2,1,0:T(8,128)(2,1)}, bf16[2,128,256]{2,1,0:T(8,128)(2,1)S(1)}, u32[]{:S(2)}, u32[]{:S(2)}) collective-permute-start(bf16[2,128,256]{2,1,0:T(8,128)(2,1)} %get-tuple-element.37), channel_id=1, source_target_pairs={{0,12},{2,14},{4,0},{6,2},{8,4},{10,6},{12,8},{14,10},{1,13},{3,15... | collective-permute-start | bytes 393224 | tf_op jit(solution)/shard_map/ppermute | solution.py:485
  161.4 6.8 %copy-start.9 = (f32[2,128,256]{2,1,0:T(8,128)}, f32[2,128,256]{2,1,0:T(8,128)S(1)}, u32[]{:S(2)}) copy-start(f32[2,128,256]{2,1,0:T(8,128)S(1)} %convert_add_fusion) | copy-start | bytes 786436
  162.1 14.8 %collective-permute-start.31 = (bf16[128,256]{1,0:T(8,128)(2,1)}, bf16[128,256]{1,0:T(8,128)(2,1)}, u32[]{:S(2)}, u32[]{:S(2)}) collective-permute-start(bf16[128,256]{1,0:T(8,128)(2,1)} %fusion.13), channel_id=1, source_target_pairs={{0,2},{2,0},{4,6},{6,4},{8,10},{10,8},{12,14},{14,12},{1,3},{3,1},... | collective-permute-start | bytes 196616 | tf_op jit(solution)/shard_map/ppermute | solution.py:481
  168.1 6.5 %copy-start.3 = (f32[512,128]{1,0:T(8,128)S(1)}, f32[512,128]{1,0:T(8,128)}, u32[]{:S(2)}) copy-start(f32[512,128]{1,0:T(8,128)} %get-tuple-element.22.refs_1_.solved_ref) | copy-start | bytes 786436
  168.1 13.8 %collective-permute-start.20 = (bf16[256,1280]{1,0:T(8,128)(2,1)}, bf16[256,1280]{1,0:T(8,128)(2,1)}, u32[]{:S(2)}, u32[]{:S(2)}) collective-permute-start(bf16[256,1280]{1,0:T(8,128)(2,1)} %get-tuple-element.25), channel_id=1, source_target_pairs={{0,2},{4,0},{8,4},{12,8},{14,12},{10,14},{6,10},{2,6},{1,3},{5,1},... | collective-permute-start | bytes 1966088 | tf_op jit(solution)/shard_map/ppermute | solution.py:614
  172.0 16.2 %collective-permute-start.18 = (bf16[256,1280]{1,0:T(8,128)(2,1)}, bf16[256,1280]{1,0:T(8,128)(2,1)S(1)}, u32[]{:S(2)}, u32[]{:S(2)}) collective-permute-start(bf16[256,1280]{1,0:T(8,128)(2,1)} %get-tuple-element.24), channel_id=1, source_target_pairs={{0,4},{4,8},{8,12},{12,14},{14,10},{10,6},{6,2},{2,0},{1,5},{5,9},... | collective-permute-start | bytes 1966088 | tf_op jit(solution)/shard_map/ppermute | solution.py:613
  174.8 27.1 %collective-permute-start.22 = (bf16[256,1024]{1,0:T(8,128)(2,1)}, bf16[256,1024]{1,0:T(8,128)(2,1)S(1)}, u32[]{:S(2)}, u32[]{:S(2)}) collective-permute-start(bf16[256,1024]{1,0:T(8,128)(2,1)} %get-tuple-element.28), channel_id=1, source_target_pairs={{0,2},{4,0},{8,4},{12,8},{14,12},{10,14},{6,10},{2,6},{1,3},{5,1},... | collective-permute-start | bytes 1572872 | tf_op jit(solution)/shard_map/ppermute | solution.py:614
  174.9 27.0 %collective-permute-start.21 = (bf16[256,1024]{1,0:T(8,128)(2,1)}, bf16[256,1024]{1,0:T(8,128)(2,1)S(1)}, u32[]{:S(2)}, u32[]{:S(2)}) collective-permute-start(bf16[256,1024]{1,0:T(8,128)(2,1)} %get-tuple-element.27), channel_id=1, source_target_pairs={{0,4},{4,8},{8,12},{12,14},{14,10},{10,6},{6,2},{2,0},{1,5},{5,9},... | collective-permute-start | bytes 1572872 | tf_op jit(solution)/shard_map/ppermute | solution.py:613
  192.0 17.3 %collective-permute-start.23 = (bf16[2,256,256]{2,1,0:T(8,128)(2,1)}, bf16[2,256,256]{2,1,0:T(8,128)(2,1)S(1)}, u32[]{:S(2)}, u32[]{:S(2)}) collective-permute-start(bf16[2,256,256]{2,1,0:T(8,128)(2,1)} %get-tuple-element.30), channel_id=1, source_target_pairs={{0,12},{4,14},{8,10},{12,6},{14,2},{10,0},{6,4},{2,8},{1,13},{5,15... | collective-permute-start | bytes 786440 | tf_op jit(solution)/shard_map/ppermute | solution.py:640
  199.2 32.3 %collective-permute-start.32 = (f32[32,128]{1,0:T(8,128)S(1)}, f32[32,128]{1,0:T(8,128)S(1)}, u32[]{:S(2)}, u32[]{:S(2)}) collective-permute-start(f32[32,128]{1,0:T(8,128)S(1)} %get-tuple-element.61), channel_id=1, source_target_pairs={{0,4},{2,6},{4,8},{6,10},{8,12},{10,14},{12,0},{14,2},{1,5},{3,7},... | collective-permute-start | bytes 49160 | tf_op jit(solution)/shard_map/ppermute | solution.py:485
  199.2 7.0 %copy-start.21 = (bf16[2,256,256]{2,1,0:T(8,128)(2,1)S(1)}, bf16[2,256,256]{2,1,0:T(8,128)(2,1)}, u32[]{:S(2)}) copy-start(bf16[2,256,256]{2,1,0:T(8,128)(2,1)} %get-tuple-element.31) | copy-start | bytes 786436
  199.2 8.9 %copy-start.12 = (bf16[5,256,256]{2,1,0:T(8,128)(2,1)S(1)}, bf16[5,256,256]{2,1,0:T(8,128)(2,1)}, u32[]{:S(2)}) copy-start(bf16[5,256,256]{2,1,0:T(8,128)(2,1)} %get-tuple-element.26) | copy-start | bytes 1966084
  199.2 32.3 %collective-permute-start.33 = (f32[32,128]{1,0:T(8,128)S(1)}, f32[32,128]{1,0:T(8,128)S(1)}, u32[]{:S(2)}, u32[]{:S(2)}) collective-permute-start(f32[32,128]{1,0:T(8,128)S(1)} %get-tuple-element.63), channel_id=1, source_target_pairs={{0,8},{2,10},{4,12},{6,14},{8,0},{10,2},{12,4},{14,6},{1,9},{3,11}... | collective-permute-start | bytes 49160 | tf_op jit(solution)/shard_map/ppermute | solution.py:485
  206.2 13.4 %copy-start.22 = (bf16[1,256,256]{2,1,0:T(8,128)(2,1)S(1)}, bf16[1,256,256]{2,1,0:T(8,128)(2,1)}, u32[]{:S(2)}) copy-start(bf16[1,256,256]{2,1,0:T(8,128)(2,1)} %get-tuple-element.33) | copy-start | bytes 393220
  206.2 14.7 %collective-permute-start.25 = (bf16[2,256,256]{2,1,0:T(8,128)(2,1)}, bf16[2,256,256]{2,1,0:T(8,128)(2,1)S(1)}, u32[]{:S(2)}, u32[]{:S(2)}) collective-permute-start(bf16[2,256,256]{2,1,0:T(8,128)(2,1)} %get-tuple-element.32), channel_id=1, source_target_pairs={{0,2},{4,0},{8,4},{12,8},{14,12},{10,14},{6,10},{2,6},{1,3},{5,1},... | collective-permute-start | bytes 786440 | tf_op jit(solution)/shard_map/ppermute | solution.py:640
  206.2 13.3 %collective-permute-start.24 = (bf16[2,256,256]{2,1,0:T(8,128)(2,1)S(1)}, bf16[2,256,256]{2,1,0:T(8,128)(2,1)S(1)}, u32[]{:S(2)}, u32[]{:S(2)}) collective-permute-start(bf16[2,256,256]{2,1,0:T(8,128)(2,1)S(1)} %copy-done.21), channel_id=1, source_target_pairs={{0,6},{4,2},{8,0},{12,4},{14,8},{10,12},{6,14},{2,10},{1,7},{5,3},... | collective-permute-start | bytes 786440 | tf_op jit(solution)/shard_map/ppermute | solution.py:640
  209.3 22.2 %collective-permute-start.34 = (f32[32,128]{1,0:T(8,128)S(1)}, f32[32,128]{1,0:T(8,128)S(1)}, u32[]{:S(2)}, u32[]{:S(2)}) collective-permute-start(f32[32,128]{1,0:T(8,128)S(1)} %get-tuple-element.62), channel_id=1, source_target_pairs={{0,12},{2,14},{4,0},{6,2},{8,4},{10,6},{12,8},{14,10},{1,13},{3,15... | collective-permute-start | bytes 49160 | tf_op jit(solution)/shard_map/ppermute | solution.py:485
  219.5 7.7 %collective-permute-start.26 = (bf16[1,256,256]{2,1,0:T(8,128)(2,1)S(1)}, bf16[1,256,256]{2,1,0:T(8,128)(2,1)S(1)}, u32[]{:S(2)}, u32[]{:S(2)}) collective-permute-start(bf16[1,256,256]{2,1,0:T(8,128)(2,1)S(1)} %copy-done.22), channel_id=1, source_target_pairs={{0,14},{4,10},{8,6},{12,2},{14,0},{10,4},{6,8},{2,12},{1,15},{5,11... | collective-permute-start | bytes 393224 | tf_op jit(solution)/shard_map/ppermute | solution.py:640
  228.5 7.9 %copy-start.23 = (s32[256]{0:T(256)S(1)}, s32[256]{0:T(256)}, u32[]{:S(2)}) copy-start(s32[256]{0:T(256)} %param.16) | copy-start | bytes 3076
  231.5 5.8 %collective-permute-start.27 = (bf16[8,256,256]{2,1,0:T(8,128)(2,1)}, bf16[8,256,256]{2,1,0:T(8,128)(2,1)S(1)}, u32[]{:S(2)}, u32[]{:S(2)}) collective-permute-start(bf16[8,256,256]{2,1,0:T(8,128)(2,1)} %for_sibling.1), channel_id=1, source_target_pairs={{0,1},{1,0},{2,3},{3,2},{4,5},{5,4},{6,7},{7,6},{8,9},{9,8},{10,11... | collective-permute-start | bytes 3145736 | tf_op jit(solution)/shard_map/ppermute | solution.py:643
  231.6 3.7 %collective-permute-start.35 = (f32[16,128]{1,0:T(8,128)S(1)}, f32[16,128]{1,0:T(8,128)S(1)}, u32[]{:S(2)}, u32[]{:S(2)}) collective-permute-start(f32[16,128]{1,0:T(8,128)S(1)} %constant_dynamic-slice_fusion), channel_id=1, source_target_pairs={{0,2},{2,0},{4,6},{6,4},{8,10},{10,8},{12,14},{14,12},{1,3},{3,1},... | collective-permute-start | bytes 24584 | tf_op jit(solution)/shard_map/ppermute | solution.py:481
  235.3 1.2 collective-permute-start.36
  (14 other events, 13.1 us)

commit v5 on v4

--- a/solution.py
+++ b/solution.py
@@ -72,26 +72,144 @@
     return found
 
 
+def project(activations, proj_in, out_grads, proj_out, after=()):
+    tokens, inner = activations.shape
+    shorter = out_grads.shape[1]
+    rank = proj_in.shape[1]
+    chunk = 2048 if inner % 2048 == 0 and shorter % 2048 == 0 else shorter
+    steps, early = inner // chunk, shorter // chunk
+
+    def kernel(act_ref, in_ref, grad_ref, out_ref, *refs):
+        sides_ref = refs[-1]
+        i = pl.program_id(0)
+
+        @pl.when(i == 0)
+        def _():
+            sides_ref[...] = jnp.zeros_like(sides_ref)
+
+        sides_ref[:, :rank] += jnp.dot(act_ref[...], in_ref[...], preferred_element_type=jnp.float32)
+
+        @pl.when(i < early)
+        def _():
+            sides_ref[:, rank:] += jnp.dot(grad_ref[...], out_ref[...], preferred_element_type=jnp.float32)
+
+    return pl.pallas_call(
+        kernel,
+        grid=(steps,),
+        in_specs=[
+            pl.BlockSpec((tokens, chunk), lambda i: (0, i)),
+            pl.BlockSpec((chunk, rank), lambda i: (i, 0)),
+            pl.BlockSpec((tokens, chunk), lambda i: (0, jnp.minimum(i, early - 1))),
+            pl.BlockSpec((chunk, rank), lambda i: (jnp.minimum(i, early - 1), 0)),
+        ]
+        + [ANYWHERE] * len(after),
+        out_specs=pl.BlockSpec((tokens, 2 * rank), lambda i: (0, 0)),
+        out_shape=jax.ShapeDtypeStruct((tokens, 2 * rank), jnp.float32),
+        compiler_params=pltpu.CompilerParams(vmem_limit_bytes=VMEM_BYTES),
+        cost_estimate=LIGHT,
+        name="project",
+    )(activations, proj_in, out_grads, proj_out, *after)
+
+
+def corner_terms(place, stored, width, pairs):
+    rows = stored.shape[0]
+    group = width // 2
+    size = group // pairs
+
+    def kernel(place_ref, left_ref, right_ref, *refs):
+        whole = refs[-1]
+        whole[...] = jnp.dot(left_ref[...].T, right_ref[...], preferred_element_type=jnp.float32)
+        for index in range(pairs):
+            first = lax.rem(place_ref[0] // 2 + index, pairs) * size
+            refs[index][...] = whole[pl.ds(pl.multiple_of(first, size), size), :]
+
+    return pl.pallas_call(
+        kernel,
+        grid_spec=pltpu.PrefetchScalarGridSpec(
+            num_scalar_prefetch=1,
+            grid=(1,),
+            in_specs=[
+                pl.BlockSpec((rows, group), lambda i, ref: (0, ref[1])),
+                pl.BlockSpec((rows, width), lambda i, ref: (0, 0)),
+            ],
+            out_specs=[pl.BlockSpec((size, width), lambda i, ref: (0, 0))] * pairs,
+            scratch_shapes=[pltpu.VMEM((group, width), jnp.float32)],
+        ),
+        out_shape=[jax.ShapeDtypeStruct((size, width), jnp.float32)] * pairs,
+        compiler_params=pltpu.CompilerParams(vmem_limit_bytes=VMEM_BYTES),
+        cost_estimate=LIGHT,
+        name="corner_terms",
+    )(place, stored, stored)
+
+
 def window_terms(ring, place, stored, vectors, group, steps, parts, after=()):
-    rows, full = stored.shape
-    new_rows = vectors.shape[0]
+    rows = stored.shape[0]
+    new_rows, full = vectors.shape
+    count = ring.count
     taps = jnp.array(steps, jnp.int32)
+    chips = [chip for slots in parts for chip in pairs_of(slots)]
+    wanted = []
+    for step in steps:
+        for offset in [0] + [chip[0] for chip in chips]:
+            apart = (step - steps[0] + offset) % count
+            if apart not in wanted:
+                wanted.append(apart)
+    at_first = [offset % count for offset in [0] + [chip[0] for chip in chips]]
 
     def kernel(place_ref, step_ref, stored_ref, vectors_ref, *refs):
-        owner = ring.position_of(place_ref[0]) + step_ref[pl.program_id(0)] + ring.count
-        owner = lax.rem(owner, ring.count)
+        outs, held, arrived = refs[len(after) : -2], refs[-2], refs[-1]
+        i = pl.program_id(0)
+        begin = ring.position_of(place_ref[0]) + step_ref[0] + count
+        owner = lax.rem(ring.position_of(place_ref[0]) + step_ref[i] + count, count)
+        moved = lax.rem(step_ref[i] - step_ref[0] + 2 * count, count)
         core = place_ref[1]
-        left = pl.ds(pl.multiple_of((2 * ring.index_at(owner) + core) * group, group), group)
-        turned = stored_ref[:, left].T
-        turned_new = vectors_ref[:, left].T
-        for slots, out_ref in zip(parts, refs[len(after) :]):
+
+        def load(apart):
+            source = pl.multiple_of(2 * ring.index_at(begin + apart) * group, 2 * group)
+            return pltpu.make_async_copy(stored_ref.at[:, pl.ds(source, 2 * group)], held.at[apart], arrived.at[apart])
+
+        @pl.when(i == 0)
+        def _():
+            for apart in wanted:
+                load(apart).start()
+
+        rest = [apart for apart in wanted if apart not in at_first]
+        if rest:
+
+            @pl.when(i == 1)
+            def _():
+                for apart in rest:
+                    load(apart).wait()
+
+        waited = set()
+
+        def ready(offset):
+            apart = offset % count
+            if apart not in waited:
+                waited.add(apart)
+
+                @pl.when(i == 0)
+                def _():
+                    load(apart).wait()
+
+            return lax.rem(moved + apart, count)
+
+        own = pl.ds(pl.multiple_of(core * group, group), group)
+        turned = held[ready(0), :, own].T
+        turned_new = vectors_ref[:, pl.ds(pl.multiple_of((2 * ring.index_at(owner) + core) * group, group), group)].T
+        for slots, out_ref in zip(parts, outs):
             for offset, blocks, first in pairs_of(slots):
+                slot = ready(offset)
                 column = 2 * ring.index_at(owner + offset)
                 if blocks == 1:
-                    column = column + jnp.where(owner < ring.half, core, 1 - core)
-                right = pl.ds(pl.multiple_of(column * group, blocks * group), blocks * group)
-                total = jnp.dot(turned, stored_ref[:, right], preferred_element_type=jnp.float32)
-                total = total + jnp.dot(turned_new, vectors_ref[:, right], preferred_element_type=jnp.float32)
+                    side = jnp.where(owner < ring.half, core, 1 - core)
+                    right = held[slot, :, pl.ds(pl.multiple_of(side * group, group), group)]
+                    column = column + side
+                else:
+                    right = held[slot]
+                total = jnp.dot(turned, right, preferred_element_type=jnp.float32)
+                right = vectors_ref[:, pl.ds(pl.multiple_of(column * group, blocks * group), blocks * group)]
+                total = total + jnp.dot(turned_new, right, preferred_element_type=jnp.float32)
                 out_ref[0, :, first * group : (first + blocks) * group] = total.astype(jnp.bfloat16)
 
     def out(slots):
@@ -105,12 +223,13 @@
         grid_spec=pltpu.PrefetchScalarGridSpec(
             num_scalar_prefetch=2,
             grid=(len(steps),),
-            in_specs=[
-                pl.BlockSpec((rows, full), lambda i, a, b: (0, 0), pipeline_mode=pl.Buffered(1)),
-                pl.BlockSpec((new_rows, full), lambda i, a, b: (0, 0), pipeline_mode=pl.Buffered(1)),
-            ]
+            in_specs=[ANYWHERE, pl.BlockSpec((new_rows, full), lambda i, a, b: (0, 0), pipeline_mode=pl.Buffered(1))]
             + [ANYWHERE] * len(after),
             out_specs=[out(slots) for slots in parts],
+            scratch_shapes=[
+                pltpu.VMEM((count, rows, 2 * group), jnp.bfloat16),
+                pltpu.SemaphoreType.DMA((count,)),
+            ],
         ),
         out_shape=[shape(slots) for slots in parts],
         compiler_params=pltpu.CompilerParams(vmem_limit_bytes=VMEM_BYTES),
@@ -135,13 +254,15 @@
                 place += 1
             outs[place][:, (k - start) * group : (k - start + 1) * group] = total.astype(jnp.bfloat16)
 
+    cuts = 4 if group >= 256 else 2
+
     def flat(columns):
-        return pl.BlockSpec((group, columns), lambda i: (0, 0))
-
-    return pl.pallas_call(
-        kernel,
-        grid=(1,),
-        in_specs=[pl.BlockSpec((1, group, count * group), lambda i: (index, 0, 0))]
+        return pl.BlockSpec((group // cuts, columns), lambda i: (i, 0))
+
+    return pl.pallas_call(
+        kernel,
+        grid=(cuts,),
+        in_specs=[pl.BlockSpec((1, group // cuts, count * group), lambda i: (index, i, 0))]
         + [flat(array.shape[1]) for array, _ in arrived]
         + [ANYWHERE] * len(after),
         out_specs=[flat(size * group) for size in sizes],
@@ -236,12 +357,18 @@
         out_ref[here, :] = out_ref[here, :] - exact_dot(work[here, rest], out_ref[rest, :])
 
 
-def solve(place, mine, other, first_cols, after=()):
+def solve(place, pairs_count, mine, other, kept, came, after=()):
     group, width = mine.shape
-    examples = first_cols.shape[0]
-
-    def kernel(place_ref, mine_ref, other_ref, first_ref, *refs):
-        out_ref, pairs_ref, matrix, right, power, inverse = refs[len(after) :]
+    examples = 2 * kept.shape[0]
+    size = kept.shape[0] // pairs_count
+
+    def kernel(place_ref, mine_ref, other_ref, kept_ref, came_ref, *refs):
+        out_ref, pairs_ref, matrix, right, power, inverse, first_ref = refs[len(after) :]
+        for start in range(0, kept_ref.shape[0], size):
+            near, far = kept_ref[start : start + size, :width], came_ref[start : start + size, :width]
+            even = lax.rem(place_ref[0], 2) == 0
+            first_ref[2 * start : 2 * start + size, :] = jnp.where(even, near, far)
+            first_ref[2 * start + size : 2 * start + 2 * size, :] = jnp.where(even, far, near)
         eye = identity(width)
         t = place_ref[1]
         matrix[pl.ds(pl.multiple_of(t * group, group), group), :] = mine_ref[...]
@@ -296,7 +423,7 @@
     whole = pl.BlockSpec(memory_space=pltpu.VMEM)
     return pl.pallas_call(
         kernel,
-        in_specs=[pl.BlockSpec(memory_space=pltpu.SMEM)] + [whole] * 3 + [ANYWHERE] * len(after),
+        in_specs=[pl.BlockSpec(memory_space=pltpu.SMEM)] + [whole] * 4 + [ANYWHERE] * len(after),
         out_shape=[
             jax.ShapeDtypeStruct((width, examples), jnp.float32),
             jax.ShapeDtypeStruct((examples, examples), jnp.float32),
@@ -306,11 +433,12 @@
             pltpu.VMEM((width, examples), jnp.float32),
             pltpu.VMEM((width, width), jnp.bfloat16),
             pltpu.VMEM((width, width), jnp.float32),
+            pltpu.VMEM((examples, width), jnp.bfloat16),
         ],
         compiler_params=pltpu.CompilerParams(vmem_limit_bytes=VMEM_BYTES),
         cost_estimate=LIGHT,
         name="solve",
-    )(place, mine, other, first_cols, *after)
+    )(place, mine, other, kept, came, *after)
 
 
 def spread_back(place, stored, solved, owners, group, after=()):
@@ -526,21 +654,14 @@
     g = 2 * d + t
     place = jnp.stack([d, t]).astype(jnp.int32)
 
-    first_stored = stored[:, :width]
-    corner_rows = lead_dot(lax.dynamic_slice_in_dim(first_stored, t * group, group, 1), first_stored)
-    corner_rows = scatter_pairs(corner_rows, pair, owners)
-    corner_rows = corner_rows + pair_swap(corner_rows, owners)
-    corner_rows = exchange_pairs(lambda index: corner_rows, pair, owners)
-    corner_rows = jnp.concatenate(natural(corner_rows, pair), axis=0)
-    corner_other = lax.ppermute(corner_rows, "tensor", SWAP)
-
-    sides = jnp.concatenate(
-        [
-            jnp.dot(activations, proj_in, preferred_element_type=jnp.float32),
-            jnp.dot(out_grads, proj_out, preferred_element_type=jnp.float32),
-        ],
-        axis=1,
-    )
+    pairs_count = owners // 2
+    corner_pieces = corner_terms(place, stored, width, pairs_count)
+    corner_rows = corner_pieces[0]
+    for step in range(1, pairs_count):
+        corner_rows = corner_rows + far_shift(corner_pieces[step], step, owners)
+    corner_payload = corner_rows
+
+    sides = project(activations, proj_in, out_grads, proj_out, [corner_pieces[0]])
     sides = sides + lax.ppermute(sides, "tensor", SWAP)
 
     examples = counts.shape[0]
@@ -563,14 +684,7 @@
         groups = [lax.dynamic_slice_in_dim(vectors, (4 * index + 2 * s + t) * group, group, 1) for s in (0, 1)]
         return jnp.concatenate([vectors[:, :width]] + groups, axis=1)
 
-    came = natural(exchange_pairs(columns_for, pair, owners), pair)
-    came = jnp.concatenate(came, axis=0)
-    kept = jnp.where(side == 0, came[:, : width + group], jnp.concatenate([came[:, :width], came[:, width + group :]], axis=1))
-    away = jnp.where(side == 0, jnp.concatenate([came[:, :width], came[:, width + group :]], axis=1), came[:, : width + group])
-    shape = (owners // 2, 1, examples, width + group)
-    known = in_order(side, kept.reshape(shape), pair_swap(away, owners).reshape(shape), 1)
-    known = known.reshape(all_examples, width + group)
-    first_cols, own_cols = known[:, :width], known[:, width:].astype(jnp.float32)
+    payloads = [columns_for(lax.rem(pair + step, pairs_count)) for step in range(pairs_count)]
 
     split = (len(ring.offsets) + 1) // 2
     far_slots = [(half, None)]
@@ -587,9 +701,24 @@
     def terms_of(steps, parts, after=()):
         return window_terms(ring, place, stored, vectors, group, steps, parts, after)
 
-    far, near = terms_of([half], [far_slots, near_slots])
+    far, near = terms_of([half], [far_slots, near_slots], payloads + [corner_payload])
     far, near = far[0], near[0]
-    second = terms_of([half - 1, 1 - half], [slots], [far])[0]
+
+    came = [payloads[0]] + [far_shift(payloads[step], step, owners) for step in range(1, pairs_count)]
+    came = jnp.concatenate(natural(came, pair), axis=0)
+    second_group = jnp.concatenate([came[:, :width], came[:, width + group :]], axis=1)
+    first_group = came[:, : width + group]
+    kept = jnp.where(side == 0, first_group, second_group)
+    away = jnp.where(side == 0, second_group, first_group)
+    corner_rows = corner_payload + pair_swap(corner_payload, owners)
+    second = terms_of([half - 1, 1 - half], [slots], [far, away, corner_rows])[0]
+    came = pair_swap(away, owners)
+    corner_rows = [corner_rows] + [far_shift(corner_rows, step, owners) for step in range(1, pairs_count)]
+    corner_rows = jnp.concatenate(natural(corner_rows, pair), axis=0)
+    corner_other = lax.ppermute(corner_rows, "tensor", SWAP)
+    shape = (pairs_count, 1, examples, group)
+    own_cols = in_order(side, kept[:, width:].reshape(shape), came[:, width:].reshape(shape), 1)
+    own_cols = own_cols.reshape(all_examples, group).astype(jnp.float32)
     far_ahead = lax.ppermute(far, "dp", ahead)
     near_back = lax.ppermute(near, "dp", back)
     last = [far_count, near_count] if half == 2 else [far_count + near_count]
@@ -598,7 +727,7 @@
 
     later_steps = [s for step in range(half - 2, 0, -1) for s in (step, -step)] + [0]
     later = terms_of(later_steps, [slots], [going[0], coming[0]])[0]
-    solved, first_pairs = solve(place, corner_rows, corner_other, first_cols, [later])
+    solved, first_pairs = solve(place, pairs_count, corner_rows, corner_other, kept, came, [later])
     token = solved
     for step in range(half - 2, 0, -1):
         last = [far_count, near_count] if step == 1 else [far_count + near_count]

time: 246 us -> 287 us (1.17); the launches traced: 244 us -> 289 us
  Pallas kernels: 86.5 us -> 115 us
  waiting for transfers between devices: 73 us -> 90.7 us
  matrix products: 11.7 us -> 2.52 us
    ppermute x15, waiting for transfers between devices: 19.5 us -> 54.7 us  [far_shift(): lax.ppermute(value, 'dp', [(index, (index + 2 * step) % count) for index...]
    pallas_call x6 -> x8, Pallas kernels: 16.8 us -> 34.5 us  [the longest x6 21.9 us: add_terms(): pl.pallas_call(kernel, grid=(cuts,), in_specs=[pl.BlockSpec((1, group //...]
    ppermute x4, waiting for transfers between devices: 30 us -> 18.4 us  [pair_swap(): lax.ppermute(value, 'dp', [(index, index ^ 1) for index in range(count)])]
    dot_general x2 -> x0, matrix products: 6.84 us -> none  [the longest x1 6.08 us: local(): jnp.dot(activations, proj_in, preferred_element_type=jnp.float32)]
    pallas_call x3, Pallas kernels: 29.4 us -> 35.5 us  [window_terms(): pl.pallas_call(kernel, grid_spec=pltpu.PrefetchScalarGridSpec(num_scalar_...]
    ppermute x4, waiting for transfers between devices: 6.27 us -> 1.21 us  [local(): going = [lax.ppermute(value, 'dp', ahead) for value in going]]
    pallas_call x1, Pallas kernels: 18.6 us -> 22.9 us  [solve(): pl.pallas_call(kernel, in_specs=[pl.BlockSpec(memory_space=pltpu.SMEM)] +...]
    unnamed x53 -> x73, local copies, waits for them, and re-layouts: 12.9 us -> 16.7 us
  transfers between devices with their start and end apart: 37 -> 37, of which waited for: 13 -> 15; matrix products, arithmetic and copies ran while one was open for 6% -> 6% of each run, Pallas kernels for 33% -> 37%
where the time goes in v5:
time: 287 us; the launch traced here: 289 us
  Pallas kernels  115 us (40%)
  waiting for transfers between devices  90.7 us (32%)
  starting transfers between devices  53.2 us (19%)
  local copies, waits for them, and re-layouts  19.2 us (7%)
  other arithmetic  6.68 us (2%)
    ppermute x15, waiting for transfers between devices, far_shift(): lax.ppermute(value, 'dp', [(index, (index + 2 * step) % count) for index...  54.7 us
    pallas_call x3, Pallas kernels, window_terms(): pl.pallas_call(kernel, grid_spec=pltpu.PrefetchScalarGridSpec(num_scalar_...  35.5 us
    pallas_call x1, Pallas kernels, solve(): pl.pallas_call(kernel, in_specs=[pl.BlockSpec(memory_space=pltpu.SMEM)] +...  22.9 us
    pallas_call x6, Pallas kernels, add_terms(): pl.pallas_call(kernel, grid=(cuts,), in_specs=[pl.BlockSpec((1, group //...  21.9 us
    ppermute x15, starting transfers between devices, far_shift(): lax.ppermute(value, 'dp', [(index, (index + 2 * step) % count) for index...  21.8 us
    ppermute x4, waiting for transfers between devices, pair_swap(): lax.ppermute(value, 'dp', [(index, index ^ 1) for index in range(count)])  18.4 us
    unnamed x73, local copies, waits for them, and re-layouts  16.7 us
    ppermute x4, waiting for transfers between devices, local(): lax.ppermute(turned[offset], 'dp', ring.shift(offset))  14.5 us
  transfers between devices with their start and end apart: 37, of which 15 were waited for; matrix products, arithmetic and copies ran while one was open for 6% of the time, Pallas kernels for 37%

profile of v5, /device:TPU:0, one launch (start us, length us, event | category | flops | bytes accessed | tf_op | source)
XLA Modules:
  0.0 288.6 jit_solution(3061751406657117653)
XLA Ops:
  1.3 3.5 %corner_terms.1 = (f32[64,512]{1,0:T(8,128)}, f32[64,512]{1,0:T(8,128)}, f32[64,512]{1,0:T(8,128)}, f32[64,512]{1,0:T(8,128)}) custom-call(s32[2]{0:T(128)} %get-tuple-element.78.place_ref, bf16[1024,4096]{1,0:T(8,128)(2,1)} %refs_7_.1, bf16[1024,4096]{1,0:T(8,128)(2,1)} %refs_7_.1), custom_call_target="tpu_custom_call" | custom-call | flops 1000000 | bytes 100000 | tf_op jit(solution)/shard_map/corner_terms/pallas_call | solution.py:126
  4.8 3.0 %collective-permute-start.1 = (f32[64,512]{1,0:T(8,128)}, f32[64,512]{1,0:T(8,128)S(1)}, u32[]{:S(2)}, u32[]{:S(2)}) collective-permute-start(f32[64,512]{1,0:T(8,128)} %get-tuple-element.25), channel_id=1, source_target_pairs={{0,4},{2,6},{4,8},{6,10},{8,12},{10,14},{12,0},{14,2},{1,5},{3,7},... | collective-permute-start | bytes 393224 | tf_op jit(solution)/shard_map/ppermute | solution.py:613
  7.8 2.6 collective-permute-start.2
  10.4 1.3 collective-permute-start.3
  11.8 2.9 %copy.19.in_ref = bf16[14336,64]{1,0:T(8,128)(2,1)} copy(bf16[14336,64]{0,1:T(8,128)(2,1)S(1)} %copy-done.5) | data formatting | bytes 3670016 | tf_op args[2]
  16.0 9.1 %project.1 = f32[256,128]{1,0:T(8,128)} custom-call(bf16[256,14336]{1,0:T(8,128)(2,1)} %act_ref.1, bf16[14336,64]{1,0:T(8,128)(2,1)} %copy.19.in_ref, bf16[256,4096]{1,0:T(8,128)(2,1)} %grad_ref.1, bf16[4096,64]{1,0:T(8,128)(2,1)} %copy.20.out_ref, f32[64,512]{1,0:T(8,128)} %get-tuple-element.24.refs_0_), custom_call_target="tpu_custom_call" | custom-call | flops 1000000 | bytes 100000 | tf_op jit(solution)/shard_map/project/pallas_call | solution.py:96
  29.7 1.7 collective-permute-start.5
  31.5 1.8 collective-permute-start.7
  33.3 1.5 collective-permute-done.5
  34.8 2.3 collective-permute-done.6
  37.8 6.7 %window_terms.3 = (bf16[1,256,1280]{2,1,0:T(8,128)(2,1)}, bf16[1,256,1024]{2,1,0:T(8,128)(2,1)}) custom-call(s32[2]{0:T(128)} %get-tuple-element.78.place_ref, s32[1]{0:T(128)} %constant.140.clone.step_ref, bf16[1024,4096]{1,0:T(8,128)(2,1)} %refs_7_.1, bf16[16,4096]{1,0:T(8,128)(2,1)} %copy-done.3, bf16[16,1024]{1,0:T(8,128)(2,1)} %get-tuple-element.69.refs_0_, ...), custom_call_target="tpu_custom_call" | custom-call | flops 1000000 | bytes 100000 | tf_op jit(solution)/shard_map/window_terms/pallas_call | solution.py:221
  44.5 1.6 collective-permute-start.9
  48.0 1.6 add.312.refs_2_
  49.5 9.9 %window_terms.4.terms_ref = bf16[2,256,2304]{2,1,0:T(8,128)(2,1)} custom-call(s32[2]{0:T(128)} %get-tuple-element.78.place_ref, s32[2]{0:T(128)} %constant.141.clone.step_ref, bf16[1024,4096]{1,0:T(8,128)(2,1)} %refs_7_.1, bf16[16,4096]{1,0:T(8,128)(2,1)} %copy-done.3, bf16[256,1280]{1,0:T(8,128)(2,1)} %bitcast.29, ...), custom_call_target="tpu_custom_call" | custom-call | flops 1000000 | bytes 100000 | tf_op jit(solution)/shard_map/window_terms/pallas_call | solution.py:221
  60.3 3.5 %add_terms.7.refs_1_ = bf16[256,2304]{1,0:T(8,128)(2,1)} custom-call(bf16[2,256,2304]{2,1,0:T(8,128)(2,1)} %window_terms.4.terms_ref, bf16[256,1024]{1,0:T(8,128)(2,1)} %copy-done.21), custom_call_target="tpu_custom_call" | custom-call | flops 1000000 | bytes 100000 | tf_op jit(solution)/shard_map/add_terms/pallas_call | solution.py:262
  63.8 1.5 collective-permute-start.17
  66.2 3.5 %add_terms.6.refs_0_ = bf16[256,2304]{1,0:T(8,128)(2,1)} custom-call(bf16[2,256,2304]{2,1,0:T(8,128)(2,1)} %window_terms.4.terms_ref, bf16[256,1280]{1,0:T(8,128)(2,1)} %copy-done.15), custom_call_target="tpu_custom_call" | custom-call | flops 1000000 | bytes 100000 | tf_op jit(solution)/shard_map/add_terms/pallas_call | solution.py:262
  72.3 26.9 %collective-permute-done.11 = f32[64,512]{1,0:T(8,128)S(1)} collective-permute-done((f32[64,512]{1,0:T(8,128)S(1)}, f32[64,512]{1,0:T(8,128)S(1)}, u32[]{:S(2)}, u32[]{:S(2)}) %collective-permute-start.11) | collective-permute-done | bytes 131104 | tf_op jit(solution)/shard_map/ppermute | solution.py:613
  99.2 1.7 collective-permute-done.12
  102.3 4.9 %collective-permute-start.15 = (bf16[64,768]{1,0:T(8,128)(2,1)S(1)}, bf16[64,768]{1,0:T(8,128)(2,1)S(1)}, u32[]{:S(2)}, u32[]{:S(2)}) collective-permute-start(bf16[64,768]{1,0:T(8,128)(2,1)S(1)} %copy-done.22), channel_id=1, source_target_pairs={{0,2},{2,0},{4,6},{6,4},{8,10},{10,8},{12,14},{14,12},{1,3},{3,1},... | collective-permute-start | bytes 294920 | tf_op jit(solution)/shard_map/ppermute | solution.py:609
  107.2 18.9 %window_terms.5.refs_0_.terms_ref.own_ref = bf16[5,256,2304]{2,1,0:T(8,128)(2,1)} custom-call(s32[2]{0:T(128)} %get-tuple-element.78.place_ref, s32[5]{0:T(128)} %constant.142.clone.step_ref, bf16[1024,4096]{1,0:T(8,128)(2,1)} %refs_7_.1, bf16[16,4096]{1,0:T(8,128)(2,1)} %copy-done.3, bf16[256,2304]{1,0:T(8,128)(2,1)} %add_terms.6.refs_0_, ...), custom_call_target="tpu_custom_call" | custom-call | flops 1000000 | bytes 100000 | tf_op jit(solution)/shard_map/window_terms/pallas_call | solution.py:221
  127.0 22.9 %solve.1 = (f32[512,128]{1,0:T(8,128)}, f32[128,128]{1,0:T(8,128)}) custom-call(s32[2]{0:T(128)} %get-tuple-element.78.place_ref, f32[256,512]{1,0:T(8,128)} %copy-done.4, f32[256,512]{1,0:T(8,128)} %copy-done.17, bf16[64,768]{1,0:T(8,128)(2,1)} %get-tuple-element.46.kept_ref, bf16[64,768]{1,0:T(8,128)(2,1)} %copy-done.24, ...), custom_call_target="tpu_custom_call" | custom-call | flops 1000000 | bytes 100000 | tf_op jit(solution)/shard_map/solve/pallas_call | solution.py:424
  150.9 3.7 %add_terms.9.refs_9_ = bf16[256,2304]{1,0:T(8,128)(2,1)} custom-call(bf16[5,256,2304]{2,1,0:T(8,128)(2,1)} %window_terms.5.refs_0_.terms_ref.own_ref, bf16[256,2304]{1,0:T(8,128)(2,1)} %copy-done.10, f32[512,128]{1,0:T(8,128)} %get-tuple-element.30.refs_1_.solved_ref), custom_call_target="tpu_custom_call" | custom-call | flops 1000000 | bytes 100000 | tf_op jit(solution)/shard_map/add_terms/pallas_call | solution.py:262
  155.7 3.7 %add_terms.8.refs_8_ = bf16[256,2304]{1,0:T(8,128)(2,1)} custom-call(bf16[5,256,2304]{2,1,0:T(8,128)(2,1)} %window_terms.5.refs_0_.terms_ref.own_ref, bf16[256,2304]{1,0:T(8,128)(2,1)} %copy-done.11, f32[512,128]{1,0:T(8,128)} %get-tuple-element.30.refs_1_.solved_ref), custom_call_target="tpu_custom_call" | custom-call | flops 1000000 | bytes 100000 | tf_op jit(solution)/shard_map/add_terms/pallas_call | solution.py:262
  159.4 2.0 collective-permute-start.16
  162.2 7.6 %spread_back.1 = (bf16[2,128,256]{2,1,0:T(8,128)(2,1)}, bf16[2,128,256]{2,1,0:T(8,128)(2,1)}, bf16[2,128,256]{2,1,0:T(8,128)(2,1)}, bf16[2,128,256]{2,1,0:T(8,128)(2,1)}) custom-call(s32[2]{0:T(128)} %get-tuple-element.78.place_ref, bf16[1024,4096]{1,0:T(8,128)(2,1)} %refs_7_.1, f32[512,128]{1,0:T(8,128)} %get-tuple-element.30.refs_1_.solved_ref, ...), custom_call_target="tpu_custom_call" | custom-call | flops 1000000 | bytes 100000 | tf_op jit(solution)/shard_map/spread_back/pallas_call | solution.py:462
  169.9 3.6 %collective-permute-start.30 = (bf16[2,128,256]{2,1,0:T(8,128)(2,1)}, bf16[2,128,256]{2,1,0:T(8,128)(2,1)S(1)}, u32[]{:S(2)}, u32[]{:S(2)}) collective-permute-start(bf16[2,128,256]{2,1,0:T(8,128)(2,1)} %get-tuple-element.45), channel_id=1, source_target_pairs={{0,12},{2,14},{4,0},{6,2},{8,4},{10,6},{12,8},{14,10},{1,13},{3,15... | collective-permute-start | bytes 393224 | tf_op jit(solution)/shard_map/ppermute | solution.py:613
  174.4 16.5 %collective-permute-done.28 = bf16[2,128,256]{2,1,0:T(8,128)(2,1)S(1)} collective-permute-done((bf16[2,128,256]{2,1,0:T(8,128)(2,1)}, bf16[2,128,256]{2,1,0:T(8,128)(2,1)S(1)}, u32[]{:S(2)}, u32[]{:S(2)}) %collective-permute-start.28) | collective-permute-done | bytes 131104 | tf_op jit(solution)/shard_map/ppermute | solution.py:613
  190.9 2.9 collective-permute-done.29
  193.8 1.7 collective-permute-done.30
  197.5 3.7 %add_terms.11 = (bf16[256,1280]{1,0:T(8,128)(2,1)}, bf16[256,1024]{1,0:T(8,128)(2,1)}) custom-call(bf16[5,256,2304]{2,1,0:T(8,128)(2,1)} %window_terms.5.refs_0_.terms_ref.own_ref, bf16[256,2304]{1,0:T(8,128)(2,1)} %copy-done.9, bf16[2,128,256]{2,1,0:T(8,128)(2,1)} %get-tuple-element.31.refs_1_), custom_call_target="tpu_custom_call" | custom-call | flops 1000000 | bytes 100000 | tf_op jit(solution)/shard_map/add_terms/pallas_call | solution.py:262
  201.1 3.6 %collective-permute-start.20 = (bf16[256,1280]{1,0:T(8,128)(2,1)}, bf16[256,1280]{1,0:T(8,128)(2,1)S(1)}, u32[]{:S(2)}, u32[]{:S(2)}) collective-permute-start(bf16[256,1280]{1,0:T(8,128)(2,1)} %get-tuple-element.33), channel_id=1, source_target_pairs={{0,2},{4,0},{8,4},{12,8},{14,12},{10,14},{6,10},{2,6},{1,3},{5,1},... | collective-permute-start | bytes 1966088 | tf_op jit(solution)/shard_map/ppermute | solution.py:743
  205.8 3.7 %add_terms.10 = (bf16[256,1280]{1,0:T(8,128)(2,1)}, bf16[256,1024]{1,0:T(8,128)(2,1)}) custom-call(bf16[5,256,2304]{2,1,0:T(8,128)(2,1)} %window_terms.5.refs_0_.terms_ref.own_ref, bf16[256,2304]{1,0:T(8,128)(2,1)} %copy-done.8, bf16[2,128,256]{2,1,0:T(8,128)(2,1)} %get-tuple-element.31.refs_1_), custom_call_target="tpu_custom_call" | custom-call | flops 1000000 | bytes 100000 | tf_op jit(solution)/shard_map/add_terms/pallas_call | solution.py:262
  209.5 2.3 collective-permute-start.31
  212.1 2.1 collective-permute-start.21
  214.2 14.9 %collective-permute-done.31 = bf16[128,256]{1,0:T(8,128)(2,1)S(1)} collective-permute-done((bf16[128,256]{1,0:T(8,128)(2,1)S(1)}, bf16[128,256]{1,0:T(8,128)(2,1)S(1)}, u32[]{:S(2)}, u32[]{:S(2)}) %collective-permute-start.31) | collective-permute-done | bytes 65568 | tf_op jit(solution)/shard_map/ppermute | solution.py:609
  231.3 3.0 %close_window.2 = (bf16[5,256,256]{2,1,0:T(8,128)(2,1)}, bf16[1,256,256]{2,1,0:T(8,128)(2,1)}, bf16[2,256,256]{2,1,0:T(8,128)(2,1)}, bf16[2,256,256]{2,1,0:T(8,128)(2,1)}) custom-call(bf16[5,256,2304]{2,1,0:T(8,128)(2,1)} %window_terms.5.refs_0_.terms_ref.own_ref, bf16[256,1280]{1,0:T(8,128)(2,1)} %copy-done.13, bf16[256,1280]{1,0:T(8,128)(2,1)} %copy-done.12), custom_call_target="tpu_custom_call" | custom-call | flops 1000000 | bytes 100000 | tf_op jit(solution)/shard_map/close_window/pallas_call | solution.py:294
  234.2 1.5 collective-permute-start.23
  235.7 2.5 collective-permute-start.32
  240.2 2.6 close_window.3
  242.9 7.0 %collective-permute-start.25 = (bf16[2,256,256]{2,1,0:T(8,128)(2,1)}, bf16[2,256,256]{2,1,0:T(8,128)(2,1)S(1)}, u32[]{:S(2)}, u32[]{:S(2)}) collective-permute-start(bf16[2,256,256]{2,1,0:T(8,128)(2,1)} %get-tuple-element.40), channel_id=1, source_target_pairs={{0,2},{4,0},{8,4},{12,8},{14,12},{10,14},{6,10},{2,6},{1,3},{5,1},... | collective-permute-start | bytes 786440 | tf_op jit(solution)/shard_map/ppermute | solution.py:769
  251.3 4.3 %collective-permute-start.34 = (f32[32,128]{1,0:T(8,128)S(1)}, f32[32,128]{1,0:T(8,128)S(1)}, u32[]{:S(2)}, u32[]{:S(2)}) collective-permute-start(f32[32,128]{1,0:T(8,128)S(1)} %get-tuple-element.67), channel_id=1, source_target_pairs={{0,12},{2,14},{4,0},{6,2},{8,4},{10,6},{12,8},{14,10},{1,13},{3,15... | collective-permute-start | bytes 49160 | tf_op jit(solution)/shard_map/ppermute | solution.py:613
  255.6 8.5 %collective-permute-done.24 = bf16[2,256,256]{2,1,0:T(8,128)(2,1)S(1)} collective-permute-done((bf16[2,256,256]{2,1,0:T(8,128)(2,1)S(1)}, bf16[2,256,256]{2,1,0:T(8,128)(2,1)S(1)}, u32[]{:S(2)}, u32[]{:S(2)}) %collective-permute-start.24) | collective-permute-done | bytes 262176 | tf_op jit(solution)/shard_map/ppermute | solution.py:769
  264.2 1.6 collective-permute-start.26
  265.8 6.0 %collective-permute-done.26 = bf16[1,256,256]{2,1,0:T(8,128)(2,1)S(1)} collective-permute-done((bf16[1,256,256]{2,1,0:T(8,128)(2,1)S(1)}, bf16[1,256,256]{2,1,0:T(8,128)(2,1)S(1)}, u32[]{:S(2)}, u32[]{:S(2)}) %collective-permute-start.26) | collective-permute-done | bytes 131104 | tf_op jit(solution)/shard_map/ppermute | solution.py:769
  273.1 2.9 %for_sibling.1 = bf16[8,256,256]{2,1,0:T(8,128)(2,1)} custom-call(s32[8]{0:T(128)} %select_n.618.table_ref, bf16[16,256,256]{2,1,0:T(8,128)(2,1)} %copy-done, bf16[16,256,256]{2,1,0:T(8,128)(2,1)} %copy-done, bf16[16,256,256]{2,1,0:T(8,128)(2,1)} %copy-done, bf16[16,256,256]{2,1,0:T(8,128)(2,1)} %copy-done), custom_call_target="tpu_custom_call" | custom-call | flops 1000000 | bytes 100000 | tf_op jit(solution)/shard_map/for_sibling/pallas_call | solution.py:536
  276.3 3.6 %collective-permute-done.35 = f32[16,128]{1,0:T(8,128)S(1)} collective-permute-done((f32[16,128]{1,0:T(8,128)S(1)}, f32[16,128]{1,0:T(8,128)S(1)}, u32[]{:S(2)}, u32[]{:S(2)}) %collective-permute-start.35) | collective-permute-done | bytes 8224 | tf_op jit(solution)/shard_map/ppermute | solution.py:609
  282.9 5.8 %finish.1 = f32[512,2048]{1,0:T(8,128)} custom-call(s32[48]{0:T(128)} %reshape.234.table_ref, s32[2]{0:T(128)} %get-tuple-element.78.place_ref, bf16[16,256,256]{2,1,0:T(8,128)(2,1)} %copy-done, bf16[16,256,256]{2,1,0:T(8,128)(2,1)} %copy-done, bf16[16,256,256]{2,1,0:T(8,128)(2,1)} %copy-done, bf16[16,256,256]{2,1,0:T(8,128)(2,1)} %copy-done, ...), custom_call_target="tpu_custom_call" | custom-call | flops 1000000 | bytes 100000 | tf_op jit(solution)/shard_map/finish/pallas_call | solution.py:585
  (161 shorter events, 32.5 us)
Async XLA Ops:
  1.3 10.5 %copy-start.5 = (bf16[14336,64]{0,1:T(8,128)(2,1)S(1)}, bf16[14336,64]{0,1:T(8,128)(2,1)}, u32[]{:S(2)}) copy-start(bf16[14336,64]{0,1:T(8,128)(2,1)} %param.12) | copy-start | bytes 5505028
  4.8 26.6 %collective-permute-start.1 = (f32[64,512]{1,0:T(8,128)}, f32[64,512]{1,0:T(8,128)S(1)}, u32[]{:S(2)}, u32[]{:S(2)}) collective-permute-start(f32[64,512]{1,0:T(8,128)} %get-tuple-element.25), channel_id=1, source_target_pairs={{0,4},{2,6},{4,8},{6,10},{8,12},{10,14},{12,0},{14,2},{1,5},{3,7},... | collective-permute-start | bytes 393224 | tf_op jit(solution)/shard_map/ppermute | solution.py:613
  7.8 23.6 %collective-permute-start.2 = (f32[64,512]{1,0:T(8,128)}, f32[64,512]{1,0:T(8,128)S(1)}, u32[]{:S(2)}, u32[]{:S(2)}) collective-permute-start(f32[64,512]{1,0:T(8,128)} %get-tuple-element.26), channel_id=1, source_target_pairs={{0,8},{2,10},{4,12},{6,14},{8,0},{10,2},{12,4},{14,6},{1,9},{3,11}... | collective-permute-start | bytes 393224 | tf_op jit(solution)/shard_map/ppermute | solution.py:613
  10.4 21.0 %collective-permute-start.3 = (f32[64,512]{1,0:T(8,128)}, f32[64,512]{1,0:T(8,128)S(1)}, u32[]{:S(2)}, u32[]{:S(2)}) collective-permute-start(f32[64,512]{1,0:T(8,128)} %get-tuple-element.27), channel_id=1, source_target_pairs={{0,12},{2,14},{4,0},{6,2},{8,4},{10,6},{12,8},{14,10},{1,13},{3,15... | collective-permute-start | bytes 393224 | tf_op jit(solution)/shard_map/ppermute | solution.py:613
  16.0 9.2 %copy-start.28 = (s32[16]{0:T(128)S(1)}, s32[16]{0:T(128)}, u32[]{:S(2)}) copy-start(s32[16]{0:T(128)} %param.15) | copy-start | bytes 196
  25.1 1.6 collective-permute-start
  29.2 4.1 %collective-permute-start.4 = (bf16[16,1024]{1,0:T(8,128)(2,1)S(1)}, bf16[16,1024]{1,0:T(8,128)(2,1)S(1)}, u32[]{:S(2)}, u32[]{:S(2)}) collective-permute-start(bf16[16,1024]{1,0:T(8,128)(2,1)S(1)} %get-tuple-element.70.refs_3_), channel_id=1, source_target_pairs={{0,12},{2,14},{4,0},{6,2},{8,4},{10,6},{12,8},{14,10},{1,13},{3,15... | collective-permute-start | bytes 98312 | tf_op jit(solution)/shard_map/ppermute | solution.py:613
  29.7 5.1 %collective-permute-start.5 = (bf16[16,1024]{1,0:T(8,128)(2,1)S(1)}, bf16[16,1024]{1,0:T(8,128)(2,1)S(1)}, u32[]{:S(2)}, u32[]{:S(2)}) collective-permute-start(bf16[16,1024]{1,0:T(8,128)(2,1)S(1)} %get-tuple-element.72.refs_2_), channel_id=1, source_target_pairs={{0,8},{2,10},{4,12},{6,14},{8,0},{10,2},{12,4},{14,6},{1,9},{3,11}... | collective-permute-start | bytes 98312 | tf_op jit(solution)/shard_map/ppermute | solution.py:613
  31.4 5.7 %collective-permute-start.6 = (bf16[16,1024]{1,0:T(8,128)(2,1)S(1)}, bf16[16,1024]{1,0:T(8,128)(2,1)S(1)}, u32[]{:S(2)}, u32[]{:S(2)}) collective-permute-start(bf16[16,1024]{1,0:T(8,128)(2,1)S(1)} %get-tuple-element.71.refs_1_), channel_id=1, source_target_pairs={{0,4},{2,6},{4,8},{6,10},{8,12},{10,14},{12,0},{14,2},{1,5},{3,7},... | collective-permute-start | bytes 98312 | tf_op jit(solution)/shard_map/ppermute | solution.py:613
  31.5 16.5 %collective-permute-start.7 = (f32[64,512]{1,0:T(8,128)S(1)}, f32[64,512]{1,0:T(8,128)S(1)}, u32[]{:S(2)}, u32[]{:S(2)}) collective-permute-start(f32[64,512]{1,0:T(8,128)S(1)} %add_add_fusion.refs_4_), channel_id=1, source_target_pairs={{0,2},{2,0},{4,6},{6,4},{8,10},{10,8},{12,14},{14,12},{1,3},{3,1},... | collective-permute-start | bytes 393224 | tf_op jit(solution)/shard_map/ppermute | solution.py:609
  44.5 15.0 %collective-permute-start.9 = (bf16[256,1024]{1,0:T(8,128)(2,1)}, bf16[256,1024]{1,0:T(8,128)(2,1)S(1)}, u32[]{:S(2)}, u32[]{:S(2)}) collective-permute-start(bf16[256,1024]{1,0:T(8,128)(2,1)} %bitcast.35), channel_id=1, source_target_pairs={{0,2},{4,0},{8,4},{12,8},{14,12},{10,14},{6,10},{2,6},{1,3},{5,1},... | collective-permute-start | bytes 1572872 | tf_op jit(solution)/shard_map/ppermute | solution.py:723
  46.1 19.3 %collective-permute-start.8 = (bf16[256,1280]{1,0:T(8,128)(2,1)}, bf16[256,1280]{1,0:T(8,128)(2,1)S(1)}, u32[]{:S(2)}, u32[]{:S(2)}) collective-permute-start(bf16[256,1280]{1,0:T(8,128)(2,1)} %bitcast.28), channel_id=1, source_target_pairs={{0,4},{4,8},{8,12},{12,14},{14,10},{10,6},{6,2},{2,0},{1,5},{5,9},... | collective-permute-start | bytes 1966088 | tf_op jit(solution)/shard_map/ppermute | solution.py:722
  63.8 86.1 %collective-permute-start.17 = (bf16[256,2304]{1,0:T(8,128)(2,1)}, bf16[256,2304]{1,0:T(8,128)(2,1)S(1)}, u32[]{:S(2)}, u32[]{:S(2)}) collective-permute-start(bf16[256,2304]{1,0:T(8,128)(2,1)} %add_terms.7.refs_1_), channel_id=1, source_target_pairs={{0,2},{4,0},{8,4},{12,8},{14,12},{10,14},{6,10},{2,6},{1,3},{5,1},... | collective-permute-start | bytes 3538952 | tf_op jit(solution)/shard_map/ppermute | solution.py:735
  69.7 32.6 %copy-start.22 = (bf16[64,768]{1,0:T(8,128)(2,1)S(1)}, bf16[64,768]{1,0:T(8,128)(2,1)}, u32[]{:S(2)}) copy-start(bf16[64,768]{1,0:T(8,128)(2,1)} %broadcast_select_fusion.1.refs_1_) | copy-start | bytes 294916
  69.8 84.9 %collective-permute-start.10 = (bf16[256,2304]{1,0:T(8,128)(2,1)}, bf16[256,2304]{1,0:T(8,128)(2,1)S(1)}, u32[]{:S(2)}, u32[]{:S(2)}) collective-permute-start(bf16[256,2304]{1,0:T(8,128)(2,1)} %add_terms.6.refs_0_), channel_id=1, source_target_pairs={{0,4},{4,8},{8,12},{12,14},{14,10},{10,6},{6,2},{2,0},{1,5},{5,9},... | collective-permute-start | bytes 3538952 | tf_op jit(solution)/shard_map/ppermute | solution.py:734
  70.3 29.0 %collective-permute-start.11 = (f32[64,512]{1,0:T(8,128)S(1)}, f32[64,512]{1,0:T(8,128)S(1)}, u32[]{:S(2)}, u32[]{:S(2)}) collective-permute-start(f32[64,512]{1,0:T(8,128)S(1)} %copy-done.7), channel_id=1, source_target_pairs={{0,12},{2,14},{4,0},{6,2},{8,4},{10,6},{12,8},{14,10},{1,13},{3,15... | collective-permute-start | bytes 393224 | tf_op jit(solution)/shard_map/ppermute | solution.py:613
  70.7 30.2 %collective-permute-start.12 = (f32[64,512]{1,0:T(8,128)S(1)}, f32[64,512]{1,0:T(8,128)S(1)}, u32[]{:S(2)}, u32[]{:S(2)}) collective-permute-start(f32[64,512]{1,0:T(8,128)S(1)} %copy-done.7), channel_id=1, source_target_pairs={{0,8},{2,10},{4,12},{6,14},{8,0},{10,2},{12,4},{14,6},{1,9},{3,11}... | collective-permute-start | bytes 393224 | tf_op jit(solution)/shard_map/ppermute | solution.py:613
  71.8 30.3 %collective-permute-start.13 = (f32[64,512]{1,0:T(8,128)S(1)}, f32[64,512]{1,0:T(8,128)S(1)}, u32[]{:S(2)}, u32[]{:S(2)}) collective-permute-start(f32[64,512]{1,0:T(8,128)S(1)} %copy-done.7), channel_id=1, source_target_pairs={{0,4},{2,6},{4,8},{6,10},{8,12},{10,14},{12,0},{14,2},{1,5},{3,7},... | collective-permute-start | bytes 393224 | tf_op jit(solution)/shard_map/ppermute | solution.py:613
  102.2 23.9 %copy-start.4 = (f32[256,512]{1,0:T(8,128)}, f32[256,512]{1,0:T(8,128)S(1)}, u32[]{:S(2)}) copy-start(f32[256,512]{1,0:T(8,128)S(1)} %pad_maximum_fusion.mine_ref) | copy-start | bytes 1572868
  102.2 23.9 %collective-permute-start.14 = (f32[256,512]{1,0:T(8,128)S(1)}, f32[256,512]{1,0:T(8,128)S(1)}, u32[]{:S(2)}, u32[]{:S(2)}) collective-permute-start(f32[256,512]{1,0:T(8,128)S(1)} %pad_maximum_fusion.mine_ref), channel_id=1, source_target_pairs={{0,1},{1,0},{2,3},{3,2},{4,5},{5,4},{6,7},{7,6},{8,9},{9,8},{10,11... | collective-permute-start | bytes 1572872 | tf_op jit(solution)/shard_map/ppermute | solution.py:718
  102.3 23.8 %collective-permute-start.15 = (bf16[64,768]{1,0:T(8,128)(2,1)S(1)}, bf16[64,768]{1,0:T(8,128)(2,1)S(1)}, u32[]{:S(2)}, u32[]{:S(2)}) collective-permute-start(bf16[64,768]{1,0:T(8,128)(2,1)S(1)} %copy-done.22), channel_id=1, source_target_pairs={{0,2},{2,0},{4,6},{6,4},{8,10},{10,8},{12,14},{14,12},{1,3},{3,1},... | collective-permute-start | bytes 294920 | tf_op jit(solution)/shard_map/ppermute | solution.py:609
  154.6 41.8 %collective-permute-start.19 = (bf16[256,2304]{1,0:T(8,128)(2,1)}, bf16[256,2304]{1,0:T(8,128)(2,1)S(1)}, u32[]{:S(2)}, u32[]{:S(2)}) collective-permute-start(bf16[256,2304]{1,0:T(8,128)(2,1)} %add_terms.9.refs_9_), channel_id=1, source_target_pairs={{0,2},{4,0},{8,4},{12,8},{14,12},{10,14},{6,10},{2,6},{1,3},{5,1},... | collective-permute-start | bytes 3538952 | tf_op jit(solution)/shard_map/ppermute | solution.py:735
  159.4 45.4 %collective-permute-start.16 = (bf16[256,2304]{1,0:T(8,128)(2,1)}, bf16[256,2304]{1,0:T(8,128)(2,1)S(1)}, u32[]{:S(2)}, u32[]{:S(2)}) collective-permute-start(bf16[256,2304]{1,0:T(8,128)(2,1)} %add_terms.8.refs_8_), channel_id=1, source_target_pairs={{0,4},{4,8},{8,12},{12,14},{14,10},{10,6},{6,2},{2,0},{1,5},{5,9},... | collective-permute-start | bytes 3538952 | tf_op jit(solution)/shard_map/ppermute | solution.py:734
  169.7 21.2 %collective-permute-start.28 = (bf16[2,128,256]{2,1,0:T(8,128)(2,1)}, bf16[2,128,256]{2,1,0:T(8,128)(2,1)S(1)}, u32[]{:S(2)}, u32[]{:S(2)}) collective-permute-start(bf16[2,128,256]{2,1,0:T(8,128)(2,1)} %get-tuple-element.43), channel_id=1, source_target_pairs={{0,4},{2,6},{4,8},{6,10},{8,12},{10,14},{12,0},{14,2},{1,5},{3,7},... | collective-permute-start | bytes 393224 | tf_op jit(solution)/shard_map/ppermute | solution.py:613
  169.7 24.0 %collective-permute-start.29 = (bf16[2,128,256]{2,1,0:T(8,128)(2,1)}, bf16[2,128,256]{2,1,0:T(8,128)(2,1)S(1)}, u32[]{:S(2)}, u32[]{:S(2)}) collective-permute-start(bf16[2,128,256]{2,1,0:T(8,128)(2,1)} %get-tuple-element.44), channel_id=1, source_target_pairs={{0,8},{2,10},{4,12},{6,14},{8,0},{10,2},{12,4},{14,6},{1,9},{3,11}... | collective-permute-start | bytes 393224 | tf_op jit(solution)/shard_map/ppermute | solution.py:613
  169.9 25.5 %collective-permute-start.30 = (bf16[2,128,256]{2,1,0:T(8,128)(2,1)}, bf16[2,128,256]{2,1,0:T(8,128)(2,1)S(1)}, u32[]{:S(2)}, u32[]{:S(2)}) collective-permute-start(bf16[2,128,256]{2,1,0:T(8,128)(2,1)} %get-tuple-element.45), channel_id=1, source_target_pairs={{0,12},{2,14},{4,0},{6,2},{8,4},{10,6},{12,8},{14,10},{1,13},{3,15... | collective-permute-start | bytes 393224 | tf_op jit(solution)/shard_map/ppermute | solution.py:613
  201.1 10.7 %slice-start = ((bf16[64,768]{1,0:T(8,128)(2,1)}), bf16[64,256]{1,0:T(8,128)(2,1)S(1)}, s32[]{:S(2)}) async-start(bf16[64,768]{1,0:T(8,128)(2,1)} %copy-done.24), calls=%async_computation | async-start | bytes 65536 | tf_op jit(solution)/shard_map/slice | solution.py:720
  201.1 10.8 %copy-start.2 = (f32[512,128]{1,0:T(8,128)S(1)}, f32[512,128]{1,0:T(8,128)}, u32[]{:S(2)}) copy-start(f32[512,128]{1,0:T(8,128)} %get-tuple-element.30.refs_1_.solved_ref) | copy-start | bytes 786436
  201.1 10.9 %copy-start.29 = (bf16[256,1024]{1,0:T(8,128)(2,1)S(1)}, bf16[256,1024]{1,0:T(8,128)(2,1)}, u32[]{:S(2)}) copy-start(bf16[256,1024]{1,0:T(8,128)(2,1)} %get-tuple-element.36) | copy-start | bytes 1572868
  201.1 27.9 %copy-start.23 = (f32[128,128]{1,0:T(8,128)S(1)}, f32[128,128]{1,0:T(8,128)}, u32[]{:S(2)}) copy-start(f32[128,128]{1,0:T(8,128)} %get-tuple-element.42) | copy-start | bytes 196612
  201.1 28.5 %collective-permute-start.20 = (bf16[256,1280]{1,0:T(8,128)(2,1)}, bf16[256,1280]{1,0:T(8,128)(2,1)S(1)}, u32[]{:S(2)}, u32[]{:S(2)}) collective-permute-start(bf16[256,1280]{1,0:T(8,128)(2,1)} %get-tuple-element.33), channel_id=1, source_target_pairs={{0,2},{4,0},{8,4},{12,8},{14,12},{10,14},{6,10},{2,6},{1,3},{5,1},... | collective-permute-start | bytes 1966088 | tf_op jit(solution)/shard_map/ppermute | solution.py:743
  209.5 20.1 %collective-permute-start.18 = (bf16[256,1280]{1,0:T(8,128)(2,1)}, bf16[256,1280]{1,0:T(8,128)(2,1)S(1)}, u32[]{:S(2)}, u32[]{:S(2)}) collective-permute-start(bf16[256,1280]{1,0:T(8,128)(2,1)} %get-tuple-element.32), channel_id=1, source_target_pairs={{0,4},{4,8},{8,12},{12,14},{14,10},{10,6},{6,2},{2,0},{1,5},{5,9},... | collective-permute-start | bytes 1966088 | tf_op jit(solution)/shard_map/ppermute | solution.py:742
  209.5 19.5 %collective-permute-start.31 = (bf16[128,256]{1,0:T(8,128)(2,1)S(1)}, bf16[128,256]{1,0:T(8,128)(2,1)S(1)}, u32[]{:S(2)}, u32[]{:S(2)}) collective-permute-start(bf16[128,256]{1,0:T(8,128)(2,1)S(1)} %fusion.11), channel_id=1, source_target_pairs={{0,2},{2,0},{4,6},{6,4},{8,10},{10,8},{12,14},{14,12},{1,3},{3,1},... | collective-permute-start | bytes 196616 | tf_op jit(solution)/shard_map/ppermute | solution.py:609
  212.0 26.2 %collective-permute-start.22 = (bf16[256,1024]{1,0:T(8,128)(2,1)S(1)}, bf16[256,1024]{1,0:T(8,128)(2,1)S(1)}, u32[]{:S(2)}, u32[]{:S(2)}) collective-permute-start(bf16[256,1024]{1,0:T(8,128)(2,1)S(1)} %copy-done.29), channel_id=1, source_target_pairs={{0,2},{4,0},{8,4},{12,8},{14,12},{10,14},{6,10},{2,6},{1,3},{5,1},... | collective-permute-start | bytes 1572872 | tf_op jit(solution)/shard_map/ppermute | solution.py:743
  212.1 27.3 %collective-permute-start.21 = (bf16[256,1024]{1,0:T(8,128)(2,1)}, bf16[256,1024]{1,0:T(8,128)(2,1)S(1)}, u32[]{:S(2)}, u32[]{:S(2)}) collective-permute-start(bf16[256,1024]{1,0:T(8,128)(2,1)} %get-tuple-element.35), channel_id=1, source_target_pairs={{0,4},{4,8},{8,12},{12,14},{14,10},{10,6},{6,2},{2,0},{1,5},{5,9},... | collective-permute-start | bytes 1572872 | tf_op jit(solution)/shard_map/ppermute | solution.py:742
  234.2 17.0 %collective-permute-start.23 = (bf16[2,256,256]{2,1,0:T(8,128)(2,1)}, bf16[2,256,256]{2,1,0:T(8,128)(2,1)S(1)}, u32[]{:S(2)}, u32[]{:S(2)}) collective-permute-start(bf16[2,256,256]{2,1,0:T(8,128)(2,1)} %get-tuple-element.38), channel_id=1, source_target_pairs={{0,12},{4,14},{8,10},{12,6},{14,2},{10,0},{6,4},{2,8},{1,13},{5,15... | collective-permute-start | bytes 786440 | tf_op jit(solution)/shard_map/ppermute | solution.py:769
  235.7 40.4 %collective-permute-start.32 = (f32[32,128]{1,0:T(8,128)S(1)}, f32[32,128]{1,0:T(8,128)S(1)}, u32[]{:S(2)}, u32[]{:S(2)}) collective-permute-start(f32[32,128]{1,0:T(8,128)S(1)} %get-tuple-element.66), channel_id=1, source_target_pairs={{0,4},{2,6},{4,8},{6,10},{8,12},{10,14},{12,0},{14,2},{1,5},{3,7},... | collective-permute-start | bytes 49160 | tf_op jit(solution)/shard_map/ppermute | solution.py:613
  238.2 11.7 %copy-start.30 = (bf16[2,256,256]{2,1,0:T(8,128)(2,1)S(1)}, bf16[2,256,256]{2,1,0:T(8,128)(2,1)}, u32[]{:S(2)}) copy-start(bf16[2,256,256]{2,1,0:T(8,128)(2,1)} %get-tuple-element.39) | copy-start | bytes 786436
  238.2 11.9 %copy-start.14 = (bf16[5,256,256]{2,1,0:T(8,128)(2,1)S(1)}, bf16[5,256,256]{2,1,0:T(8,128)(2,1)}, u32[]{:S(2)}) copy-start(bf16[5,256,256]{2,1,0:T(8,128)(2,1)} %get-tuple-element.34) | copy-start | bytes 1966084
  238.2 37.9 %collective-permute-start.33 = (f32[32,128]{1,0:T(8,128)S(1)}, f32[32,128]{1,0:T(8,128)S(1)}, u32[]{:S(2)}, u32[]{:S(2)}) collective-permute-start(f32[32,128]{1,0:T(8,128)S(1)} %get-tuple-element.68), channel_id=1, source_target_pairs={{0,8},{2,10},{4,12},{6,14},{8,0},{10,2},{12,4},{14,6},{1,9},{3,11}... | collective-permute-start | bytes 49160 | tf_op jit(solution)/shard_map/ppermute | solution.py:613
  242.9 21.3 %copy-start.31 = (bf16[1,256,256]{2,1,0:T(8,128)(2,1)S(1)}, bf16[1,256,256]{2,1,0:T(8,128)(2,1)}, u32[]{:S(2)}) copy-start(bf16[1,256,256]{2,1,0:T(8,128)(2,1)} %get-tuple-element.41) | copy-start | bytes 393220
  242.9 22.9 %collective-permute-start.25 = (bf16[2,256,256]{2,1,0:T(8,128)(2,1)}, bf16[2,256,256]{2,1,0:T(8,128)(2,1)S(1)}, u32[]{:S(2)}, u32[]{:S(2)}) collective-permute-start(bf16[2,256,256]{2,1,0:T(8,128)(2,1)} %get-tuple-element.40), channel_id=1, source_target_pairs={{0,2},{4,0},{8,4},{12,8},{14,12},{10,14},{6,10},{2,6},{1,3},{5,1},... | collective-permute-start | bytes 786440 | tf_op jit(solution)/shard_map/ppermute | solution.py:769
  249.9 14.2 %collective-permute-start.24 = (bf16[2,256,256]{2,1,0:T(8,128)(2,1)S(1)}, bf16[2,256,256]{2,1,0:T(8,128)(2,1)S(1)}, u32[]{:S(2)}, u32[]{:S(2)}) collective-permute-start(bf16[2,256,256]{2,1,0:T(8,128)(2,1)S(1)} %copy-done.30), channel_id=1, source_target_pairs={{0,6},{4,2},{8,0},{12,4},{14,8},{10,12},{6,14},{2,10},{1,7},{5,3},... | collective-permute-start | bytes 786440 | tf_op jit(solution)/shard_map/ppermute | solution.py:769
  251.3 24.8 %collective-permute-start.34 = (f32[32,128]{1,0:T(8,128)S(1)}, f32[32,128]{1,0:T(8,128)S(1)}, u32[]{:S(2)}, u32[]{:S(2)}) collective-permute-start(f32[32,128]{1,0:T(8,128)S(1)} %get-tuple-element.67), channel_id=1, source_target_pairs={{0,12},{2,14},{4,0},{6,2},{8,4},{10,6},{12,8},{14,10},{1,13},{3,15... | collective-permute-start | bytes 49160 | tf_op jit(solution)/shard_map/ppermute | solution.py:613
  264.2 7.7 %collective-permute-start.26 = (bf16[1,256,256]{2,1,0:T(8,128)(2,1)S(1)}, bf16[1,256,256]{2,1,0:T(8,128)(2,1)S(1)}, u32[]{:S(2)}, u32[]{:S(2)}) collective-permute-start(bf16[1,256,256]{2,1,0:T(8,128)(2,1)S(1)} %copy-done.31), channel_id=1, source_target_pairs={{0,14},{4,10},{8,6},{12,2},{14,0},{10,4},{6,8},{2,12},{1,15},{5,11... | collective-permute-start | bytes 393224 | tf_op jit(solution)/shard_map/ppermute | solution.py:769
  276.1 5.8 %collective-permute-start.27 = (bf16[8,256,256]{2,1,0:T(8,128)(2,1)}, bf16[8,256,256]{2,1,0:T(8,128)(2,1)S(1)}, u32[]{:S(2)}, u32[]{:S(2)}) collective-permute-start(bf16[8,256,256]{2,1,0:T(8,128)(2,1)} %for_sibling.1), channel_id=1, source_target_pairs={{0,1},{1,0},{2,3},{3,2},{4,5},{5,4},{6,7},{7,6},{8,9},{9,8},{10,11... | collective-permute-start | bytes 3145736 | tf_op jit(solution)/shard_map/ppermute | solution.py:772
  276.2 3.7 %collective-permute-start.35 = (f32[16,128]{1,0:T(8,128)S(1)}, f32[16,128]{1,0:T(8,128)S(1)}, u32[]{:S(2)}, u32[]{:S(2)}) collective-permute-start(f32[16,128]{1,0:T(8,128)S(1)} %constant_dynamic-slice_fusion), channel_id=1, source_target_pairs={{0,2},{2,0},{4,6},{6,4},{8,10},{10,8},{12,14},{14,12},{1,3},{3,1},... | collective-permute-start | bytes 24584 | tf_op jit(solution)/shard_map/ppermute | solution.py:609
  279.9 1.2 collective-permute-start.36
  (23 other events, 78.7 us)

commit v6 on v4

--- a/solution.py
+++ b/solution.py
@@ -11,6 +11,7 @@
 EXACT = lax.Precision.HIGHEST
 SWAP = [(0, 1), (1, 0)]
 VMEM_BYTES = 56 * 1024 * 1024
+SMALL_BYTES = 12 * 1024 * 1024
 LIGHT = pl.CostEstimate(flops=10**6, bytes_accessed=10**5, transcendentals=0)
 ANYWHERE = pl.BlockSpec(memory_space=pl.ANY)
 
@@ -75,27 +76,45 @@
 def window_terms(ring, place, stored, vectors, group, steps, parts, after=()):
     rows, full = stored.shape
     new_rows = vectors.shape[0]
-    taps = jnp.array(steps, jnp.int32)
-
-    def kernel(place_ref, step_ref, stored_ref, vectors_ref, *refs):
-        owner = ring.position_of(place_ref[0]) + step_ref[pl.program_id(0)] + ring.count
-        owner = lax.rem(owner, ring.count)
-        core = place_ref[1]
-        left = pl.ds(pl.multiple_of((2 * ring.index_at(owner) + core) * group, group), group)
-        turned = stored_ref[:, left].T
-        turned_new = vectors_ref[:, left].T
-        for slots, out_ref in zip(parts, refs[len(after) :]):
-            for offset, blocks, first in pairs_of(slots):
-                column = 2 * ring.index_at(owner + offset)
+    chips = [(part,) + chip for part, slots in enumerate(parts) for chip in pairs_of(slots)]
+    taps = jnp.array(list(steps) + [offset for _, offset, _, _ in chips], jnp.int32)
+
+    def owner_of(i, place_ref, taps_ref):
+        return lax.rem(ring.position_of(place_ref[0]) + taps_ref[i] + ring.count, ring.count)
+
+    def chip_of(i, k, place_ref, taps_ref):
+        return ring.index_at(owner_of(i, place_ref, taps_ref) + taps_ref[len(steps) + k])
+
+    def kernel(place_ref, taps_ref, left_ref, right_ref, left_new_ref, right_new_ref, *refs):
+        outs, turned, turned_new = refs[len(after) : -2], refs[-2], refs[-1]
+        i, k = pl.program_id(0), pl.program_id(1)
+        owner = owner_of(i, place_ref, taps_ref)
+
+        @pl.when(k == 0)
+        def _():
+            turned[...] = left_ref[...].T
+            turned_new[...] = left_new_ref[...].T
+
+        for index, (part, _, blocks, first) in enumerate(chips):
+
+            @pl.when(k == index)
+            def _():
+                columns = slice(0, 2 * group)
                 if blocks == 1:
-                    column = column + jnp.where(owner < ring.half, core, 1 - core)
-                right = pl.ds(pl.multiple_of(column * group, blocks * group), blocks * group)
-                total = jnp.dot(turned, stored_ref[:, right], preferred_element_type=jnp.float32)
-                total = total + jnp.dot(turned_new, vectors_ref[:, right], preferred_element_type=jnp.float32)
-                out_ref[0, :, first * group : (first + blocks) * group] = total.astype(jnp.bfloat16)
+                    side = jnp.where(owner < ring.half, place_ref[1], 1 - place_ref[1])
+                    columns = pl.ds(pl.multiple_of(side * group, group), group)
+                total = jnp.dot(turned[...], right_ref[:, columns], preferred_element_type=jnp.float32)
+                total = total + jnp.dot(turned_new[...], right_new_ref[:, columns], preferred_element_type=jnp.float32)
+                outs[part][0, :, first * group : (first + blocks) * group] = total.astype(jnp.bfloat16)
+
+    def left_map(i, k, place_ref, taps_ref):
+        return 0, 2 * ring.index_at(owner_of(i, place_ref, taps_ref)) + place_ref[1]
+
+    def right_map(i, k, place_ref, taps_ref):
+        return 0, chip_of(i, k, place_ref, taps_ref)
 
     def out(slots):
-        return pl.BlockSpec((1, group, len(slots) * group), lambda i, a, b: (i, 0, 0))
+        return pl.BlockSpec((1, group, len(slots) * group), lambda i, k, a, b: (i, 0, 0))
 
     def shape(slots):
         return jax.ShapeDtypeStruct((len(steps), group, len(slots) * group), jnp.bfloat16)
@@ -104,19 +123,22 @@
         kernel,
         grid_spec=pltpu.PrefetchScalarGridSpec(
             num_scalar_prefetch=2,
-            grid=(len(steps),),
+            grid=(len(steps), len(chips)),
             in_specs=[
-                pl.BlockSpec((rows, full), lambda i, a, b: (0, 0), pipeline_mode=pl.Buffered(1)),
-                pl.BlockSpec((new_rows, full), lambda i, a, b: (0, 0), pipeline_mode=pl.Buffered(1)),
+                pl.BlockSpec((rows, group), left_map),
+                pl.BlockSpec((rows, 2 * group), right_map),
+                pl.BlockSpec((new_rows, group), left_map),
+                pl.BlockSpec((new_rows, 2 * group), right_map),
             ]
             + [ANYWHERE] * len(after),
             out_specs=[out(slots) for slots in parts],
+            scratch_shapes=[pltpu.VMEM((group, rows), jnp.bfloat16), pltpu.VMEM((group, new_rows), jnp.bfloat16)],
         ),
         out_shape=[shape(slots) for slots in parts],
         compiler_params=pltpu.CompilerParams(vmem_limit_bytes=VMEM_BYTES),
         cost_estimate=LIGHT,
         name="window_terms",
-    )(place, taps, stored, vectors, *after)
+    )(place, taps, stored, stored, vectors, vectors, *after)
 
 
 def add_terms(terms, index, arrived, sizes, group, after=()):
@@ -146,7 +168,7 @@
         + [ANYWHERE] * len(after),
         out_specs=[flat(size * group) for size in sizes],
         out_shape=[jax.ShapeDtypeStruct((group, size * group), jnp.bfloat16) for size in sizes],
-        compiler_params=pltpu.CompilerParams(vmem_limit_bytes=VMEM_BYTES),
+        compiler_params=pltpu.CompilerParams(vmem_limit_bytes=SMALL_BYTES),
         cost_estimate=LIGHT,
         name="add_terms",
     )(terms, *[array for array, _ in arrived], *after)
@@ -176,7 +198,7 @@
         in_specs=[pl.BlockSpec((1,) + terms.shape[1:], lambda i: (index, 0, 0)), flat, flat],
         out_specs=[pl.BlockSpec((size, group, group), lambda i: (0, 0, 0)) for size in sizes],
         out_shape=[jax.ShapeDtypeStruct((size, group, group), jnp.bfloat16) for size in sizes],
-        compiler_params=pltpu.CompilerParams(vmem_limit_bytes=VMEM_BYTES),
+        compiler_params=pltpu.CompilerParams(vmem_limit_bytes=SMALL_BYTES),
         cost_estimate=LIGHT,
         name="close_window",
     )(terms, ahead, back)
@@ -236,12 +258,18 @@
         out_ref[here, :] = out_ref[here, :] - exact_dot(work[here, rest], out_ref[rest, :])
 
 
-def solve(place, mine, other, first_cols, after=()):
+def solve(place, pairs_count, mine, other, kept, came, after=()):
     group, width = mine.shape
-    examples = first_cols.shape[0]
-
-    def kernel(place_ref, mine_ref, other_ref, first_ref, *refs):
-        out_ref, pairs_ref, matrix, right, power, inverse = refs[len(after) :]
+    examples = 2 * kept.shape[0]
+    size = kept.shape[0] // pairs_count
+
+    def kernel(place_ref, mine_ref, other_ref, kept_ref, came_ref, *refs):
+        out_ref, pairs_ref, matrix, right, power, inverse, first_ref = refs[len(after) :]
+        for start in range(0, kept_ref.shape[0], size):
+            near, far = kept_ref[start : start + size, :width], came_ref[start : start + size, :width]
+            even = lax.rem(place_ref[0], 2) == 0
+            first_ref[2 * start : 2 * start + size, :] = jnp.where(even, near, far)
+            first_ref[2 * start + size : 2 * start + 2 * size, :] = jnp.where(even, far, near)
         eye = identity(width)
         t = place_ref[1]
         matrix[pl.ds(pl.multiple_of(t * group, group), group), :] = mine_ref[...]
@@ -296,7 +324,7 @@
     whole = pl.BlockSpec(memory_space=pltpu.VMEM)
     return pl.pallas_call(
         kernel,
-        in_specs=[pl.BlockSpec(memory_space=pltpu.SMEM)] + [whole] * 3 + [ANYWHERE] * len(after),
+        in_specs=[pl.BlockSpec(memory_space=pltpu.SMEM)] + [whole] * 4 + [ANYWHERE] * len(after),
         out_shape=[
             jax.ShapeDtypeStruct((width, examples), jnp.float32),
             jax.ShapeDtypeStruct((examples, examples), jnp.float32),
@@ -306,11 +334,12 @@
             pltpu.VMEM((width, examples), jnp.float32),
             pltpu.VMEM((width, width), jnp.bfloat16),
             pltpu.VMEM((width, width), jnp.float32),
+            pltpu.VMEM((examples, width), jnp.bfloat16),
         ],
         compiler_params=pltpu.CompilerParams(vmem_limit_bytes=VMEM_BYTES),
         cost_estimate=LIGHT,
         name="solve",
-    )(place, mine, other, first_cols, *after)
+    )(place, mine, other, kept, came, *after)
 
 
 def spread_back(place, stored, solved, owners, group, after=()):
@@ -354,6 +383,40 @@
     )(place, stored, solved, *([stored] * owners), *after)
 
 
+def pair_products(place, pairs, own_cols, first_pairs, mine, other, solved, after=()):
+    examples, group = own_cols.shape
+    size = examples // pairs
+
+    def kernel(place_ref, own_ref, first_ref, mine_ref, other_ref, solved_ref, *refs):
+        outs, whole = refs[len(after) : -1], refs[-1]
+        g = 2 * place_ref[0] + place_ref[1]
+        own = own_ref[...]
+        damped = solved_ref[pl.ds(pl.multiple_of(place_ref[1] * group, group), group), :].T
+        rest = own - lax.dot_general(
+            first_ref[...], own, (((0,), (0,)), ((), ())), precision=EXACT, preferred_element_type=jnp.float32
+        )
+        rest = rest - mine_ref[...] - other_ref[...].astype(jnp.float32) - jnp.where(g < 2, damping * damped, 0.0)
+        products = lax.dot_general(
+            rest, rest, (((1,), (1,)), ((), ())), precision=EXACT, preferred_element_type=jnp.float32
+        )
+        whole[...] = products + jnp.where(g == 0, first_ref[...], 0.0)
+        for index in range(pairs):
+            start = lax.rem(place_ref[0] // 2 + index, pairs) * size
+            outs[index][...] = whole[pl.ds(pl.multiple_of(start, size), size), :]
+
+    vmem = pl.BlockSpec(memory_space=pltpu.VMEM)
+    return pl.pallas_call(
+        kernel,
+        in_specs=[pl.BlockSpec(memory_space=pltpu.SMEM)] + [vmem] * 5 + [ANYWHERE] * len(after),
+        out_specs=[vmem] * pairs,
+        out_shape=[jax.ShapeDtypeStruct((size, examples), jnp.float32)] * pairs,
+        scratch_shapes=[pltpu.VMEM((examples, examples), jnp.float32)],
+        compiler_params=pltpu.CompilerParams(vmem_limit_bytes=SMALL_BYTES),
+        cost_estimate=LIGHT,
+        name="pair_products",
+    )(place, own_cols, first_pairs, mine, other, solved, *after)
+
+
 def assembly_tables(ring, slots, d, t):
     start = [0] * ring.count
     arrived = [0] * ring.count
@@ -416,7 +479,7 @@
             out_specs=pl.BlockSpec((wide, group, group), lambda c, ref: (c, 0, 0)),
         ),
         out_shape=jax.ShapeDtypeStruct((total, group, group), jnp.bfloat16),
-        compiler_params=pltpu.CompilerParams(vmem_limit_bytes=VMEM_BYTES),
+        compiler_params=pltpu.CompilerParams(vmem_limit_bytes=SMALL_BYTES),
         cost_estimate=LIGHT,
         name="for_sibling",
     )(table, *([blocks] * wide))
@@ -463,7 +526,7 @@
             out_specs=pl.BlockSpec((group, 2 * wide * group), lambda r, c, ref, place: (r, c)),
         ),
         out_shape=jax.ShapeDtypeStruct((2 * group, 2 * half * group), jnp.float32),
-        compiler_params=pltpu.CompilerParams(vmem_limit_bytes=VMEM_BYTES),
+        compiler_params=pltpu.CompilerParams(vmem_limit_bytes=SMALL_BYTES),
         cost_estimate=LIGHT,
         name="finish",
     )(table, place, *([blocks] * len(order)), *([other] * len(order)))
@@ -526,13 +589,10 @@
     g = 2 * d + t
     place = jnp.stack([d, t]).astype(jnp.int32)
 
+    pairs_count = owners // 2
     first_stored = stored[:, :width]
     corner_rows = lead_dot(lax.dynamic_slice_in_dim(first_stored, t * group, group, 1), first_stored)
-    corner_rows = scatter_pairs(corner_rows, pair, owners)
-    corner_rows = corner_rows + pair_swap(corner_rows, owners)
-    corner_rows = exchange_pairs(lambda index: corner_rows, pair, owners)
-    corner_rows = jnp.concatenate(natural(corner_rows, pair), axis=0)
-    corner_other = lax.ppermute(corner_rows, "tensor", SWAP)
+    corner_payload = scatter_pairs(corner_rows, pair, owners)
 
     sides = jnp.concatenate(
         [
@@ -563,14 +623,7 @@
         groups = [lax.dynamic_slice_in_dim(vectors, (4 * index + 2 * s + t) * group, group, 1) for s in (0, 1)]
         return jnp.concatenate([vectors[:, :width]] + groups, axis=1)
 
-    came = natural(exchange_pairs(columns_for, pair, owners), pair)
-    came = jnp.concatenate(came, axis=0)
-    kept = jnp.where(side == 0, came[:, : width + group], jnp.concatenate([came[:, :width], came[:, width + group :]], axis=1))
-    away = jnp.where(side == 0, jnp.concatenate([came[:, :width], came[:, width + group :]], axis=1), came[:, : width + group])
-    shape = (owners // 2, 1, examples, width + group)
-    known = in_order(side, kept.reshape(shape), pair_swap(away, owners).reshape(shape), 1)
-    known = known.reshape(all_examples, width + group)
-    first_cols, own_cols = known[:, :width], known[:, width:].astype(jnp.float32)
+    payloads = [columns_for(lax.rem(pair + step, pairs_count)) for step in range(pairs_count)]
 
     split = (len(ring.offsets) + 1) // 2
     far_slots = [(half, None)]
@@ -587,18 +640,33 @@
     def terms_of(steps, parts, after=()):
         return window_terms(ring, place, stored, vectors, group, steps, parts, after)
 
-    far, near = terms_of([half], [far_slots, near_slots])
+    came = [payloads[0]] + [far_shift(payloads[step], step, owners) for step in range(1, pairs_count)]
+    came = jnp.concatenate(natural(came, pair), axis=0)
+    second_group = jnp.concatenate([came[:, :width], came[:, width + group :]], axis=1)
+    first_group = came[:, : width + group]
+    kept = jnp.where(side == 0, first_group, second_group)
+    away = jnp.where(side == 0, second_group, first_group)
+    received = pair_swap(away, owners)
+    far, near = terms_of([half], [far_slots, near_slots], [away, corner_payload])
     far, near = far[0], near[0]
+
+    corner_rows = corner_payload + pair_swap(corner_payload, owners)
     second = terms_of([half - 1, 1 - half], [slots], [far])[0]
+    corner_rows = [corner_rows] + [far_shift(corner_rows, step, owners) for step in range(1, pairs_count)]
+    corner_rows = jnp.concatenate(natural(corner_rows, pair), axis=0)
+    corner_other = lax.ppermute(corner_rows, "tensor", SWAP)
+    shape = (pairs_count, 1, examples, group)
+    own_cols = in_order(side, kept[:, width:].reshape(shape), received[:, width:].reshape(shape), 1)
+    own_cols = own_cols.reshape(all_examples, group).astype(jnp.float32)
     far_ahead = lax.ppermute(far, "dp", ahead)
     near_back = lax.ppermute(near, "dp", back)
     last = [far_count, near_count] if half == 2 else [far_count + near_count]
-    going = add_terms(second, 0, [(far_ahead, 0)], last, group)
-    coming = add_terms(second, 1, [(near_back, far_count)], last, group)
+    going = add_terms(second, 0, [(far_ahead, 0)], last, group, [corner_rows, received])
+    coming = add_terms(second, 1, [(near_back, far_count)], last, group, [corner_rows, received])
 
     later_steps = [s for step in range(half - 2, 0, -1) for s in (step, -step)] + [0]
     later = terms_of(later_steps, [slots], [going[0], coming[0]])[0]
-    solved, first_pairs = solve(place, corner_rows, corner_other, first_cols, [later])
+    solved, first_pairs = solve(place, pairs_count, corner_rows, corner_other, kept, received, [later])
     token = solved
     for step in range(half - 2, 0, -1):
         last = [far_count, near_count] if step == 1 else [far_count + near_count]
@@ -617,18 +685,8 @@
     for step in range(1, owners // 2):
         terms = terms + far_shift(pieces[step], step, owners).astype(jnp.float32)
     away = jnp.where(side == 0, terms[1], terms[0]).astype(jnp.bfloat16)
-    terms = jnp.where(side == 0, terms[0], terms[1]) + pair_swap(away, owners).astype(jnp.float32)
-    damped = lax.dynamic_slice_in_dim(solved.T, lax.rem(g, 2) * group, group, 1)
-    damped = jnp.where(g < 2, damping * damped, 0.0)
-    rest = own_cols - lead_dot(first_pairs, own_cols, EXACT) - terms - damped
-    pairs = lax.dot_general(rest, rest, (((1,), (1,)), ((), ())), precision=EXACT, preferred_element_type=jnp.float32)
-    pairs = pairs + jnp.where(g == 0, first_pairs, 0.0)
-    pairs = scatter_pairs(pairs, pair, owners)
-    away = lax.dynamic_slice_in_dim(pairs, (1 - side) * examples, examples, 0)
-    pairs = lax.dynamic_slice_in_dim(pairs, side * examples, examples, 0) + pair_swap(away, owners)
-    pairs = pairs + lax.ppermute(pairs, "tensor", SWAP)
-    chosen = (query_ids[:, None] == jnp.arange(all_examples, dtype=jnp.int32)[None, :]).astype(jnp.float32)
-    scores = lax.dot_general(chosen, pairs, (((1,), (1,)), ((), ())), precision=EXACT, preferred_element_type=jnp.float32) / R
+    terms = jnp.where(side == 0, terms[0], terms[1])
+    terms_other = pair_swap(away, owners)
 
     far = close_window(later, 0, going[0], coming[0], far_slots, group)
     near = close_window(later, far_count, going[1], coming[1], near_slots, group)
@@ -637,7 +695,19 @@
         chips = [chip for chip in pairs_of(slots) if chip[0] != 0]
         for (offset, _, _), block in zip(chips, found[1:]):
             turned[offset] = block
-    came = [lax.ppermute(turned[offset], "dp", ring.shift(offset)) for offset in ring.offsets + [half]]
+    shifted = {
+        offset: lax.ppermute(turned[offset], "dp", ring.shift(offset))
+        for offset in [half] + ring.offsets
+    }
+    came = [shifted[offset] for offset in ring.offsets + [half]]
+    early = [shifted[offset] for offset in [half] + ring.offsets[:split]]
+    pairs = pair_products(place, pairs_count, own_cols, first_pairs, terms, terms_other, solved, early)
+    pairs = pairs[0] + sum(far_shift(pairs[step], step, owners) for step in range(1, pairs_count))
+    away = lax.dynamic_slice_in_dim(pairs, (1 - side) * examples, examples, 0)
+    pairs = lax.dynamic_slice_in_dim(pairs, side * examples, examples, 0) + pair_swap(away, owners)
+    pairs = pairs + lax.ppermute(pairs, "tensor", SWAP)
+    chosen = (query_ids[:, None] == jnp.arange(all_examples, dtype=jnp.int32)[None, :]).astype(jnp.float32)
+    scores = lax.dot_general(chosen, pairs, (((1,), (1,)), ((), ())), precision=EXACT, preferred_element_type=jnp.float32) / R
     blocks = jnp.concatenate([far[0], near[0]] + came, axis=0)
     send_table, final_table = assembly_tables(ring, far_slots + near_slots, d, t)
     other = lax.ppermute(for_sibling(send_table, blocks, group), "tensor", SWAP)

time: 246 us -> 239 us (0.972)
  Pallas kernels: 86.5 us -> 78.4 us
  starting transfers between devices: 50.7 us -> 56 us
  waiting for transfers between devices: 73 us -> 68.8 us
  matrix products: 11.7 us -> 8.62 us
    ppermute x4, waiting for transfers between devices: 2.6 us -> 31.3 us  [local(): coming = [lax.ppermute(value, 'dp', back) for value in coming]]
    pallas_call x3, Pallas kernels: 29.4 us -> 46.3 us  [window_terms(): pl.pallas_call(kernel, grid_spec=pltpu.PrefetchScalarGridSpec(num_scalar_...]
    ppermute x15, waiting for transfers between devices: 19.5 us -> 4.13 us  [far_shift(): lax.ppermute(value, 'dp', [(index, (index + 2 * step) % count) for index...]
    pallas_call x6, Pallas kernels: 16.8 us -> 4.97 us  [add_terms(): pl.pallas_call(kernel, grid=(1,), in_specs=[pl.BlockSpec((1, group, count...]
    ppermute x4, waiting for transfers between devices: 14.1 us -> 5.95 us  [local(): lax.ppermute(turned[offset], 'dp', ring.shift(offset))]
    ppermute x4, waiting for transfers between devices: 30 us -> 23 us  [pair_swap(): lax.ppermute(value, 'dp', [(index, index ^ 1) for index in range(count)])]
    pallas_call x1, Pallas kernels: 18.6 us -> 12.8 us  [solve(): pl.pallas_call(kernel, in_specs=[pl.BlockSpec(memory_space=pltpu.SMEM)] +...]
    ppermute x4, starting transfers between devices: 10.5 us -> 16.1 us  [local(): lax.ppermute(turned[offset], 'dp', ring.shift(offset))]
  transfers between devices with their start and end apart: 37 -> 37, of which waited for: 13 -> 15; matrix products, arithmetic and copies ran while one was open for 6% -> 5% of each run, Pallas kernels for 33% -> 29%
where the time goes in v6:
time: 239 us; the launch traced here: 236 us
  Pallas kernels  78.4 us (33%)
  waiting for transfers between devices  68.8 us (29%)
  starting transfers between devices  56 us (23%)
  local copies, waits for them, and re-layouts  18.5 us (8%)
  matrix products  8.62 us (4%)
  other arithmetic  4.38 us (2%)
    pallas_call x3, Pallas kernels, window_terms(): pl.pallas_call(kernel, grid_spec=pltpu.PrefetchScalarGridSpec(num_scalar_...  46.3 us
    ppermute x4, waiting for transfers between devices, local(): coming = [lax.ppermute(value, 'dp', back) for value in coming]  31.3 us
    ppermute x15, starting transfers between devices, far_shift(): lax.ppermute(value, 'dp', [(index, (index + 2 * step) % count) for index...  26.8 us
    ppermute x4, waiting for transfers between devices, pair_swap(): lax.ppermute(value, 'dp', [(index, index ^ 1) for index in range(count)])  23 us
    ppermute x4, starting transfers between devices, local(): lax.ppermute(turned[offset], 'dp', ring.shift(offset))  16.1 us
    unnamed x59, local copies, waits for them, and re-layouts  14.6 us
    pallas_call x1, Pallas kernels, solve(): pl.pallas_call(kernel, in_specs=[pl.BlockSpec(memory_space=pltpu.SMEM)] +...  12.8 us
    pallas_call x1, Pallas kernels, spread_back(): pl.pallas_call(kernel, grid_spec=pltpu.PrefetchScalarGridSpec(num_scalar_...  7.56 us
  transfers between devices with their start and end apart: 37, of which 15 were waited for; matrix products, arithmetic and copies ran while one was open for 5% of the time, Pallas kernels for 29%

profile of v6, /device:TPU:0, one launch (start us, length us, event | category | flops | bytes accessed | tf_op | source)
XLA Modules:
  0.0 236.0 jit_solution(12404706370650539509)
XLA Ops:
  0.7 1.8 slice-done.1
  3.7 3.0 %collective-permute-start.4 = (f32[64,512]{1,0:T(8,128)}, f32[64,512]{1,0:T(8,128)S(1)}, u32[]{:S(2)}, u32[]{:S(2)}) collective-permute-start(f32[64,512]{1,0:T(8,128)} %get-tuple-element.52), channel_id=1, source_target_pairs={{0,4},{2,6},{4,8},{6,10},{8,12},{10,14},{12,0},{14,2},{1,5},{3,7},... | collective-permute-start | bytes 393224 | tf_op jit(solution)/shard_map/ppermute | solution.py:548
  6.7 2.6 %collective-permute-start.5 = (f32[64,512]{1,0:T(8,128)S(1)}, f32[64,512]{1,0:T(8,128)S(1)}, u32[]{:S(2)}, u32[]{:S(2)}) collective-permute-start(f32[64,512]{1,0:T(8,128)S(1)} %get-tuple-element.54), channel_id=1, source_target_pairs={{0,8},{2,10},{4,12},{6,14},{8,0},{10,2},{12,4},{14,6},{1,9},{3,11}... | collective-permute-start | bytes 393224 | tf_op jit(solution)/shard_map/ppermute | solution.py:548
  9.3 1.3 collective-permute-start.6
  10.7 5.4 %fusion.30 = f32[256,64]{0,1:T(8,128)S(1)} fusion(bf16[256,14336]{1,0:T(8,128)(2,1)} %param.10, bf16[14336,64]{0,1:T(8,128)(2,1)S(1)} %copy-done.19), kind=kOutput, calls=%fused_computation.119 | convolution fusion | flops 469762048 | bytes 9240576 | tf_op jit(solution)/shard_map/dot_general | solution.py:599
  20.5 1.7 collective-permute-start.2
  22.2 1.6 add_add_fusion.refs_1_
  24.1 1.5 collective-permute-done.2
  25.6 2.3 collective-permute-done.3
  29.4 7.2 %window_terms.3 = (bf16[1,256,1280]{2,1,0:T(8,128)(2,1)}, bf16[1,256,1024]{2,1,0:T(8,128)(2,1)}) custom-call(s32[2]{0:T(128)} %pad_add_fusion.1.place_ref, s32[6]{0:T(128)} %constant.138.clone.taps_ref, bf16[1024,4096]{1,0:T(8,128)(2,1)} %refs_7_.1, bf16[1024,4096]{1,0:T(8,128)(2,1)} %refs_7_.1, bf16[16,4096]{1,0:T(8,128)(2,1)} %copy-done.18, ...), custom_call_target="tpu_custom_call" | custom-call | flops 1000000 | bytes 100000 | tf_op jit(solution)/shard_map/window_terms/pallas_call | solution.py:122
  36.6 2.0 collective-permute-start.8
  38.7 16.1 %collective-permute-done.8 = f32[64,512]{1,0:T(8,128)S(1)} collective-permute-done((f32[64,512]{1,0:T(8,128)S(1)}, f32[64,512]{1,0:T(8,128)S(1)}, u32[]{:S(2)}, u32[]{:S(2)}) %collective-permute-start.8) | collective-permute-done | bytes 131104 | tf_op jit(solution)/shard_map/ppermute | solution.py:544
  55.2 3.6 %collective-permute-start.9 = (f32[64,512]{1,0:T(8,128)S(1)}, f32[64,512]{1,0:T(8,128)S(1)}, u32[]{:S(2)}, u32[]{:S(2)}) collective-permute-start(f32[64,512]{1,0:T(8,128)S(1)} %add.308), channel_id=1, source_target_pairs={{0,12},{2,14},{4,0},{6,2},{8,4},{10,6},{12,8},{14,10},{1,13},{3,15... | collective-permute-start | bytes 393224 | tf_op jit(solution)/shard_map/ppermute | solution.py:548
  58.8 12.1 %window_terms.4.terms_ref = bf16[2,256,2304]{2,1,0:T(8,128)(2,1)} custom-call(s32[2]{0:T(128)} %pad_add_fusion.1.place_ref, s32[7]{0:T(128)} %constant.139.clone.taps_ref, bf16[1024,4096]{1,0:T(8,128)(2,1)} %refs_7_.1, bf16[1024,4096]{1,0:T(8,128)(2,1)} %refs_7_.1, bf16[16,4096]{1,0:T(8,128)(2,1)} %copy-done.18, bf16[16,4096]{1,0:T(8,128)(2,1)} %copy-done.18, ...), custom_call_target="tpu_custom_call" | custom-call | flops 1000000 | bytes 100000 | tf_op jit(solution)/shard_map/window_terms/pallas_call | solution.py:122
  71.2 4.4 %collective-permute-done.12.refs_2_.came_ref = bf16[64,768]{1,0:T(8,128)(2,1)S(1)} collective-permute-done((bf16[64,768]{1,0:T(8,128)(2,1)S(1)}, bf16[64,768]{1,0:T(8,128)(2,1)S(1)}, u32[]{:S(2)}, u32[]{:S(2)}) %collective-permute-start.12) | collective-permute-done | bytes 98336 | tf_op jit(solution)/shard_map/ppermute | solution.py:544
  75.6 1.7 copy-done.5
  78.5 1.5 collective-permute-start.14
  80.0 27.0 %window_terms.5.refs_0_.terms_ref.own_ref = bf16[5,256,2304]{2,1,0:T(8,128)(2,1)} custom-call(s32[2]{0:T(128)} %pad_add_fusion.1.place_ref, s32[10]{0:T(128)} %constant.140.clone.taps_ref, bf16[1024,4096]{1,0:T(8,128)(2,1)} %refs_7_.1, bf16[1024,4096]{1,0:T(8,128)(2,1)} %refs_7_.1, bf16[16,4096]{1,0:T(8,128)(2,1)} %copy-done.18, ...), custom_call_target="tpu_custom_call" | custom-call | flops 1000000 | bytes 100000 | tf_op jit(solution)/shard_map/window_terms/pallas_call | solution.py:122
  107.8 12.8 %solve.1 = (f32[512,128]{1,0:T(8,128)}, f32[128,128]{1,0:T(8,128)}) custom-call(s32[2]{0:T(128)} %pad_add_fusion.1.place_ref, f32[256,512]{1,0:T(8,128)} %copy-done.6, f32[256,512]{1,0:T(8,128)} %copy-done.21, bf16[64,768]{1,0:T(8,128)(2,1)} %get-tuple-element.46.kept_ref, bf16[64,768]{1,0:T(8,128)(2,1)} %copy-done.15, ...), custom_call_target="tpu_custom_call" | custom-call | flops 1000000 | bytes 100000 | tf_op jit(solution)/shard_map/solve/pallas_call | solution.py:325
  120.6 2.7 %copy-done.1 = bf16[5,256,2304]{2,1,0:T(8,128)(2,1)S(1)} copy-done((bf16[5,256,2304]{2,1,0:T(8,128)(2,1)S(1)}, bf16[5,256,2304]{2,1,0:T(8,128)(2,1)}, u32[]{:S(2)}) %copy-start.1) | copy-done | bytes 5898264
  124.2 1.3 add_terms.9.refs_9_
  127.1 1.3 copy-done.14
  128.6 1.5 collective-permute-start.16
  131.3 7.6 %spread_back.1 = (bf16[2,128,256]{2,1,0:T(8,128)(2,1)}, bf16[2,128,256]{2,1,0:T(8,128)(2,1)}, bf16[2,128,256]{2,1,0:T(8,128)(2,1)}, bf16[2,128,256]{2,1,0:T(8,128)(2,1)}) custom-call(s32[2]{0:T(128)} %pad_add_fusion.1.place_ref, bf16[1024,4096]{1,0:T(8,128)(2,1)} %refs_7_.1, f32[512,128]{1,0:T(8,128)} %get-tuple-element.26.refs_1_.solved_ref, ...), custom_call_target="tpu_custom_call" | custom-call | flops 1000000 | bytes 100000 | tf_op jit(solution)/shard_map/spread_back/pallas_call | solution.py:363
  140.6 2.2 collective-permute-start.30
  142.8 15.6 %collective-permute-done.19.refs_0_ = bf16[256,2304]{1,0:T(8,128)(2,1)} collective-permute-done((bf16[256,2304]{1,0:T(8,128)(2,1)}, bf16[256,2304]{1,0:T(8,128)(2,1)}, u32[]{:S(2)}, u32[]{:S(2)}) %collective-permute-start.19) | collective-permute-done | bytes 1179680 | tf_op jit(solution)/shard_map/ppermute | solution.py:674
  158.4 2.7 %copy-done.2 = bf16[5,256,2304]{2,1,0:T(8,128)(2,1)S(1)} copy-done((bf16[5,256,2304]{2,1,0:T(8,128)(2,1)S(1)}, bf16[5,256,2304]{2,1,0:T(8,128)(2,1)}, u32[]{:S(2)}) %copy-start.2) | copy-done | bytes 5898264
  162.0 1.5 add_terms.11
  163.6 1.5 add_terms.10
  165.1 2.4 %collective-permute-start.18 = (bf16[256,1280]{1,0:T(8,128)(2,1)S(1)}, bf16[256,1280]{1,0:T(8,128)(2,1)S(1)}, u32[]{:S(2)}, u32[]{:S(2)}) collective-permute-start(bf16[256,1280]{1,0:T(8,128)(2,1)S(1)} %get-tuple-element.28), channel_id=1, source_target_pairs={{0,4},{4,8},{8,12},{12,14},{14,10},{10,6},{6,2},{2,0},{1,5},{5,9},... | collective-permute-start | bytes 1966088 | tf_op jit(solution)/shard_map/ppermute | solution.py:681
  167.6 2.1 collective-permute-start.21
  169.8 11.8 %collective-permute-done.20.back_ref = bf16[256,1280]{1,0:T(8,128)(2,1)S(1)} collective-permute-done((bf16[256,1280]{1,0:T(8,128)(2,1)S(1)}, bf16[256,1280]{1,0:T(8,128)(2,1)S(1)}, u32[]{:S(2)}, u32[]{:S(2)}) %collective-permute-start.20) | collective-permute-done | bytes 655392 | tf_op jit(solution)/shard_map/ppermute | solution.py:682
  181.5 1.3 collective-permute-done.18.ahead_ref
  183.2 3.3 %collective-permute-start.23 = (bf16[2,256,256]{2,1,0:T(8,128)(2,1)S(1)}, bf16[2,256,256]{2,1,0:T(8,128)(2,1)S(1)}, u32[]{:S(2)}, u32[]{:S(2)}) collective-permute-start(bf16[2,256,256]{2,1,0:T(8,128)(2,1)S(1)} %get-tuple-element.34), channel_id=1, source_target_pairs={{0,12},{4,14},{8,10},{12,6},{14,2},{10,0},{6,4},{2,8},{1,13},{5,15... | collective-permute-start | bytes 786440 | tf_op jit(solution)/shard_map/ppermute | solution.py:699
  187.0 1.5 collective-permute-start.31
  188.5 4.0 %collective-permute-done.22.back_ref = bf16[256,1024]{1,0:T(8,128)(2,1)S(1)} collective-permute-done((bf16[256,1024]{1,0:T(8,128)(2,1)S(1)}, bf16[256,1024]{1,0:T(8,128)(2,1)S(1)}, u32[]{:S(2)}, u32[]{:S(2)}) %collective-permute-start.22) | collective-permute-done | bytes 524320 | tf_op jit(solution)/shard_map/ppermute | solution.py:682
  192.5 1.4 collective-permute-done.21.ahead_ref
  194.3 12.2 %collective-permute-start.26 = (bf16[1,256,256]{2,1,0:T(8,128)(2,1)S(1)}, bf16[1,256,256]{2,1,0:T(8,128)(2,1)S(1)}, u32[]{:S(2)}, u32[]{:S(2)}) collective-permute-start(bf16[1,256,256]{2,1,0:T(8,128)(2,1)S(1)} %get-tuple-element.37), channel_id=1, source_target_pairs={{0,14},{4,10},{8,6},{12,2},{14,0},{10,4},{6,8},{2,12},{1,15},{5,11... | collective-permute-start | bytes 393224 | tf_op jit(solution)/shard_map/ppermute | solution.py:699
  206.6 2.8 %collective-permute-done.26.refs_0_ = bf16[1,256,256]{2,1,0:T(8,128)(2,1)S(1)} collective-permute-done((bf16[1,256,256]{2,1,0:T(8,128)(2,1)S(1)}, bf16[1,256,256]{2,1,0:T(8,128)(2,1)S(1)}, u32[]{:S(2)}, u32[]{:S(2)}) %collective-permute-start.26) | collective-permute-done | bytes 131104 | tf_op jit(solution)/shard_map/ppermute | solution.py:699
  209.5 3.1 %collective-permute-done.24.refs_2_ = bf16[2,256,256]{2,1,0:T(8,128)(2,1)S(1)} collective-permute-done((bf16[2,256,256]{2,1,0:T(8,128)(2,1)S(1)}, bf16[2,256,256]{2,1,0:T(8,128)(2,1)S(1)}, u32[]{:S(2)}, u32[]{:S(2)}) %collective-permute-start.24) | collective-permute-done | bytes 262176 | tf_op jit(solution)/shard_map/ppermute | solution.py:699
  212.6 1.3 pair_products.1
  213.8 1.2 collective-permute-start.32
  215.1 5.6 %collective-permute-start.33 = (f32[32,128]{1,0:T(8,128)S(1)}, f32[32,128]{1,0:T(8,128)S(1)}, u32[]{:S(2)}, u32[]{:S(2)}) collective-permute-start(f32[32,128]{1,0:T(8,128)S(1)} %get-tuple-element.44), channel_id=1, source_target_pairs={{0,8},{2,10},{4,12},{6,14},{8,0},{10,2},{12,4},{14,6},{1,9},{3,11}... | collective-permute-start | bytes 49160 | tf_op jit(solution)/shard_map/ppermute | solution.py:548
  220.7 2.8 %collective-permute-start.34 = (f32[32,128]{1,0:T(8,128)S(1)}, f32[32,128]{1,0:T(8,128)S(1)}, u32[]{:S(2)}, u32[]{:S(2)}) collective-permute-start(f32[32,128]{1,0:T(8,128)S(1)} %get-tuple-element.45), channel_id=1, source_target_pairs={{0,12},{2,14},{4,0},{6,2},{8,4},{10,6},{12,8},{14,10},{1,13},{3,15... | collective-permute-start | bytes 49160 | tf_op jit(solution)/shard_map/ppermute | solution.py:548
  223.7 1.7 for_sibling.1
  226.6 2.5 %collective-permute-done.35 = f32[16,128]{1,0:T(8,128)S(1)} collective-permute-done((f32[16,128]{1,0:T(8,128)S(1)}, f32[16,128]{1,0:T(8,128)S(1)}, u32[]{:S(2)}, u32[]{:S(2)}) %collective-permute-start.35) | collective-permute-done | bytes 8224 | tf_op jit(solution)/shard_map/ppermute | solution.py:544
  231.2 1.6 copy-done.4
  232.7 3.3 %finish.1 = f32[512,2048]{1,0:T(8,128)} custom-call(s32[48]{0:T(128)S(1)} %reshape.236.table_ref, s32[2]{0:T(128)S(1)} %copy-done.17, bf16[16,256,256]{2,1,0:T(8,128)(2,1)S(1)} %copy-done.4, bf16[16,256,256]{2,1,0:T(8,128)(2,1)S(1)} %copy-done.4, bf16[16,256,256]{2,1,0:T(8,128)(2,1)S(1)} %copy-done.4, bf16[16,256,256]{2,1,0:T(8,128)(2,1)S(1)} %copy-done.4, ...), custom_call_target="tpu_custom_call" | custom-call | flops 1000000 | bytes 100000 | tf_op jit(solution)/shard_map/finish/pallas_call | solution.py:520
  (154 shorter events, 21.3 us)
Async XLA Ops:
  0.6 15.4 %copy-start = (bf16[256,4096]{1,0:T(8,128)(2,1)S(1)}, bf16[256,4096]{1,0:T(8,128)(2,1)}, u32[]{:S(2)}) copy-start(bf16[256,4096]{1,0:T(8,128)(2,1)} %param.11) | copy-start | bytes 6291460
  2.5 8.2 %copy-start.19 = (bf16[14336,64]{0,1:T(8,128)(2,1)S(1)}, bf16[14336,64]{0,1:T(8,128)(2,1)}, u32[]{:S(2)}) copy-start(bf16[14336,64]{0,1:T(8,128)(2,1)} %param.12) | copy-start | bytes 5505028
  3.7 18.5 %collective-permute-start.4 = (f32[64,512]{1,0:T(8,128)}, f32[64,512]{1,0:T(8,128)S(1)}, u32[]{:S(2)}, u32[]{:S(2)}) collective-permute-start(f32[64,512]{1,0:T(8,128)} %get-tuple-element.52), channel_id=1, source_target_pairs={{0,4},{2,6},{4,8},{6,10},{8,12},{10,14},{12,0},{14,2},{1,5},{3,7},... | collective-permute-start | bytes 393224 | tf_op jit(solution)/shard_map/ppermute | solution.py:548
  6.7 15.5 %collective-permute-start.5 = (f32[64,512]{1,0:T(8,128)S(1)}, f32[64,512]{1,0:T(8,128)S(1)}, u32[]{:S(2)}, u32[]{:S(2)}) collective-permute-start(f32[64,512]{1,0:T(8,128)S(1)} %get-tuple-element.54), channel_id=1, source_target_pairs={{0,8},{2,10},{4,12},{6,14},{8,0},{10,2},{12,4},{14,6},{1,9},{3,11}... | collective-permute-start | bytes 393224 | tf_op jit(solution)/shard_map/ppermute | solution.py:548
  9.3 6.8 %copy-start.23 = (bf16[4096,64]{0,1:T(8,128)(2,1)S(1)}, bf16[4096,64]{0,1:T(8,128)(2,1)}, u32[]{:S(2)}) copy-start(bf16[4096,64]{0,1:T(8,128)(2,1)} %param.13) | copy-start | bytes 1572868
  9.3 12.9 %collective-permute-start.6 = (f32[64,512]{1,0:T(8,128)S(1)}, f32[64,512]{1,0:T(8,128)S(1)}, u32[]{:S(2)}, u32[]{:S(2)}) collective-permute-start(f32[64,512]{1,0:T(8,128)S(1)} %get-tuple-element.53), channel_id=1, source_target_pairs={{0,12},{2,14},{4,0},{6,2},{8,4},{10,6},{12,8},{14,10},{1,13},{3,15... | collective-permute-start | bytes 393224 | tf_op jit(solution)/shard_map/ppermute | solution.py:548
  16.9 1.4 collective-permute-start
  19.9 9.4 %copy-start.18 = (bf16[16,4096]{1,0:T(8,128)(2,1)}, bf16[16,4096]{1,0:T(8,128)(2,1)S(1)}, u32[]{:S(2)}) copy-start(bf16[16,4096]{1,0:T(8,128)(2,1)S(1)} %convert_element_type.49.left_new_ref.right_new_ref) | copy-start | bytes 393220
  20.0 4.1 %collective-permute-start.1 = (bf16[16,1024]{1,0:T(8,128)(2,1)S(1)}, bf16[16,1024]{1,0:T(8,128)(2,1)S(1)}, u32[]{:S(2)}, u32[]{:S(2)}) collective-permute-start(bf16[16,1024]{1,0:T(8,128)(2,1)S(1)} %get-tuple-element.71), channel_id=1, source_target_pairs={{0,12},{2,14},{4,0},{6,2},{8,4},{10,6},{12,8},{14,10},{1,13},{3,15... | collective-permute-start | bytes 98312 | tf_op jit(solution)/shard_map/ppermute | solution.py:548
  20.5 5.1 %collective-permute-start.2 = (bf16[16,1024]{1,0:T(8,128)(2,1)S(1)}, bf16[16,1024]{1,0:T(8,128)(2,1)S(1)}, u32[]{:S(2)}, u32[]{:S(2)}) collective-permute-start(bf16[16,1024]{1,0:T(8,128)(2,1)S(1)} %get-tuple-element.70), channel_id=1, source_target_pairs={{0,8},{2,10},{4,12},{6,14},{8,0},{10,2},{12,4},{14,6},{1,9},{3,11}... | collective-permute-start | bytes 98312 | tf_op jit(solution)/shard_map/ppermute | solution.py:548
  22.2 5.7 %collective-permute-start.3 = (bf16[16,1024]{1,0:T(8,128)(2,1)S(1)}, bf16[16,1024]{1,0:T(8,128)(2,1)S(1)}, u32[]{:S(2)}, u32[]{:S(2)}) collective-permute-start(bf16[16,1024]{1,0:T(8,128)(2,1)S(1)} %get-tuple-element.69), channel_id=1, source_target_pairs={{0,4},{2,6},{4,8},{6,10},{8,12},{10,14},{12,0},{14,2},{1,5},{3,7},... | collective-permute-start | bytes 98312 | tf_op jit(solution)/shard_map/ppermute | solution.py:548
  29.4 7.2 %copy-start.20 = (f32[64,512]{1,0:T(8,128)S(1)}, f32[64,512]{1,0:T(8,128)}, u32[]{:S(2)}) copy-start(f32[64,512]{1,0:T(8,128)} %add_add_fusion.refs_1_) | copy-start | bytes 393220
  36.6 41.0 %collective-permute-start.7 = (bf16[256,1280]{1,0:T(8,128)(2,1)}, bf16[256,1280]{1,0:T(8,128)(2,1)S(1)}, u32[]{:S(2)}, u32[]{:S(2)}) collective-permute-start(bf16[256,1280]{1,0:T(8,128)(2,1)} %bitcast.28), channel_id=1, source_target_pairs={{0,4},{4,8},{8,12},{12,14},{14,10},{10,6},{6,2},{2,0},{1,5},{5,9},... | collective-permute-start | bytes 1966088 | tf_op jit(solution)/shard_map/ppermute | solution.py:661
  36.6 18.2 %collective-permute-start.8 = (f32[64,512]{1,0:T(8,128)S(1)}, f32[64,512]{1,0:T(8,128)S(1)}, u32[]{:S(2)}, u32[]{:S(2)}) collective-permute-start(f32[64,512]{1,0:T(8,128)S(1)} %copy-done.20), channel_id=1, source_target_pairs={{0,2},{2,0},{4,6},{6,4},{8,10},{10,8},{12,14},{14,12},{1,3},{3,1},... | collective-permute-start | bytes 393224 | tf_op jit(solution)/shard_map/ppermute | solution.py:544
  38.6 37.0 %collective-permute-start.13 = (bf16[256,1024]{1,0:T(8,128)(2,1)}, bf16[256,1024]{1,0:T(8,128)(2,1)S(1)}, u32[]{:S(2)}, u32[]{:S(2)}) collective-permute-start(bf16[256,1024]{1,0:T(8,128)(2,1)} %bitcast.33), channel_id=1, source_target_pairs={{0,2},{4,0},{8,4},{12,8},{14,12},{10,14},{6,10},{2,6},{1,3},{5,1},... | collective-permute-start | bytes 1572872 | tf_op jit(solution)/shard_map/ppermute | solution.py:662
  54.9 16.1 %copy-start.24 = (bf16[64,768]{1,0:T(8,128)(2,1)S(1)}, bf16[64,768]{1,0:T(8,128)(2,1)}, u32[]{:S(2)}) copy-start(bf16[64,768]{1,0:T(8,128)(2,1)} %broadcast_select_fusion.1.refs_0_) | copy-start | bytes 294916
  54.9 16.1 %collective-permute-start.10 = (f32[64,512]{1,0:T(8,128)S(1)}, f32[64,512]{1,0:T(8,128)S(1)}, u32[]{:S(2)}, u32[]{:S(2)}) collective-permute-start(f32[64,512]{1,0:T(8,128)S(1)} %add.308), channel_id=1, source_target_pairs={{0,8},{2,10},{4,12},{6,14},{8,0},{10,2},{12,4},{14,6},{1,9},{3,11}... | collective-permute-start | bytes 393224 | tf_op jit(solution)/shard_map/ppermute | solution.py:548
  54.9 16.1 %collective-permute-start.11 = (f32[64,512]{1,0:T(8,128)S(1)}, f32[64,512]{1,0:T(8,128)S(1)}, u32[]{:S(2)}, u32[]{:S(2)}) collective-permute-start(f32[64,512]{1,0:T(8,128)S(1)} %add.308), channel_id=1, source_target_pairs={{0,4},{2,6},{4,8},{6,10},{8,12},{10,14},{12,0},{14,2},{1,5},{3,7},... | collective-permute-start | bytes 393224 | tf_op jit(solution)/shard_map/ppermute | solution.py:548
  55.2 15.8 %collective-permute-start.9 = (f32[64,512]{1,0:T(8,128)S(1)}, f32[64,512]{1,0:T(8,128)S(1)}, u32[]{:S(2)}, u32[]{:S(2)}) collective-permute-start(f32[64,512]{1,0:T(8,128)S(1)} %add.308), channel_id=1, source_target_pairs={{0,12},{2,14},{4,0},{6,2},{8,4},{10,6},{12,8},{14,10},{1,13},{3,15... | collective-permute-start | bytes 393224 | tf_op jit(solution)/shard_map/ppermute | solution.py:548
  70.9 4.7 %collective-permute-start.12 = (bf16[64,768]{1,0:T(8,128)(2,1)S(1)}, bf16[64,768]{1,0:T(8,128)(2,1)S(1)}, u32[]{:S(2)}, u32[]{:S(2)}) collective-permute-start(bf16[64,768]{1,0:T(8,128)(2,1)S(1)} %copy-done.24), channel_id=1, source_target_pairs={{0,2},{2,0},{4,6},{6,4},{8,10},{10,8},{12,14},{14,12},{1,3},{3,1},... | collective-permute-start | bytes 294920 | tf_op jit(solution)/shard_map/ppermute | solution.py:544
  71.2 8.8 %copy-start.6 = (f32[256,512]{1,0:T(8,128)}, f32[256,512]{1,0:T(8,128)S(1)}, u32[]{:S(2)}) copy-start(f32[256,512]{1,0:T(8,128)S(1)} %pad_maximum_fusion.refs_1_.mine_ref) | copy-start | bytes 1572868
  77.5 43.1 %collective-permute-start.17 = (bf16[256,2304]{1,0:T(8,128)(2,1)S(1)}, bf16[256,2304]{1,0:T(8,128)(2,1)S(1)}, u32[]{:S(2)}, u32[]{:S(2)}) collective-permute-start(bf16[256,2304]{1,0:T(8,128)(2,1)S(1)} %add_terms.7.refs_1_), channel_id=1, source_target_pairs={{0,2},{4,0},{8,4},{12,8},{14,12},{10,14},{6,10},{2,6},{1,3},{5,1},... | collective-permute-start | bytes 3538952 | tf_op jit(solution)/shard_map/ppermute | solution.py:674
  78.5 47.5 %collective-permute-start.14 = (bf16[256,2304]{1,0:T(8,128)(2,1)S(1)}, bf16[256,2304]{1,0:T(8,128)(2,1)S(1)}, u32[]{:S(2)}, u32[]{:S(2)}) collective-permute-start(bf16[256,2304]{1,0:T(8,128)(2,1)S(1)} %add_terms.6.refs_0_), channel_id=1, source_target_pairs={{0,4},{4,8},{8,12},{12,14},{14,10},{10,6},{6,2},{2,0},{1,5},{5,9},... | collective-permute-start | bytes 3538952 | tf_op jit(solution)/shard_map/ppermute | solution.py:673
  80.0 27.0 %collective-permute-start.15 = (f32[256,512]{1,0:T(8,128)S(1)}, f32[256,512]{1,0:T(8,128)S(1)}, u32[]{:S(2)}, u32[]{:S(2)}) collective-permute-start(f32[256,512]{1,0:T(8,128)S(1)} %pad_maximum_fusion.refs_1_.mine_ref), channel_id=1, source_target_pairs={{0,1},{1,0},{2,3},{3,2},{4,5},{5,4},{6,7},{7,6},{8,9},{9,8},{10,11... | collective-permute-start | bytes 1572872 | tf_op jit(solution)/shard_map/ppermute | solution.py:657
  124.2 7.1 %slice-start = ((bf16[64,768]{1,0:T(8,128)(2,1)}), bf16[64,256]{1,0:T(8,128)(2,1)S(1)}, s32[]{:S(2)}) async-start(bf16[64,768]{1,0:T(8,128)(2,1)} %copy-done.15), calls=%async_computation | async-start | bytes 65536 | tf_op jit(solution)/shard_map/slice | solution.py:659
  125.5 32.9 %collective-permute-start.19 = (bf16[256,2304]{1,0:T(8,128)(2,1)}, bf16[256,2304]{1,0:T(8,128)(2,1)}, u32[]{:S(2)}, u32[]{:S(2)}) collective-permute-start(bf16[256,2304]{1,0:T(8,128)(2,1)} %add_terms.9.refs_9_), channel_id=1, source_target_pairs={{0,2},{4,0},{8,4},{12,8},{14,12},{10,14},{6,10},{2,6},{1,3},{5,1},... | collective-permute-start | bytes 3538952 | tf_op jit(solution)/shard_map/ppermute | solution.py:674
  128.6 35.0 %collective-permute-start.16 = (bf16[256,2304]{1,0:T(8,128)(2,1)S(1)}, bf16[256,2304]{1,0:T(8,128)(2,1)}, u32[]{:S(2)}, u32[]{:S(2)}) collective-permute-start(bf16[256,2304]{1,0:T(8,128)(2,1)S(1)} %add_terms.8.refs_8_), channel_id=1, source_target_pairs={{0,4},{4,8},{8,12},{12,14},{14,10},{10,6},{6,2},{2,0},{1,5},{5,9},... | collective-permute-start | bytes 3538952 | tf_op jit(solution)/shard_map/ppermute | solution.py:673
  138.8 28.7 %collective-permute-start.28 = (bf16[2,128,256]{2,1,0:T(8,128)(2,1)}, bf16[2,128,256]{2,1,0:T(8,128)(2,1)S(1)}, u32[]{:S(2)}, u32[]{:S(2)}) collective-permute-start(bf16[2,128,256]{2,1,0:T(8,128)(2,1)} %get-tuple-element.39), channel_id=1, source_target_pairs={{0,4},{2,6},{4,8},{6,10},{8,12},{10,14},{12,0},{14,2},{1,5},{3,7},... | collective-permute-start | bytes 393224 | tf_op jit(solution)/shard_map/ppermute | solution.py:548
  139.6 28.0 %collective-permute-start.29 = (bf16[2,128,256]{2,1,0:T(8,128)(2,1)}, bf16[2,128,256]{2,1,0:T(8,128)(2,1)S(1)}, u32[]{:S(2)}, u32[]{:S(2)}) collective-permute-start(bf16[2,128,256]{2,1,0:T(8,128)(2,1)} %get-tuple-element.40), channel_id=1, source_target_pairs={{0,8},{2,10},{4,12},{6,14},{8,0},{10,2},{12,4},{14,6},{1,9},{3,11}... | collective-permute-start | bytes 393224 | tf_op jit(solution)/shard_map/ppermute | solution.py:548
  140.6 29.0 %collective-permute-start.30 = (bf16[2,128,256]{2,1,0:T(8,128)(2,1)}, bf16[2,128,256]{2,1,0:T(8,128)(2,1)S(1)}, u32[]{:S(2)}, u32[]{:S(2)}) collective-permute-start(bf16[2,128,256]{2,1,0:T(8,128)(2,1)} %get-tuple-element.41), channel_id=1, source_target_pairs={{0,12},{2,14},{4,0},{6,2},{8,4},{10,6},{12,8},{14,10},{1,13},{3,15... | collective-permute-start | bytes 393224 | tf_op jit(solution)/shard_map/ppermute | solution.py:548
  163.5 18.0 %collective-permute-start.20 = (bf16[256,1280]{1,0:T(8,128)(2,1)S(1)}, bf16[256,1280]{1,0:T(8,128)(2,1)S(1)}, u32[]{:S(2)}, u32[]{:S(2)}) collective-permute-start(bf16[256,1280]{1,0:T(8,128)(2,1)S(1)} %get-tuple-element.29), channel_id=1, source_target_pairs={{0,2},{4,0},{8,4},{12,8},{14,12},{10,14},{6,10},{2,6},{1,3},{5,1},... | collective-permute-start | bytes 1966088 | tf_op jit(solution)/shard_map/ppermute | solution.py:682
  165.1 17.7 %collective-permute-start.18 = (bf16[256,1280]{1,0:T(8,128)(2,1)S(1)}, bf16[256,1280]{1,0:T(8,128)(2,1)S(1)}, u32[]{:S(2)}, u32[]{:S(2)}) collective-permute-start(bf16[256,1280]{1,0:T(8,128)(2,1)S(1)} %get-tuple-element.28), channel_id=1, source_target_pairs={{0,4},{4,8},{8,12},{12,14},{14,10},{10,6},{6,2},{2,0},{1,5},{5,9},... | collective-permute-start | bytes 1966088 | tf_op jit(solution)/shard_map/ppermute | solution.py:681
  167.5 25.0 %collective-permute-start.22 = (bf16[256,1024]{1,0:T(8,128)(2,1)S(1)}, bf16[256,1024]{1,0:T(8,128)(2,1)S(1)}, u32[]{:S(2)}, u32[]{:S(2)}) collective-permute-start(bf16[256,1024]{1,0:T(8,128)(2,1)S(1)} %get-tuple-element.32), channel_id=1, source_target_pairs={{0,2},{4,0},{8,4},{12,8},{14,12},{10,14},{6,10},{2,6},{1,3},{5,1},... | collective-permute-start | bytes 1572872 | tf_op jit(solution)/shard_map/ppermute | solution.py:682
  167.6 26.3 %collective-permute-start.21 = (bf16[256,1024]{1,0:T(8,128)(2,1)S(1)}, bf16[256,1024]{1,0:T(8,128)(2,1)S(1)}, u32[]{:S(2)}, u32[]{:S(2)}) collective-permute-start(bf16[256,1024]{1,0:T(8,128)(2,1)S(1)} %get-tuple-element.31), channel_id=1, source_target_pairs={{0,4},{4,8},{8,12},{12,14},{14,10},{10,6},{6,2},{2,0},{1,5},{5,9},... | collective-permute-start | bytes 1572872 | tf_op jit(solution)/shard_map/ppermute | solution.py:681
  183.2 26.3 %collective-permute-start.23 = (bf16[2,256,256]{2,1,0:T(8,128)(2,1)S(1)}, bf16[2,256,256]{2,1,0:T(8,128)(2,1)S(1)}, u32[]{:S(2)}, u32[]{:S(2)}) collective-permute-start(bf16[2,256,256]{2,1,0:T(8,128)(2,1)S(1)} %get-tuple-element.34), channel_id=1, source_target_pairs={{0,12},{4,14},{8,10},{12,6},{14,2},{10,0},{6,4},{2,8},{1,13},{5,15... | collective-permute-start | bytes 786440 | tf_op jit(solution)/shard_map/ppermute | solution.py:699
  186.4 26.1 %collective-permute-start.24 = (bf16[2,256,256]{2,1,0:T(8,128)(2,1)S(1)}, bf16[2,256,256]{2,1,0:T(8,128)(2,1)S(1)}, u32[]{:S(2)}, u32[]{:S(2)}) collective-permute-start(bf16[2,256,256]{2,1,0:T(8,128)(2,1)S(1)} %get-tuple-element.35), channel_id=1, source_target_pairs={{0,6},{4,2},{8,0},{12,4},{14,8},{10,12},{6,14},{2,10},{1,7},{5,3},... | collective-permute-start | bytes 786440 | tf_op jit(solution)/shard_map/ppermute | solution.py:699
  187.0 19.6 %collective-permute-start.31 = (bf16[128,256]{1,0:T(8,128)(2,1)S(1)}, bf16[128,256]{1,0:T(8,128)(2,1)S(1)}, u32[]{:S(2)}, u32[]{:S(2)}) collective-permute-start(bf16[128,256]{1,0:T(8,128)(2,1)S(1)} %fusion.11), channel_id=1, source_target_pairs={{0,2},{2,0},{4,6},{6,4},{8,10},{10,8},{12,14},{14,12},{1,3},{3,1},... | collective-permute-start | bytes 196616 | tf_op jit(solution)/shard_map/ppermute | solution.py:544
  194.2 18.4 %copy-start.11 = (f32[512,128]{1,0:T(8,128)S(1)}, f32[512,128]{1,0:T(8,128)}, u32[]{:S(2)}) copy-start(f32[512,128]{1,0:T(8,128)} %get-tuple-element.26.refs_1_.solved_ref) | copy-start | bytes 786436
  194.2 18.4 %copy-start.16 = (f32[128,128]{1,0:T(8,128)S(1)}, f32[128,128]{1,0:T(8,128)}, u32[]{:S(2)}) copy-start(f32[128,128]{1,0:T(8,128)} %get-tuple-element.38.first_ref) | copy-start | bytes 196612
  194.2 18.4 %copy-start.17 = (s32[2]{0:T(128)S(1)}, s32[2]{0:T(128)}, u32[]{:S(2)}) copy-start(s32[2]{0:T(128)} %pad_add_fusion.1.place_ref) | copy-start | bytes 28
  194.2 29.4 %collective-permute-start.25 = (bf16[2,256,256]{2,1,0:T(8,128)(2,1)S(1)}, bf16[2,256,256]{2,1,0:T(8,128)(2,1)S(1)}, u32[]{:S(2)}, u32[]{:S(2)}) collective-permute-start(bf16[2,256,256]{2,1,0:T(8,128)(2,1)S(1)} %get-tuple-element.36), channel_id=1, source_target_pairs={{0,2},{4,0},{8,4},{12,8},{14,12},{10,14},{6,10},{2,6},{1,3},{5,1},... | collective-permute-start | bytes 786440 | tf_op jit(solution)/shard_map/ppermute | solution.py:699
  194.3 15.2 %collective-permute-start.26 = (bf16[1,256,256]{2,1,0:T(8,128)(2,1)S(1)}, bf16[1,256,256]{2,1,0:T(8,128)(2,1)S(1)}, u32[]{:S(2)}, u32[]{:S(2)}) collective-permute-start(bf16[1,256,256]{2,1,0:T(8,128)(2,1)S(1)} %get-tuple-element.37), channel_id=1, source_target_pairs={{0,14},{4,10},{8,6},{12,2},{14,0},{10,4},{6,8},{2,12},{1,15},{5,11... | collective-permute-start | bytes 393224 | tf_op jit(solution)/shard_map/ppermute | solution.py:699
  213.8 11.5 %collective-permute-start.32 = (f32[32,128]{1,0:T(8,128)S(1)}, f32[32,128]{1,0:T(8,128)S(1)}, u32[]{:S(2)}, u32[]{:S(2)}) collective-permute-start(f32[32,128]{1,0:T(8,128)S(1)} %get-tuple-element.43), channel_id=1, source_target_pairs={{0,4},{2,6},{4,8},{6,10},{8,12},{10,14},{12,0},{14,2},{1,5},{3,7},... | collective-permute-start | bytes 49160 | tf_op jit(solution)/shard_map/ppermute | solution.py:548
  215.1 10.2 %collective-permute-start.33 = (f32[32,128]{1,0:T(8,128)S(1)}, f32[32,128]{1,0:T(8,128)S(1)}, u32[]{:S(2)}, u32[]{:S(2)}) collective-permute-start(f32[32,128]{1,0:T(8,128)S(1)} %get-tuple-element.44), channel_id=1, source_target_pairs={{0,8},{2,10},{4,12},{6,14},{8,0},{10,2},{12,4},{14,6},{1,9},{3,11}... | collective-permute-start | bytes 49160 | tf_op jit(solution)/shard_map/ppermute | solution.py:548
  220.7 4.7 %collective-permute-start.34 = (f32[32,128]{1,0:T(8,128)S(1)}, f32[32,128]{1,0:T(8,128)S(1)}, u32[]{:S(2)}, u32[]{:S(2)}) collective-permute-start(f32[32,128]{1,0:T(8,128)S(1)} %get-tuple-element.45), channel_id=1, source_target_pairs={{0,12},{2,14},{4,0},{6,2},{8,4},{10,6},{12,8},{14,10},{1,13},{3,15... | collective-permute-start | bytes 49160 | tf_op jit(solution)/shard_map/ppermute | solution.py:548
  225.3 5.8 %collective-permute-start.27 = (bf16[8,256,256]{2,1,0:T(8,128)(2,1)}, bf16[8,256,256]{2,1,0:T(8,128)(2,1)S(1)}, u32[]{:S(2)}, u32[]{:S(2)}) collective-permute-start(bf16[8,256,256]{2,1,0:T(8,128)(2,1)} %for_sibling.1), channel_id=1, source_target_pairs={{0,1},{1,0},{2,3},{3,2},{4,5},{5,4},{6,7},{7,6},{8,9},{9,8},{10,11... | collective-permute-start | bytes 3145736 | tf_op jit(solution)/shard_map/ppermute | solution.py:713
  225.4 3.7 %collective-permute-start.35 = (f32[16,128]{1,0:T(8,128)S(1)}, f32[16,128]{1,0:T(8,128)S(1)}, u32[]{:S(2)}, u32[]{:S(2)}) collective-permute-start(f32[16,128]{1,0:T(8,128)S(1)} %constant_dynamic-slice_fusion), channel_id=1, source_target_pairs={{0,2},{2,0},{4,6},{6,4},{8,10},{10,8},{12,14},{14,12},{1,3},{3,1},... | collective-permute-start | bytes 24584 | tf_op jit(solution)/shard_map/ppermute | solution.py:544
  229.1 1.2 collective-permute-start.36
  (18 other events, 38.1 us)
